TPU v7x, 32 devices: a whole 2x2x4 slice. The times are simulated.
32 devices in a mesh: seq: 8 (over z, y), grp: 4 (over x, core).
Axes of the slice: x: 2, y: 2, z: 4, core: 2. Of those that a mesh axis runs over, the one named last changes fastest.
Arguments:
- frames_in: bfloat16 [128, 256, 1024], P(('grp', 'seq')), may hold values from -6 to 6
- action_codes: int32 [128], P(('grp', 'seq')), may hold values from 0 to 7
- cotangent: bfloat16 [128, 256, 1024], P(('grp', 'seq')), may hold values from -40 to 40, as said below
- attn_master: float32 [2, 1024, 4096], P(None, 'seq'), as said below
- attn_first: float32 [2, 1024, 4096], P(None, 'seq'), may hold values from -0.0014648438 to 0.0014648438
- attn_second: float32 [2, 1024, 4096], P(None, 'seq'), may hold values from 6e-08 to 2.4e-07
- ffn_master: float32 [2, 1024, 4096], P(None, 'seq'), may hold values from -0.1875 to 0.1875
- ffn_first: float32 [2, 1024, 4096], P(None, 'seq'), may hold values from -0.0014648438 to 0.0014648438
- ffn_second: float32 [2, 1024, 4096], P(None, 'seq'), may hold values from 6e-08 to 2.4e-07
- small_master: float32 [11, 1024], P(None, 'seq'), as said below
- small_first: float32 [11, 1024], P(None, 'seq'), may hold values from -0.0014648438 to 0.0014648438
- small_second: float32 [11, 1024], P(None, 'seq'), may hold values from 6e-08 to 2.4e-07
Outputs:
- block_out: bfloat16 [128, 256, 1024], P(('grp', 'seq'))
- input_grad: bfloat16 [128, 256, 1024], P(('grp', 'seq'))
- grad_norm: float32 [], replicated
- attn_updated: float32 [2, 1024, 4096], P(None, 'seq')
- attn_first_new: float32 [2, 1024, 4096], P(None, 'seq')
- attn_second_new: float32 [2, 1024, 4096], P(None, 'seq')
- ffn_updated: float32 [2, 1024, 4096], P(None, 'seq')
- ffn_first_new: float32 [2, 1024, 4096], P(None, 'seq')
- ffn_second_new: float32 [2, 1024, 4096], P(None, 'seq')
- small_updated: float32 [11, 1024], P(None, 'seq')
- small_first_new: float32 [11, 1024], P(None, 'seq')
- small_second_new: float32 [11, 1024], P(None, 'seq')
Inputs may be any that keep to these rules, and one draw needn't show every extreme that they name: `attn_master`: attention weights of order 1024 to the power -1/2, output columns larger. `small_master`: gains positive, between 0.3 and 3.5, table rows of order one half. `cotangent`: entries of order one, their spread varying by feature within a factor of six.
All inputs are finite; a program needn't handle non-finite values.
Results may differ from a plain program's by a relative error of at most 0.02.
Values may be sent and summed in bfloat16 or wider, within the bound.
No kernel may reach another device: no remote copies, remote signals or barrier semaphores. Data moves between devices by JAX's collectives and lax.ppermute only.
A program may use at most 384 MiB of HBM per device.

v0:
```python
import jax
import jax.numpy as jnp
from jax import lax
from jax.sharding import PartitionSpec as P

H = 16
HD = 64
FPV = 16
CODES = 8
STEP = 5


eps_norm = 1e-05
beta_first = 0.5
beta_second = 0.5
rate_matrix = 0.02
rate_small = 0.3
decay_rate = 0.1
eps_adam = 1e-08
masked_score = -1000000000.0


def layer_norm(values, gain_vec):
    centre = values - jnp.mean(values, axis=-1, keepdims=True)
    spread = jnp.mean(centre * centre, axis=-1, keepdims=True)
    return centre * lax.rsqrt(spread + eps_norm) * gain_vec


def project(left_side, right_side):
    return jnp.einsum("...d,de->...e", left_side, right_side, preferred_element_type=jnp.float32)


def project_back(left_side, right_side):
    return jnp.einsum("...e,de->...d", left_side, right_side, preferred_element_type=jnp.float32)


def weight_grad(left_side, right_side):
    left_rows = left_side.reshape(-1, left_side.shape[-1])
    right_rows = right_side.reshape(-1, right_side.shape[-1])
    return jnp.einsum("nd,ne->de", left_rows, right_rows, preferred_element_type=jnp.float32)


def softmax_back(attn_probs, probs_grad):
    return attn_probs * (probs_grad - jnp.sum(probs_grad * attn_probs, axis=-1, keepdims=True))


def adamw(weight, moment_one, moment_two, gradient, step_rate, decay_coef):
    first_new = beta_first * moment_one + (1.0 - beta_first) * gradient
    second_new = beta_second * moment_two + (1.0 - beta_second) * gradient * gradient
    fix_first = 1.0 - beta_first**STEP
    fix_second = 1.0 - beta_second**STEP
    update = first_new / fix_first / (jnp.sqrt(second_new / fix_second) + eps_adam)
    return (weight - step_rate * (update + decay_coef * weight), first_new, second_new)


def column_piece(full_array, grp_place, columns):
    return lax.dynamic_slice_in_dim(full_array, grp_place * columns, columns, 2)


def shards(
    frames_in,
    action_codes,
    cotangent,
    attn_master,
    attn_first,
    attn_second,
    ffn_master,
    ffn_first,
    ffn_second,
    small_master,
    small_first,
    small_second,
):
    attn_w, ffn_w, small_w = (
        lax.all_gather(attn_master.astype(jnp.bfloat16), "seq", axis=1, tiled=True),
        lax.all_gather(ffn_master.astype(jnp.bfloat16), "seq", axis=1, tiled=True),
        lax.all_gather(small_master.astype(jnp.bfloat16), "seq", axis=1, tiled=True),
    )
    frames, positions, model_width = frames_in.shape
    triple = 3 * model_width
    score_scale = HD ** (-0.5)
    gains = small_w[:3].astype(jnp.float32)
    onehot = (action_codes[:, None] == jnp.arange(CODES)[None, :]).astype(jnp.bfloat16)
    code_shift = jnp.dot(onehot, small_w[3:], preferred_element_type=jnp.float32)
    resid_zero = frames_in.astype(jnp.float32) + code_shift[:, None, :]
    normed_one = layer_norm(resid_zero, gains[0]).astype(jnp.bfloat16)
    packed_s = (
        project(normed_one, attn_w[0, :, :triple])
        .astype(jnp.bfloat16)
        .reshape(frames, positions, 3, H, HD)
    )
    query_s, key_s, value_s = (packed_s[:, :, 0], packed_s[:, :, 1], packed_s[:, :, 2])
    scores_s = (
        jnp.einsum("fqhc,fkhc->fhqk", query_s, key_s, preferred_element_type=jnp.float32)
        * score_scale
    )
    probs_s = jax.nn.softmax(scores_s, axis=-1)
    lowp_s = probs_s.astype(jnp.bfloat16)
    heads_s = (
        jnp.einsum("fhqk,fkhc->fqhc", lowp_s, value_s, preferred_element_type=jnp.float32)
        .astype(jnp.bfloat16)
        .reshape(frames, positions, model_width)
    )
    resid_one = resid_zero + project(heads_s, attn_w[0, :, triple:])
    normed_two = layer_norm(resid_one, gains[1]).astype(jnp.bfloat16)
    normed_pos = lax.all_to_all(normed_two, "seq", split_axis=1, concat_axis=0, tiled=True)
    group, local_pos = (normed_pos.shape[0], normed_pos.shape[1])
    videos = group // FPV
    packed_t = (
        project(normed_pos, attn_w[1, :, :triple])
        .astype(jnp.bfloat16)
        .reshape(videos, FPV, local_pos, 3, H, HD)
    )
    query_t, key_t, value_t = (packed_t[:, :, :, 0], packed_t[:, :, :, 1], packed_t[:, :, :, 2])
    causal = jnp.arange(FPV)[:, None] >= jnp.arange(FPV)[None, :]
    scores_t = (
        jnp.einsum("vtphc,vuphc->vphtu", query_t, key_t, preferred_element_type=jnp.float32)
        * score_scale
    )
    probs_t = jax.nn.softmax(jnp.where(causal, scores_t, masked_score), axis=-1)
    lowp_t = probs_t.astype(jnp.bfloat16)
    heads_pos = (
        jnp.einsum("vphtu,vuphc->vtphc", lowp_t, value_t, preferred_element_type=jnp.float32)
        .astype(jnp.bfloat16)
        .reshape(group, local_pos, model_width)
    )
    heads_t = lax.all_to_all(heads_pos, "seq", split_axis=0, concat_axis=1, tiled=True)
    resid_two = resid_one + project(heads_t, attn_w[1, :, triple:])
    normed_three = layer_norm(resid_two, gains[2]).astype(jnp.bfloat16)
    ffn_pre = project(normed_three, ffn_w[0])
    ffn_act, gelu_pull = jax.vjp(jax.nn.gelu, ffn_pre)
    act_low = ffn_act.astype(jnp.bfloat16)
    block_out = (resid_two + project_back(act_low, ffn_w[1])).astype(jnp.bfloat16)
    out_grad = cotangent.astype(jnp.float32)
    down_grad = weight_grad(cotangent, act_low)
    pre_grad = gelu_pull(project(cotangent, ffn_w[1]))[0].astype(jnp.bfloat16)
    up_grad = weight_grad(normed_three, pre_grad)
    _, norm_pull = jax.vjp(layer_norm, resid_two, gains[2])
    back_three, gain_three = norm_pull(project_back(pre_grad, ffn_w[0]))
    grad_two = out_grad + back_three
    branch_t = grad_two.astype(jnp.bfloat16)
    out_t_grad = weight_grad(heads_t, branch_t)
    heads_t_grad = project_back(branch_t, attn_w[1, :, triple:]).astype(jnp.bfloat16)
    heads_pos_grad = lax.all_to_all(
        heads_t_grad, "seq", split_axis=1, concat_axis=0, tiled=True
    ).reshape(videos, FPV, local_pos, H, HD)
    probs_t_grad = jnp.einsum(
        "vtphc,vuphc->vphtu", heads_pos_grad, value_t, preferred_element_type=jnp.float32
    )
    value_t_grad = jnp.einsum(
        "vphtu,vtphc->vuphc", lowp_t, heads_pos_grad, preferred_element_type=jnp.float32
    )
    score_t_grad = softmax_back(probs_t, probs_t_grad).astype(jnp.bfloat16)
    query_t_grad = (
        jnp.einsum("vphtu,vuphc->vtphc", score_t_grad, key_t, preferred_element_type=jnp.float32)
        * score_scale
    )
    key_t_grad = (
        jnp.einsum("vphtu,vtphc->vuphc", score_t_grad, query_t, preferred_element_type=jnp.float32)
        * score_scale
    )
    packed_t_grad = (
        jnp.stack([query_t_grad, key_t_grad, value_t_grad], axis=3)
        .astype(jnp.bfloat16)
        .reshape(group, local_pos, triple)
    )
    qkv_t_grad = weight_grad(normed_pos, packed_t_grad)
    normed_two_grad = lax.all_to_all(
        project_back(packed_t_grad, attn_w[1, :, :triple]).astype(jnp.bfloat16),
        "seq",
        split_axis=0,
        concat_axis=1,
        tiled=True,
    ).astype(jnp.float32)
    _, norm_pull = jax.vjp(layer_norm, resid_one, gains[1])
    back_two, gain_two = norm_pull(normed_two_grad)
    grad_one = grad_two + back_two
    branch_s = grad_one.astype(jnp.bfloat16)
    out_s_grad = weight_grad(heads_s, branch_s)
    heads_s_grad = (
        project_back(branch_s, attn_w[0, :, triple:])
        .astype(jnp.bfloat16)
        .reshape(frames, positions, H, HD)
    )
    probs_s_grad = jnp.einsum(
        "fqhc,fkhc->fhqk", heads_s_grad, value_s, preferred_element_type=jnp.float32
    )
    value_s_grad = jnp.einsum(
        "fhqk,fqhc->fkhc", lowp_s, heads_s_grad, preferred_element_type=jnp.float32
    )
    score_s_grad = softmax_back(probs_s, probs_s_grad).astype(jnp.bfloat16)
    query_s_grad = (
        jnp.einsum("fhqk,fkhc->fqhc", score_s_grad, key_s, preferred_element_type=jnp.float32)
        * score_scale
    )
    key_s_grad = (
        jnp.einsum("fhqk,fqhc->fkhc", score_s_grad, query_s, preferred_element_type=jnp.float32)
        * score_scale
    )
    packed_s_grad = (
        jnp.stack([query_s_grad, key_s_grad, value_s_grad], axis=2)
        .astype(jnp.bfloat16)
        .reshape(frames, positions, triple)
    )
    qkv_s_grad = weight_grad(normed_one, packed_s_grad)
    _, norm_pull = jax.vjp(layer_norm, resid_zero, gains[0])
    back_one, gain_one = norm_pull(project_back(packed_s_grad, attn_w[0, :, :triple]))
    grad_zero = grad_one + back_one
    input_grad = grad_zero.astype(jnp.bfloat16)
    table_grad = jnp.dot(
        onehot.astype(jnp.float32).T, jnp.sum(grad_zero, axis=1), precision=lax.Precision.HIGHEST
    )
    grad_attn = jnp.stack(
        [
            jnp.concatenate([qkv_s_grad, out_s_grad], axis=1),
            jnp.concatenate([qkv_t_grad, out_t_grad], axis=1),
        ]
    )
    grad_ffn = jnp.stack([up_grad, down_grad])
    grad_small = jnp.concatenate([jnp.stack([gain_one, gain_two, gain_three]), table_grad], axis=0)
    small_decay = jnp.where(jnp.arange(3 + CODES)[:, None] >= 3, decay_rate, 0.0)
    sum_attn, sum_ffn, sum_small = (
        lax.psum_scatter(grad_attn, "seq", scatter_dimension=1, tiled=True),
        lax.psum_scatter(grad_ffn, "seq", scatter_dimension=1, tiled=True),
        lax.psum_scatter(grad_small, "seq", scatter_dimension=1, tiled=True),
    )
    quarter_attn, quarter_ffn = (
        lax.psum_scatter(
            sum_attn.astype(jnp.bfloat16), "grp", scatter_dimension=2, tiled=True
        ).astype(jnp.float32),
        lax.psum_scatter(
            sum_ffn.astype(jnp.bfloat16), "grp", scatter_dimension=2, tiled=True
        ).astype(jnp.float32),
    )
    sum_small = lax.psum(sum_small, "grp")
    local_squares = (
        jnp.sum(quarter_attn * quarter_attn)
        + jnp.sum(quarter_ffn * quarter_ffn)
        + jnp.sum(sum_small * sum_small) / lax.axis_size("grp")
    )
    total_squares = lax.psum(local_squares, ("seq", "grp"))
    grad_norm = jnp.sqrt(total_squares)
    clip_factor = 1.0 / jnp.maximum(grad_norm, 1.0)
    grp_place = lax.axis_index("grp")
    attn_cols = quarter_attn.shape[2]
    ffn_cols = quarter_ffn.shape[2]
    attn_part = adamw(
        column_piece(attn_master, grp_place, attn_cols),
        column_piece(attn_first, grp_place, attn_cols),
        column_piece(attn_second, grp_place, attn_cols),
        quarter_attn * clip_factor,
        rate_matrix,
        decay_rate,
    )
    ffn_part = adamw(
        column_piece(ffn_master, grp_place, ffn_cols),
        column_piece(ffn_first, grp_place, ffn_cols),
        column_piece(ffn_second, grp_place, ffn_cols),
        quarter_ffn * clip_factor,
        rate_matrix,
        decay_rate,
    )
    gathered = (
        lax.all_gather(attn_part[0].astype(jnp.bfloat16), "grp", axis=2, tiled=True).astype(
            jnp.float32
        ),
        lax.all_gather(attn_part[1].astype(jnp.bfloat16), "grp", axis=2, tiled=True).astype(
            jnp.float32
        ),
        lax.all_gather(attn_part[2].astype(jnp.bfloat16), "grp", axis=2, tiled=True).astype(
            jnp.float32
        ),
        lax.all_gather(ffn_part[0].astype(jnp.bfloat16), "grp", axis=2, tiled=True).astype(
            jnp.float32
        ),
        lax.all_gather(ffn_part[1].astype(jnp.bfloat16), "grp", axis=2, tiled=True).astype(
            jnp.float32
        ),
        lax.all_gather(ffn_part[2].astype(jnp.bfloat16), "grp", axis=2, tiled=True).astype(
            jnp.float32
        ),
    )
    attn_new = gathered[:3]
    ffn_new = gathered[3:]
    small_new = adamw(
        small_master, small_first, small_second, sum_small * clip_factor, rate_small, small_decay
    )
    return (
        block_out,
        input_grad,
        grad_norm,
        attn_new[0],
        attn_new[1],
        attn_new[2],
        ffn_new[0],
        ffn_new[1],
        ffn_new[2],
        small_new[0],
        small_new[1],
        small_new[2],
    )


def solution(mesh):
    placed = (
        P(("grp", "seq"), None, None),
        P(("grp", "seq")),
        P(("grp", "seq"), None, None),
        P(None, "seq", None),
        P(None, "seq", None),
        P(None, "seq", None),
        P(None, "seq", None),
        P(None, "seq", None),
        P(None, "seq", None),
        P(None, "seq"),
        P(None, "seq"),
        P(None, "seq"),
    )
    return jax.shard_map(
        shards,
        mesh=mesh,
        in_specs=placed,
        out_specs=(
            P(("grp", "seq"), None, None),
            P(("grp", "seq"), None, None),
            P(),
            P(None, "seq", None),
            P(None, "seq", None),
            P(None, "seq", None),
            P(None, "seq", None),
            P(None, "seq", None),
            P(None, "seq", None),
            P(None, "seq"),
            P(None, "seq"),
            P(None, "seq"),
        ),
        check_vma=False,
    )
```

profile of v0, /device:TPU:0, one launch (start us, length us, event | category | flops | bytes accessed | tf_op | source)
XLA Modules:
  0.0 2157.0 jit_solution(13840560140288135245)
XLA Ops:
  15.1 28.2 %all_gather.27 = bf16[11,1024]{1,0:T(8,128)(2,1)S(1)} all-gather(bf16[11,128]{1,0:T(8,128)(2,1)S(1)} %convert_element_type.189), channel_id=1, replica_groups=mesh['seq'=8,'grp'=4] {'seq'}, dimensions={1}, use_global_device_ids=true | all-gather | bytes 25344 | tf_op jit(solution)/shard_map/all_gather | solution.py:77
  48.2 193.6 %all-gather.9.cloned.1.call-done = bf16[2,1024,4096]{2,1,0:T(8,128)(2,1)} async-done(((bf16[2,128,4096]{2,1,0:T(8,128)(2,1)}), bf16[2,1024,4096]{2,1,0:T(8,128)(2,1)}) %all-gather.9.cloned.1.call-update) | async-done | bytes 16777232 | tf_op jit(solution)/shard_map/all_gather | solution.py:75
  241.8 11.1 convolution_convert_fusion.1
  253.0 8.8 copy.148
  261.7 10.3 fusion.54
  272.1 19.5 fusion.86
  291.6 8.1 fusion.47
  299.8 5.0 fusion.87
  313.5 90.0 %all-to-all-done = bf16[4,256,1024]{2,0,1:T(4,128)(2,1)S(1)} async-done(((bf16[4,256,1024]{2,0,1:T(4,128)(2,1)}), bf16[4,256,1024]{2,0,1:T(4,128)(2,1)S(1)}, u32[]{:S(2)}, u32[]{:S(2)}) %all-to-all-start) | async-done | bytes 2097184 | tf_op jit(solution)/shard_map/all_to_all | solution.py:106
  405.7 11.4 convolution_convert_fusion
  417.1 16.0 reshape.206
  433.1 7.7 fusion.84
  442.8 8.2 fusion.37
  451.1 10.3 fusion.88
  461.4 7.6 convert_bitcast_fusion.1
  472.1 5.5 reshape.207
  477.6 72.5 %all_to_all.60 = bf16[32,32,1024]{2,1,0:T(8,128)(2,1)S(1)} all-to-all(bf16[32,32,1024]{2,1,0:T(8,128)(2,1)S(1)} %reshape.207), channel_id=1, replica_groups=mesh['seq'=8,'grp'=4] {'seq'}, dimensions={0} | all-to-all | bytes 4194304 | tf_op jit(solution)/shard_map/all_to_all | solution.py:127
  550.3 4.8 fusion.89
  557.8 16.6 fusion.14
  574.4 16.0 convolution_bitcast_fusion
  590.4 22.9 %fusion.8 = bf16[4,256,4096]{2,1,0:T(8,128)(2,1)} fusion(f32[4,256,4096]{2,1,0:T(8,128)} %fusion.14, bf16[4,256,1024]{2,1,0:T(8,128)(2,1)S(1)} %copy-done.18, bf16[2,1024,4096]{2,1,0:T(8,128)(2,1)} %all-gather.11.cloned.1.call-done), kind=kOutput, calls=%fused_computation.12 | convolution fusion | flops 8673820672 | bytes 35651584 | tf_op jit(solution)/shard_map/...d,de->...e/dot_general | solution.py:30
  613.4 15.5 convolution_bitcast_fusion.1
  628.8 23.2 %pad_maximum_fusion.1 = f32[2,1024,4096]{2,1,0:T(8,128)} fusion(f32[1,1024,4096]{2,1,0:T(8,128)} %convolution_bitcast_fusion, f32[1,1024,4096]{2,1,0:T(8,128)} %convolution_bitcast_fusion.1), kind=kLoop, calls=%fused_computation.3 | loop fusion | flops 8388608 | bytes 67108864 | tf_op jit(solution)/shard_map/stack | solution.py:219
  652.0 16.4 multiply_reduce_fusion.3
  671.8 4.7 convolution_convert_fusion.3
  678.2 100.3 %all_to_all.61 = bf16[4,256,1024]{2,0,1:T(4,128)(2,1)S(1)} all-to-all(bf16[4,256,1024]{2,0,1:T(4,128)(2,1)S(1)} %copy.163), channel_id=1, replica_groups=mesh['seq'=8,'grp'=4] {'seq'}, dimensions={1} | all-to-all | bytes 4194304 | tf_op jit(solution)/shard_map/all_to_all | solution.py:144
  783.2 15.4 multiply_reduce_fusion.2
  798.6 7.5 multiply_convert_fusion.4
  812.6 9.8 convert_bitcast_fusion
  822.4 5.8 pad_maximum_fusion.2
  828.3 6.6 copy.168
  834.8 16.5 convert_element_type.211
  851.4 11.7 fusion.52
  872.1 4.4 fusion.93
  876.5 16.5 convert_element_type.223
  893.0 12.2 fusion.92
  905.1 57.7 %all-to-all-done.3 = bf16[32,32,1024]{2,1,0:T(8,128)(2,1)S(1)} async-done(((bf16[32,32,1024]{2,1,0:T(8,128)(2,1)}), bf16[32,32,1024]{2,1,0:T(8,128)(2,1)S(1)}, u32[]{:S(2)}, u32[]{:S(2)}) %all-to-all-start.3) | async-done | bytes 2097184 | tf_op jit(solution)/shard_map/all_to_all | solution.py:168
  973.6 5.4 convolution_convert_fusion.2
  983.0 13.8 multiply_reduce_fusion
  996.8 12.2 multiply_convert_fusion
  1014.6 10.8 convert_bitcast_fusion.2
  1027.7 8.9 copy.176
  1036.6 5.4 copy.206
  1044.4 9.4 fusion.90
  1053.8 21.1 maximum_bitcast_fusion
  1075.0 23.3 %pad_maximum_fusion = f32[2,1024,4096]{2,1,0:T(8,128)} fusion(f32[1,1024,4096]{2,1,0:T(8,128)} %get-tuple-element.54, f32[1,1024,4096]{2,1,0:T(8,128)} %get-tuple-element.53), kind=kLoop, calls=%fused_computation.2 | loop fusion | flops 8388608 | bytes 67108864 | tf_op jit(solution)/shard_map/stack | solution.py:213
  1101.9 10.1 multiply_reduce_fusion.5
  1118.6 163.0 %reduce-scatter.10.cloned.1.call-done = f32[2,128,4096]{2,1,0:T(8,128)} async-done(((f32[2,1024,4096]{2,1,0:T(8,128)}), f32[2,128,4096]{2,1,0:T(8,128)}) %reduce-scatter.10.cloned.1.call-update) | async-done | bytes 4194320 | tf_op jit(solution)/shard_map/reduce_scatter | solution.py:224
  1285.4 542.0 %reduce-scatter.6.cloned.1.call-done = f32[2,128,4096]{2,1,0:T(8,128)} async-done(((f32[2,1024,4096]{2,1,0:T(8,128)}), f32[2,128,4096]{2,1,0:T(8,128)}) %reduce-scatter.6.cloned.1.call-update) | async-done | bytes 4194320 | tf_op jit(solution)/shard_map/reduce_scatter | solution.py:223
  1831.3 52.4 %reduce-scatter.14.cloned.1.call-done = f32[11,128]{1,0:T(8,128)} async-done(((f32[11,1024]{1,0:T(8,128)}), f32[11,128]{1,0:T(8,128)}) %reduce-scatter.14.cloned.1.call-update) | async-done | bytes 5648 | tf_op jit(solution)/shard_map/reduce_scatter | solution.py:225
  1883.8 5.9 psum.14
  1890.9 26.3 %reduce-scatter.12.cloned.1.call-done = bf16[2,128,1024]{2,1,0:T(8,128)(2,1)} async-done(((bf16[2,128,4096]{2,1,0:T(8,128)(2,1)}), bf16[2,128,1024]{2,1,0:T(8,128)(2,1)}) %reduce-scatter.12.cloned.1.call-update) | async-done | bytes 524304 | tf_op jit(solution)/shard_map/reduce_scatter | solution.py:231
  1919.2 32.7 %reduce-scatter.8.cloned.1.call-done = bf16[2,128,1024]{2,1,0:T(8,128)(2,1)} async-done(((bf16[2,128,4096]{2,1,0:T(8,128)(2,1)}), bf16[2,128,1024]{2,1,0:T(8,128)(2,1)}) %reduce-scatter.8.cloned.1.call-update) | async-done | bytes 524304 | tf_op jit(solution)/shard_map/reduce_scatter | solution.py:228
  1955.1 39.4 %psum.15 = f32[]{:T(128)} all-reduce(f32[]{:T(128)S(6)} %add.147), channel_id=1, replica_groups=mesh['seq'=8,'grp'=4] {'seq','grp'}, use_global_device_ids=true, to_apply=%region_31.32 | all-reduce | flops 1 | bytes 8 | tf_op jit(solution)/shard_map/psum | solution.py:241
  1995.2 4.3 fusion.67
  2000.9 4.2 fusion.66
  2006.5 18.4 add_convert_fusion
  2025.6 4.1 convert_element_type.229
  2029.7 18.2 all-gather.15.cloned.1.call-done
  2048.0 4.1 convert_element_type.231
  2052.1 20.5 all-gather.17.cloned.1.call-done
  2076.7 20.1 all-gather.19.cloned.1.call-done
  2100.9 19.9 all-gather.21.cloned.1.call-done
  2124.9 20.1 all-gather.23.cloned.1.call-done
  (223 shorter events, 123.6 us)
Async XLA Ops:
  7.2 234.7 %all-gather.9.cloned.1.call-start = ((), (), s32[]{:S(2)}) async-start(), calls=%async_computation.9 | async-start | bytes 18874368 | tf_op jit(solution)/shard_map/all_gather | solution.py:75
  11.0 4.0 copy-start.54
  11.1 32.3 %copy-start.60 = (s32[4]{0:T(128)S(1)}, s32[4]{0:T(128)}, u32[]{:S(2)}) copy-start(s32[4]{0:T(128)} %param.13) | copy-start | bytes 52
  11.1 32.5 %copy-start.4 = (bf16[4,256,1024]{2,1,0:T(8,128)(2,1)S(1)}, bf16[4,256,1024]{2,1,0:T(8,128)(2,1)}, u32[]{:S(2)}) copy-start(bf16[4,256,1024]{2,1,0:T(8,128)(2,1)} %param.12) | copy-start | bytes 6291460
  11.1 546.7 %all-gather.11.cloned.1.call-start = ((), (), s32[]{:S(2)}) async-start(), calls=%async_computation.10 | async-start | bytes 18874368 | tf_op jit(solution)/shard_map/all_gather | solution.py:76
  43.5 256.2 %copy-start.34 = (f32[4,1024]{1,0:T(4,128)}, f32[4,1024]{1,0:T(4,128)S(1)}, u32[]{:S(2)}) copy-start(f32[4,1024]{1,0:T(4,128)S(1)} %fusion.68) | copy-start | bytes 49156
  45.5 260.8 %copy-start.42 = (f32[1,1024]{1,0:T(1,128)}, f32[1,1024]{1,0:T(1,128)S(1)}, u32[]{:S(2)}) copy-start(f32[1,1024]{1,0:T(1,128)S(1)} %get-tuple-element.36) | copy-start | bytes 12292
  291.6 8.1 copy-start.36
  299.7 5.0 copy-start.22
  309.9 93.7 %all-to-all-start = ((bf16[4,256,1024]{2,0,1:T(4,128)(2,1)}), bf16[4,256,1024]{2,0,1:T(4,128)(2,1)S(1)}, u32[]{:S(2)}, u32[]{:S(2)}) async-start(bf16[4,256,1024]{2,0,1:T(4,128)(2,1)} %copy.154), calls=%async_computation | async-start | bytes 4194304 | tf_op jit(solution)/shard_map/all_to_all | solution.py:106
  313.5 968.1 %reduce-scatter.10.cloned.1.call-start = ((), (), s32[]{:S(2)}) async-start(), calls=%async_computation.13 | async-start | bytes 37748736 | tf_op jit(solution)/shard_map/reduce_scatter | solution.py:224
  440.8 10.2 copy-start.10
  461.4 7.6 copy-start.16
  461.4 7.6 copy-start.32
  477.6 72.7 %copy-start.1 = (f32[4,256,1024]{2,1,0:T(8,128)S(1)}, f32[4,256,1024]{2,1,0:T(8,128)}, u32[]{:S(2)}) copy-start(f32[4,256,1024]{2,1,0:T(8,128)} %copy-done) | copy-start | bytes 12582916
  550.3 4.8 copy-start.24
  557.8 16.6 copy-start.18
  590.4 22.9 %copy-start.13 = (f32[4,256,1024]{2,1,0:T(8,128)S(1)}, f32[4,256,1024]{2,1,0:T(8,128)}, u32[]{:S(2)}) copy-start(f32[4,256,1024]{2,1,0:T(8,128)} %copy-done.12) | copy-start | bytes 12582916
  652.0 16.4 copy-start.14
  671.8 4.7 copy-start.27
  779.2 4.0 copy-start.33
  798.6 7.5 copy-start.11
  806.1 3.5 copy-start.7
  863.0 99.8 %all-to-all-start.3 = ((bf16[32,32,1024]{2,1,0:T(8,128)(2,1)}), bf16[32,32,1024]{2,1,0:T(8,128)(2,1)S(1)}, u32[]{:S(2)}, u32[]{:S(2)}) async-start(bf16[32,32,1024]{2,1,0:T(8,128)(2,1)} %fusion.52), calls=%async_computation.3 | async-start | bytes 4194304 | tf_op jit(solution)/shard_map/all_to_all | solution.py:168
  866.6 960.8 %reduce-scatter.6.cloned.1.call-start = ((), (), s32[]{:S(2)}) async-start(), calls=%async_computation.11 | async-start | bytes 37748736 | tf_op jit(solution)/shard_map/reduce_scatter | solution.py:223
  866.7 5.4 copy-start.25
  866.7 5.4 copy-start.28
  905.1 58.2 %copy-start.39 = (f32[4,256]{1,0:T(4,128)S(1)}, f32[4,256]{1,0:T(4,128)}, u32[]{:S(2)}) copy-start(f32[4,256]{1,0:T(4,128)} %copy-done.38) | copy-start | bytes 12292
  905.1 58.2 %copy-start.43 = (f32[1,1024]{1,0:T(1,128)S(1)}, f32[1,1024]{1,0:T(1,128)}, u32[]{:S(2)}) copy-start(f32[1,1024]{1,0:T(1,128)} %copy-done.42) | copy-start | bytes 12292
  962.8 2.2 copy-start.2
  965.8 2.8 copy-start.9
  965.9 2.9 copy-start.19
  973.6 35.4 %slice-start = ((s8[6291456]{0:T(1024)(128)(4,1)}), s8[2097152]{0:T(1024)(128)(4,1)S(1)}, s32[]{:S(2)}) async-start(s8[6291456]{0:T(1024)(128)(4,1)} %bitcast.222), calls=%async_computation.22 | async-start | bytes 4194304
  979.0 4.0 copy-start.37
  983.0 26.0 %slice-start.1 = ((s8[6291456]{0:T(1024)(128)(4,1)}), s8[4194304]{0:T(1024)(128)(4,1)S(1)}, s32[]{:S(2)}) async-start(s8[6291456]{0:T(1024)(128)(4,1)} %bitcast.222), calls=%async_computation.23 | async-start | bytes 8388608
  1014.6 10.8 copy-start.17
  1027.7 8.9 copy-start.3
  1036.6 5.4 copy-start.26
  1036.6 5.4 copy-start.31
  1042.0 2.4 copy-start.21
  1044.4 9.4 copy-start.20
  1098.2 3.6 copy-start.5
  1098.3 3.6 copy-start.35
  1098.3 3.6 copy-start.41
  1098.3 3.6 copy-start.47
  1098.3 785.5 %reduce-scatter.14.cloned.1.call-start = ((), (), s32[]{:S(2)}) async-start(), calls=%async_computation.15 | async-start | bytes 73728 | tf_op jit(solution)/shard_map/reduce_scatter | solution.py:225
  1101.9 10.1 copy-start.51
  1101.9 10.1 copy-start.45
  1112.0 2.2 copy-start.15
  1114.2 3.4 copy-start.61
  1114.2 3.6 copy-start.56
  1114.2 3.7 copy-start.59
  1118.5 798.6 %reduce-scatter.12.cloned.1.call-start = ((), (), s32[]{:S(2)}) async-start(), calls=%async_computation.14 | async-start | bytes 2621440 | tf_op jit(solution)/shard_map/reduce_scatter | solution.py:231
  1285.4 666.5 %reduce-scatter.8.cloned.1.call-start = ((), (), s32[]{:S(2)}) async-start(), calls=%async_computation.12 | async-start | bytes 2621440 | tf_op jit(solution)/shard_map/reduce_scatter | solution.py:228
  1831.3 194.4 %all-gather.13.cloned.1.call-start = ((), (), s32[]{:S(2)}) async-start(), calls=%async_computation.16 | async-start | bytes 2621440 | tf_op jit(solution)/shard_map/all_gather | solution.py:264
  1917.2 83.7 %copy-start.29 = (bf16[2,128,1024]{2,1,0:T(8,128)(2,1)S(1)}, bf16[2,128,1024]{2,1,0:T(8,128)(2,1)}, u32[]{:S(2)}) copy-start(bf16[2,128,1024]{2,1,0:T(8,128)(2,1)} %reduce-scatter.12.cloned.1.call-done) | copy-start | bytes 1572868
  1999.5 48.4 %all-gather.15.cloned.1.call-start = ((), (), s32[]{:S(2)}) async-start(), calls=%async_computation.17 | async-start | bytes 2621440 | tf_op jit(solution)/shard_map/all_gather | solution.py:267
  2000.3 72.3 %all-gather.17.cloned.1.call-start = ((), (), s32[]{:S(2)}) async-start(), calls=%async_computation.18 | async-start | bytes 2621440 | tf_op jit(solution)/shard_map/all_gather | solution.py:270
  2000.8 95.9 %all-gather.19.cloned.1.call-start = ((), (), s32[]{:S(2)}) async-start(), calls=%async_computation.19 | async-start | bytes 2621440 | tf_op jit(solution)/shard_map/all_gather | solution.py:273
  2005.1 115.7 %all-gather.21.cloned.1.call-start = ((), (), s32[]{:S(2)}) async-start(), calls=%async_computation.20 | async-start | bytes 2621440 | tf_op jit(solution)/shard_map/all_gather | solution.py:276
  2005.7 139.3 %all-gather.23.cloned.1.call-start = ((), (), s32[]{:S(2)}) async-start(), calls=%async_computation.21 | async-start | bytes 2621440 | tf_op jit(solution)/shard_map/all_gather | solution.py:279
  2006.5 18.5 copy-start.55
  2006.5 18.5 copy-start.57
  2006.5 18.5 copy-start.58
  (15 other events, 20.3 us)
Sparse Core Ops, SparseCore 0:
  11.2 230.6 all-gather.8
  244.6 294.3 all-gather.10
  652.1 629.3 reduce-scatter.9
  1285.2 542.2 reduce-scatter.5
  1831.0 52.7 reduce-scatter.13
  1886.7 30.4 reduce-scatter.11
  1920.4 31.3 reduce-scatter.7
  1999.6 23.5 all-gather.12
  2025.3 22.5 all-gather.14
  2049.9 22.5 all-gather.16
  2074.1 22.5 all-gather.18
  2098.2 22.5 all-gather.20
  2122.4 22.5 all-gather.22
where the time goes:
time: 2170 us; the launch traced here: 2160 us
  waiting for transfers between devices  1260 us (58%)
  matrix products  295 us (14%)
  blocking collectives  246 us (11%)
  other arithmetic  199 us (9%)
  local copies, waits for them, and re-layouts  131 us (6%)
    reduce_scatter x1, waiting for transfers between devices, shards(): lax.psum_scatter(grad_attn, 'seq', scatter_dimension=1, tiled=True)  542 us
    all_gather x1, waiting for transfers between devices, shards(): lax.all_gather(attn_master.astype(jnp.bfloat16), 'seq', axis=1, tiled=True)  194 us
    reduce_scatter x1, waiting for transfers between devices, shards(): lax.psum_scatter(grad_ffn, 'seq', scatter_dimension=1, tiled=True)  163 us
    all_to_all x1, blocking collectives, shards(): lax.all_to_all(heads_t_grad, 'seq', split_axis=1, concat_axis=0, tiled=True)  100 us
    all_to_all x1, waiting for transfers between devices, shards(): lax.all_to_all(normed_two, 'seq', split_axis=1, concat_axis=0, tiled=True)  90 us
    all_to_all x1, blocking collectives, shards(): lax.all_to_all(heads_pos, 'seq', split_axis=0, concat_axis=1, tiled=True)  72.5 us
    dot_general x6, matrix products, project(): jnp.einsum('...d,de->...e', left_side, right_side, preferred_element_type...  71.9 us
    dot_general x6, matrix products, project_back(): jnp.einsum('...e,de->...d', left_side, right_side, preferred_element_type...  66.8 us
  transfers between devices with their start and end apart: 15, of which 13 were waited for; matrix products, arithmetic and copies ran while one was open for 23% of the time, Pallas kernels for 0%

commit v1 on v0

v1 whole, which is shorter than its diff:
```python
import functools

import jax
import jax.numpy as jnp
from jax import lax
from jax.experimental import pallas as pl
from jax.experimental.pallas import tpu as pltpu
from jax.sharding import PartitionSpec as P

HD = 64
FPV = 16
CODES = 8
STEP = 5
BF = jnp.bfloat16
F32 = jnp.float32

eps_norm = 1e-05
beta_first = 0.5
beta_second = 0.5
rate_matrix = 0.02
rate_small = 0.3
decay_rate = 0.1
eps_adam = 1e-08
masked_score = -1000000000.0
score_scale = HD**-0.5

CORE, XPOS, YPOS, ZPOS, MEMBER = range(5)
ANY = pl.BlockSpec(memory_space=pl.ANY)
MIB = 1 << 20


def dot_nn(a, b):
    return lax.dot_general(a, b, (((1,), (0,)), ((), ())), preferred_element_type=F32)


def dot_nt(a, b):
    return lax.dot_general(a, b, (((1,), (1,)), ((), ())), preferred_element_type=F32)


def swap(value, axis, bit):
    size = lax.axis_size(axis)
    return lax.ppermute(value, axis, [(i, i ^ bit) for i in range(size)])


def shift_z(value, step):
    size = lax.axis_size("seq")
    return lax.ppermute(value, "seq", [(i, (i + 2 * step) % size) for i in range(size)])


def z_groups():
    size = lax.axis_size("seq")
    return [list(range(first, size, 2)) for first in range(2)]


def gather_z(piece):
    nz = lax.axis_size("seq") // 2
    if nz <= 4:
        return jnp.stack([piece] + [shift_z(piece, k) for k in range(1, nz)])
    whole = lax.all_gather(piece, "seq", axis_index_groups=z_groups())
    here = lax.axis_index("seq") // 2
    return jnp.take(whole, (here - jnp.arange(nz)) % nz, axis=0)


def scatter_z(parts):
    nz = lax.axis_size("seq") // 2
    if nz <= 4:
        come = [parts[0]] + [shift_z(parts[k], k) for k in range(1, nz)]
        total = come[0].astype(F32)
        for item in come[1:]:
            total = total + item.astype(F32)
        return total.astype(BF)
    here = lax.axis_index("seq") // 2
    ordered = jnp.take(parts, (jnp.arange(nz) - here) % nz, axis=0)
    return lax.psum_scatter(ordered, "seq", axis_index_groups=z_groups())


def column_part(block, start, width):
    return lax.dynamic_slice_in_dim(block, start, width, 2)


def gather_weights(block, kind, place):
    width = block.shape[2]
    if kind == "zyx":
        part = width // 4
        piece = column_part(block, (place[CORE] * 2 + place[XPOS]) * part, part)
    else:
        part = width // 2
        piece = column_part(block, place[CORE] * part, part)
    below = gather_z(piece)
    beside = swap(below, "seq", 1)
    stacks = [(below, 0, 0), (beside, 1, 0)]
    if kind == "zyx":
        stacks += [(swap(s, "grp", 2), y, 1) for s, y, _ in stacks]
    out = [(s, (y, 0, x)) for s, y, x in stacks]
    out += [(swap(s, "grp", 1), (y, 1, x)) for s, y, x in stacks]
    return [s for s, _ in out], [m if kind == "zyx" else (m[0], m[1], None) for _, m in out]


def add_low(a, b):
    return (a.astype(F32) + b.astype(F32)).astype(BF)


def reduce_grads(parts, kind):
    half = [add_low(parts[0][x], swap(parts[1][x], "grp", 1)) for x in range(2)]
    if kind == "xyz":
        quarter = add_low(half[0], swap(half[1], "grp", 2))
        rows = add_low(quarter[0], swap(quarter[1], "seq", 1))
        return scatter_z(rows)
    rows = [add_low(h[0], swap(h[1], "seq", 1)) for h in half]
    ends = [scatter_z(r) for r in rows]
    return add_low(ends[0], swap(ends[1], "grp", 2))


def share_quarters(quarter):
    beside = swap(quarter, "grp", 2)
    return [quarter, beside, swap(quarter, "grp", 1), swap(beside, "grp", 1)]


def exchange(pieces):
    return [pieces[0]] + [swap(pieces[j], "seq", j) for j in range(1, len(pieces))]


def start_weights(place, stacks, metas, target, sem):
    for stack, (y_rel, c_rel, x_rel) in zip(stacks, metas):
        nz, _, rows, width = stack.shape
        column = place[CORE] ^ c_rel
        if x_rel is not None:
            column = column * 2 + (place[XPOS] ^ x_rel)
        column = pl.multiple_of(column * width, 128)

        def one(k, carry, stack=stack, y_rel=y_rel, rows=rows, width=width, column=column, nz=nz):
            shard = lax.rem(place[ZPOS] - k + nz, nz) * 2 + (place[YPOS] ^ y_rel)
            row = pl.multiple_of(shard * rows, rows)
            pltpu.make_async_copy(
                stack.at[k], target.at[:, pl.ds(row, rows), pl.ds(column, width)], sem
            ).start()
            return carry

        if nz <= 4:
            for k in range(nz):
                one(k, 0)
        else:
            lax.fori_loop(0, nz, one, 0)


def wait_all(target, sem):
    pltpu.make_async_copy(target, target, sem).wait()


def start_grads(place, source, index, outs, sem):
    for rel, out in enumerate(outs):
        _, nz, _, rows, width = out.shape
        column = (place[CORE] ^ (rel // 2)) * 2 + (place[XPOS] ^ (rel % 2))
        column = pl.multiple_of(column * width, 128)
        for y_rel in range(2):

            def one(k, carry, out=out, y_rel=y_rel, column=column, nz=nz, rows=rows, width=width):
                shard = lax.rem(place[ZPOS] + k, nz) * 2 + (place[YPOS] ^ y_rel)
                row = pl.multiple_of(shard * rows, rows)
                pltpu.make_async_copy(
                    source.at[pl.ds(row, rows), pl.ds(column, width)],
                    out.at[y_rel, k, index],
                    sem,
                ).start()
                return carry

            if nz <= 4:
                for k in range(nz):
                    one(k, 0)
            else:
                lax.fori_loop(0, nz, one, 0)


def norm_parts(values):
    centre = values - jnp.mean(values, axis=-1, keepdims=True)
    spread = jnp.mean(centre * centre, axis=-1, keepdims=True)
    scale = lax.rsqrt(spread + eps_norm)
    return centre * scale, scale


def norm_back(values, h_grad, gain):
    xhat, scale = norm_parts(values)
    e = h_grad * gain
    inner = jnp.mean(e * xhat, axis=-1, keepdims=True)
    v_grad = scale * (e - jnp.mean(e, axis=-1, keepdims=True) - xhat * inner)
    return v_grad, jnp.sum(h_grad * xhat, axis=0, keepdims=True)


def two_heads(x):
    lane = lax.broadcasted_iota(jnp.int32, x.shape, 1)
    zero = jnp.zeros_like(x)
    return jnp.where(lane < HD, x, zero), jnp.where(lane < HD, zero, x)


def video_mask(rows, positions):
    key = lax.broadcasted_iota(jnp.int32, (rows, rows), 0)
    query = lax.broadcasted_iota(jnp.int32, (rows, rows), 1)
    return (lax.rem(key, positions) == lax.rem(query, positions)) & (key <= query)


def attend(packed_ref, heads_ref, lse_ref, mask):
    width = heads_ref.shape[-1]
    for pair in range(width // 128):
        lo = pair * 128
        queries = two_heads(packed_ref[0, :, lo : lo + 128] * jnp.asarray(score_scale, BF))
        keys = packed_ref[0, :, width + lo : width + lo + 128]
        values_t = packed_ref[0, :, 2 * width + lo : 2 * width + lo + 128].T
        out = []
        for half in range(2):
            scores = dot_nt(keys, queries[half])
            if mask is not None:
                scores = jnp.where(mask, scores, masked_score)
            top = jnp.max(scores, axis=0, keepdims=True)
            probs = jnp.exp(scores - top)
            total = jnp.sum(probs, axis=0, keepdims=True)
            mixed = dot_nn(values_t[half * HD : half * HD + HD], probs.astype(BF))
            out.append(mixed / total)
            lse_ref[0, 2 * pair + half : 2 * pair + half + 1, :] = top + jnp.log(total)
        heads_ref[0, :, lo : lo + 128] = jnp.concatenate(out, axis=0).astype(BF).T


def attend_back(packed_ref, heads_ref, heads_grad_ref, lse_ref, grad_ref, mask):
    width = heads_ref.shape[-1]
    for pair in range(width // 128):
        lo = pair * 128
        query = packed_ref[0, :, lo : lo + 128] * jnp.asarray(score_scale, BF)
        key = packed_ref[0, :, width + lo : width + lo + 128]
        value = packed_ref[0, :, 2 * width + lo : 2 * width + lo + 128]
        heads_grad = heads_grad_ref[:, lo : lo + 128]
        key_t = key.T
        mixed_t = (heads_grad.astype(F32) * heads_ref[0, :, lo : lo + 128].astype(F32)).T
        queries, head_grads = two_heads(query), two_heads(heads_grad)
        probs_two, score_two, query_grad = [], [], []
        for half in range(2):
            scores = dot_nt(key, queries[half])
            if mask is not None:
                scores = jnp.where(mask, scores, masked_score)
            probs = jnp.exp(scores - lse_ref[0, 2 * pair + half : 2 * pair + half + 1, :])
            delta = jnp.sum(mixed_t[half * HD : half * HD + HD], axis=0, keepdims=True)
            probs_grad = dot_nt(value, head_grads[half])
            score_grad = (probs * (probs_grad - delta)).astype(BF)
            probs_two.append(probs.astype(BF))
            score_two.append(score_grad)
            query_grad.append(dot_nn(key_t[half * HD : half * HD + HD], score_grad))
        value_grad = dot_nn(jnp.concatenate(probs_two, 1), jnp.concatenate(head_grads, 0))
        key_grad = dot_nn(jnp.concatenate(score_two, 1), jnp.concatenate(queries, 0))
        grad_ref[0, :, lo : lo + 128] = (
            (jnp.concatenate(query_grad, 0) * score_scale).astype(BF).T
        )
        grad_ref[0, :, width + lo : width + lo + 128] = key_grad.astype(BF)
        grad_ref[0, :, 2 * width + lo : 2 * width + lo + 128] = value_grad.astype(BF)


def gelu_both(pre):
    root = 0.7978845608028654
    square = pre * pre
    bend = jnp.tanh(root * pre * (1.0 + 0.044715 * square))
    half = 0.5 * (1.0 + bend)
    slope = half + 0.5 * pre * (1.0 - bend * bend) * (root * (1.0 + 3 * 0.044715 * square))
    return pre * half, slope


def spatial_fwd_body(
    metas_qkv, metas_out, place, frames_ref, shift_ref, gain_ref, *refs
):
    n_qkv, n_out = len(metas_qkv), len(metas_out)
    qkv_stacks, out_stacks = refs[:n_qkv], refs[n_qkv : n_qkv + n_out]
    refs = refs[n_qkv + n_out :]
    packed_ref, heads_ref, lse_ref, normed_ref = refs[:4]
    piece_refs = refs[4:8]
    w_qkv, w_out, resid, sems = refs[8:]
    step = pl.program_id(0)

    @pl.when(step == 0)
    def _():
        start_weights(place, qkv_stacks, metas_qkv, w_qkv, sems.at[0])
        start_weights(place, out_stacks, metas_out, w_out, sems.at[1])
        wait_all(w_qkv, sems.at[0])
        wait_all(w_out, sems.at[1])

    values = frames_ref[0].astype(F32) + shift_ref[0]
    xhat, _ = norm_parts(values)
    normed = (xhat * gain_ref[0:1, :]).astype(BF)
    normed_ref[0] = normed
    width = normed.shape[1]
    for b in range(3):
        packed_ref[0, :, b * width : (b + 1) * width] = dot_nn(normed, w_qkv[b]).astype(BF)
    attend(packed_ref, heads_ref, lse_ref, None)
    resid[...] = (values + dot_nn(heads_ref[0], w_out[0])).astype(BF)
    count = piece_refs[0].shape[1]
    for j, piece in enumerate(piece_refs):
        first = pl.multiple_of((place[MEMBER] ^ j) * count, count)
        piece[0] = resid[pl.ds(first, count), :]


def temporal_fwd_body(metas, place, *refs):
    n = len(metas)
    piece_refs, gain_ref, stacks = refs[:4], refs[4], refs[5 : 5 + n]
    packed_ref, heads_ref, lse_ref, normed_ref, tokens_ref, resid_ref, third_ref = refs[5 + n : 12 + n]
    weights, tokens, sems = refs[12 + n :]
    step = pl.program_id(0)

    @pl.when(step == 0)
    def _():
        start_weights(place, stacks, metas, weights, sems.at[0])

    frames, positions = piece_refs[0].shape[0], piece_refs[0].shape[1]
    for j, piece in enumerate(piece_refs):
        tokens[pl.ds((place[MEMBER] ^ j) * frames, frames)] = piece[...]
    low = tokens[...].reshape(tokens_ref.shape[1:])
    tokens_ref[0] = low
    values = low.astype(F32)
    xhat, _ = norm_parts(values)
    normed = (xhat * gain_ref[1:2, :]).astype(BF)
    normed_ref[0] = normed

    @pl.when(step == 0)
    def _():
        wait_all(weights, sems.at[0])

    width = normed.shape[1]
    for b in range(3):
        packed_ref[0, :, b * width : (b + 1) * width] = dot_nn(normed, weights[b]).astype(BF)
    attend(packed_ref, heads_ref, lse_ref, video_mask(low.shape[0], positions))
    resid = values + dot_nn(heads_ref[0], weights[3])
    resid_ref[0] = resid
    xhat, _ = norm_parts(resid)
    third_ref[0] = (xhat * gain_ref[2:3, :]).astype(BF)


def ffn_body(metas, first, last, place, *refs):
    n = len(metas)
    third_ref, cot_ref, resid_ref, dx_in = refs[:4]
    stacks = refs[4 : 4 + n]
    outs = refs[4 + n : 8 + n]
    refs = refs[8 + n :]
    if last:
        dx_out, piece_refs, refs = refs[0], refs[1:5], refs[5:]
    else:
        resid_out, dx_out, refs = refs[0], refs[1], refs[2:]
    third, cot, third_t, cot_t, acc, dx, weights, act, pre_grad, staging, sems = refs
    tokens, width = third.shape
    blocks = weights.shape[0] // 2
    chunk = 256
    loads = [(third_ref, third, 0), (cot_ref, cot, 1), (resid_ref, acc, 2)]
    if not first:
        loads.append((dx_in, dx, 3))
    for source, target, s in loads:
        pltpu.make_async_copy(source, target, sems.at[s]).start()
    start_weights(place, stacks, metas, weights, sems.at[4])
    for source, target, s in loads[:2]:
        pltpu.make_async_copy(source, target, sems.at[s]).wait()
    for r in range(tokens // chunk):
        rows = slice(r * chunk, (r + 1) * chunk)
        third_t[:, rows] = third[rows, :].T
        cot_t[:, rows] = cot[rows, :].T
    wait_all(weights, sems.at[4])
    for source, target, s in loads[2:]:
        pltpu.make_async_copy(source, target, sems.at[s]).wait()
    for b in range(blocks):
        for r in range(tokens // chunk):
            rows = slice(r * chunk, (r + 1) * chunk)
            pre = dot_nn(third[rows, :], weights[b])
            act_grad = dot_nn(cot[rows, :], weights[blocks + b])
            act_now, slope = gelu_both(pre)
            act_now = act_now.astype(BF)
            grad_now = (act_grad * slope).astype(BF)
            act[rows, :] = act_now
            pre_grad[rows, :] = grad_now
            acc[rows, :] += dot_nt(act_now, weights[blocks + b])
            back = dot_nt(grad_now, weights[b])
            if first and b == 0:
                dx[rows, :] = back
            else:
                dx[rows, :] += back
        staging[b] = dot_nn(third_t[...], pre_grad[...]).astype(BF)
        start_grads(place, staging.at[b], b, outs, sems.at[5])
        staging[blocks + b] = dot_nn(cot_t[...], act[...]).astype(BF)
        start_grads(place, staging.at[blocks + b], blocks + b, outs, sems.at[5])
    pltpu.make_async_copy(dx, dx_out, sems.at[6]).start()
    if last:
        low = third
        low[...] = acc[...].astype(BF)
        frames, positions = piece_refs[0].shape[:2]
        tiles = tokens // 256
        per_tile = positions // tiles
        for j, piece in enumerate(piece_refs):
            for tile in range(tiles):
                for f in range(frames):
                    row = pl.multiple_of(
                        tile * (tokens // tiles)
                        + ((place[MEMBER] ^ j) * frames + f) * per_tile,
                        per_tile,
                    )
                    pltpu.make_async_copy(
                        low.at[pl.ds(row, per_tile)],
                        piece.at[f, pl.ds(tile * per_tile, per_tile)],
                        sems.at[7],
                    ).start()
        wait_all(low, sems.at[7])
    else:
        pltpu.make_async_copy(acc, resid_out, sems.at[7]).start()
        pltpu.make_async_copy(acc, resid_out, sems.at[7]).wait()
    pltpu.make_async_copy(dx, dx_out, sems.at[6]).wait()
    wait_all(staging, sems.at[5])


def add_gain(step, ref, row, value):
    @pl.when(step == 0)
    def _():
        ref[row : row + 1, :] = value

    @pl.when(step > 0)
    def _():
        ref[row : row + 1, :] += value


def temporal_bwd_body(metas, place, *refs):
    n = len(metas)
    dx_ref, cot_ref, resid_ref, tokens_ref, packed_ref, heads_ref, lse_ref, gain_ref = refs[:8]
    stacks = refs[8 : 8 + n]
    branch_ref, grad_ref, gains_out = refs[8 + n : 11 + n]
    piece_refs = refs[11 + n : 15 + n]
    weights, heads_grad, total, sems = refs[15 + n :]
    step = pl.program_id(0)

    @pl.when(step == 0)
    def _():
        start_weights(place, stacks, metas, weights, sems.at[0])

    back, gain_three = norm_back(resid_ref[0], dx_ref[0], gain_ref[2:3, :])
    add_gain(step, gains_out, 1, gain_three)
    grad_two = cot_ref[0].astype(F32) + back
    branch = grad_two.astype(BF)
    branch_ref[0] = branch

    @pl.when(step == 0)
    def _():
        wait_all(weights, sems.at[0])

    heads_grad[...] = dot_nt(branch, weights[3]).astype(BF)
    frames, positions = piece_refs[0].shape[0], piece_refs[0].shape[1]
    attend_back(
        packed_ref, heads_ref, heads_grad, lse_ref, grad_ref, video_mask(branch.shape[0], positions)
    )
    width = branch.shape[1]
    normed_grad = dot_nt(grad_ref[0, :, :width], weights[0])
    for b in range(1, 3):
        normed_grad = normed_grad + dot_nt(grad_ref[0, :, b * width : (b + 1) * width], weights[b])
    back, gain_two = norm_back(tokens_ref[0].astype(F32), normed_grad, gain_ref[1:2, :])
    add_gain(step, gains_out, 0, gain_two)
    total[...] = (grad_two + back).astype(BF).reshape(total.shape)
    for j, piece in enumerate(piece_refs):
        piece[...] = total[pl.ds((place[MEMBER] ^ j) * frames, frames)]


def spatial_bwd_body(metas_qkv, metas_out, place, *refs):
    n_qkv, n_out = len(metas_qkv), len(metas_out)
    piece_refs = refs[:4]
    frames_ref, shift_ref, packed_ref, heads_ref, lse_ref, gain_ref = refs[4:10]
    refs = refs[10:]
    qkv_stacks, out_stacks = refs[:n_qkv], refs[n_qkv : n_qkv + n_out]
    refs = refs[n_qkv + n_out :]
    branch_ref, grad_ref, input_ref, gain_out, column_out = refs[:5]
    w_qkv, w_out, heads_grad, sems = refs[5:]
    step = pl.program_id(0)

    @pl.when(step == 0)
    def _():
        start_weights(place, out_stacks, metas_out, w_out, sems.at[1])
        start_weights(place, qkv_stacks, metas_qkv, w_qkv, sems.at[0])
        wait_all(w_out, sems.at[1])
        wait_all(w_qkv, sems.at[0])

    count = piece_refs[0].shape[1]
    for j, piece in enumerate(piece_refs):
        first = pl.multiple_of((place[MEMBER] ^ j) * count, count)
        branch_ref[0, pl.ds(first, count), :] = piece[0]
    branch = branch_ref[0]
    heads_grad[...] = dot_nt(branch, w_out[0]).astype(BF)
    attend_back(packed_ref, heads_ref, heads_grad, lse_ref, grad_ref, None)
    width = branch.shape[1]
    normed_grad = dot_nt(grad_ref[0, :, :width], w_qkv[0])
    for b in range(1, 3):
        normed_grad = normed_grad + dot_nt(grad_ref[0, :, b * width : (b + 1) * width], w_qkv[b])
    values = frames_ref[0].astype(F32) + shift_ref[0]
    back, gain_one = norm_back(values, normed_grad, gain_ref[0:1, :])
    add_gain(step, gain_out, 0, gain_one)
    grad_zero = branch.astype(F32) + back
    input_ref[0] = grad_zero.astype(BF)
    column_out[0] = jnp.sum(grad_zero, axis=0, keepdims=True)


def weight_grad_body(place, normed_ref, heads_ref, grad_ref, branch_ref, *refs):
    outs = refs[:4]
    normed, heads, grad, branch, normed_t, heads_t, staging, sems = refs[4:]
    loads = [(normed_ref, normed), (grad_ref, grad), (heads_ref, heads), (branch_ref, branch)]
    for s, (source, target) in enumerate(loads):
        pltpu.make_async_copy(source, target, sems.at[s]).start()
    tokens, width = normed.shape
    chunk = 256

    def wait(s):
        pltpu.make_async_copy(loads[s][0], loads[s][1], sems.at[s]).wait()

    def turn(source, target):
        for r in range(tokens // chunk):
            rows = slice(r * chunk, (r + 1) * chunk)
            target[:, rows] = source[rows, :].T

    wait(0)
    turn(normed, normed_t)
    wait(1)
    for b in range(3):
        staging[b] = dot_nn(normed_t[...], grad[:, b * width : (b + 1) * width]).astype(BF)
        start_grads(place, staging.at[b], b, outs, sems.at[4])
    wait(2)
    turn(heads, heads_t)
    wait(3)
    staging[3] = dot_nn(heads_t[...], branch[...]).astype(BF)
    start_grads(place, staging.at[3], 3, outs, sems.at[4])
    wait_all(staging, sems.at[4])


def update(weight, moment_one, moment_two, gradient, step_rate, decay_coef):
    first_new = beta_first * moment_one + (1.0 - beta_first) * gradient
    second_new = beta_second * moment_two + (1.0 - beta_second) * gradient * gradient
    fix_first = 1.0 - beta_first**STEP
    fix_second = 1.0 - beta_second**STEP
    change = first_new / fix_first / (jnp.sqrt(second_new / fix_second) + eps_adam)
    return weight - step_rate * (change + decay_coef * weight), first_new, second_new


def update_body(pick, place, clip, *refs):
    lots = [refs[:4], refs[4:8]]
    master, first, second, master_new, first_new, second_new = refs[8:]
    which = pick(pl.program_id(0), pl.program_id(1))
    for lot, pieces in enumerate(lots):

        @pl.when(which == lot)
        def _(pieces=pieces):
            for rel, piece in enumerate(pieces):
                width = piece.shape[2]
                column = (place[CORE] ^ (rel // 2)) * 2 + (place[XPOS] ^ (rel % 2))
                at = pl.ds(pl.multiple_of(column * width, 128), width)
                new = update(
                    master[0, :, at],
                    first[0, :, at],
                    second[0, :, at],
                    piece[0].astype(F32) * clip[0],
                    rate_matrix,
                    decay_rate,
                )
                master_new[0, :, at], first_new[0, :, at], second_new[0, :, at] = new


def join_body(place, *refs):
    pieces, out_ref, sems = refs[:4], refs[4], refs[5]
    count = pieces[0].shape[1]
    copies = []
    for j, piece in enumerate(pieces):
        first = pl.multiple_of((place[MEMBER] ^ j) * count, count)
        copies.append(
            pltpu.make_async_copy(piece, out_ref.at[:, pl.ds(first, count)], sems.at[j])
        )
    for copy in copies:
        copy.start()
    for copy in copies:
        copy.wait()


def tile_body(place, *refs):
    pieces, out_ref, tokens = refs[:4], refs[4], refs[5]
    frames = pieces[0].shape[0]
    for j, piece in enumerate(pieces):
        tokens[pl.ds((place[MEMBER] ^ j) * frames, frames)] = piece[...]
    out_ref[0] = tokens[...].reshape(out_ref.shape[1:])


def call(body, place, args, in_specs, out_specs, out_shape, scratch, grid=(1,), limit=60, flops=0, scalars=1):
    return pl.pallas_call(
        body,
        out_shape=out_shape,
        grid_spec=pltpu.PrefetchScalarGridSpec(
            num_scalar_prefetch=scalars,
            grid=grid,
            in_specs=in_specs,
            out_specs=out_specs,
            scratch_shapes=scratch,
        ),
        compiler_params=pltpu.CompilerParams(vmem_limit_bytes=limit * MIB),
        cost_estimate=pl.CostEstimate(flops=flops, bytes_accessed=16 * MIB, transcendentals=0),
    )(*place, *args)


def tile(*shape):
    return pl.BlockSpec((1,) + shape, lambda i, *_: (i,) + (0,) * len(shape))


def fixed(*shape):
    return pl.BlockSpec(shape, lambda i, *_: (0,) * len(shape))


def shape_of(*shape, dtype=BF):
    return jax.ShapeDtypeStruct(shape, dtype)


def shards(
    frames_in,
    action_codes,
    cotangent,
    attn_master,
    attn_first,
    attn_second,
    ffn_master,
    ffn_first,
    ffn_second,
    small_master,
    small_first,
    small_second,
):
    frames, positions, width = frames_in.shape
    heads_n = width // HD
    members = FPV // frames
    part = positions // members
    spot = positions // FPV
    tiles = part // spot
    rows_tile = FPV * spot
    tokens = tiles * rows_tile
    seq_size = lax.axis_size("seq")
    nz = seq_size // 2
    seq, grp = lax.axis_index("seq"), lax.axis_index("grp")
    place = jnp.stack([grp % 2, grp // 2, seq % 2, seq // 2, seq % members]).astype(jnp.int32)
    spots = (place,)
    local_rows = attn_master.shape[1]

    def blocks(master, picks):
        return jnp.stack(
            [master[m, :, b * width : (b + 1) * width] for m, b in picks]
        ).astype(BF)

    qkv_s, meta_qkv_s = gather_weights(blocks(attn_master, [(0, 0), (0, 1), (0, 2)]), "zy", place)
    small_low = small_master.astype(BF)
    if seq_size <= 8:
        small_all = jnp.stack(
            [small_low] + [lax.ppermute(small_low, "seq", [(i, i ^ j) for i in range(seq_size)]) for j in range(1, seq_size)]
        )
        small_all = jnp.take(small_all, jnp.arange(seq_size) ^ seq, axis=0)
    else:
        small_all = lax.all_gather(small_low, "seq")
    small_w = small_all.transpose(1, 0, 2).reshape(small_low.shape[0], width)
    out_s, meta_out_s = gather_weights(blocks(attn_master, [(0, 3)]), "zyx", place)
    all_t, meta_t = gather_weights(blocks(attn_master, [(1, b) for b in range(4)]), "zyx", place)
    ffn_groups = []
    for group, kind in ((0, "zyx"), (1, "zy")):
        picks = [(m, 2 * group + b) for m in range(2) for b in range(2)]
        ffn_groups.append(gather_weights(blocks(ffn_master, picks), kind, place))

    gains = small_w[:3].astype(F32)
    onehot = (action_codes[:, None] == jnp.arange(CODES)[None, :]).astype(BF)
    code_shift = jnp.dot(onehot, small_w[3:], preferred_element_type=F32)[:, None, :]

    def position_part(array, j):
        return lax.dynamic_slice_in_dim(array, (place[MEMBER] ^ j) * part, part, 1)

    cot_pieces = exchange([position_part(cotangent, j) for j in range(members)])
    piece_spec = pl.BlockSpec((frames, spot, width), lambda i, *_: (0, i, 0))
    cot_tiles = call(
        tile_body,
        spots,
        cot_pieces,
        [piece_spec] * members,
        tile(rows_tile, width),
        shape_of(tiles, rows_tile, width),
        [pltpu.VMEM((FPV, spot, width), BF)],
        grid=(tiles,),
    )

    part_spec = pl.BlockSpec((1, part, width), lambda i, *_: (i, 0, 0))
    sems = pltpu.SemaphoreType.DMA
    result = call(
        functools.partial(spatial_fwd_body, meta_qkv_s, meta_out_s),
        spots,
        [frames_in, code_shift, gains, *qkv_s, *out_s],
        [tile(positions, width), tile(1, width), fixed(3, width)] + [ANY] * (len(qkv_s) + len(out_s)),
        [tile(positions, 3 * width), tile(positions, width), tile(heads_n, positions), tile(positions, width)]
        + [part_spec] * members,
        [
            shape_of(frames, positions, 3 * width),
            shape_of(frames, positions, width),
            shape_of(frames, heads_n, positions, dtype=F32),
            shape_of(frames, positions, width),
        ]
        + [shape_of(frames, part, width)] * members,
        [
            pltpu.VMEM((3, width, width), BF),
            pltpu.VMEM((1, width, width), BF),
            pltpu.VMEM((positions, width), BF),
            sems((2,)),
        ],
        grid=(frames,),
        flops=9 * 10**9,
    )
    packed_s, heads_s, lse_s, normed_s = result[:4]
    token_pieces = exchange(result[4:])

    tile_shapes = shape_of(tiles, rows_tile, width)
    packed_t, heads_t, lse_t, normed_t, tokens_t, resid_two, third = call(
        functools.partial(temporal_fwd_body, meta_t),
        spots,
        [*token_pieces, gains, *all_t],
        [piece_spec] * members + [fixed(3, width)] + [ANY] * len(all_t),
        [tile(rows_tile, 3 * width), tile(rows_tile, width), tile(heads_n, rows_tile)]
        + [tile(rows_tile, width)] * 4,
        [
            shape_of(tiles, rows_tile, 3 * width),
            tile_shapes,
            shape_of(tiles, heads_n, rows_tile, dtype=F32),
            tile_shapes,
            tile_shapes,
            shape_of(tiles, rows_tile, width, dtype=F32),
            tile_shapes,
        ],
        [pltpu.VMEM((4, width, width), BF), pltpu.VMEM((FPV, spot, width), BF), sems((1,))],
        grid=(tiles,),
        flops=9 * 10**9,
    )

    grad_shape = shape_of(2, nz, 4, local_rows, width // 4)
    flat = lambda array: array.reshape(tokens, width)
    resid_now, dx = flat(resid_two), flat(resid_two)
    ffn_grads = []
    full32 = shape_of(tokens, width, dtype=F32)
    for group, (stacks, metas) in enumerate(ffn_groups):
        first, last = group == 0, group == len(ffn_groups) - 1
        ends = [full32] + [shape_of(frames, part, width)] * members if last else [full32, full32]
        outs = call(
            functools.partial(ffn_body, metas, first, last),
            spots,
            [flat(third), flat(cot_tiles), resid_now, dx, *stacks],
            [ANY] * (4 + len(stacks)),
            [ANY] * (4 + len(ends)),
            [grad_shape] * 4 + ends,
            [pltpu.VMEM((tokens, width), BF)] * 2
            + [pltpu.VMEM((width, tokens), BF)] * 2
            + [pltpu.VMEM((tokens, width), F32)] * 2
            + [pltpu.VMEM((4, width, width), BF)]
            + [pltpu.VMEM((tokens, width), BF)] * 2
            + [pltpu.VMEM((4, width, width), BF), sems((8,))],
            flops=26 * 10**9,
        )
        ffn_grads.append(outs[:4])
        if last:
            dx, block_pieces = outs[4], outs[5:]
        else:
            resid_now, dx = outs[4], outs[5]

    def reduced(parts, kind):
        return reduce_grads([[parts[0], parts[1]], [parts[2], parts[3]]], kind)

    quarters = {"ffn0": reduced(ffn_grads[0], "xyz"), "ffn1": reduced(ffn_grads[1], "yzx")}

    block_pieces = exchange(block_pieces)
    join = functools.partial(
        call,
        join_body,
        spots,
        in_specs=[ANY] * members,
        out_specs=ANY,
        out_shape=shape_of(frames, positions, width),
        scratch=[sems((members,))],
    )
    block_out = join(block_pieces)

    outs = call(
        functools.partial(temporal_bwd_body, meta_t),
        spots,
        [dx.reshape(resid_two.shape), cot_tiles, resid_two, tokens_t, packed_t, heads_t, lse_t, gains, *all_t],
        [tile(rows_tile, width)] * 4
        + [tile(rows_tile, 3 * width), tile(rows_tile, width), tile(heads_n, rows_tile), fixed(3, width)]
        + [ANY] * len(all_t),
        [tile(rows_tile, width), tile(rows_tile, 3 * width), fixed(2, width)] + [piece_spec] * members,
        [tile_shapes, shape_of(tiles, rows_tile, 3 * width), shape_of(2, width, dtype=F32)]
        + [shape_of(frames, part, width)] * members,
        [
            pltpu.VMEM((4, width, width), BF),
            pltpu.VMEM((rows_tile, width), BF),
            pltpu.VMEM((FPV, spot, width), BF),
            sems((1,)),
        ],
        grid=(tiles,),
        flops=10 * 10**9,
    )
    branch_t, grad_t, gains_two = outs[:3]
    grad_pieces = exchange(outs[3:])

    def weight_grads(normed, heads, grad, branch):
        return call(
            weight_grad_body,
            spots,
            [flat(normed), flat(heads), grad.reshape(tokens, 3 * width), flat(branch)],
            [ANY] * 4,
            [ANY] * 4,
            [grad_shape] * 4,
            [pltpu.VMEM((tokens, width), BF)] * 2
            + [pltpu.VMEM((tokens, 3 * width), BF), pltpu.VMEM((tokens, width), BF)]
            + [pltpu.VMEM((width, tokens), BF)] * 2
            + [pltpu.VMEM((4, width, width), BF), sems((5,))],
            flops=9 * 10**9,
        )

    quarters["attn1"] = reduced(weight_grads(normed_t, heads_t, grad_t, branch_t), "xyz")

    branch_s, grad_s, input_grad, gain_one, columns = call(
        functools.partial(spatial_bwd_body, meta_qkv_s, meta_out_s),
        spots,
        [*grad_pieces, frames_in, code_shift, packed_s, heads_s, lse_s, gains, *qkv_s, *out_s],
        [part_spec] * members
        + [tile(positions, width), tile(1, width), tile(positions, 3 * width), tile(positions, width)]
        + [tile(heads_n, positions), fixed(3, width)]
        + [ANY] * (len(qkv_s) + len(out_s)),
        [tile(positions, width), tile(positions, 3 * width), tile(positions, width), fixed(1, width), tile(1, width)],
        [
            shape_of(frames, positions, width),
            shape_of(frames, positions, 3 * width),
            shape_of(frames, positions, width),
            shape_of(1, width, dtype=F32),
            shape_of(frames, 1, width, dtype=F32),
        ],
        [
            pltpu.VMEM((3, width, width), BF),
            pltpu.VMEM((1, width, width), BF),
            pltpu.VMEM((positions, width), BF),
            sems((2,)),
        ],
        grid=(frames,),
        flops=10 * 10**9,
    )
    quarters["attn0"] = reduced(weight_grads(normed_s, heads_s, grad_s, branch_s), "yzx")

    table_grad = jnp.dot(
        onehot.astype(F32).T, columns[:, 0, :], precision=lax.Precision.HIGHEST
    )
    small_grad = lax.psum(
        jnp.concatenate([gain_one, gains_two, table_grad], axis=0), ("seq", "grp")
    )

    squares = sum(jnp.sum(jnp.square(q.astype(F32))) for q in quarters.values())
    total_squares = lax.psum(squares, ("seq", "grp")) + jnp.sum(small_grad * small_grad)
    grad_norm = jnp.sqrt(total_squares)
    clip_factor = 1.0 / jnp.maximum(grad_norm, 1.0)
    shared = {name: share_quarters(q) for name, q in quarters.items()}

    def updated(lots, pick, index, master, first, second):
        piece = lambda lot: pl.BlockSpec((1, local_rows, width // 4), lambda m, b, *_: (index(lot, m, b), 0, 0))
        block = pl.BlockSpec((1, local_rows, width), lambda m, b, *_: (m, 0, b))
        return call(
            functools.partial(update_body, pick),
            (place, clip_factor.reshape(1)),
            [*lots[0], *lots[1], master, first, second],
            [piece(0)] * 4 + [piece(1)] * 4 + [block] * 3,
            [block] * 3,
            [shape_of(*master.shape, dtype=F32)] * 3,
            [],
            grid=(2, master.shape[2] // width),
            scalars=2,
        )

    attn_new = updated(
        [shared["attn0"], shared["attn1"]],
        lambda m, b: m,
        lambda lot, m, b: jnp.where(m == lot, b, 3 if lot == 0 else 0),
        attn_master,
        attn_first,
        attn_second,
    )
    ffn_new = updated(
        [shared["ffn0"], shared["ffn1"]],
        lambda m, b: b // 2,
        lambda lot, m, b: m * 2 + b % 2,
        ffn_master,
        ffn_first,
        ffn_second,
    )
    small_decay = jnp.where(jnp.arange(3 + CODES)[:, None] >= 3, decay_rate, 0.0)
    small_cols = small_master.shape[1]
    small_mine = lax.dynamic_slice_in_dim(small_grad, seq * small_cols, small_cols, 1)
    small_new = update(
        small_master, small_first, small_second, small_mine * clip_factor, rate_small, small_decay
    )
    return (block_out, input_grad, grad_norm, *attn_new, *ffn_new, *small_new)


def solution(mesh):
    token = P(("grp", "seq"), None, None)
    matrix = P(None, "seq", None)
    small = P(None, "seq")
    return jax.shard_map(
        shards,
        mesh=mesh,
        in_specs=(token, P(("grp", "seq")), token) + (matrix,) * 6 + (small,) * 3,
        out_specs=(token, token, P()) + (matrix,) * 6 + (small,) * 3,
        check_vma=False,
    )
```

time: 2170 us -> 963 us (0.44)
  waiting for transfers between devices: 1260 us -> 344 us
  Pallas kernels: 0 us -> 362 us
  matrix products: 295 us -> 0.46 us
  blocking collectives: 246 us -> 41.2 us
  other arithmetic: 199 us -> 38.6 us
  starting transfers between devices: 7.74 us -> 148 us
  local copies, waits for them, and re-layouts: 131 us -> 16 us
    reduce_scatter x5 -> x0, waiting for transfers between devices: 816 us -> none  [the longest x1 542 us: shards(): lax.psum_scatter(grad_attn, 'seq', scatter_dimension=1, tiled=True)]
    pallas_call x0 -> x12, Pallas kernels: none -> 362 us  [call(): pl.pallas_call(body, out_shape=out_shape, grid_spec=pltpu.PrefetchScalarG...]
    ppermute x0 -> x109, waiting for transfers between devices: none -> 344 us  [the longest x69 239 us: swap(): return lax.ppermute(value, axis, [(i, i ^ bit) for i in range(size)])]
    dot_general x32 -> x2, matrix products: 295 us -> 0.46 us  [the longest x1 0.27 us: shards(): jnp.dot(onehot.astype(F32).T, columns[:, 0, :], precision=lax.Precision.H...]
    all_gather x8 -> x0, waiting for transfers between devices: 293 us -> none  [the longest x1 194 us: shards(): lax.all_gather(attn_master.astype(jnp.bfloat16), 'seq', axis=1, tiled=True)]
    all_to_all x2 -> x0, blocking collectives: 173 us -> none  [the longest x1 100 us: shards(): lax.all_to_all(heads_t_grad, 'seq', split_axis=1, concat_axis=0, tiled=True)]
    ppermute x0 -> x109, starting transfers between devices: none -> 148 us  [the longest x69 73.5 us: swap(): return lax.ppermute(value, axis, [(i, i ^ bit) for i in range(size)])]
    all_to_all x2 -> x0, waiting for transfers between devices: 148 us -> none  [the longest x1 90 us: shards(): lax.all_to_all(normed_two, 'seq', split_axis=1, concat_axis=0, tiled=True)]
  transfers between devices with their start and end apart: 15 -> 109, of which waited for: 13 -> 30; matrix products, arithmetic and copies ran while one was open for 23% -> 5% of each run, Pallas kernels for 0% -> 36%
where the time goes in v1:
time: 963 us; the launch traced here: 958 us
  Pallas kernels  362 us (38%)
  waiting for transfers between devices  344 us (36%)
  starting transfers between devices  148 us (15%)
  blocking collectives  41.2 us (4%)
  other arithmetic  38.6 us (4%)
  local copies, waits for them, and re-layouts  16 us (2%)
    pallas_call x12, Pallas kernels, call(): pl.pallas_call(body, out_shape=out_shape, grid_spec=pltpu.PrefetchScalarG...  362 us
    ppermute x69, waiting for transfers between devices, swap(): return lax.ppermute(value, axis, [(i, i ^ bit) for i in range(size)])  239 us
    ppermute x33, waiting for transfers between devices, shift_z(): lax.ppermute(value, 'seq', [(i, (i + 2 * step) % size) for i in range(siz...  105 us
    ppermute x69, starting transfers between devices, swap(): return lax.ppermute(value, axis, [(i, i ^ bit) for i in range(size)])  73.5 us
    ppermute x33, starting transfers between devices, shift_z(): lax.ppermute(value, 'seq', [(i, (i + 2 * step) % size) for i in range(siz...  62 us
    psum x1, blocking collectives, shards(): lax.psum(squares, ('seq', 'grp')) + jnp.sum(small_grad * small_grad)  41.2 us
  transfers between devices with their start and end apart: 109, of which 30 were waited for; matrix products, arithmetic and copies ran while one was open for 5% of the time, Pallas kernels for 36%

profile of v1, /device:TPU:0, one launch (start us, length us, event | category | flops | bytes accessed | tf_op | source)
XLA Modules:
  0.0 958.1 jit_solution(15394918064610209737)
XLA Ops:
  1.9 3.0 collective-permute-start
  6.5 3.0 collective-permute-start.3
  10.8 2.5 convert.49
  17.4 3.6 collective-permute-start.5
  22.0 4.3 collective-permute-start.40
  29.1 13.9 %collective-permute-done.13 = bf16[1,128,256]{2,1,0:T(8,128)(2,1)S(1)} collective-permute-done((bf16[1,128,256]{2,1,0:T(8,128)(2,1)S(1)}, bf16[1,128,256]{2,1,0:T(8,128)(2,1)S(1)}, u32[]{:S(2)}, u32[]{:S(2)}) %collective-permute-start.13) | collective-permute-done | bytes 65568 | tf_op jit(solution)/shard_map/ppermute | solution.py:47
  43.0 7.7 collective-permute-done.14
  52.1 2.7 collective-permute-start.27
  63.2 10.1 %collective-permute-done.27 = bf16[4,128,256]{2,1,0:T(8,128)(2,1)} collective-permute-done((bf16[4,128,256]{2,1,0:T(8,128)(2,1)}, bf16[4,128,256]{2,1,0:T(8,128)(2,1)}, u32[]{:S(2)}, u32[]{:S(2)}) %collective-permute-start.27) | collective-permute-done | bytes 262176 | tf_op jit(solution)/shard_map/ppermute | solution.py:47
  73.3 3.9 collective-permute-start.9
  77.2 2.5 constant_dynamic-slice_fusion
  81.3 18.2 %collective-permute-start.37 = (bf16[4,64,1024]{2,1,0:T(8,128)(2,1)S(1)}, bf16[4,64,1024]{2,1,0:T(8,128)(2,1)S(1)}, u32[]{:S(2)}, u32[]{:S(2)}) collective-permute-start(bf16[4,64,1024]{2,1,0:T(8,128)(2,1)S(1)} %get-tuple-element.150), channel_id=1, source_target_pairs={{0,8},{4,12},{8,0},{12,4},{16,24},{20,28},{24,16},{28,20},{1,9},{5... | collective-permute-start | bytes 1572872 | tf_op jit(solution)/shard_map/ppermute | solution.py:42
  99.6 3.6 collective-permute-done.8
  103.2 5.2 collective-permute-start.38
  108.4 3.2 collective-permute-done.9
  116.1 26.5 %collective-permute-done.37.refs_2_ = bf16[4,64,1024]{2,1,0:T(8,128)(2,1)S(1)} collective-permute-done((bf16[4,64,1024]{2,1,0:T(8,128)(2,1)S(1)}, bf16[4,64,1024]{2,1,0:T(8,128)(2,1)S(1)}, u32[]{:S(2)}, u32[]{:S(2)}) %collective-permute-start.37) | collective-permute-done | bytes 524320 | tf_op jit(solution)/shard_map/ppermute | solution.py:42
  142.8 14.6 %collective-permute-done.38.refs_3_ = bf16[4,64,1024]{2,1,0:T(8,128)(2,1)S(1)} collective-permute-done((bf16[4,64,1024]{2,1,0:T(8,128)(2,1)S(1)}, bf16[4,64,1024]{2,1,0:T(8,128)(2,1)S(1)}, u32[]{:S(2)}, u32[]{:S(2)}) %collective-permute-start.38) | collective-permute-done | bytes 524320 | tf_op jit(solution)/shard_map/ppermute | solution.py:42
  161.1 6.6 collective-permute-done.51
  174.1 12.6 %collective-permute-done.42.refs_5_ = bf16[4,4,128,256]{3,2,1,0:T(8,128)(2,1)} collective-permute-done((bf16[4,4,128,256]{3,2,1,0:T(8,128)(2,1)S(1)}, bf16[4,4,128,256]{3,2,1,0:T(8,128)(2,1)}, u32[]{:S(2)}, u32[]{:S(2)}) %collective-permute-start.42) | collective-permute-done | bytes 1048608 | tf_op jit(solution)/shard_map/ppermute | solution.py:42
  187.2 6.6 collective-permute-done.43.refs_6_
  194.5 14.0 %collective-permute-done.29.refs_6_.refs_9_ = bf16[4,4,128,256]{3,2,1,0:T(8,128)(2,1)} collective-permute-done((bf16[4,4,128,256]{3,2,1,0:T(8,128)(2,1)S(1)}, bf16[4,4,128,256]{3,2,1,0:T(8,128)(2,1)}, u32[]{:S(2)}, u32[]{:S(2)}) %collective-permute-start.29) | collective-permute-done | bytes 1048608 | tf_op jit(solution)/shard_map/ppermute | solution.py:42
  210.6 5.7 collective-permute-done.30.refs_7_.refs_10_
  220.9 17.9 %collective-permute-done.31.refs_8_.refs_11_ = bf16[4,4,128,256]{3,2,1,0:T(8,128)(2,1)} collective-permute-done((bf16[4,4,128,256]{3,2,1,0:T(8,128)(2,1)}, bf16[4,4,128,256]{3,2,1,0:T(8,128)(2,1)}, u32[]{:S(2)}, u32[]{:S(2)}) %collective-permute-start.31) | collective-permute-done | bytes 1048608 | tf_op jit(solution)/shard_map/ppermute | solution.py:42
  240.3 35.8 %shard_map.211 = (bf16[4,256,3072]{2,1,0:T(8,128)(2,1)}, bf16[4,256,1024]{2,1,0:T(8,128)(2,1)}, f32[4,16,256]{2,1,0:T(8,128)}, bf16[4,256,1024]{2,1,0:T(8,128)(2...) custom-call(s32[5]{0:T(128)} %stack.141.place, ...), custom_call_target="tpu_custom_call" | custom-call | flops 8999999488 | bytes 16777216 | tf_op jit(solution)/shard_map/pallas_call | solution.py:581
  276.6 3.0 collective-permute-start.25
  279.6 27.7 %collective-permute-done.23.refs_1_ = bf16[4,64,1024]{2,1,0:T(8,128)(2,1)S(1)} collective-permute-done((bf16[4,64,1024]{2,1,0:T(8,128)(2,1)}, bf16[4,64,1024]{2,1,0:T(8,128)(2,1)S(1)}, u32[]{:S(2)}, u32[]{:S(2)}) %collective-permute-start.23) | collective-permute-done | bytes 524320 | tf_op jit(solution)/shard_map/ppermute | solution.py:42
  307.9 4.6 shard_map.213.refs_1_
  312.5 37.3 %shard_map.212 = (bf16[4,256,3072]{2,1,0:T(8,128)(2,1)}, bf16[4,256,1024]{2,1,0:T(8,128)(2,1)}, f32[4,16,256]{2,1,0:T(8,128)}, bf16[4,256,1024]{2,1,0:T(8,128)(2...) custom-call(s32[5]{0:T(128)} %stack.141.place, ...), custom_call_target="tpu_custom_call" | custom-call | flops 8999999488 | bytes 16777216 | tf_op jit(solution)/shard_map/pallas_call | solution.py:581
  350.4 40.5 %shard_map.214 = (bf16[2,4,4,128,256]{4,3,2,1,0:T(8,128)(2,1)}, bf16[2,4,4,128,256]{4,3,2,1,0:T(8,128)(2,1)}, bf16[2,4,4,128,256]{4,3,2,1,0:T(8,128)(2,1)}, bf16...) custom-call(s32[5]{0:T(128)} %stack.141.place, bf16[1024,1024]{1,0:T(8,128)(2,1)} %bitcast.204, ...), custom_call_target="tpu_custom_call" | custom-call | flops 25999998976 | bytes 16777216 | tf_op jit(solution)/shard_map/pallas_call | solution.py:581
  391.4 41.3 %shard_map.215 = (bf16[2,4,4,128,256]{4,3,2,1,0:T(8,128)(2,1)}, bf16[2,4,4,128,256]{4,3,2,1,0:T(8,128)(2,1)}, bf16[2,4,4,128,256]{4,3,2,1,0:T(8,128)(2,1)}, bf16...) custom-call(s32[5]{0:T(128)} %stack.141.place, ...), custom_call_target="tpu_custom_call" | custom-call | flops 25999998976 | bytes 16777216 | tf_op jit(solution)/shard_map/pallas_call | solution.py:581
  432.8 41.9 %shard_map.217 = (bf16[4,256,1024]{2,1,0:T(8,128)(2,1)}, bf16[4,256,3072]{2,1,0:T(8,128)(2,1)}, f32[2,1024]{1,0:T(2,128)}, bf16[4,64,1024]{2,1,0:T(8,128)(2,1)},...) custom-call(s32[5]{0:T(128)} %stack.141.place, ...), custom_call_target="tpu_custom_call" | custom-call | flops 10000000000 | bytes 16777216 | tf_op jit(solution)/shard_map/pallas_call | solution.py:581
  478.3 15.0 %shard_map.219 = (bf16[2,4,4,128,256]{4,3,2,1,0:T(8,128)(2,1)}, bf16[2,4,4,128,256]{4,3,2,1,0:T(8,128)(2,1)}, bf16[2,4,4,128,256]{4,3,2,1,0:T(8,128)(2,1)}, bf16[2,4,4,128,256]{4,3,2,1,0:T(8,128)(2,1)}) custom-call(s32[5]{0:T(128)} %stack.141.place, bf16[1024,1024]{1,0:T(8,128)(2,1)} %bitcast.203, bf16[1024,1024]{1,0:T(8,128)(2,1)} %bitcast.202, ...), custom_call_target="tpu_custom_call" | custom-call | flops 8999999488 | bytes 16777216 | tf_op jit(solution)/shard_map/pallas_call | solution.py:581
  494.0 7.3 collective-permute-done.60.refs_3_
  502.1 38.0 %shard_map.218 = (bf16[4,256,1024]{2,1,0:T(8,128)(2,1)}, bf16[4,256,3072]{2,1,0:T(8,128)(2,1)}, bf16[4,256,1024]{2,1,0:T(8,128)(2,1)}, f32[1,1024]{1,0:T(1,128)}, f32[4,1,1024]{2,1,0:T(1,128)}) custom-call(s32[5]{0:T(128)} %stack.141.place, bf16[4,64,1024]{2,1,0:T(8,128)(2,1)} %get-tuple-element.85.refs_0_, bf16[4,64,1024]{2,1,0:T(8,128)(2,1)} %copy-done.51, ...), custom_call_target="tpu_custom_call" | custom-call | flops 10000000000 | bytes 16777216 | tf_op jit(solution)/shard_map/pallas_call | solution.py:581
  540.1 15.2 %shard_map.220 = (bf16[2,4,4,128,256]{4,3,2,1,0:T(8,128)(2,1)}, bf16[2,4,4,128,256]{4,3,2,1,0:T(8,128)(2,1)}, bf16[2,4,4,128,256]{4,3,2,1,0:T(8,128)(2,1)}, bf16[2,4,4,128,256]{4,3,2,1,0:T(8,128)(2,1)}) custom-call(s32[5]{0:T(128)} %stack.141.place, bf16[1024,1024]{1,0:T(8,128)(2,1)} %bitcast.201, bf16[1024,1024]{1,0:T(8,128)(2,1)} %bitcast.200, ...), custom_call_target="tpu_custom_call" | custom-call | flops 8999999488 | bytes 16777216 | tf_op jit(solution)/shard_map/pallas_call | solution.py:581
  555.9 2.5 add_convert_fusion.8
  562.7 2.5 add_convert_fusion.3
  566.8 2.4 add_convert_fusion.6
  570.8 2.5 add_convert_fusion.1
  574.2 17.1 %collective-permute-done.74 = bf16[4,4,128,256]{3,2,1,0:T(8,128)(2,1)S(1)} collective-permute-done((bf16[4,4,128,256]{3,2,1,0:T(8,128)(2,1)S(1)}, bf16[4,4,128,256]{3,2,1,0:T(8,128)(2,1)S(1)}, u32[]{:S(2)}, u32[]{:S(2)}) %collective-permute-start.74) | collective-permute-done | bytes 1048608 | tf_op jit(solution)/shard_map/ppermute | solution.py:42
  594.7 18.3 %collective-permute-done.69 = bf16[4,4,128,256]{3,2,1,0:T(8,128)(2,1)S(1)} collective-permute-done((bf16[4,4,128,256]{3,2,1,0:T(8,128)(2,1)S(1)}, bf16[4,4,128,256]{3,2,1,0:T(8,128)(2,1)S(1)}, u32[]{:S(2)}, u32[]{:S(2)}) %collective-permute-start.69) | collective-permute-done | bytes 1048608 | tf_op jit(solution)/shard_map/ppermute | solution.py:42
  617.0 5.9 collective-permute-done.77
  628.1 21.0 %collective-permute-done.92 = bf16[4,4,128,256]{3,2,1,0:T(8,128)(2,1)S(1)} collective-permute-done((bf16[4,4,128,256]{3,2,1,0:T(8,128)(2,1)S(1)}, bf16[4,4,128,256]{3,2,1,0:T(8,128)(2,1)S(1)}, u32[]{:S(2)}, u32[]{:S(2)}) %collective-permute-start.92) | collective-permute-done | bytes 1048608 | tf_op jit(solution)/shard_map/ppermute | solution.py:42
  650.9 31.8 %collective-permute-done.87 = bf16[4,4,128,256]{3,2,1,0:T(8,128)(2,1)S(1)} collective-permute-done((bf16[4,4,128,256]{3,2,1,0:T(8,128)(2,1)S(1)}, bf16[4,4,128,256]{3,2,1,0:T(8,128)(2,1)S(1)}, u32[]{:S(2)}, u32[]{:S(2)}) %collective-permute-start.87) | collective-permute-done | bytes 1048608 | tf_op jit(solution)/shard_map/ppermute | solution.py:42
  683.4 4.2 collective-permute-start.94
  688.9 5.0 collective-permute-done.93
  695.4 5.8 collective-permute-done.94
  701.1 5.6 collective-permute-start.70
  706.8 3.4 collective-permute-start.71
  715.0 16.0 %collective-permute-done.71 = bf16[4,128,256]{2,1,0:T(8,128)(2,1)S(1)} collective-permute-done((bf16[4,128,256]{2,1,0:T(8,128)(2,1)S(1)}, bf16[4,128,256]{2,1,0:T(8,128)(2,1)S(1)}, u32[]{:S(2)}, u32[]{:S(2)}) %collective-permute-start.71) | collective-permute-done | bytes 262176 | tf_op jit(solution)/shard_map/ppermute | solution.py:47
  731.6 11.7 %collective-permute-start.65 = (bf16[4,128,256]{2,1,0:T(8,128)(2,1)S(1)}, bf16[4,128,256]{2,1,0:T(8,128)(2,1)S(1)}, u32[]{:S(2)}, u32[]{:S(2)}) collective-permute-start(bf16[4,128,256]{2,1,0:T(8,128)(2,1)S(1)} %get-tuple-element.174), channel_id=1, source_target_pairs={{0,8},{4,12},{8,16},{12,20},{16,24},{20,28},{24,0},{28,4},{1,9},{5... | collective-permute-start | bytes 786440 | tf_op jit(solution)/shard_map/ppermute | solution.py:47
  743.7 2.9 collective-permute-start.66
  746.6 12.5 %collective-permute-done.89 = bf16[4,128,256]{2,1,0:T(8,128)(2,1)S(1)} collective-permute-done((bf16[4,128,256]{2,1,0:T(8,128)(2,1)S(1)}, bf16[4,128,256]{2,1,0:T(8,128)(2,1)S(1)}, u32[]{:S(2)}, u32[]{:S(2)}) %collective-permute-start.89) | collective-permute-done | bytes 262176 | tf_op jit(solution)/shard_map/ppermute | solution.py:47
  759.1 8.5 collective-permute-start.83
  770.7 10.8 %collective-permute-done.66 = bf16[4,128,256]{2,1,0:T(8,128)(2,1)S(1)} collective-permute-done((bf16[4,128,256]{2,1,0:T(8,128)(2,1)S(1)}, bf16[4,128,256]{2,1,0:T(8,128)(2,1)S(1)}, u32[]{:S(2)}, u32[]{:S(2)}) %collective-permute-start.66) | collective-permute-done | bytes 262176 | tf_op jit(solution)/shard_map/ppermute | solution.py:47
  781.6 2.5 collective-permute-start.56
  784.1 4.3 collective-permute-start.57
  789.7 3.1 collective-permute-done.84
  795.6 6.3 collective-permute-done.56.refs_2_
  802.4 10.7 %collective-permute-done.57.refs_3_ = bf16[4,64,1024]{2,1,0:T(8,128)(2,1)S(1)} collective-permute-done((bf16[4,64,1024]{2,1,0:T(8,128)(2,1)S(1)}, bf16[4,64,1024]{2,1,0:T(8,128)(2,1)S(1)}, u32[]{:S(2)}, u32[]{:S(2)}) %collective-permute-start.57) | collective-permute-done | bytes 524320 | tf_op jit(solution)/shard_map/ppermute | solution.py:42
  817.2 65.3 %shard_map.216 = bf16[4,256,1024]{2,1,0:T(8,128)(2,1)} custom-call(s32[5]{0:T(128)} %stack.141.place, bf16[4,64,1024]{2,1,0:T(8,128)(2,1)} %get-tuple-element.76.refs_0_, bf16[4,64,1024]{2,1,0:T(8,128)(2,1)} %copy-done.20, bf16[4,64,1024]{2,1,0:T(8,128)(2,1)} %copy-done.22, bf16[4,64,1024]{2,1,0:T(8,128)(2,1)} %copy-done.23), custom_call_target="tpu_custom_call" | custom-call | bytes 16777216 | tf_op jit(solution)/shard_map/pallas_call | solution.py:581
  882.6 41.2 %all-reduce = (f32[]{:T(128)}, f32[11,1024]{1,0:T(8,128)S(1)}) all-reduce(f32[]{:T(128)S(6)} %add.245, f32[11,1024]{1,0:T(8,128)S(1)} %pad_maximum_fusion.5), channel_id=1, replica_groups=mesh['seq'=8,'grp'=4] {'seq','grp'}, use_global_device_ids=true, to_apply=%region_4.5 | all-reduce | flops 11265 | bytes 90120 | tf_op jit(solution)/shard_map/psum | solution.py:849
  927.0 13.9 %shard_map.222 = (f32[2,128,4096]{2,1,0:T(8,128)}, f32[2,128,4096]{2,1,0:T(8,128)}, f32[2,128,4096]{2,1,0:T(8,128)}) custom-call(s32[5]{0:T(128)} %stack.141.place, f32[1]{0:T(128)} %bitcast.86.clip, bf16[4,128,256]{2,1,0:T(8,128)(2,1)} %copy-done.14, bf16[4,128,256]{2,1,0:T(8,128)(2,1)} %copy-done.29, ...), custom_call_target="tpu_custom_call" | custom-call | bytes 16777216 | tf_op jit(solution)/shard_map/pallas_call | solution.py:581
  943.2 13.5 %shard_map.221 = (f32[2,128,4096]{2,1,0:T(8,128)}, f32[2,128,4096]{2,1,0:T(8,128)}, f32[2,128,4096]{2,1,0:T(8,128)}) custom-call(s32[5]{0:T(128)} %stack.141.place, f32[1]{0:T(128)} %bitcast.86.clip, bf16[4,128,256]{2,1,0:T(8,128)(2,1)} %copy-done.17, bf16[4,128,256]{2,1,0:T(8,128)(2,1)} %copy-done.30, bf16[4,128,256]{2,1,0:T(8,128)(2,1)} %copy-done.32, ...), custom_call_target="tpu_custom_call" | custom-call | bytes 16777216 | tf_op jit(solution)/shard_map/pallas_call | solution.py:581
  (365 shorter events, 100.5 us)
Async XLA Ops:
  21.1 33.8 %collective-permute-start.39 = (bf16[4,128,256]{2,1,0:T(8,128)(2,1)}, bf16[4,128,256]{2,1,0:T(8,128)(2,1)}, u32[]{:S(2)}, u32[]{:S(2)}) collective-permute-start(bf16[4,128,256]{2,1,0:T(8,128)(2,1)} %fusion.31), channel_id=1, source_target_pairs={{0,8},{4,12},{8,16},{12,20},{16,24},{20,28},{24,0},{28,4},{1,9},{5... | collective-permute-start | bytes 786440 | tf_op jit(solution)/shard_map/ppermute | solution.py:47
  22.0 35.4 %collective-permute-start.40 = (bf16[4,128,256]{2,1,0:T(8,128)(2,1)}, bf16[4,128,256]{2,1,0:T(8,128)(2,1)}, u32[]{:S(2)}, u32[]{:S(2)}) collective-permute-start(bf16[4,128,256]{2,1,0:T(8,128)(2,1)} %fusion.31), channel_id=1, source_target_pairs={{0,16},{4,20},{8,24},{12,28},{16,0},{20,4},{24,8},{28,12},{1,17},{... | collective-permute-start | bytes 786440 | tf_op jit(solution)/shard_map/ppermute | solution.py:47
  26.2 32.6 %collective-permute-start.41 = (bf16[4,128,256]{2,1,0:T(8,128)(2,1)}, bf16[4,128,256]{2,1,0:T(8,128)(2,1)}, u32[]{:S(2)}, u32[]{:S(2)}) collective-permute-start(bf16[4,128,256]{2,1,0:T(8,128)(2,1)} %fusion.31), channel_id=1, source_target_pairs={{0,24},{4,28},{8,0},{12,4},{16,8},{20,12},{24,16},{28,20},{1,25},{... | collective-permute-start | bytes 786440 | tf_op jit(solution)/shard_map/ppermute | solution.py:47
  62.1 37.3 %collective-permute-start.7 = (bf16[3,128,512]{2,1,0:T(8,128)(2,1)}, bf16[3,128,512]{2,1,0:T(8,128)(2,1)}, u32[]{:S(2)}, u32[]{:S(2)}) collective-permute-start(bf16[3,128,512]{2,1,0:T(8,128)(2,1)} %fusion.28), channel_id=1, source_target_pairs={{0,8},{4,12},{8,16},{12,20},{16,24},{20,28},{24,0},{28,4},{1,9},{5... | collective-permute-start | bytes 1179656 | tf_op jit(solution)/shard_map/ppermute | solution.py:47
  73.3 29.9 %collective-permute-start.8 = (bf16[3,128,512]{2,1,0:T(8,128)(2,1)}, bf16[3,128,512]{2,1,0:T(8,128)(2,1)S(1)}, u32[]{:S(2)}, u32[]{:S(2)}) collective-permute-start(bf16[3,128,512]{2,1,0:T(8,128)(2,1)} %fusion.28), channel_id=1, source_target_pairs={{0,16},{4,20},{8,24},{12,28},{16,0},{20,4},{24,8},{28,12},{1,17},{... | collective-permute-start | bytes 1179656 | tf_op jit(solution)/shard_map/ppermute | solution.py:47
  73.3 38.2 %collective-permute-start.9 = (bf16[3,128,512]{2,1,0:T(8,128)(2,1)}, bf16[3,128,512]{2,1,0:T(8,128)(2,1)S(1)}, u32[]{:S(2)}, u32[]{:S(2)}) collective-permute-start(bf16[3,128,512]{2,1,0:T(8,128)(2,1)} %fusion.28), channel_id=1, source_target_pairs={{0,24},{4,28},{8,0},{12,4},{16,8},{20,12},{24,16},{28,20},{1,25},{... | collective-permute-start | bytes 1179656 | tf_op jit(solution)/shard_map/ppermute | solution.py:47
  79.8 36.2 %collective-permute-start.36 = (bf16[4,64,1024]{2,1,0:T(8,128)(2,1)S(1)}, bf16[4,64,1024]{2,1,0:T(8,128)(2,1)S(1)}, u32[]{:S(2)}, u32[]{:S(2)}) collective-permute-start(bf16[4,64,1024]{2,1,0:T(8,128)(2,1)S(1)} %get-tuple-element.148), channel_id=1, source_target_pairs={{0,4},{4,0},{8,12},{12,8},{16,20},{20,16},{24,28},{28,24},{1,5},{5... | collective-permute-start | bytes 1572872 | tf_op jit(solution)/shard_map/ppermute | solution.py:42
  81.3 61.3 %collective-permute-start.37 = (bf16[4,64,1024]{2,1,0:T(8,128)(2,1)S(1)}, bf16[4,64,1024]{2,1,0:T(8,128)(2,1)S(1)}, u32[]{:S(2)}, u32[]{:S(2)}) collective-permute-start(bf16[4,64,1024]{2,1,0:T(8,128)(2,1)S(1)} %get-tuple-element.150), channel_id=1, source_target_pairs={{0,8},{4,12},{8,0},{12,4},{16,24},{20,28},{24,16},{28,20},{1,9},{5... | collective-permute-start | bytes 1572872 | tf_op jit(solution)/shard_map/ppermute | solution.py:42
  103.2 54.3 %collective-permute-start.38 = (bf16[4,64,1024]{2,1,0:T(8,128)(2,1)S(1)}, bf16[4,64,1024]{2,1,0:T(8,128)(2,1)S(1)}, u32[]{:S(2)}, u32[]{:S(2)}) collective-permute-start(bf16[4,64,1024]{2,1,0:T(8,128)(2,1)S(1)} %get-tuple-element.147), channel_id=1, source_target_pairs={{0,12},{4,8},{8,4},{12,0},{16,28},{20,24},{24,20},{28,16},{1,13},{... | collective-permute-start | bytes 1572872 | tf_op jit(solution)/shard_map/ppermute | solution.py:42
  111.5 47.4 %collective-permute-start.49 = (bf16[4,128,512]{2,1,0:T(8,128)(2,1)S(1)}, bf16[4,128,512]{2,1,0:T(8,128)(2,1)S(1)}, u32[]{:S(2)}, u32[]{:S(2)}) collective-permute-start(bf16[4,128,512]{2,1,0:T(8,128)(2,1)S(1)} %fusion.8), channel_id=1, source_target_pairs={{0,8},{4,12},{8,16},{12,20},{16,24},{20,28},{24,0},{28,4},{1,9},{5... | collective-permute-start | bytes 1572872 | tf_op jit(solution)/shard_map/ppermute | solution.py:47
  114.5 59.2 %collective-permute-start.10 = (bf16[4,3,128,512]{3,2,1,0:T(8,128)(2,1)}, bf16[4,3,128,512]{3,2,1,0:T(8,128)(2,1)}, u32[]{:S(2)}, u32[]{:S(2)}) collective-permute-start(bf16[4,3,128,512]{3,2,1,0:T(8,128)(2,1)} %pad_maximum_fusion.1.refs_0_.refs_10_), channel_id=1, source_target_pairs={{0,4},{4,0},{8,12},{12,8},{16,20},{20,16},{24,28},{28,24},{1,5},{5... | collective-permute-start | bytes 4718600 | tf_op jit(solution)/shard_map/ppermute | solution.py:42
  116.0 44.5 %collective-permute-start.50 = (bf16[4,128,512]{2,1,0:T(8,128)(2,1)S(1)}, bf16[4,128,512]{2,1,0:T(8,128)(2,1)S(1)}, u32[]{:S(2)}, u32[]{:S(2)}) collective-permute-start(bf16[4,128,512]{2,1,0:T(8,128)(2,1)S(1)} %fusion.8), channel_id=1, source_target_pairs={{0,16},{4,20},{8,24},{12,28},{16,0},{20,4},{24,8},{28,12},{1,17},{... | collective-permute-start | bytes 1572872 | tf_op jit(solution)/shard_map/ppermute | solution.py:47
  142.5 25.2 %collective-permute-start.51 = (bf16[4,128,512]{2,1,0:T(8,128)(2,1)S(1)}, bf16[4,128,512]{2,1,0:T(8,128)(2,1)S(1)}, u32[]{:S(2)}, u32[]{:S(2)}) collective-permute-start(bf16[4,128,512]{2,1,0:T(8,128)(2,1)S(1)} %fusion.8), channel_id=1, source_target_pairs={{0,24},{4,28},{8,0},{12,4},{16,8},{20,12},{24,16},{28,20},{1,25},{... | collective-permute-start | bytes 1572872 | tf_op jit(solution)/shard_map/ppermute | solution.py:47
  160.5 26.2 %collective-permute-start.42 = (bf16[4,4,128,256]{3,2,1,0:T(8,128)(2,1)S(1)}, bf16[4,4,128,256]{3,2,1,0:T(8,128)(2,1)}, u32[]{:S(2)}, u32[]{:S(2)}) collective-permute-start(bf16[4,4,128,256]{3,2,1,0:T(8,128)(2,1)S(1)} %pad_maximum_fusion.3.refs_4_), channel_id=1, source_target_pairs={{0,4},{4,0},{8,12},{12,8},{16,20},{20,16},{24,28},{28,24},{1,5},{5... | collective-permute-start | bytes 3145736 | tf_op jit(solution)/shard_map/ppermute | solution.py:42
  167.7 26.1 %collective-permute-start.43 = (bf16[4,4,128,256]{3,2,1,0:T(8,128)(2,1)S(1)}, bf16[4,4,128,256]{3,2,1,0:T(8,128)(2,1)}, u32[]{:S(2)}, u32[]{:S(2)}) collective-permute-start(bf16[4,4,128,256]{3,2,1,0:T(8,128)(2,1)S(1)} %pad_maximum_fusion.3.refs_4_), channel_id=1, source_target_pairs={{0,2},{1,3},{2,0},{3,1},{4,6},{5,7},{6,4},{7,5},{8,10},{9,11},{10,... | collective-permute-start | bytes 3145736 | tf_op jit(solution)/shard_map/ppermute | solution.py:42
  171.9 36.6 %collective-permute-start.29 = (bf16[4,4,128,256]{3,2,1,0:T(8,128)(2,1)S(1)}, bf16[4,4,128,256]{3,2,1,0:T(8,128)(2,1)}, u32[]{:S(2)}, u32[]{:S(2)}) collective-permute-start(bf16[4,4,128,256]{3,2,1,0:T(8,128)(2,1)S(1)} %pad_maximum_fusion.2.refs_5_.refs_8_), channel_id=1, source_target_pairs={{0,4},{4,0},{8,12},{12,8},{16,20},{20,16},{24,28},{28,24},{1,5},{5... | collective-permute-start | bytes 3145736 | tf_op jit(solution)/shard_map/ppermute | solution.py:42
  173.5 44.3 %collective-permute-start.11 = (bf16[4,3,128,512]{3,2,1,0:T(8,128)(2,1)}, bf16[4,3,128,512]{3,2,1,0:T(8,128)(2,1)}, u32[]{:S(2)}, u32[]{:S(2)}) collective-permute-start(bf16[4,3,128,512]{3,2,1,0:T(8,128)(2,1)} %pad_maximum_fusion.1.refs_0_.refs_10_), channel_id=1, source_target_pairs={{0,1},{1,0},{2,3},{3,2},{4,5},{5,4},{6,7},{7,6},{8,9},{9,8},{10,11... | collective-permute-start | bytes 4718600 | tf_op jit(solution)/shard_map/ppermute | solution.py:42
  173.7 66.6 %collective-permute-start.12 = (bf16[4,3,128,512]{3,2,1,0:T(8,128)(2,1)}, bf16[4,3,128,512]{3,2,1,0:T(8,128)(2,1)}, u32[]{:S(2)}, u32[]{:S(2)}) collective-permute-start(bf16[4,3,128,512]{3,2,1,0:T(8,128)(2,1)} %collective-permute-done.10.refs_1_.refs_11_), channel_id=1, source_target_pairs={{0,1},{1,0},{2,3},{3,2},{4,5},{5,4},{6,7},{7,6},{8,9},{9,8},{10,11... | collective-permute-start | bytes 4718600 | tf_op jit(solution)/shard_map/ppermute | solution.py:42
  186.6 29.7 %collective-permute-start.30 = (bf16[4,4,128,256]{3,2,1,0:T(8,128)(2,1)S(1)}, bf16[4,4,128,256]{3,2,1,0:T(8,128)(2,1)}, u32[]{:S(2)}, u32[]{:S(2)}) collective-permute-start(bf16[4,4,128,256]{3,2,1,0:T(8,128)(2,1)S(1)} %pad_maximum_fusion.2.refs_5_.refs_8_), channel_id=1, source_target_pairs={{0,2},{1,3},{2,0},{3,1},{4,6},{5,7},{6,4},{7,5},{8,10},{9,11},{10,... | collective-permute-start | bytes 3145736 | tf_op jit(solution)/shard_map/ppermute | solution.py:42
  208.5 30.3 %collective-permute-start.31 = (bf16[4,4,128,256]{3,2,1,0:T(8,128)(2,1)}, bf16[4,4,128,256]{3,2,1,0:T(8,128)(2,1)}, u32[]{:S(2)}, u32[]{:S(2)}) collective-permute-start(bf16[4,4,128,256]{3,2,1,0:T(8,128)(2,1)} %collective-permute-done.29.refs_6_.refs_9_), channel_id=1, source_target_pairs={{0,2},{1,3},{2,0},{3,1},{4,6},{5,7},{6,4},{7,5},{8,10},{9,11},{10,... | collective-permute-start | bytes 3145736 | tf_op jit(solution)/shard_map/ppermute | solution.py:42
  216.3 60.3 %collective-permute-start.33 = (bf16[4,4,128,256]{3,2,1,0:T(8,128)(2,1)}, bf16[4,4,128,256]{3,2,1,0:T(8,128)(2,1)}, u32[]{:S(2)}, u32[]{:S(2)}) collective-permute-start(bf16[4,4,128,256]{3,2,1,0:T(8,128)(2,1)} %collective-permute-done.29.refs_6_.refs_9_), channel_id=1, source_target_pairs={{0,1},{1,0},{2,3},{3,2},{4,5},{5,4},{6,7},{7,6},{8,9},{9,8},{10,11... | collective-permute-start | bytes 3145736 | tf_op jit(solution)/shard_map/ppermute | solution.py:42
  216.3 59.7 %collective-permute-start.44 = (bf16[4,4,128,256]{3,2,1,0:T(8,128)(2,1)}, bf16[4,4,128,256]{3,2,1,0:T(8,128)(2,1)}, u32[]{:S(2)}, u32[]{:S(2)}) collective-permute-start(bf16[4,4,128,256]{3,2,1,0:T(8,128)(2,1)} %collective-permute-done.42.refs_5_), channel_id=1, source_target_pairs={{0,2},{1,3},{2,0},{3,1},{4,6},{5,7},{6,4},{7,5},{8,10},{9,11},{10,... | collective-permute-start | bytes 3145736 | tf_op jit(solution)/shard_map/ppermute | solution.py:42
  217.8 58.9 %collective-permute-start.34 = (bf16[4,4,128,256]{3,2,1,0:T(8,128)(2,1)}, bf16[4,4,128,256]{3,2,1,0:T(8,128)(2,1)}, u32[]{:S(2)}, u32[]{:S(2)}) collective-permute-start(bf16[4,4,128,256]{3,2,1,0:T(8,128)(2,1)} %collective-permute-done.30.refs_7_.refs_10_), channel_id=1, source_target_pairs={{0,1},{1,0},{2,3},{3,2},{4,5},{5,4},{6,7},{7,6},{8,9},{9,8},{10,11... | collective-permute-start | bytes 3145736 | tf_op jit(solution)/shard_map/ppermute | solution.py:42
  238.8 111.5 %collective-permute-start.52 = (bf16[4,4,128,512]{3,2,1,0:T(8,128)(2,1)S(1)}, bf16[4,4,128,512]{3,2,1,0:T(8,128)(2,1)}, u32[]{:S(2)}, u32[]{:S(2)}) collective-permute-start(bf16[4,4,128,512]{3,2,1,0:T(8,128)(2,1)S(1)} %pad_maximum_fusion.refs_4_), channel_id=1, source_target_pairs={{0,4},{4,0},{8,12},{12,8},{16,20},{20,16},{24,28},{28,24},{1,5},{5... | collective-permute-start | bytes 6291464 | tf_op jit(solution)/shard_map/ppermute | solution.py:42
  240.3 39.3 %collective-permute-start.35 = (bf16[4,4,128,256]{3,2,1,0:T(8,128)(2,1)}, bf16[4,4,128,256]{3,2,1,0:T(8,128)(2,1)}, u32[]{:S(2)}, u32[]{:S(2)}) collective-permute-start(bf16[4,4,128,256]{3,2,1,0:T(8,128)(2,1)} %collective-permute-done.31.refs_8_.refs_11_), channel_id=1, source_target_pairs={{0,1},{1,0},{2,3},{3,2},{4,5},{5,4},{6,7},{7,6},{8,9},{9,8},{10,11... | collective-permute-start | bytes 3145736 | tf_op jit(solution)/shard_map/ppermute | solution.py:42
  276.0 31.3 %collective-permute-start.23 = (bf16[4,64,1024]{2,1,0:T(8,128)(2,1)}, bf16[4,64,1024]{2,1,0:T(8,128)(2,1)S(1)}, u32[]{:S(2)}, u32[]{:S(2)}) collective-permute-start(bf16[4,64,1024]{2,1,0:T(8,128)(2,1)} %get-tuple-element.69), channel_id=1, source_target_pairs={{0,4},{4,0},{8,12},{12,8},{16,20},{20,16},{24,28},{28,24},{1,5},{5... | collective-permute-start | bytes 1572872 | tf_op jit(solution)/shard_map/ppermute | solution.py:42
  276.6 30.7 %collective-permute-start.24 = (bf16[4,64,1024]{2,1,0:T(8,128)(2,1)}, bf16[4,64,1024]{2,1,0:T(8,128)(2,1)}, u32[]{:S(2)}, u32[]{:S(2)}) collective-permute-start(bf16[4,64,1024]{2,1,0:T(8,128)(2,1)} %get-tuple-element.70), channel_id=1, source_target_pairs={{0,8},{4,12},{8,0},{12,4},{16,24},{20,28},{24,16},{28,20},{1,9},{5... | collective-permute-start | bytes 1572872 | tf_op jit(solution)/shard_map/ppermute | solution.py:42
  276.6 31.2 %collective-permute-start.25 = (bf16[4,64,1024]{2,1,0:T(8,128)(2,1)}, bf16[4,64,1024]{2,1,0:T(8,128)(2,1)}, u32[]{:S(2)}, u32[]{:S(2)}) collective-permute-start(bf16[4,64,1024]{2,1,0:T(8,128)(2,1)} %get-tuple-element.71), channel_id=1, source_target_pairs={{0,12},{4,8},{8,4},{12,0},{16,28},{20,24},{24,20},{28,16},{1,13},{... | collective-permute-start | bytes 1572872 | tf_op jit(solution)/shard_map/ppermute | solution.py:42
  279.6 70.2 %collective-permute-start.45 = (bf16[4,4,128,256]{3,2,1,0:T(8,128)(2,1)S(1)}, bf16[4,4,128,256]{3,2,1,0:T(8,128)(2,1)}, u32[]{:S(2)}, u32[]{:S(2)}) collective-permute-start(bf16[4,4,128,256]{3,2,1,0:T(8,128)(2,1)S(1)} %pad_maximum_fusion.3.refs_4_), channel_id=1, source_target_pairs={{0,1},{1,0},{2,3},{3,2},{4,5},{5,4},{6,7},{7,6},{8,9},{9,8},{10,11... | collective-permute-start | bytes 3145736 | tf_op jit(solution)/shard_map/ppermute | solution.py:42
  307.3 43.1 %collective-permute-start.46 = (bf16[4,4,128,256]{3,2,1,0:T(8,128)(2,1)}, bf16[4,4,128,256]{3,2,1,0:T(8,128)(2,1)}, u32[]{:S(2)}, u32[]{:S(2)}) collective-permute-start(bf16[4,4,128,256]{3,2,1,0:T(8,128)(2,1)} %collective-permute-done.42.refs_5_), channel_id=1, source_target_pairs={{0,1},{1,0},{2,3},{3,2},{4,5},{5,4},{6,7},{7,6},{8,9},{9,8},{10,11... | collective-permute-start | bytes 3145736 | tf_op jit(solution)/shard_map/ppermute | solution.py:42
  307.3 43.1 %collective-permute-start.47 = (bf16[4,4,128,256]{3,2,1,0:T(8,128)(2,1)}, bf16[4,4,128,256]{3,2,1,0:T(8,128)(2,1)}, u32[]{:S(2)}, u32[]{:S(2)}) collective-permute-start(bf16[4,4,128,256]{3,2,1,0:T(8,128)(2,1)} %collective-permute-done.43.refs_6_), channel_id=1, source_target_pairs={{0,1},{1,0},{2,3},{3,2},{4,5},{5,4},{6,7},{7,6},{8,9},{9,8},{10,11... | collective-permute-start | bytes 3145736 | tf_op jit(solution)/shard_map/ppermute | solution.py:42
  307.8 42.6 %collective-permute-start.48 = (bf16[4,4,128,256]{3,2,1,0:T(8,128)(2,1)}, bf16[4,4,128,256]{3,2,1,0:T(8,128)(2,1)}, u32[]{:S(2)}, u32[]{:S(2)}) collective-permute-start(bf16[4,4,128,256]{3,2,1,0:T(8,128)(2,1)} %collective-permute-done.44.refs_7_), channel_id=1, source_target_pairs={{0,1},{1,0},{2,3},{3,2},{4,5},{5,4},{6,7},{7,6},{8,9},{9,8},{10,11... | collective-permute-start | bytes 3145736 | tf_op jit(solution)/shard_map/ppermute | solution.py:42
  349.8 41.7 %collective-permute-start.53 = (bf16[4,4,128,512]{3,2,1,0:T(8,128)(2,1)S(1)}, bf16[4,4,128,512]{3,2,1,0:T(8,128)(2,1)}, u32[]{:S(2)}, u32[]{:S(2)}) collective-permute-start(bf16[4,4,128,512]{3,2,1,0:T(8,128)(2,1)S(1)} %pad_maximum_fusion.refs_4_), channel_id=1, source_target_pairs={{0,1},{1,0},{2,3},{3,2},{4,5},{5,4},{6,7},{7,6},{8,9},{9,8},{10,11... | collective-permute-start | bytes 6291464 | tf_op jit(solution)/shard_map/ppermute | solution.py:42
  350.3 41.1 %collective-permute-start.54 = (bf16[4,4,128,512]{3,2,1,0:T(8,128)(2,1)}, bf16[4,4,128,512]{3,2,1,0:T(8,128)(2,1)}, u32[]{:S(2)}, u32[]{:S(2)}) collective-permute-start(bf16[4,4,128,512]{3,2,1,0:T(8,128)(2,1)} %collective-permute-done.52.refs_5_), channel_id=1, source_target_pairs={{0,1},{1,0},{2,3},{3,2},{4,5},{5,4},{6,7},{7,6},{8,9},{9,8},{10,11... | collective-permute-start | bytes 6291464 | tf_op jit(solution)/shard_map/ppermute | solution.py:42
  390.9 164.4 %collective-permute-start.62 = (bf16[2,4,4,128,256]{4,3,2,1,0:T(8,128)(2,1)}, bf16[2,4,4,128,256]{4,3,2,1,0:T(8,128)(2,1)}, u32[]{:S(2)}, u32[]{:S(2)}) collective-permute-start(bf16[2,4,4,128,256]{4,3,2,1,0:T(8,128)(2,1)} %get-tuple-element.96), channel_id=1, source_target_pairs={{0,1},{1,0},{2,3},{3,2},{4,5},{5,4},{6,7},{7,6},{8,9},{9,8},{10,11... | collective-permute-start | bytes 6291464 | tf_op jit(solution)/shard_map/ppermute | solution.py:42
  493.3 67.8 %collective-permute-start.80 = (bf16[2,4,4,128,256]{4,3,2,1,0:T(8,128)(2,1)}, bf16[2,4,4,128,256]{4,3,2,1,0:T(8,128)(2,1)}, u32[]{:S(2)}, u32[]{:S(2)}) collective-permute-start(bf16[2,4,4,128,256]{4,3,2,1,0:T(8,128)(2,1)} %get-tuple-element.107), channel_id=1, source_target_pairs={{0,1},{1,0},{2,3},{3,2},{4,5},{5,4},{6,7},{7,6},{8,9},{9,8},{10,11... | collective-permute-start | bytes 6291464 | tf_op jit(solution)/shard_map/ppermute | solution.py:42
  493.4 71.8 %collective-permute-start.68 = (bf16[2,4,4,128,256]{4,3,2,1,0:T(8,128)(2,1)}, bf16[2,4,4,128,256]{4,3,2,1,0:T(8,128)(2,1)}, u32[]{:S(2)}, u32[]{:S(2)}) collective-permute-start(bf16[2,4,4,128,256]{4,3,2,1,0:T(8,128)(2,1)} %get-tuple-element.98), channel_id=1, source_target_pairs={{0,1},{1,0},{2,3},{3,2},{4,5},{5,4},{6,7},{7,6},{8,9},{9,8},{10,11... | collective-permute-start | bytes 6291464 | tf_op jit(solution)/shard_map/ppermute | solution.py:42
  493.9 64.5 %collective-permute-start.73 = (bf16[2,4,4,128,256]{4,3,2,1,0:T(8,128)(2,1)}, bf16[2,4,4,128,256]{4,3,2,1,0:T(8,128)(2,1)}, u32[]{:S(2)}, u32[]{:S(2)}) collective-permute-start(bf16[2,4,4,128,256]{4,3,2,1,0:T(8,128)(2,1)} %get-tuple-element.100), channel_id=1, source_target_pairs={{0,1},{1,0},{2,3},{3,2},{4,5},{5,4},{6,7},{7,6},{8,9},{9,8},{10,11... | collective-permute-start | bytes 6291464 | tf_op jit(solution)/shard_map/ppermute | solution.py:42
  558.4 66.3 %collective-permute-start.61 = (bf16[2,4,4,128,256]{4,3,2,1,0:T(8,128)(2,1)S(1)}, bf16[2,4,4,128,256]{4,3,2,1,0:T(8,128)(2,1)S(1)}, u32[]{:S(2)}, u32[]{:S(2)}) collective-permute-start(bf16[2,4,4,128,256]{4,3,2,1,0:T(8,128)(2,1)S(1)} %copy-done.46), channel_id=1, source_target_pairs={{0,1},{1,0},{2,3},{3,2},{4,5},{5,4},{6,7},{7,6},{8,9},{9,8},{10,11... | collective-permute-start | bytes 6291464 | tf_op jit(solution)/shard_map/ppermute | solution.py:42
  561.1 64.1 %collective-permute-start.63 = (bf16[2,4,4,128,256]{4,3,2,1,0:T(8,128)(2,1)S(1)}, bf16[2,4,4,128,256]{4,3,2,1,0:T(8,128)(2,1)S(1)}, u32[]{:S(2)}, u32[]{:S(2)}) collective-permute-start(bf16[2,4,4,128,256]{4,3,2,1,0:T(8,128)(2,1)S(1)} %add_convert_fusion.8), channel_id=1, source_target_pairs={{0,2},{1,3},{2,0},{3,1},{4,6},{5,7},{6,4},{7,5},{8,10},{9,11},{10,... | collective-permute-start | bytes 6291464 | tf_op jit(solution)/shard_map/ppermute | solution.py:42
  565.2 26.1 %collective-permute-start.74 = (bf16[4,4,128,256]{3,2,1,0:T(8,128)(2,1)S(1)}, bf16[4,4,128,256]{3,2,1,0:T(8,128)(2,1)S(1)}, u32[]{:S(2)}, u32[]{:S(2)}) collective-permute-start(bf16[4,4,128,256]{3,2,1,0:T(8,128)(2,1)S(1)} %slice_bitcast_fusion.6), channel_id=1, source_target_pairs={{0,4},{4,0},{8,12},{12,8},{16,20},{20,16},{24,28},{28,24},{1,5},{5... | collective-permute-start | bytes 3145736 | tf_op jit(solution)/shard_map/ppermute | solution.py:42
  569.3 43.7 %collective-permute-start.69 = (bf16[4,4,128,256]{3,2,1,0:T(8,128)(2,1)S(1)}, bf16[4,4,128,256]{3,2,1,0:T(8,128)(2,1)S(1)}, u32[]{:S(2)}, u32[]{:S(2)}) collective-permute-start(bf16[4,4,128,256]{3,2,1,0:T(8,128)(2,1)S(1)} %slice_bitcast_fusion.8), channel_id=1, source_target_pairs={{0,4},{4,0},{8,12},{12,8},{16,20},{20,16},{24,28},{28,24},{1,5},{5... | collective-permute-start | bytes 3145736 | tf_op jit(solution)/shard_map/ppermute | solution.py:42
  613.0 70.4 %collective-permute-start.79 = (bf16[2,4,4,128,256]{4,3,2,1,0:T(8,128)(2,1)S(1)}, bf16[2,4,4,128,256]{4,3,2,1,0:T(8,128)(2,1)S(1)}, u32[]{:S(2)}, u32[]{:S(2)}) collective-permute-start(bf16[2,4,4,128,256]{4,3,2,1,0:T(8,128)(2,1)S(1)} %copy-done.47), channel_id=1, source_target_pairs={{0,1},{1,0},{2,3},{3,2},{4,5},{5,4},{6,7},{7,6},{8,9},{9,8},{10,11... | collective-permute-start | bytes 6291464 | tf_op jit(solution)/shard_map/ppermute | solution.py:42
  613.0 74.6 %collective-permute-start.81 = (bf16[2,4,4,128,256]{4,3,2,1,0:T(8,128)(2,1)S(1)}, bf16[2,4,4,128,256]{4,3,2,1,0:T(8,128)(2,1)S(1)}, u32[]{:S(2)}, u32[]{:S(2)}) collective-permute-start(bf16[2,4,4,128,256]{4,3,2,1,0:T(8,128)(2,1)S(1)} %add_convert_fusion.3), channel_id=1, source_target_pairs={{0,2},{1,3},{2,0},{3,1},{4,6},{5,7},{6,4},{7,5},{8,10},{9,11},{10,... | collective-permute-start | bytes 6291464 | tf_op jit(solution)/shard_map/ppermute | solution.py:42
  622.9 26.1 %collective-permute-start.92 = (bf16[4,4,128,256]{3,2,1,0:T(8,128)(2,1)S(1)}, bf16[4,4,128,256]{3,2,1,0:T(8,128)(2,1)S(1)}, u32[]{:S(2)}, u32[]{:S(2)}) collective-permute-start(bf16[4,4,128,256]{3,2,1,0:T(8,128)(2,1)S(1)} %slice_bitcast_fusion), channel_id=1, source_target_pairs={{0,4},{4,0},{8,12},{12,8},{16,20},{20,16},{24,28},{28,24},{1,5},{5... | collective-permute-start | bytes 3145736 | tf_op jit(solution)/shard_map/ppermute | solution.py:42
  624.6 85.6 %collective-permute-start.55 = (bf16[4,64,1024]{2,1,0:T(8,128)(2,1)S(1)}, bf16[4,64,1024]{2,1,0:T(8,128)(2,1)S(1)}, u32[]{:S(2)}, u32[]{:S(2)}) collective-permute-start(bf16[4,64,1024]{2,1,0:T(8,128)(2,1)S(1)} %copy-done.50), channel_id=1, source_target_pairs={{0,4},{4,0},{8,12},{12,8},{16,20},{20,16},{24,28},{28,24},{1,5},{5... | collective-permute-start | bytes 1572872 | tf_op jit(solution)/shard_map/ppermute | solution.py:42
  625.2 57.5 %collective-permute-start.87 = (bf16[4,4,128,256]{3,2,1,0:T(8,128)(2,1)S(1)}, bf16[4,4,128,256]{3,2,1,0:T(8,128)(2,1)S(1)}, u32[]{:S(2)}, u32[]{:S(2)}) collective-permute-start(bf16[4,4,128,256]{3,2,1,0:T(8,128)(2,1)S(1)} %slice_bitcast_fusion.2), channel_id=1, source_target_pairs={{0,4},{4,0},{8,12},{12,8},{16,20},{20,16},{24,28},{28,24},{1,5},{5... | collective-permute-start | bytes 3145736 | tf_op jit(solution)/shard_map/ppermute | solution.py:42
  649.0 63.6 %collective-permute-start.64 = (bf16[4,4,128,256]{3,2,1,0:T(8,128)(2,1)S(1)}, bf16[4,4,128,256]{3,2,1,0:T(8,128)(2,1)S(1)}, u32[]{:S(2)}, u32[]{:S(2)}) collective-permute-start(bf16[4,4,128,256]{3,2,1,0:T(8,128)(2,1)S(1)} %slice_bitcast_fusion.10), channel_id=1, source_target_pairs={{0,4},{4,0},{8,12},{12,8},{16,20},{20,16},{24,28},{28,24},{1,5},{5... | collective-permute-start | bytes 3145736 | tf_op jit(solution)/shard_map/ppermute | solution.py:42
  693.9 37.7 %collective-permute-start.82 = (bf16[4,4,128,256]{3,2,1,0:T(8,128)(2,1)S(1)}, bf16[4,4,128,256]{3,2,1,0:T(8,128)(2,1)S(1)}, u32[]{:S(2)}, u32[]{:S(2)}) collective-permute-start(bf16[4,4,128,256]{3,2,1,0:T(8,128)(2,1)S(1)} %slice_bitcast_fusion.4), channel_id=1, source_target_pairs={{0,4},{4,0},{8,12},{12,8},{16,20},{20,16},{24,28},{28,24},{1,5},{5... | collective-permute-start | bytes 3145736 | tf_op jit(solution)/shard_map/ppermute | solution.py:42
  715.0 28.8 %collective-permute-start.88 = (bf16[4,128,256]{2,1,0:T(8,128)(2,1)S(1)}, bf16[4,128,256]{2,1,0:T(8,128)(2,1)S(1)}, u32[]{:S(2)}, u32[]{:S(2)}) collective-permute-start(bf16[4,128,256]{2,1,0:T(8,128)(2,1)S(1)} %get-tuple-element.159), channel_id=1, source_target_pairs={{0,8},{4,12},{8,16},{12,20},{16,24},{20,28},{24,0},{28,4},{1,9},{5... | collective-permute-start | bytes 786440 | tf_op jit(solution)/shard_map/ppermute | solution.py:47
  731.0 28.1 %collective-permute-start.89 = (bf16[4,128,256]{2,1,0:T(8,128)(2,1)S(1)}, bf16[4,128,256]{2,1,0:T(8,128)(2,1)S(1)}, u32[]{:S(2)}, u32[]{:S(2)}) collective-permute-start(bf16[4,128,256]{2,1,0:T(8,128)(2,1)S(1)} %get-tuple-element.161), channel_id=1, source_target_pairs={{0,16},{4,20},{8,24},{12,28},{16,0},{20,4},{24,8},{28,12},{1,17},{... | collective-permute-start | bytes 786440 | tf_op jit(solution)/shard_map/ppermute | solution.py:47
  731.0 28.1 %collective-permute-start.90 = (bf16[4,128,256]{2,1,0:T(8,128)(2,1)S(1)}, bf16[4,128,256]{2,1,0:T(8,128)(2,1)S(1)}, u32[]{:S(2)}, u32[]{:S(2)}) collective-permute-start(bf16[4,128,256]{2,1,0:T(8,128)(2,1)S(1)} %get-tuple-element.160), channel_id=1, source_target_pairs={{0,24},{4,28},{8,0},{12,4},{16,8},{20,12},{24,16},{28,20},{1,25},{... | collective-permute-start | bytes 786440 | tf_op jit(solution)/shard_map/ppermute | solution.py:47
  731.0 36.6 %collective-permute-start.96 = (bf16[4,128,256]{2,1,0:T(8,128)(2,1)S(1)}, bf16[4,128,256]{2,1,0:T(8,128)(2,1)S(1)}, u32[]{:S(2)}, u32[]{:S(2)}) collective-permute-start(bf16[4,128,256]{2,1,0:T(8,128)(2,1)S(1)} %fusion.11), channel_id=1, source_target_pairs={{0,2},{1,3},{2,0},{3,1},{4,6},{5,7},{6,4},{7,5},{8,10},{9,11},{10,... | collective-permute-start | bytes 786440 | tf_op jit(solution)/shard_map/ppermute | solution.py:42
  731.6 36.0 %collective-permute-start.65 = (bf16[4,128,256]{2,1,0:T(8,128)(2,1)S(1)}, bf16[4,128,256]{2,1,0:T(8,128)(2,1)S(1)}, u32[]{:S(2)}, u32[]{:S(2)}) collective-permute-start(bf16[4,128,256]{2,1,0:T(8,128)(2,1)S(1)} %get-tuple-element.174), channel_id=1, source_target_pairs={{0,8},{4,12},{8,16},{12,20},{16,24},{20,28},{24,0},{28,4},{1,9},{5... | collective-permute-start | bytes 786440 | tf_op jit(solution)/shard_map/ppermute | solution.py:47
  743.7 37.8 %collective-permute-start.66 = (bf16[4,128,256]{2,1,0:T(8,128)(2,1)S(1)}, bf16[4,128,256]{2,1,0:T(8,128)(2,1)S(1)}, u32[]{:S(2)}, u32[]{:S(2)}) collective-permute-start(bf16[4,128,256]{2,1,0:T(8,128)(2,1)S(1)} %get-tuple-element.176), channel_id=1, source_target_pairs={{0,16},{4,20},{8,24},{12,28},{16,0},{20,4},{24,8},{28,12},{1,17},{... | collective-permute-start | bytes 786440 | tf_op jit(solution)/shard_map/ppermute | solution.py:47
  759.1 30.1 %collective-permute-start.83 = (bf16[4,128,256]{2,1,0:T(8,128)(2,1)S(1)}, bf16[4,128,256]{2,1,0:T(8,128)(2,1)S(1)}, u32[]{:S(2)}, u32[]{:S(2)}) collective-permute-start(bf16[4,128,256]{2,1,0:T(8,128)(2,1)S(1)} %get-tuple-element.165), channel_id=1, source_target_pairs={{0,8},{4,12},{8,16},{12,20},{16,24},{20,28},{24,0},{28,4},{1,9},{5... | collective-permute-start | bytes 786440 | tf_op jit(solution)/shard_map/ppermute | solution.py:47
  767.5 25.3 %collective-permute-start.84 = (bf16[4,128,256]{2,1,0:T(8,128)(2,1)S(1)}, bf16[4,128,256]{2,1,0:T(8,128)(2,1)S(1)}, u32[]{:S(2)}, u32[]{:S(2)}) collective-permute-start(bf16[4,128,256]{2,1,0:T(8,128)(2,1)S(1)} %get-tuple-element.167), channel_id=1, source_target_pairs={{0,16},{4,20},{8,24},{12,28},{16,0},{20,4},{24,8},{28,12},{1,17},{... | collective-permute-start | bytes 786440 | tf_op jit(solution)/shard_map/ppermute | solution.py:47
  767.6 25.3 %collective-permute-start.85 = (bf16[4,128,256]{2,1,0:T(8,128)(2,1)S(1)}, bf16[4,128,256]{2,1,0:T(8,128)(2,1)S(1)}, u32[]{:S(2)}, u32[]{:S(2)}) collective-permute-start(bf16[4,128,256]{2,1,0:T(8,128)(2,1)S(1)} %get-tuple-element.166), channel_id=1, source_target_pairs={{0,24},{4,28},{8,0},{12,4},{16,8},{20,12},{24,16},{28,20},{1,25},{... | collective-permute-start | bytes 786440 | tf_op jit(solution)/shard_map/ppermute | solution.py:47
  784.1 29.0 %collective-permute-start.57 = (bf16[4,64,1024]{2,1,0:T(8,128)(2,1)S(1)}, bf16[4,64,1024]{2,1,0:T(8,128)(2,1)S(1)}, u32[]{:S(2)}, u32[]{:S(2)}) collective-permute-start(bf16[4,64,1024]{2,1,0:T(8,128)(2,1)S(1)} %copy-done.48), channel_id=1, source_target_pairs={{0,12},{4,8},{8,4},{12,0},{16,28},{20,24},{24,20},{28,16},{1,13},{... | collective-permute-start | bytes 1572872 | tf_op jit(solution)/shard_map/ppermute | solution.py:42
  795.6 128.2 %collective-permute-start.108 = (bf16[4,128,256]{2,1,0:T(8,128)(2,1)S(1)}, bf16[4,128,256]{2,1,0:T(8,128)(2,1)S(1)}, u32[]{:S(2)}, u32[]{:S(2)}) collective-permute-start(bf16[4,128,256]{2,1,0:T(8,128)(2,1)S(1)} %collective-permute-done.106.refs_5_), channel_id=1, source_target_pairs={{0,1},{1,0},{2,3},{3,2},{4,5},{5,4},{6,7},{7,6},{8,9},{9,8},{10,11... | collective-permute-start | bytes 786440 | tf_op jit(solution)/shard_map/ppermute | solution.py:42
  801.9 122.0 %collective-permute-start.97 = (bf16[4,128,256]{2,1,0:T(8,128)(2,1)S(1)}, bf16[4,128,256]{2,1,0:T(8,128)(2,1)S(1)}, u32[]{:S(2)}, u32[]{:S(2)}) collective-permute-start(bf16[4,128,256]{2,1,0:T(8,128)(2,1)S(1)} %get-tuple-element.130.refs_0_), channel_id=1, source_target_pairs={{0,2},{1,3},{2,0},{3,1},{4,6},{5,7},{6,4},{7,5},{8,10},{9,11},{10,... | collective-permute-start | bytes 786440 | tf_op jit(solution)/shard_map/ppermute | solution.py:42
  813.1 111.2 %collective-permute-start.104 = (bf16[4,128,256]{2,1,0:T(8,128)(2,1)S(1)}, bf16[4,128,256]{2,1,0:T(8,128)(2,1)}, u32[]{:S(2)}, u32[]{:S(2)}) collective-permute-start(bf16[4,128,256]{2,1,0:T(8,128)(2,1)S(1)} %get-tuple-element.136.refs_0_), channel_id=1, source_target_pairs={{0,1},{1,0},{2,3},{3,2},{4,5},{5,4},{6,7},{7,6},{8,9},{9,8},{10,11... | collective-permute-start | bytes 786440 | tf_op jit(solution)/shard_map/ppermute | solution.py:42
  813.2 113.7 %collective-permute-start.105 = (bf16[4,128,256]{2,1,0:T(8,128)(2,1)S(1)}, bf16[4,128,256]{2,1,0:T(8,128)(2,1)}, u32[]{:S(2)}, u32[]{:S(2)}) collective-permute-start(bf16[4,128,256]{2,1,0:T(8,128)(2,1)S(1)} %collective-permute-done.103.refs_1_), channel_id=1, source_target_pairs={{0,1},{1,0},{2,3},{3,2},{4,5},{5,4},{6,7},{7,6},{8,9},{9,8},{10,11... | collective-permute-start | bytes 786440 | tf_op jit(solution)/shard_map/ppermute | solution.py:42
  813.7 110.8 %collective-permute-start.100 = (bf16[4,128,256]{2,1,0:T(8,128)(2,1)S(1)}, bf16[4,128,256]{2,1,0:T(8,128)(2,1)}, u32[]{:S(2)}, u32[]{:S(2)}) collective-permute-start(bf16[4,128,256]{2,1,0:T(8,128)(2,1)S(1)} %get-tuple-element.132.refs_4_), channel_id=1, source_target_pairs={{0,2},{1,3},{2,0},{3,1},{4,6},{5,7},{6,4},{7,5},{8,10},{9,11},{10,... | collective-permute-start | bytes 786440 | tf_op jit(solution)/shard_map/ppermute | solution.py:42
  (107 other events, 2499.0 us)

commit v2 on v1

v2 whole, which is shorter than its diff:
```python
import functools

import jax
import jax.numpy as jnp
from jax import lax
from jax.experimental import pallas as pl
from jax.experimental.pallas import tpu as pltpu
from jax.sharding import PartitionSpec as P

HD = 64
FPV = 16
CODES = 8
STEP = 5
BF = jnp.bfloat16
F32 = jnp.float32

eps_norm = 1e-05
beta_first = 0.5
beta_second = 0.5
rate_matrix = 0.02
rate_small = 0.3
decay_rate = 0.1
eps_adam = 1e-08
masked_score = -1000000000.0
score_scale = HD**-0.5

CORE, XPOS, YPOS, ZPOS, MEMBER = range(5)
ANY = pl.BlockSpec(memory_space=pl.ANY)
MIB = 1 << 20


def dot_nn(a, b):
    return lax.dot_general(a, b, (((1,), (0,)), ((), ())), preferred_element_type=F32)


def dot_nt(a, b):
    return lax.dot_general(a, b, (((1,), (1,)), ((), ())), preferred_element_type=F32)


def after(value, *others):
    return lax.optimization_barrier((value, *others))[0] if others else value


def swap(value, axis, bit):
    size = lax.axis_size(axis)
    return lax.ppermute(value, axis, [(i, i ^ bit) for i in range(size)])


def shift_z(value, step):
    size = lax.axis_size("seq")
    return lax.ppermute(value, "seq", [(i, (i + 2 * step) % size) for i in range(size)])


def z_groups():
    size = lax.axis_size("seq")
    return [list(range(first, size, 2)) for first in range(2)]


def gather_z(piece):
    nz = lax.axis_size("seq") // 2
    if nz <= 4:
        return jnp.stack([piece] + [shift_z(piece, k) for k in range(1, nz)])
    whole = lax.all_gather(piece, "seq", axis_index_groups=z_groups())
    here = lax.axis_index("seq") // 2
    return jnp.take(whole, (here - jnp.arange(nz)) % nz, axis=0)


def scatter_z(parts, *others):
    nz = lax.axis_size("seq") // 2
    if nz <= 4:
        come = [parts[0]] + [shift_z(parts[k], k) for k in range(1, nz)]
        total = come[0].astype(F32)
        for item in come[1:]:
            total = total + after(item, *others).astype(F32)
        return total.astype(BF)
    here = lax.axis_index("seq") // 2
    ordered = jnp.take(jnp.stack(parts), (jnp.arange(nz) - here) % nz, axis=0)
    return lax.psum_scatter(ordered, "seq", axis_index_groups=z_groups())


def column_part(block, start, width):
    return lax.dynamic_slice_in_dim(block, start, width, 2)


def quarter_mine(block, place):
    part = block.shape[2] // 4
    return column_part(block, (place[CORE] * 2 + place[XPOS]) * part, part)


def gather_weights(block, kind, place, begin=(), beside_after=(), across_after=(), cross=()):
    width = block.shape[2]
    if kind == "zyx":
        part = width // 4
        piece = column_part(block, (place[CORE] * 2 + place[XPOS]) * part, part)
    else:
        part = width // 2
        piece = column_part(block, place[CORE] * part, part)
    piece = after(piece, *begin)
    below = gather_z(piece)
    beside = swap(after(below, *beside_after), "seq", 1)
    stacks = [(below, 0, 0), (beside, 1, 0)]
    if kind == "zyx":
        stacks += [(swap(after(s, *across_after), "grp", 2), y, 1) for s, y, _ in stacks]
    out = [(s, (y, 0, x)) for s, y, x in stacks]
    out += [(swap(after(s, *cross), "grp", 1), (y, 1, x)) for s, y, x in stacks]
    return [s for s, _ in out], [m if kind == "zyx" else (m[0], m[1], None) for _, m in out]


def add_low(a, b):
    return (a.astype(F32) + b.astype(F32)).astype(BF)


def send_core(parts):
    return parts[0], swap(parts[1], "grp", 1)


def step_one(here, there):
    return add_low(here[0], there[0]), add_low(here[1], there[1])


def send_one(kept, sent, kind):
    return kept, swap(sent, "grp", 2) if kind == "xyz" else swap(sent, "seq", 1)


def step_two(kept, come, kind):
    if kind == "xyz":
        return add_low(kept[0], come[0]), add_low(kept[1], come[1])
    sums = [add_low(kept[k], come[k]) for k in range(kept.shape[0])]
    return sums[0], sums[1:]


def send_two(kept, sent, kind, *others):
    if kind == "xyz":
        return kept, swap(sent, "seq", 1)
    ends = scatter_z([kept, *sent], *others)
    return ends[0], ends[1]


def step_three(kept, come, kind):
    if kind == "xyz":
        sums = [add_low(kept[k], come[k]) for k in range(kept.shape[0])]
        return sums[0], sums[1:]
    return kept, come


def send_three(kept, sent, kind, *others):
    if kind == "xyz":
        return scatter_z([kept, *sent], *others)
    return add_low(kept, after(swap(sent, "grp", 2), *others))


def pinned(state, *others):
    return state[0], after(state[1], *others)


def before(value, *states):
    return after(value, *jax.tree.leaves(states))


def share_quarters(quarter):
    beside = swap(quarter, "grp", 2)
    return [quarter, beside, swap(quarter, "grp", 1), swap(beside, "grp", 1)]


def all_sum(value):
    for axis in ("grp", "seq"):
        size = lax.axis_size(axis)
        if size & (size - 1):
            value = lax.psum(value, axis)
            continue
        bit = 1
        while bit < size:
            if 4 * bit <= size:
                a, b, c = (swap(value, axis, bit * k) for k in (1, 2, 3))
                low = (lax.axis_index(axis) // (2 * bit)) % 2 == 0
                near, far = value + a, b + c
                value = jnp.where(low, near, far) + jnp.where(low, far, near)
                bit *= 4
            else:
                value = value + swap(value, axis, bit)
                bit *= 2
    return value


def exchange(pieces):
    return [pieces[0]] + [swap(pieces[j], "seq", j) for j in range(1, len(pieces))]


def start_weights(place, stacks, metas, target, sem):
    for stack, (y_rel, c_rel, x_rel) in zip(stacks, metas):
        nz, _, rows, width = stack.shape
        column = place[CORE] ^ c_rel
        if x_rel is not None:
            column = column * 2 + (place[XPOS] ^ x_rel)
        column = pl.multiple_of(column * width, 128)

        def one(k, carry, stack=stack, y_rel=y_rel, rows=rows, width=width, column=column, nz=nz):
            shard = lax.rem(place[ZPOS] - k + nz, nz) * 2 + (place[YPOS] ^ y_rel)
            row = pl.multiple_of(shard * rows, rows)
            pltpu.make_async_copy(
                stack.at[k], target.at[:, pl.ds(row, rows), pl.ds(column, width)], sem
            ).start()
            return carry

        if nz <= 4:
            for k in range(nz):
                one(k, 0)
        else:
            lax.fori_loop(0, nz, one, 0)


def quarter_column(g, width):
    return (g % 2 * 2 + g // 2) * width


def start_whole(stack, first, target, sem):
    count, _, rows, width = stack.shape
    n = target.shape[0]

    def one(s, carry):
        row = s * rows if isinstance(s, int) else pl.multiple_of(s * rows, rows)
        for g in range(4):
            pltpu.make_async_copy(
                stack.at[s * 4 + g, pl.ds(first, n)],
                target.at[:, pl.ds(row, rows), pl.ds(quarter_column(g, width), width)],
                sem,
            ).start()
        return carry

    if count <= 32:
        for s in range(count // 4):
            one(s, 0)
    else:
        lax.fori_loop(0, count // 4, one, 0)


def wait_all(target, sem):
    pltpu.make_async_copy(target, target, sem).wait()


def start_grads(place, kind, source, index, outs, sem):
    nz = outs[0].shape[2 if kind == "xyz" else 1]
    rows, width = outs[0].shape[-2:]
    for rel in range(4):
        out, x_rel = outs[rel // 2], rel % 2
        column = (place[CORE] ^ (rel // 2)) * 2 + (place[XPOS] ^ x_rel)
        column = pl.multiple_of(column * width, 128)
        for y_rel in range(2):

            def one(k, carry, out=out, x_rel=x_rel, y_rel=y_rel, column=column):
                shard = lax.rem(place[ZPOS] + k, nz) * 2 + (place[YPOS] ^ y_rel)
                row = pl.multiple_of(shard * rows, rows)
                target = out.at[x_rel, y_rel, k, index]
                if kind != "xyz":
                    target = out.at[y_rel, k, x_rel, index]
                pltpu.make_async_copy(
                    source.at[pl.ds(row, rows), pl.ds(column, width)], target, sem
                ).start()
                return carry

            if nz <= 4:
                for k in range(nz):
                    one(k, 0)
            else:
                lax.fori_loop(0, nz, one, 0)


def norm_parts(values):
    centre = values - jnp.mean(values, axis=-1, keepdims=True)
    spread = jnp.mean(centre * centre, axis=-1, keepdims=True)
    scale = lax.rsqrt(spread + eps_norm)
    return centre * scale, scale


def norm_back(values, h_grad, gain):
    xhat, scale = norm_parts(values)
    e = h_grad * gain
    inner = jnp.mean(e * xhat, axis=-1, keepdims=True)
    v_grad = scale * (e - jnp.mean(e, axis=-1, keepdims=True) - xhat * inner)
    return v_grad, jnp.sum(h_grad * xhat, axis=0, keepdims=True)


def two_heads(x):
    lane = lax.broadcasted_iota(jnp.int32, x.shape, 1)
    zero = jnp.zeros_like(x)
    return jnp.where(lane < HD, x, zero), jnp.where(lane < HD, zero, x)


def video_mask(rows, positions):
    key = lax.broadcasted_iota(jnp.int32, (rows, rows), 0)
    query = lax.broadcasted_iota(jnp.int32, (rows, rows), 1)
    return (lax.rem(key, positions) == lax.rem(query, positions)) & (key <= query)


def attend(packed_ref, heads_ref, lse_ref, mask):
    width = heads_ref.shape[-1]
    for pair in range(width // 128):
        lo = pair * 128
        queries = two_heads(packed_ref[0, :, lo : lo + 128] * jnp.asarray(score_scale, BF))
        keys = packed_ref[0, :, width + lo : width + lo + 128]
        values_t = packed_ref[0, :, 2 * width + lo : 2 * width + lo + 128].T
        out = []
        for half in range(2):
            scores = dot_nt(keys, queries[half])
            if mask is not None:
                scores = jnp.where(mask, scores, masked_score)
            top = jnp.max(scores, axis=0, keepdims=True)
            probs = jnp.exp(scores - top)
            total = jnp.sum(probs, axis=0, keepdims=True)
            mixed = dot_nn(values_t[half * HD : half * HD + HD], probs.astype(BF))
            out.append(mixed / total)
            lse_ref[0, 2 * pair + half : 2 * pair + half + 1, :] = top + jnp.log(total)
        heads_ref[0, :, lo : lo + 128] = jnp.concatenate(out, axis=0).astype(BF).T


def attend_back(packed_ref, heads_ref, heads_grad_ref, lse_ref, grad_ref, mask):
    width = heads_ref.shape[-1]
    for pair in range(width // 128):
        lo = pair * 128
        query = packed_ref[0, :, lo : lo + 128] * jnp.asarray(score_scale, BF)
        key = packed_ref[0, :, width + lo : width + lo + 128]
        value = packed_ref[0, :, 2 * width + lo : 2 * width + lo + 128]
        heads_grad = heads_grad_ref[0, :, lo : lo + 128]
        key_t = key.T
        mixed_t = (heads_grad.astype(F32) * heads_ref[0, :, lo : lo + 128].astype(F32)).T
        queries, head_grads = two_heads(query), two_heads(heads_grad)
        probs_two, score_two, query_grad = [], [], []
        for half in range(2):
            scores = dot_nt(key, queries[half])
            if mask is not None:
                scores = jnp.where(mask, scores, masked_score)
            probs = jnp.exp(scores - lse_ref[0, 2 * pair + half : 2 * pair + half + 1, :])
            delta = jnp.sum(mixed_t[half * HD : half * HD + HD], axis=0, keepdims=True)
            probs_grad = dot_nt(value, head_grads[half])
            score_grad = (probs * (probs_grad - delta)).astype(BF)
            probs_two.append(probs.astype(BF))
            score_two.append(score_grad)
            query_grad.append(dot_nn(key_t[half * HD : half * HD + HD], score_grad))
        value_grad = dot_nn(jnp.concatenate(probs_two, 1), jnp.concatenate(head_grads, 0))
        key_grad = dot_nn(jnp.concatenate(score_two, 1), jnp.concatenate(queries, 0))
        grad_ref[0, :, lo : lo + 128] = (
            (jnp.concatenate(query_grad, 0) * score_scale).astype(BF).T
        )
        grad_ref[0, :, width + lo : width + lo + 128] = key_grad.astype(BF)
        grad_ref[0, :, 2 * width + lo : 2 * width + lo + 128] = value_grad.astype(BF)


def gelu_both(pre):
    root = 0.7978845608028654
    square = pre * pre
    bend = jnp.tanh(root * pre * (1.0 + 0.044715 * square))
    half = 0.5 * (1.0 + bend)
    slope = half + 0.5 * pre * (1.0 - bend * bend) * (root * (1.0 + 3 * 0.044715 * square))
    return pre * half, slope


def start_layer(place, lots, refs, weights, sems):
    for i, (first, count, metas) in enumerate(lots):
        stacks, refs = refs[: len(metas)], refs[len(metas) :]
        start_weights(place, stacks, metas, weights.at[pl.ds(first, count)], sems.at[i])


def wait_layer(lots, weights, sems):
    for i, (first, count, _) in enumerate(lots):
        wait_all(weights.at[pl.ds(first, count)], sems.at[i])


def stacks_of(lots):
    return sum(len(metas) for _, _, metas in lots)


def project_in(values, gain, weights, normed_ref, packed_ref):
    xhat, _ = norm_parts(values)
    normed = (xhat * gain).astype(BF)
    normed_ref[0] = normed
    width = normed.shape[1]
    for b in range(3):
        packed_ref[0, :, b * width : (b + 1) * width] = dot_nn(normed, weights[b]).astype(BF)


def load_layer(place, lots, stacks, weights, sems):
    @pl.when(pl.program_id(0) == 0)
    def _():
        start_layer(place, lots, stacks, weights, sems)


def await_layer(lots, weights, sems):
    @pl.when(pl.program_id(0) == 0)
    def _():
        wait_layer(lots, weights, sems)


def spatial_in_body(lots, place, frames_ref, shift_ref, gain_ref, *refs):
    n = stacks_of(lots)
    stacks, (packed_ref, normed_ref, weights, sems) = refs[:n], refs[n:]
    load_layer(place, lots, stacks, weights, sems)
    await_layer(lots, weights, sems)
    values = frames_ref[0].astype(F32) + shift_ref[0]
    project_in(values, gain_ref[0:1, :], weights, normed_ref, packed_ref)


def temporal_fwd_body(place, *refs):
    piece_refs, gain_ref, stack = refs[:4], refs[4], refs[5]
    packed_ref, heads_ref, lse_ref, normed_ref, tokens_ref, resid_ref, third_ref = refs[6:13]
    weights, tokens, sems = refs[13:]
    load_whole(stack, weights, sems)
    frames, positions = piece_refs[0].shape[0], piece_refs[0].shape[1]
    for j, piece in enumerate(piece_refs):
        tokens[pl.ds((place[MEMBER] ^ j) * frames, frames)] = piece[...]
    low = tokens[...].reshape(tokens_ref.shape[1:])
    tokens_ref[0] = low
    values = low.astype(F32)
    await_whole(weights, sems)
    project_in(values, gain_ref[1:2, :], weights, normed_ref, packed_ref)
    attend(packed_ref, heads_ref, lse_ref, video_mask(low.shape[0], positions))
    resid = values + dot_nn(heads_ref[0], weights[3])
    resid_ref[0] = resid
    xhat, _ = norm_parts(resid)
    third_ref[0] = (xhat * gain_ref[2:3, :]).astype(BF)


def load_whole(stack, weights, sems):
    @pl.when(pl.program_id(0) == 0)
    def _():
        start_whole(stack, 0, weights, sems.at[0])


def await_whole(weights, sems):
    @pl.when(pl.program_id(0) == 0)
    def _():
        wait_all(weights, sems.at[0])


def attend_body(positions, place, packed_ref, heads_ref, lse_ref):
    mask = video_mask(packed_ref.shape[1], positions) if positions else None
    attend(packed_ref, heads_ref, lse_ref, mask)


def spatial_out_body(lots, place, heads_ref, frames_ref, shift_ref, *refs):
    n = stacks_of(lots)
    stacks, refs = refs[:n], refs[n:]
    piece_refs, (weights, resid, sems) = refs[:4], refs[4:]
    load_layer(place, lots, stacks, weights, sems)
    values = frames_ref[0].astype(F32) + shift_ref[0]
    await_layer(lots, weights, sems)
    resid[...] = (values + dot_nn(heads_ref[0], weights[lots[0][1] - 1])).astype(BF)
    count = piece_refs[0].shape[1]
    for j, piece in enumerate(piece_refs):
        first = pl.multiple_of((place[MEMBER] ^ j) * count, count)
        piece[0] = resid[pl.ds(first, count), :]


def ffn_body(group, base, last, kind, place, *refs):
    first = group == 0
    third_ref, cot_ref, resid_ref, stack = refs[:4]
    refs = refs[4:]
    if not first:
        dx_in, *refs = refs
    outs, refs = refs[:2], refs[2:]
    if last:
        dx_out, piece_refs, refs = refs[0], refs[1:5], refs[5:]
    else:
        resid_out, dx_out, refs = refs[0], refs[1], refs[2:]
    third, cot, third_t, cot_t, acc, dx, weights, act, pre_grad, staging, sems = refs
    tokens, width = third.shape
    blocks = weights.shape[0] // 2
    chunk = 256
    loads = [(third_ref, third, 0), (cot_ref, cot, 1), (resid_ref, acc, 2)]
    if not first:
        loads.append((dx_in, dx, 3))
    for source, target, s in loads:
        pltpu.make_async_copy(source, target, sems.at[s]).start()
    start_whole(stack, base, weights, sems.at[4])
    for source, target, s in loads[:2]:
        pltpu.make_async_copy(source, target, sems.at[s]).wait()
    for r in range(tokens // chunk):
        rows = slice(r * chunk, (r + 1) * chunk)
        third_t[:, rows] = third[rows, :].T
        cot_t[:, rows] = cot[rows, :].T
    wait_all(weights, sems.at[4])
    for source, target, s in loads[2:]:
        pltpu.make_async_copy(source, target, sems.at[s]).wait()

    def send(source, index):
        start_grads(place, kind, source, index, outs, sems.at[5])

    for b in range(blocks):
        for r in range(tokens // chunk):
            rows = slice(r * chunk, (r + 1) * chunk)
            pre = dot_nn(third[rows, :], weights[b])
            act_grad = dot_nn(cot[rows, :], weights[blocks + b])
            act_now, slope = gelu_both(pre)
            act_now = act_now.astype(BF)
            grad_now = (act_grad * slope).astype(BF)
            act[rows, :] = act_now
            pre_grad[rows, :] = grad_now
            acc[rows, :] += dot_nt(act_now, weights[blocks + b])
            back = dot_nt(grad_now, weights[b])
            if first and b == 0:
                dx[rows, :] = back
            else:
                dx[rows, :] += back
        staging[b] = dot_nn(third_t[...], pre_grad[...]).astype(BF)
        send(staging.at[b], b)
        staging[blocks + b] = dot_nn(cot_t[...], act[...]).astype(BF)
        send(staging.at[blocks + b], blocks + b)
    pltpu.make_async_copy(dx, dx_out, sems.at[6]).start()
    if last:
        low = third
        low[...] = acc[...].astype(BF)
        frames, positions = piece_refs[0].shape[:2]
        tiles = tokens // (FPV * 16)
        per_tile = positions // tiles
        for j, piece in enumerate(piece_refs):
            for tile in range(tiles):
                for f in range(frames):
                    row = pl.multiple_of(
                        tile * (tokens // tiles)
                        + ((place[MEMBER] ^ j) * frames + f) * per_tile,
                        per_tile,
                    )
                    pltpu.make_async_copy(
                        low.at[pl.ds(row, per_tile)],
                        piece.at[f, pl.ds(tile * per_tile, per_tile)],
                        sems.at[7],
                    ).start()
        wait_all(low, sems.at[7])
    else:
        pltpu.make_async_copy(acc, resid_out, sems.at[7]).start()
        pltpu.make_async_copy(acc, resid_out, sems.at[7]).wait()
    pltpu.make_async_copy(dx, dx_out, sems.at[6]).wait()
    wait_all(staging, sems.at[5])


def add_gain(step, ref, row, value):
    @pl.when(step == 0)
    def _():
        ref[row : row + 1, :] = value

    @pl.when(step > 0)
    def _():
        ref[row : row + 1, :] += value


def temporal_bwd_body(
    place, dx_ref, cot_ref, resid_ref, tokens_ref, packed_ref, heads_ref, lse_ref, gain_ref, stack, *refs
):
    branch_ref, grad_ref, gains_out = refs[:3]
    piece_refs = refs[3:7]
    weights, heads_grad, total, sems = refs[7:]
    step = pl.program_id(0)
    load_whole(stack, weights, sems)
    back, gain_three = norm_back(resid_ref[0], dx_ref[0], gain_ref[2:3, :])
    add_gain(step, gains_out, 1, gain_three)
    grad_two = cot_ref[0].astype(F32) + back
    branch = grad_two.astype(BF)
    branch_ref[0] = branch
    await_whole(weights, sems)
    heads_grad[0] = dot_nt(branch, weights[3]).astype(BF)
    frames, positions = piece_refs[0].shape[0], piece_refs[0].shape[1]
    mask = video_mask(branch.shape[0], positions)
    attend_back(packed_ref, heads_ref, heads_grad, lse_ref, grad_ref, mask)
    normed_grad = project_back(grad_ref, weights)
    back, gain_two = norm_back(tokens_ref[0].astype(F32), normed_grad, gain_ref[1:2, :])
    add_gain(step, gains_out, 0, gain_two)
    total[...] = (grad_two + back).astype(BF).reshape(total.shape)
    for j, piece in enumerate(piece_refs):
        piece[...] = total[pl.ds((place[MEMBER] ^ j) * frames, frames)]


def spatial_branch_body(lots, place, *refs):
    n = stacks_of(lots)
    piece_refs, stacks = refs[:4], refs[4 : 4 + n]
    branch_ref, heads_grad_ref, weights, sems = refs[4 + n :]
    load_layer(place, lots, stacks, weights, sems)
    count = piece_refs[0].shape[1]
    for j, piece in enumerate(piece_refs):
        first = pl.multiple_of((place[MEMBER] ^ j) * count, count)
        branch_ref[0, pl.ds(first, count), :] = piece[0]
    await_layer(lots, weights, sems)
    heads_grad_ref[0] = dot_nt(branch_ref[0], weights[lots[0][1] - 1]).astype(BF)


def attend_back_body(positions, place, packed_ref, heads_ref, heads_grad_ref, lse_ref, grad_ref):
    mask = video_mask(packed_ref.shape[1], positions) if positions else None
    attend_back(packed_ref, heads_ref, heads_grad_ref, lse_ref, grad_ref, mask)


def project_back(grad_ref, weights):
    width = weights.shape[1]
    out = dot_nt(grad_ref[0, :, :width], weights[0])
    for b in range(1, 3):
        out = out + dot_nt(grad_ref[0, :, b * width : (b + 1) * width], weights[b])
    return out


def spatial_end_body(lots, place, grad_ref, frames_ref, shift_ref, branch_ref, gain_ref, *refs):
    n = stacks_of(lots)
    stacks, (input_ref, gain_out, column_out, weights, sems) = refs[:n], refs[n:]
    load_layer(place, lots, stacks, weights, sems)
    await_layer(lots, weights, sems)
    normed_grad = project_back(grad_ref, weights)
    values = frames_ref[0].astype(F32) + shift_ref[0]
    back, gain_one = norm_back(values, normed_grad, gain_ref[0:1, :])
    add_gain(pl.program_id(0), gain_out, 0, gain_one)
    grad_zero = branch_ref[0].astype(F32) + back
    input_ref[0] = grad_zero.astype(BF)
    column_out[0] = jnp.sum(grad_zero, axis=0, keepdims=True)


def weight_grad_body(kinds, lots, place, *refs):
    pairs = 1 + max(pair for lot in lots for pair, _ in lot)
    sides, refs = refs[: 2 * pairs], refs[2 * pairs :]
    outs, refs = refs[: 2 * len(lots)], refs[2 * len(lots) :]
    held, refs = refs[: 2 * pairs], refs[2 * pairs :]
    turned, (staging, sems) = refs[:pairs], refs[pairs:]
    for s, (source, target) in enumerate(zip(sides, held)):
        pltpu.make_async_copy(source, target, sems.at[s]).start()
    tokens, width = held[0].shape
    chunk = 256
    done = set()
    at = 0
    for i, lot in enumerate(lots):
        for index, (pair, block) in enumerate(lot):
            if pair not in done:
                done.add(pair)
                wait_all(held[2 * pair], sems.at[2 * pair])
                for r in range(tokens // chunk):
                    rows = slice(r * chunk, (r + 1) * chunk)
                    turned[pair][:, rows] = held[2 * pair][rows, :].T
                wait_all(held[2 * pair + 1], sems.at[2 * pair + 1])
            columns = slice(block * width, (block + 1) * width)
            staging[at] = dot_nn(turned[pair][...], held[2 * pair + 1][:, columns]).astype(BF)
            start_grads(place, kinds[i], staging.at[at], index, outs[2 * i : 2 * i + 2], sems.at[2 * pairs])
            at += 1
    wait_all(staging, sems.at[2 * pairs])


def update(weight, moment_one, moment_two, gradient, step_rate, decay_coef):
    first_new = beta_first * moment_one + (1.0 - beta_first) * gradient
    second_new = beta_second * moment_two + (1.0 - beta_second) * gradient * gradient
    fix_first = 1.0 - beta_first**STEP
    fix_second = 1.0 - beta_second**STEP
    change = first_new * (step_rate / fix_first) / (jnp.sqrt(second_new * (1.0 / fix_second)) + eps_adam)
    return weight - (change + (step_rate * decay_coef) * weight), first_new, second_new


def update_body(lots, place, clip, *refs):
    pieces, refs = refs[: 4 * len(lots)], refs[4 * len(lots) :]
    master, first, second, master_new, first_new, second_new = refs
    matrix, block = pl.program_id(0), pl.program_id(1)
    for i, lot in enumerate(lots):
        mine = functools.reduce(
            jnp.logical_or, [(matrix == m) & (block == b) for m, b in lot]
        )

        @pl.when(mine)
        def _(i=i):
            for rel, piece in enumerate(pieces[4 * i : 4 * i + 4]):
                width = piece.shape[2]
                column = (place[CORE] ^ (rel // 2)) * 2 + (place[XPOS] ^ (rel % 2))
                at = pl.ds(pl.multiple_of(column * width, 128), width)
                new = update(
                    master[0, :, at],
                    first[0, :, at],
                    second[0, :, at],
                    piece[0].astype(F32) * clip[0],
                    rate_matrix,
                    decay_rate,
                )
                master_new[0, :, at], first_new[0, :, at], second_new[0, :, at] = new


def join_body(place, *refs):
    pieces, out_ref = refs[:4], refs[4]
    count = pieces[0].shape[1]
    for j, piece in enumerate(pieces):
        first = pl.multiple_of((place[MEMBER] ^ j) * count, count)
        out_ref[0, pl.ds(first, count), :] = piece[0]


def tile_body(place, *refs):
    pieces, out_ref, tokens = refs[:4], refs[4], refs[5]
    frames = pieces[0].shape[0]
    for j, piece in enumerate(pieces):
        tokens[pl.ds((place[MEMBER] ^ j) * frames, frames)] = piece[...]
    out_ref[0] = tokens[...].reshape(out_ref.shape[1:])


def call(body, place, args, in_specs, out_specs, out_shape, scratch, grid=(1,), limit=60, us=10, scalars=1, aliases={}):
    return pl.pallas_call(
        body,
        out_shape=out_shape,
        grid_spec=pltpu.PrefetchScalarGridSpec(
            num_scalar_prefetch=scalars,
            grid=grid,
            in_specs=in_specs,
            out_specs=out_specs,
            scratch_shapes=scratch,
        ),
        input_output_aliases=aliases,
        compiler_params=pltpu.CompilerParams(vmem_limit_bytes=limit * MIB),
        cost_estimate=pl.CostEstimate(flops=us * 10**9, bytes_accessed=MIB, transcendentals=0),
    )(*place, *args)


def tile(*shape):
    return pl.BlockSpec((1,) + shape, lambda i, *_: (i,) + (0,) * len(shape))


def fixed(*shape):
    return pl.BlockSpec(shape, lambda i, *_: (0,) * len(shape))


def shape_of(*shape, dtype=BF):
    return jax.ShapeDtypeStruct(shape, dtype)


def shards(
    frames_in,
    action_codes,
    cotangent,
    attn_master,
    attn_first,
    attn_second,
    ffn_master,
    ffn_first,
    ffn_second,
    small_master,
    small_first,
    small_second,
):
    frames, positions, width = frames_in.shape
    heads_n = width // HD
    members = FPV // frames
    part = positions // members
    spot = positions // FPV
    tiles = part // spot
    rows_tile = FPV * spot
    tokens = tiles * rows_tile
    seq_size = lax.axis_size("seq")
    nz = seq_size // 2
    seq, grp = lax.axis_index("seq"), lax.axis_index("grp")
    place = jnp.stack([grp % 2, grp // 2, seq % 2, seq // 2, seq % members]).astype(jnp.int32)
    spots = (place,)
    local_rows = attn_master.shape[1]

    def blocks(master, picks):
        return jnp.stack([master[m, :, b * width : (b + 1) * width] for m, b in picks]).astype(BF)

    small_low = small_master.astype(BF)
    if seq_size & (seq_size - 1) == 0:
        small_all = small_low[None]
        bit = 1
        while bit < seq_size:
            small_all = jnp.concatenate([small_all, swap(small_all, "seq", bit)])
            bit *= 2
        small_all = jnp.take(small_all, jnp.arange(seq_size) ^ seq, axis=0)
    else:
        small_all = lax.all_gather(small_low, "seq")
    small_w = small_all.transpose(1, 0, 2).reshape(small_low.shape[0], width)

    qk_s, meta_qk_s = gather_weights(blocks(attn_master, [(0, 0), (0, 1)]), "zyx", place)
    v_s, meta_v_s = gather_weights(
        blocks(attn_master, [(0, 2)]), "zy", place, begin=(qk_s[0],)
    )
    lots_in_s, in_s = ((0, 2, meta_qk_s), (2, 1, meta_v_s)), [*qk_s, *v_s]

    ffn_picks = [(m, 2 * group + b) for group in range(2) for m in range(2) for b in range(2)]
    early = jnp.concatenate(
        [
            quarter_mine(blocks(attn_master, [(1, b) for b in range(4)]), place),
            quarter_mine(blocks(ffn_master, ffn_picks[:4]), place),
        ]
    )
    late = quarter_mine(blocks(ffn_master, ffn_picks[4:]), place)
    early_all = lax.all_gather(early, ("seq", "grp"))
    gains = small_w[:3].astype(F32)
    onehot = (action_codes[:, None] == jnp.arange(CODES)[None, :]).astype(BF)
    code_shift = jnp.dot(onehot, small_w[3:], preferred_element_type=F32)[:, None, :]

    piece_spec = pl.BlockSpec((frames, spot, width), lambda i, *_: (0, i, 0))
    part_spec = pl.BlockSpec((1, part, width), lambda i, *_: (i, 0, 0))
    sems = pltpu.SemaphoreType.DMA

    def held(count):
        return [pltpu.VMEM((count, width, width), BF)]

    def layer(body, lots, stacks, args, in_specs, out_specs, out_shape, scratch, us):
        return call(
            functools.partial(body, lots),
            spots,
            [*args, *stacks],
            in_specs + [ANY] * len(stacks),
            out_specs,
            out_shape,
            held(sum(count for _, count, _ in lots)) + scratch + [sems((len(lots),))],
            grid=(frames,),
            limit=60,
            us=us,
        )

    wide, flat_tile = tile(positions, 3 * width), tile(positions, width)
    wide_shape = shape_of(frames, positions, 3 * width)
    tile_shape = shape_of(frames, positions, width)
    tile32_shape = shape_of(frames, positions, width, dtype=F32)
    lse_spec, lse_shape = tile(heads_n, positions), shape_of(frames, heads_n, positions, dtype=F32)
    piece_shapes = [shape_of(frames, part, width)] * members
    gain_shape = shape_of(1, width, dtype=F32)

    def attention(packed, step):
        return call(
            functools.partial(attend_body, step),
            spots,
            [packed],
            [wide],
            [flat_tile, lse_spec],
            [tile_shape, lse_shape],
            [],
            grid=(frames,),
            limit=60,
            us=22,
        )

    def attention_back(packed, heads, heads_grad, lse, step):
        return call(
            functools.partial(attend_back_body, step),
            spots,
            [packed, heads, heads_grad, lse],
            [wide, flat_tile, flat_tile, lse_spec],
            wide,
            wide_shape,
            [],
            grid=(frames,),
            limit=60,
            us=26,
        )

    packed_s, normed_s = layer(
        spatial_in_body,
        lots_in_s,
        in_s,
        [frames_in, code_shift, gains],
        [flat_tile, tile(1, width), fixed(3, width)],
        [wide, flat_tile],
        [wide_shape, tile_shape],
        [],
        12,
    )
    late_all = lax.all_gather(after(late, packed_s), ("seq", "grp"))
    heads_s, lse_s = attention(packed_s, 0)
    out_s, meta_out_s = gather_weights(
        blocks(attn_master, [(0, 3)]), "zyx", place, begin=(v_s[0],), across_after=(packed_s,), cross=(heads_s,)
    )
    lots_out_s = ((0, 1, meta_out_s),)
    pieces = layer(
        spatial_out_body,
        lots_out_s,
        out_s,
        [heads_s, frames_in, code_shift],
        [flat_tile, flat_tile, tile(1, width)],
        [part_spec] * members,
        piece_shapes,
        [pltpu.VMEM((positions, width), BF)],
        6,
    )
    token_pieces = exchange(pieces)

    packed_t, heads_t, lse_t, normed_t, tokens_t, resid_two, third = call(
        temporal_fwd_body,
        spots,
        [*token_pieces, gains, early_all],
        [piece_spec] * members + [fixed(3, width), ANY],
        [wide, flat_tile, lse_spec] + [flat_tile] * 4,
        [wide_shape, tile_shape, lse_shape, tile_shape, tile_shape, tile32_shape, tile_shape],
        held(4) + [pltpu.VMEM((FPV, spot, width), BF), sems((1,))],
        grid=(tiles,),
        us=37,
    )

    def position_part(array, j):
        return lax.dynamic_slice_in_dim(array, (place[MEMBER] ^ j) * part, part, 1)

    cot_pieces = exchange(
        [after(position_part(cotangent, j), *token_pieces) for j in range(members)]
    )
    cot_tiles = call(
        tile_body,
        spots,
        [before(cot_pieces[0], third), *cot_pieces[1:]],
        [piece_spec] * members,
        tile(rows_tile, width),
        shape_of(tiles, rows_tile, width),
        [pltpu.VMEM((FPV, spot, width), BF)],
        grid=(tiles,),
    )

    def split_shape(kind, n):
        lead = (2, 2, nz) if kind == "xyz" else (2, nz, 2)
        return shape_of(*lead, n, local_rows, width // 4)

    flat = lambda array: array.reshape(tokens, width)
    resid_now = flat(resid_two)
    full32 = shape_of(tokens, width, dtype=F32)
    parts_f = []
    groups = 2
    for group in range(groups):
        last = group == groups - 1
        ends = [full32] + [shape_of(frames, part, width)] * members if last else [full32, full32]
        args = [flat(third), flat(cot_tiles), resid_now, late_all if group else early_all]
        if group:
            args += [dx]
        outs = call(
            functools.partial(ffn_body, group, 0 if group else 4, last, "xyz"),
            spots,
            args,
            [ANY] * len(args),
            [ANY] * (2 + len(ends)),
            [split_shape("xyz", 4)] * 2 + ends,
            [pltpu.VMEM((tokens, width), BF)] * 2
            + [pltpu.VMEM((width, tokens), BF)] * 2
            + [pltpu.VMEM((tokens, width), F32)] * 2
            + [pltpu.VMEM((4, width, width), BF)]
            + [pltpu.VMEM((tokens, width), BF)] * 2
            + [pltpu.VMEM((4, width, width), BF), sems((8,))],
            us=41,
        )
        parts_f.append(outs[:2])
        if last:
            dx, block_pieces = outs[2], outs[3:]
        else:
            resid_now, dx = outs[2:]
            sum_e = send_core(outs[:2])

    quarters = {}
    sum_f = send_core(parts_f[1])
    sum_e = step_one(*pinned(sum_e, dx))
    dx = before(dx, sum_e)
    sum_e = send_one(*sum_e, "xyz")
    outs = call(
        temporal_bwd_body,
        spots,
        [dx.reshape(resid_two.shape), cot_tiles, resid_two, tokens_t, packed_t, heads_t, lse_t, gains, early_all],
        [flat_tile] * 4 + [wide, flat_tile, lse_spec, fixed(3, width), ANY],
        [flat_tile, wide, fixed(2, width)] + [piece_spec] * members,
        [tile_shape, wide_shape, shape_of(2, width, dtype=F32)] + piece_shapes,
        held(4)
        + [
            pltpu.VMEM((1, positions, width), BF),
            pltpu.VMEM((FPV, spot, width), BF),
            sems((1,)),
        ],
        grid=(tiles,),
        us=38,
    )
    branch_t, grad_t, gains_two = outs[:3]
    grad_pieces = exchange(outs[3:])
    block_pieces = exchange(block_pieces)
    join = functools.partial(
        call,
        body=join_body,
        place=spots,
        in_specs=[part_spec] * members,
        out_specs=tile(positions, width),
        out_shape=shape_of(frames, positions, width),
        scratch=[],
        grid=(frames,),
    )
    block_out = join(args=[before(block_pieces[0], grad_t), *block_pieces[1:]])


    def weight_grads(kinds, sides, *lots):
        sides = [side.reshape(tokens, -1) for side in sides]
        outs = call(
            functools.partial(weight_grad_body, kinds, lots),
            spots,
            sides,
            [ANY] * len(sides),
            [ANY] * (2 * len(lots)),
            [split_shape(kind, len(lot)) for kind, lot in zip(kinds, lots) for _ in range(2)],
            [pltpu.VMEM(side.shape, BF) for side in sides]
            + [pltpu.VMEM((width, tokens), BF)] * (len(sides) // 2)
            + [pltpu.VMEM((sum(map(len, lots)), width, width), BF), sems((len(sides) + 1,))],
            us=15,
        )
        return [outs[2 * i : 2 * i + 2] for i in range(len(lots))]

    kinds = ("xyz", "yzx")
    sum_f = step_one(*pinned(sum_f, grad_t))
    (parts_t,) = weight_grads(
        ("xyz",),
        [normed_t, before(grad_t, sum_f, block_out), heads_t, branch_t],
        [(0, 0), (0, 1), (0, 2), (1, 0)],
    )
    sum_f = send_one(*sum_f, "xyz")
    sum_t = send_core(parts_t)

    branch_s, heads_grad_s = layer(
        spatial_branch_body,
        lots_out_s,
        out_s,
        [before(grad_pieces[0], parts_t), *grad_pieces[1:]],
        [part_spec] * members,
        [flat_tile] * 2,
        [tile_shape] * 2,
        [],
        7,
    )
    sum_e = step_two(*pinned(sum_e, branch_s), "xyz")
    sum_t = step_one(*pinned(sum_t, branch_s))
    grad_s = attention_back(packed_s, heads_s, before(heads_grad_s, sum_e, sum_t), lse_s, 0)
    sum_e, sum_t = send_two(*sum_e, "xyz"), send_one(*sum_t, "xyz")
    sum_e = step_three(*pinned(sum_e, grad_s), "xyz")
    sum_f = step_two(*pinned(sum_f, grad_s), "xyz")
    parts_s = weight_grads(
        kinds,
        [normed_s, before(grad_s, sum_e, sum_f), heads_s, branch_s],
        [(0, 0), (0, 1)],
        [(0, 2), (1, 0)],
    )
    quarters["ffn0"] = send_three(*sum_e, "xyz", parts_s[0][0])
    sum_f = send_two(*sum_f, "xyz")
    sums_s = [send_core(parts) for parts in parts_s]
    sum_f = step_three(*pinned(sum_f, parts_s[0][0]), "xyz")
    sum_t = step_two(*pinned(sum_t, parts_s[0][0]), "xyz")
    input_grad, gain_one, columns = layer(
        spatial_end_body,
        lots_in_s,
        in_s,
        [grad_s, frames_in, code_shift, before(branch_s, parts_s, sum_t, sum_f), gains],
        [wide, flat_tile, tile(1, width), flat_tile, fixed(3, width)],
        [flat_tile, fixed(1, width), tile(1, width)],
        [tile_shape, gain_shape, shape_of(frames, 1, width, dtype=F32)],
        [],
        14,
    )
    sum_t = send_two(*sum_t, "xyz")
    quarters["ffn1"] = send_three(*sum_f, "xyz", columns)
    sums_s = [step_one(*pinned(s, columns)) for s in sums_s]
    sums_s = [send_one(*s, kind) for s, kind in zip(sums_s, kinds)]
    sum_t = step_three(*pinned(sum_t, columns), "xyz")
    quarters["t"] = send_three(*sum_t, "xyz")
    sums_s = [send_two(*step_two(*s, kind), kind) for s, kind in zip(sums_s, kinds)]
    sums_s = [send_three(*step_three(*s, kind), kind) for s, kind in zip(sums_s, kinds)]
    quarters["qk"], quarters["vo"] = sums_s

    table_grad = jnp.dot(
        onehot.astype(F32).T, columns[:, 0, :], precision=lax.Precision.HIGHEST
    )
    squares = sum(jnp.sum(jnp.square(q.astype(F32))) for q in quarters.values())
    sums = all_sum(
        jnp.concatenate(
            [gain_one, gains_two, table_grad, jnp.broadcast_to(squares, (1, width))], axis=0
        )
    )
    small_grad = sums[:-1]

    total_squares = sums[-1, 0] + jnp.sum(small_grad * small_grad)
    grad_norm = jnp.sqrt(total_squares)
    clip_factor = 1.0 / jnp.maximum(grad_norm, 1.0)
    shared = {name: share_quarters(q) for name, q in quarters.items()}

    def updated(lots, master, first, second):
        def piece(lot):
            def at(m, b, *_):
                entry = 0
                for k, (matrix, block) in enumerate(lot):
                    entry = jnp.where((m == matrix) & (b == block), k, entry)
                return entry, 0, 0

            return pl.BlockSpec((1, local_rows, width // 4), at)

        block = pl.BlockSpec((1, local_rows, width), lambda m, b, *_: (m, 0, b))
        return call(
            functools.partial(update_body, [lot for _, lot in lots]),
            (place, clip_factor.reshape(1)),
            [p for name, _ in lots for p in shared[name]] + [master, first, second],
            [piece(lot) for _, lot in lots for _ in range(4)] + [block] * 3,
            [block] * 3,
            [shape_of(*master.shape, dtype=F32)] * 3,
            [],
            grid=(2, master.shape[2] // width),
            scalars=2,
        )

    attn_new = updated(
        [("qk", [(0, 0), (0, 1)]), ("vo", [(0, 2), (0, 3)]), ("t", [(1, b) for b in range(4)])],
        attn_master,
        attn_first,
        attn_second,
    )
    ffn_new = updated([("ffn0", ffn_picks[:4]), ("ffn1", ffn_picks[4:])], ffn_master, ffn_first, ffn_second)
    small_decay = jnp.where(jnp.arange(3 + CODES)[:, None] >= 3, decay_rate, 0.0)
    small_cols = small_master.shape[1]
    small_mine = lax.dynamic_slice_in_dim(small_grad, seq * small_cols, small_cols, 1)
    small_new = update(
        small_master, small_first, small_second, small_mine * clip_factor, rate_small, small_decay
    )
    return (block_out, input_grad, grad_norm, *attn_new, *ffn_new, *small_new)


def solution(mesh):
    token = P(("grp", "seq"), None, None)
    matrix = P(None, "seq", None)
    small = P(None, "seq")
    return jax.shard_map(
        shards,
        mesh=mesh,
        in_specs=(token, P(("grp", "seq")), token) + (matrix,) * 6 + (small,) * 3,
        out_specs=(token, token, P()) + (matrix,) * 6 + (small,) * 3,
        check_vma=False,
    )
```

time: 963 us -> 760 us (0.79)
  waiting for transfers between devices: 344 us -> 218 us
  Pallas kernels: 362 us -> 320 us
  blocking collectives: 41.2 us -> 0 us
  starting transfers between devices: 148 us -> 117 us
  other arithmetic: 38.6 us -> 60.4 us
  between operations: 7.35 us -> 21 us
    ppermute x69, waiting for transfers between devices: 239 us -> 173 us  [swap(): return lax.ppermute(value, axis, [(i, i ^ bit) for i in range(size)])]
    ppermute x33 -> x24, waiting for transfers between devices: 105 us -> 44.9 us  [shift_z(): lax.ppermute(value, 'seq', [(i, (i + 2 * step) % size) for i in range(siz...]
    pallas_call x12 -> x16, Pallas kernels: 362 us -> 320 us  [call(): pl.pallas_call(body, out_shape=out_shape, grid_spec=pltpu.PrefetchScalarG...]
    psum x1 -> x0, blocking collectives: 41.2 us -> none  [shards(): lax.psum(squares, ('seq', 'grp')) + jnp.sum(small_grad * small_grad)]
    convert_element_type x14, other arithmetic: 17.3 us -> 43.6 us  [add_low(): return (a.astype(F32) + b.astype(F32)).astype(BF)]
    ppermute x7 -> x0, starting transfers between devices: 12.4 us -> none  [shards(): lax.ppermute(small_low, 'seq', [(i, i ^ j) for i in range(seq_size)])]
    ppermute x69, starting transfers between devices: 73.5 us -> 61.5 us  [swap(): return lax.ppermute(value, axis, [(i, i ^ bit) for i in range(size)])]
    ppermute x33 -> x24, starting transfers between devices: 62 us -> 55.2 us  [shift_z(): lax.ppermute(value, 'seq', [(i, (i + 2 * step) % size) for i in range(siz...]
  transfers between devices with their start and end apart: 109 -> 95, of which waited for: 30 -> 41; matrix products, arithmetic and copies ran while one was open for 5% -> 8% of each run, Pallas kernels for 36% -> 38%
where the time goes in v2:
time: 760 us; the launch traced here: 754 us
  Pallas kernels  320 us (42%)
  waiting for transfers between devices  218 us (29%)
  starting transfers between devices  117 us (15%)
  other arithmetic  60.4 us (8%)
  between operations  21 us (3%)
  local copies, waits for them, and re-layouts  17.6 us (2%)
    pallas_call x16, Pallas kernels, call(): pl.pallas_call(body, out_shape=out_shape, grid_spec=pltpu.PrefetchScalarG...  320 us
    ppermute x69, waiting for transfers between devices, swap(): return lax.ppermute(value, axis, [(i, i ^ bit) for i in range(size)])  173 us
    ppermute x69, starting transfers between devices, swap(): return lax.ppermute(value, axis, [(i, i ^ bit) for i in range(size)])  61.5 us
    ppermute x24, starting transfers between devices, shift_z(): lax.ppermute(value, 'seq', [(i, (i + 2 * step) % size) for i in range(siz...  55.2 us
    ppermute x24, waiting for transfers between devices, shift_z(): lax.ppermute(value, 'seq', [(i, (i + 2 * step) % size) for i in range(siz...  44.9 us
    convert_element_type x14, other arithmetic, add_low(): return (a.astype(F32) + b.astype(F32)).astype(BF)  43.6 us
  transfers between devices with their start and end apart: 95, of which 41 were waited for; matrix products, arithmetic and copies ran while one was open for 8% of the time, Pallas kernels for 38%

profile of v2, /device:TPU:0, one launch (start us, length us, event | category | flops | bytes accessed | tf_op | source)
XLA Modules:
  0.0 753.8 jit_solution(14662261551335161513)
XLA Ops:
  15.2 3.1 collective-permute-start.3
  24.7 4.8 collective-permute-done.4
  31.7 7.4 collective-permute-start.13
  39.1 3.6 collective-permute-start.14
  43.5 4.7 collective-permute-done.13
  55.3 3.1 collective-permute-start.1
  58.5 2.6 collective-permute-done.1
  62.6 3.5 collective-permute-done.2
  67.4 6.8 collective-permute-done.16.refs_9_
  74.2 8.1 %collective-permute-done.8.refs_3_ = bf16[4,2,128,256]{3,2,1,0:T(8,128)(2,1)} collective-permute-done((bf16[4,2,128,256]{3,2,1,0:T(8,128)(2,1)S(1)}, bf16[4,2,128,256]{3,2,1,0:T(8,128)(2,1)}, u32[]{:S(2)}, u32[]{:S(2)}) %collective-permute-start.8) | collective-permute-done | bytes 524320 | tf_op jit(solution)/shard_map/ppermute | solution.py:46
  85.7 14.0 %shard_map.211 = (bf16[4,256,3072]{2,1,0:T(8,128)(2,1)}, bf16[4,256,1024]{2,1,0:T(8,128)(2,1)}) custom-call(s32[5]{0:T(128)} %stack.84.place, bf16[4,256,1024]{2,1,0:T(8,128)(2,1)} %frames_ref.5, f32[4,1,1024]{2,1,0:T(1,128)} %broadcast_in_dim.33.shift_ref, f32[3,1024]{1,0:T(4,128)} %fusion.82.gain_ref.refs_4_, bf16[4,2,128,256]{3,2,1,0:T(8,128)(2,1)} %copy-done.10, ...), custom_call_target="tpu_custom_call" | custom-call | flops 12000000000 | bytes 1048576 | tf_op jit(solution)/shard_map/pallas_call | solution.py:691
  104.1 3.1 collective-permute-start.21
  108.7 5.3 collective-permute-done.20
  115.7 12.7 %collective-permute-done.22.refs_1_.refs_5_ = bf16[4,1,128,256]{3,2,1,0:T(8,128)(2,1)S(1)} collective-permute-done((bf16[4,1,128,256]{3,2,1,0:T(8,128)(2,1)S(1)}, bf16[4,1,128,256]{3,2,1,0:T(8,128)(2,1)S(1)}, u32[]{:S(2)}, u32[]{:S(2)}) %collective-permute-start.22) | collective-permute-done | bytes 262176 | tf_op jit(solution)/shard_map/ppermute | solution.py:46
  128.4 2.6 collective-permute-start.24
  131.1 22.3 %shard_map.212 = (bf16[4,256,1024]{2,1,0:T(8,128)(2,1)}, f32[4,16,256]{2,1,0:T(8,128)}) custom-call(s32[5]{0:T(128)} %stack.84.place, bf16[4,256,3072]{2,1,0:T(8,128)(2,1)} %get-tuple-element.101.packed_ref), custom_call_target="tpu_custom_call" | custom-call | flops 22000001024 | bytes 1048576 | tf_op jit(solution)/shard_map/pallas_call | solution.py:691
  156.9 8.2 %shard_map.213 = (bf16[4,64,1024]{2,1,0:T(8,128)(2,1)}, bf16[4,64,1024]{2,1,0:T(8,128)(2,1)}, bf16[4,64,1024]{2,1,0:T(8,128)(2,1)}, bf16[4,64,1024]{2,1,0:T(8,128)(2,1)}) custom-call(s32[5]{0:T(128)} %stack.84.place, bf16[4,256,1024]{2,1,0:T(8,128)(2,1)} %get-tuple-element.102.heads_ref, bf16[4,256,1024]{2,1,0:T(8,128)(2,1)} %frames_ref.5, ...), custom_call_target="tpu_custom_call" | custom-call | flops 6000000000 | bytes 1048576 | tf_op jit(solution)/shard_map/pallas_call | solution.py:691
  167.3 5.6 collective-permute-start.30
  174.1 7.8 %collective-permute-done.29.refs_1_ = bf16[4,64,1024]{2,1,0:T(8,128)(2,1)} collective-permute-done((bf16[4,64,1024]{2,1,0:T(8,128)(2,1)}, bf16[4,64,1024]{2,1,0:T(8,128)(2,1)}, u32[]{:S(2)}, u32[]{:S(2)}) %collective-permute-start.29) | collective-permute-done | bytes 524320 | tf_op jit(solution)/shard_map/ppermute | solution.py:46
  181.9 8.1 %collective-permute-done.30.refs_2_ = bf16[4,64,1024]{2,1,0:T(8,128)(2,1)} collective-permute-done((bf16[4,64,1024]{2,1,0:T(8,128)(2,1)}, bf16[4,64,1024]{2,1,0:T(8,128)(2,1)}, u32[]{:S(2)}, u32[]{:S(2)}) %collective-permute-start.30) | collective-permute-done | bytes 524320 | tf_op jit(solution)/shard_map/ppermute | solution.py:46
  190.0 23.1 %collective-permute-done.31.refs_3_ = bf16[4,64,1024]{2,1,0:T(8,128)(2,1)} collective-permute-done((bf16[4,64,1024]{2,1,0:T(8,128)(2,1)}, bf16[4,64,1024]{2,1,0:T(8,128)(2,1)}, u32[]{:S(2)}, u32[]{:S(2)}) %collective-permute-start.31) | collective-permute-done | bytes 524320 | tf_op jit(solution)/shard_map/ppermute | solution.py:46
  216.5 37.0 %shard_map.214 = (bf16[4,256,3072]{2,1,0:T(8,128)(2,1)}, bf16[4,256,1024]{2,1,0:T(8,128)(2,1)}, f32[4,16,256]{2,1,0:T(8,128)}, bf16[4,256,1024]{2,1,0:T(8,128)(2...) custom-call(s32[5]{0:T(128)} %stack.84.place, ...), custom_call_target="tpu_custom_call" | custom-call | flops 36999999488 | bytes 1048576 | tf_op jit(solution)/shard_map/pallas_call | solution.py:691
  255.3 5.0 shard_map.215.cot_ref
  260.2 40.8 %shard_map.216 = (bf16[2,2,4,4,128,256]{5,4,3,2,1,0:T(8,128)(2,1)}, bf16[2,2,4,4,128,256]{5,4,3,2,1,0:T(8,128)(2,1)}, f32[1024,1024]{1,0:T(8,128)}, f32[1024,1024]{1,0:T(8,128)}) custom-call(s32[5]{0:T(128)} %stack.84.place, bf16[1024,1024]{1,0:T(8,128)(2,1)} %bitcast.297, bf16[1024,1024]{1,0:T(8,128)(2,1)} %bitcast.295, f32[1024,1024]{1,0:T(8,128)} %bitcast.288, ...), custom_call_target="tpu_custom_call" | custom-call | flops 41000001536 | bytes 1048576 | tf_op jit(solution)/shard_map/pallas_call | solution.py:691
  301.2 41.3 %shard_map.217 = (bf16[2,2,4,4,128,256]{5,4,3,2,1,0:T(8,128)(2,1)}, bf16[2,2,4,4,128,256]{5,4,3,2,1,0:T(8,128)(2,1)}, f32[1024,1024]{1,0:T(8,128)}, bf16[4,64,10...) custom-call(s32[5]{0:T(128)} %stack.84.place, ...), custom_call_target="tpu_custom_call" | custom-call | flops 41000001536 | bytes 1048576 | tf_op jit(solution)/shard_map/pallas_call | solution.py:691
  346.5 5.6 add_convert_fusion.3
  352.1 41.5 %shard_map.218 = (bf16[4,256,1024]{2,1,0:T(8,128)(2,1)}, bf16[4,256,3072]{2,1,0:T(8,128)(2,1)}, f32[2,1024]{1,0:T(2,128)}, bf16[4,64,1024]{2,1,0:T(8,128)(2,1)},...) custom-call(s32[5]{0:T(128)} %stack.84.place, ...), custom_call_target="tpu_custom_call" | custom-call | flops 38000001024 | bytes 1048576 | tf_op jit(solution)/shard_map/pallas_call | solution.py:691
  393.6 5.2 add_convert_fusion.1
  400.6 4.9 shard_map.219
  405.5 15.2 %shard_map.220 = (bf16[2,2,4,4,128,256]{5,4,3,2,1,0:T(8,128)(2,1)}, bf16[2,2,4,4,128,256]{5,4,3,2,1,0:T(8,128)(2,1)}) custom-call(s32[5]{0:T(128)} %stack.84.place, bf16[1024,1024]{1,0:T(8,128)(2,1)} %bitcast.294, bf16[1024,3072]{1,0:T(8,128)(2,1)} %bitcast.287, bf16[1024,1024]{1,0:T(8,128)(2,1)} %bitcast.293, bf16[1024,1024]{1,0:T(8,128)(2,1)} %bitcast.299), custom_call_target="tpu_custom_call" | custom-call | flops 15000000512 | bytes 1048576 | tf_op jit(solution)/shard_map/pallas_call | solution.py:691
  425.9 10.5 %collective-permute-done.40.refs_1_ = bf16[4,64,1024]{2,1,0:T(8,128)(2,1)S(1)} collective-permute-done((bf16[4,64,1024]{2,1,0:T(8,128)(2,1)S(1)}, bf16[4,64,1024]{2,1,0:T(8,128)(2,1)S(1)}, u32[]{:S(2)}, u32[]{:S(2)}) %collective-permute-start.40) | collective-permute-done | bytes 524320 | tf_op jit(solution)/shard_map/ppermute | solution.py:46
  439.2 9.8 %collective-permute-done.42.refs_3_ = bf16[4,64,1024]{2,1,0:T(8,128)(2,1)} collective-permute-done((bf16[4,64,1024]{2,1,0:T(8,128)(2,1)S(1)}, bf16[4,64,1024]{2,1,0:T(8,128)(2,1)}, u32[]{:S(2)}, u32[]{:S(2)}) %collective-permute-start.42) | collective-permute-done | bytes 524320 | tf_op jit(solution)/shard_map/ppermute | solution.py:46
  448.9 7.9 %shard_map.221 = (bf16[4,256,1024]{2,1,0:T(8,128)(2,1)}, bf16[4,256,1024]{2,1,0:T(8,128)(2,1)}) custom-call(s32[5]{0:T(128)} %stack.84.place, bf16[4,64,1024]{2,1,0:T(8,128)(2,1)} %get-tuple-element.148.refs_0_, bf16[4,64,1024]{2,1,0:T(8,128)(2,1)} %copy-done.41, bf16[4,64,1024]{2,1,0:T(8,128)(2,1)} %copy-done.43, ...), custom_call_target="tpu_custom_call" | custom-call | flops 7000000000 | bytes 1048576 | tf_op jit(solution)/shard_map/pallas_call | solution.py:691
  456.8 12.8 %collective-permute-done.43 = bf16[2,4,4,128,256]{4,3,2,1,0:T(8,128)(2,1)} collective-permute-done((bf16[2,4,4,128,256]{4,3,2,1,0:T(8,128)(2,1)}, bf16[2,4,4,128,256]{4,3,2,1,0:T(8,128)(2,1)}, u32[]{:S(2)}, u32[]{:S(2)}) %collective-permute-start.43) | collective-permute-done | bytes 2097184 | tf_op jit(solution)/shard_map/ppermute | solution.py:46
  469.6 4.1 fusion.7
  474.9 4.4 add_convert_fusion
  480.8 23.1 %shard_map.222.grad_ref = bf16[4,256,3072]{2,1,0:T(8,128)(2,1)} custom-call(s32[5]{0:T(128)} %stack.84.place, bf16[4,256,3072]{2,1,0:T(8,128)(2,1)} %get-tuple-element.101.packed_ref, bf16[4,256,1024]{2,1,0:T(8,128)(2,1)} %get-tuple-element.102.heads_ref, bf16[4,256,1024]{2,1,0:T(8,128)(2,1)} %get-tuple-element.156.heads_grad_ref, ...), custom_call_target="tpu_custom_call" | custom-call | flops 25999998976 | bytes 1048576 | tf_op jit(solution)/shard_map/pallas_call | solution.py:691
  503.9 10.6 %collective-permute-done.46 = bf16[2,4,4,128,256]{4,3,2,1,0:T(8,128)(2,1)} collective-permute-done((bf16[2,4,4,128,256]{4,3,2,1,0:T(8,128)(2,1)}, bf16[2,4,4,128,256]{4,3,2,1,0:T(8,128)(2,1)}, u32[]{:S(2)}, u32[]{:S(2)}) %collective-permute-start.46) | collective-permute-done | bytes 2097184 | tf_op jit(solution)/shard_map/ppermute | solution.py:46
  514.6 3.8 fusion.4
  521.8 15.2 %shard_map.223 = (bf16[2,2,4,2,128,256]{5,4,3,2,1,0:T(8,128)(2,1)}, bf16[2,2,4,2,128,256]{5,4,3,2,1,0:T(8,128)(2,1)}, bf16[2,4,2,2,128,256]{5,4,3,2,1,0:T(8,128)(2,1)}, bf16[2,4,2,2,128,256]{5,4,3,2,1,0:T(8,128)(2,1)}) custom-call(s32[5]{0:T(128)} %stack.84.place, bf16[1024,1024]{1,0:T(8,128)(2,1)} %bitcast.290, bf16[1024,3072]{1,0:T(8,128)(2,1)} %bitcast.286, ...), custom_call_target="tpu_custom_call" | custom-call | flops 15000000512 | bytes 1048576 | tf_op jit(solution)/shard_map/pallas_call | solution.py:691
  537.7 2.7 collective-permute-start.50
  545.3 13.7 %collective-permute-done.47 = bf16[2,4,4,128,256]{4,3,2,1,0:T(8,128)(2,1)} collective-permute-done((bf16[2,4,4,128,256]{4,3,2,1,0:T(8,128)(2,1)}, bf16[2,4,4,128,256]{4,3,2,1,0:T(8,128)(2,1)}, u32[]{:S(2)}, u32[]{:S(2)}) %collective-permute-start.47) | collective-permute-done | bytes 2097184 | tf_op jit(solution)/shard_map/ppermute | solution.py:46
  559.0 3.0 collective-permute-start.51
  562.1 3.3 fusion.3
  565.4 16.0 %shard_map.224 = (bf16[4,256,1024]{2,1,0:T(8,128)(2,1)}, f32[1,1024]{1,0:T(1,128)}, f32[4,1,1024]{2,1,0:T(1,128)}) custom-call(s32[5]{0:T(128)} %stack.84.place, bf16[4,256,3072]{2,1,0:T(8,128)(2,1)} %shard_map.222.grad_ref, bf16[4,256,1024]{2,1,0:T(8,128)(2,1)} %frames_ref.5, f32[4,1,1024]{2,1,0:T(1,128)} %broadcast_in_dim.33.shift_ref, ...), custom_call_target="tpu_custom_call" | custom-call | flops 14000000000 | bytes 1048576 | tf_op jit(solution)/shard_map/pallas_call | solution.py:691
  582.7 4.1 add_convert_fusion.7
  587.7 3.3 add_convert_fusion.9
  592.5 2.8 collective-permute-start.54
  598.9 7.1 collective-permute-done.53
  609.2 4.1 collective-permute-done.66
  622.6 13.2 %collective-permute-done.55 = bf16[4,4,128,256]{3,2,1,0:T(8,128)(2,1)} collective-permute-done((bf16[4,4,128,256]{3,2,1,0:T(8,128)(2,1)}, bf16[4,4,128,256]{3,2,1,0:T(8,128)(2,1)}, u32[]{:S(2)}, u32[]{:S(2)}) %collective-permute-start.55) | collective-permute-done | bytes 1048608 | tf_op jit(solution)/shard_map/ppermute | solution.py:46
  637.2 3.3 collective-permute-start.57
  640.5 4.9 collective-permute-start.58
  648.2 9.4 %collective-permute-done.57 = bf16[4,128,256]{2,1,0:T(8,128)(2,1)S(1)} collective-permute-done((bf16[4,128,256]{2,1,0:T(8,128)(2,1)S(1)}, bf16[4,128,256]{2,1,0:T(8,128)(2,1)S(1)}, u32[]{:S(2)}, u32[]{:S(2)}) %collective-permute-start.57) | collective-permute-done | bytes 262176 | tf_op jit(solution)/shard_map/ppermute | solution.py:51
  660.1 6.1 collective-permute-start.62
  671.9 4.5 collective-permute-done.63
  680.5 3.1 collective-permute-done.72
  685.3 3.3 collective-permute-start.75
  691.1 2.7 collective-permute-done.76
  695.5 2.7 collective-permute-done.87.refs_1_
  698.7 3.8 collective-permute-done.90.refs_5_
  707.8 6.3 collective-permute-done.81.refs_5_
  715.3 13.8 %shard_map.226 = (f32[2,128,4096]{2,1,0:T(8,128)}, f32[2,128,4096]{2,1,0:T(8,128)}, f32[2,128,4096]{2,1,0:T(8,128)}) custom-call(s32[5]{0:T(128)} %stack.84.place, f32[1]{0:T(128)} %bitcast.97.clip, bf16[4,128,256]{2,1,0:T(8,128)(2,1)} %get-tuple-element.200.refs_0_, bf16[4,128,256]{2,1,0:T(8,128)(2,1)} %copy-done.51, bf16[4,128,256]{2,1,0:T(8,128)(2,1)} %copy-done.52, ...), custom_call_target="tpu_custom_call" | custom-call | flops 10000000000 | bytes 1048576 | tf_op jit(solution)/shard_map/pallas_call | solution.py:691
  732.0 13.6 %shard_map.225 = (f32[2,128,4096]{2,1,0:T(8,128)}, f32[2,128,4096]{2,1,0:T(8,128)}, f32[2,128,4096]{2,1,0:T(8,128)}) custom-call(s32[5]{0:T(128)} %stack.84.place, f32[1]{0:T(128)} %bitcast.97.clip, bf16[2,128,256]{2,1,0:T(8,128)(2,1)} %copy-done.20, bf16[2,128,256]{2,1,0:T(8,128)(2,1)} %copy-done.63, bf16[2,128,256]{2,1,0:T(8,128)(2,1)} %copy-done.64, ...), custom_call_target="tpu_custom_call" | custom-call | flops 10000000000 | bytes 1048576 | tf_op jit(solution)/shard_map/pallas_call | solution.py:691
  (341 shorter events, 123.0 us)
Async XLA Ops:
  7.2 209.4 %all-gather.5.cloned.1.call-start = ((), (), s32[]{:S(2)}) async-start(), calls=%async_computation | async-start | bytes 17301504 | tf_op jit(solution)/shard_map/all_gather | solution.py:777
  15.1 286.1 %all-gather.7.cloned.1.call-start = ((), (), s32[]{:S(2)}) async-start(), calls=%async_computation.1 | async-start | bytes 8650752 | tf_op jit(solution)/shard_map/all_gather | solution.py:850
  29.6 24.2 %collective-permute-start.6 = (bf16[4,2,128,256]{3,2,1,0:T(8,128)(2,1)S(1)}, bf16[4,2,128,256]{3,2,1,0:T(8,128)(2,1)S(1)}, u32[]{:S(2)}, u32[]{:S(2)}) collective-permute-start(bf16[4,2,128,256]{3,2,1,0:T(8,128)(2,1)S(1)} %pad_maximum_fusion.refs_0_), channel_id=1, source_target_pairs={{0,4},{4,0},{8,12},{12,8},{16,20},{20,16},{24,28},{28,24},{1,5},{5... | collective-permute-start | bytes 1572872 | tf_op jit(solution)/shard_map/ppermute | solution.py:46
  31.2 24.1 %collective-permute-start = (bf16[1,11,128]{2,1,0:T(8,128)(2,1)S(1)}, bf16[1,11,128]{2,1,0:T(8,128)(2,1)S(1)}, u32[]{:S(2)}, u32[]{:S(2)}) collective-permute-start(bf16[1,11,128]{2,1,0:T(8,128)(2,1)S(1)} %convert_bitcast_fusion), channel_id=1, source_target_pairs={{0,4},{4,0},{8,12},{12,8},{16,20},{20,16},{24,28},{28,24},{1,5},{5... | collective-permute-start | bytes 8456 | tf_op jit(solution)/shard_map/ppermute | solution.py:46
  31.7 16.4 %collective-permute-start.13 = (bf16[1,128,512]{2,1,0:T(8,128)(2,1)S(1)}, bf16[1,128,512]{2,1,0:T(8,128)(2,1)S(1)}, u32[]{:S(2)}, u32[]{:S(2)}) collective-permute-start(bf16[1,128,512]{2,1,0:T(8,128)(2,1)S(1)} %constant_dynamic-slice_fusion.5), channel_id=1, source_target_pairs={{0,8},{4,12},{8,16},{12,20},{16,24},{20,28},{24,0},{28,4},{1,9},{5... | collective-permute-start | bytes 393224 | tf_op jit(solution)/shard_map/ppermute | solution.py:51
  39.1 13.1 %collective-permute-start.14 = (bf16[1,128,512]{2,1,0:T(8,128)(2,1)S(1)}, bf16[1,128,512]{2,1,0:T(8,128)(2,1)S(1)}, u32[]{:S(2)}, u32[]{:S(2)}) collective-permute-start(bf16[1,128,512]{2,1,0:T(8,128)(2,1)S(1)} %constant_dynamic-slice_fusion.5), channel_id=1, source_target_pairs={{0,16},{4,20},{8,24},{12,28},{16,0},{20,4},{24,8},{28,12},{1,17},{... | collective-permute-start | bytes 393224 | tf_op jit(solution)/shard_map/ppermute | solution.py:51
  48.1 18.6 %collective-permute-start.7 = (bf16[4,2,128,256]{3,2,1,0:T(8,128)(2,1)S(1)}, bf16[4,2,128,256]{3,2,1,0:T(8,128)(2,1)S(1)}, u32[]{:S(2)}, u32[]{:S(2)}) collective-permute-start(bf16[4,2,128,256]{3,2,1,0:T(8,128)(2,1)S(1)} %pad_maximum_fusion.refs_0_), channel_id=1, source_target_pairs={{0,2},{1,3},{2,0},{3,1},{4,6},{5,7},{6,4},{7,5},{8,10},{9,11},{10,... | collective-permute-start | bytes 1572872 | tf_op jit(solution)/shard_map/ppermute | solution.py:46
  52.2 15.1 %collective-permute-start.9 = (bf16[4,2,128,256]{3,2,1,0:T(8,128)(2,1)S(1)}, bf16[4,2,128,256]{3,2,1,0:T(8,128)(2,1)}, u32[]{:S(2)}, u32[]{:S(2)}) collective-permute-start(bf16[4,2,128,256]{3,2,1,0:T(8,128)(2,1)S(1)} %pad_maximum_fusion.refs_0_), channel_id=1, source_target_pairs={{0,1},{1,0},{2,3},{3,2},{4,5},{5,4},{6,7},{7,6},{8,9},{9,8},{10,11... | collective-permute-start | bytes 1572872 | tf_op jit(solution)/shard_map/ppermute | solution.py:46
  52.3 21.9 %collective-permute-start.16 = (bf16[4,1,128,512]{3,2,1,0:T(8,128)(2,1)S(1)}, bf16[4,1,128,512]{3,2,1,0:T(8,128)(2,1)S(1)}, u32[]{:S(2)}, u32[]{:S(2)}) collective-permute-start(bf16[4,1,128,512]{3,2,1,0:T(8,128)(2,1)S(1)} %pad_maximum_fusion.1.refs_8_), channel_id=1, source_target_pairs={{0,4},{4,0},{8,12},{12,8},{16,20},{20,16},{24,28},{28,24},{1,5},{5... | collective-permute-start | bytes 1572872 | tf_op jit(solution)/shard_map/ppermute | solution.py:46
  53.8 28.4 %collective-permute-start.8 = (bf16[4,2,128,256]{3,2,1,0:T(8,128)(2,1)S(1)}, bf16[4,2,128,256]{3,2,1,0:T(8,128)(2,1)}, u32[]{:S(2)}, u32[]{:S(2)}) collective-permute-start(bf16[4,2,128,256]{3,2,1,0:T(8,128)(2,1)S(1)} %collective-permute-done.6.refs_1_), channel_id=1, source_target_pairs={{0,2},{1,3},{2,0},{3,1},{4,6},{5,7},{6,4},{7,5},{8,10},{9,11},{10,... | collective-permute-start | bytes 1572872 | tf_op jit(solution)/shard_map/ppermute | solution.py:46
  66.7 17.1 %collective-permute-start.17 = (bf16[4,1,128,512]{3,2,1,0:T(8,128)(2,1)S(1)}, bf16[4,1,128,512]{3,2,1,0:T(8,128)(2,1)S(1)}, u32[]{:S(2)}, u32[]{:S(2)}) collective-permute-start(bf16[4,1,128,512]{3,2,1,0:T(8,128)(2,1)S(1)} %pad_maximum_fusion.1.refs_8_), channel_id=1, source_target_pairs={{0,1},{1,0},{2,3},{3,2},{4,5},{5,4},{6,7},{7,6},{8,9},{9,8},{10,11... | collective-permute-start | bytes 1572872 | tf_op jit(solution)/shard_map/ppermute | solution.py:46
  66.8 17.0 %collective-permute-start.10 = (bf16[4,2,128,256]{3,2,1,0:T(8,128)(2,1)S(1)}, bf16[4,2,128,256]{3,2,1,0:T(8,128)(2,1)S(1)}, u32[]{:S(2)}, u32[]{:S(2)}) collective-permute-start(bf16[4,2,128,256]{3,2,1,0:T(8,128)(2,1)S(1)} %collective-permute-done.6.refs_1_), channel_id=1, source_target_pairs={{0,1},{1,0},{2,3},{3,2},{4,5},{5,4},{6,7},{7,6},{8,9},{9,8},{10,11... | collective-permute-start | bytes 1572872 | tf_op jit(solution)/shard_map/ppermute | solution.py:46
  67.3 16.5 %collective-permute-start.11 = (bf16[4,2,128,256]{3,2,1,0:T(8,128)(2,1)S(1)}, bf16[4,2,128,256]{3,2,1,0:T(8,128)(2,1)S(1)}, u32[]{:S(2)}, u32[]{:S(2)}) collective-permute-start(bf16[4,2,128,256]{3,2,1,0:T(8,128)(2,1)S(1)} %collective-permute-done.7.refs_2_), channel_id=1, source_target_pairs={{0,1},{1,0},{2,3},{3,2},{4,5},{5,4},{6,7},{7,6},{8,9},{9,8},{10,11... | collective-permute-start | bytes 1572872 | tf_op jit(solution)/shard_map/ppermute | solution.py:46
  114.1 14.4 %collective-permute-start.22 = (bf16[4,1,128,256]{3,2,1,0:T(8,128)(2,1)S(1)}, bf16[4,1,128,256]{3,2,1,0:T(8,128)(2,1)S(1)}, u32[]{:S(2)}, u32[]{:S(2)}) collective-permute-start(bf16[4,1,128,256]{3,2,1,0:T(8,128)(2,1)S(1)} %pad_maximum_fusion.3.refs_0_.refs_4_), channel_id=1, source_target_pairs={{0,4},{4,0},{8,12},{12,8},{16,20},{20,16},{24,28},{28,24},{1,5},{5... | collective-permute-start | bytes 786440 | tf_op jit(solution)/shard_map/ppermute | solution.py:46
  128.4 25.5 %collective-permute-start.24 = (bf16[4,1,128,256]{3,2,1,0:T(8,128)(2,1)S(1)}, bf16[4,1,128,256]{3,2,1,0:T(8,128)(2,1)S(1)}, u32[]{:S(2)}, u32[]{:S(2)}) collective-permute-start(bf16[4,1,128,256]{3,2,1,0:T(8,128)(2,1)S(1)} %collective-permute-done.22.refs_1_.refs_5_), channel_id=1, source_target_pairs={{0,2},{1,3},{2,0},{3,1},{4,6},{5,7},{6,4},{7,5},{8,10},{9,11},{10,... | collective-permute-start | bytes 786440 | tf_op jit(solution)/shard_map/ppermute | solution.py:46
  131.0 23.0 %collective-permute-start.23 = (bf16[4,1,128,256]{3,2,1,0:T(8,128)(2,1)S(1)}, bf16[4,1,128,256]{3,2,1,0:T(8,128)(2,1)S(1)}, u32[]{:S(2)}, u32[]{:S(2)}) collective-permute-start(bf16[4,1,128,256]{3,2,1,0:T(8,128)(2,1)S(1)} %pad_maximum_fusion.3.refs_0_.refs_4_), channel_id=1, source_target_pairs={{0,2},{1,3},{2,0},{3,1},{4,6},{5,7},{6,4},{7,5},{8,10},{9,11},{10,... | collective-permute-start | bytes 786440 | tf_op jit(solution)/shard_map/ppermute | solution.py:46
  165.0 16.9 %collective-permute-start.29 = (bf16[4,64,1024]{2,1,0:T(8,128)(2,1)}, bf16[4,64,1024]{2,1,0:T(8,128)(2,1)}, u32[]{:S(2)}, u32[]{:S(2)}) collective-permute-start(bf16[4,64,1024]{2,1,0:T(8,128)(2,1)} %get-tuple-element.111), channel_id=1, source_target_pairs={{0,4},{4,0},{8,12},{12,8},{16,20},{20,16},{24,28},{28,24},{1,5},{5... | collective-permute-start | bytes 1572872 | tf_op jit(solution)/shard_map/ppermute | solution.py:46
  167.3 22.7 %collective-permute-start.30 = (bf16[4,64,1024]{2,1,0:T(8,128)(2,1)}, bf16[4,64,1024]{2,1,0:T(8,128)(2,1)}, u32[]{:S(2)}, u32[]{:S(2)}) collective-permute-start(bf16[4,64,1024]{2,1,0:T(8,128)(2,1)} %get-tuple-element.112), channel_id=1, source_target_pairs={{0,8},{4,12},{8,0},{12,4},{16,24},{20,28},{24,16},{28,20},{1,9},{5... | collective-permute-start | bytes 1572872 | tf_op jit(solution)/shard_map/ppermute | solution.py:46
  172.8 40.2 %collective-permute-start.31 = (bf16[4,64,1024]{2,1,0:T(8,128)(2,1)}, bf16[4,64,1024]{2,1,0:T(8,128)(2,1)}, u32[]{:S(2)}, u32[]{:S(2)}) collective-permute-start(bf16[4,64,1024]{2,1,0:T(8,128)(2,1)} %get-tuple-element.113), channel_id=1, source_target_pairs={{0,12},{4,8},{8,4},{12,0},{16,28},{20,24},{24,20},{28,16},{1,13},{... | collective-permute-start | bytes 1572872 | tf_op jit(solution)/shard_map/ppermute | solution.py:46
  213.0 40.5 %collective-permute-start.34 = (bf16[4,64,1024]{2,1,0:T(8,128)(2,1)}, bf16[4,64,1024]{2,1,0:T(8,128)(2,1)S(1)}, u32[]{:S(2)}, u32[]{:S(2)}) collective-permute-start(bf16[4,64,1024]{2,1,0:T(8,128)(2,1)} %get-tuple-element.119), channel_id=1, source_target_pairs={{0,12},{4,8},{8,4},{12,0},{16,28},{20,24},{24,20},{28,16},{1,13},{... | collective-permute-start | bytes 1572872 | tf_op jit(solution)/shard_map/ppermute | solution.py:46
  213.0 40.5 %collective-permute-start.33 = (bf16[4,64,1024]{2,1,0:T(8,128)(2,1)S(1)}, bf16[4,64,1024]{2,1,0:T(8,128)(2,1)S(1)}, u32[]{:S(2)}, u32[]{:S(2)}) collective-permute-start(bf16[4,64,1024]{2,1,0:T(8,128)(2,1)S(1)} %get-tuple-element.118), channel_id=1, source_target_pairs={{0,8},{4,12},{8,0},{12,4},{16,24},{20,28},{24,16},{28,20},{1,9},{5... | collective-permute-start | bytes 1572872 | tf_op jit(solution)/shard_map/ppermute | solution.py:46
  215.2 38.3 %collective-permute-start.32 = (bf16[4,64,1024]{2,1,0:T(8,128)(2,1)S(1)}, bf16[4,64,1024]{2,1,0:T(8,128)(2,1)S(1)}, u32[]{:S(2)}, u32[]{:S(2)}) collective-permute-start(bf16[4,64,1024]{2,1,0:T(8,128)(2,1)S(1)} %get-tuple-element.117), channel_id=1, source_target_pairs={{0,4},{4,0},{8,12},{12,8},{16,20},{20,16},{24,28},{28,24},{1,5},{5... | collective-permute-start | bytes 1572872 | tf_op jit(solution)/shard_map/ppermute | solution.py:46
  301.1 45.4 %collective-permute-start.35 = (bf16[2,2,4,4,128,256]{5,4,3,2,1,0:T(8,128)(2,1)}, bf16[2,2,4,4,128,256]{5,4,3,2,1,0:T(8,128)(2,1)}, u32[]{:S(2)}, u32[]{:S(2)}) collective-permute-start(bf16[2,2,4,4,128,256]{5,4,3,2,1,0:T(8,128)(2,1)} %get-tuple-element.127), channel_id=1, source_target_pairs={{0,1},{1,0},{2,3},{3,2},{4,5},{5,4},{6,7},{7,6},{8,9},{9,8},{10,11... | collective-permute-start | bytes 12582920 | tf_op jit(solution)/shard_map/ppermute | solution.py:46
  342.5 51.2 %collective-permute-start.39 = (bf16[2,2,4,4,128,256]{5,4,3,2,1,0:T(8,128)(2,1)}, bf16[2,2,4,4,128,256]{5,4,3,2,1,0:T(8,128)(2,1)}, u32[]{:S(2)}, u32[]{:S(2)}) collective-permute-start(bf16[2,2,4,4,128,256]{5,4,3,2,1,0:T(8,128)(2,1)} %get-tuple-element.142), channel_id=1, source_target_pairs={{0,1},{1,0},{2,3},{3,2},{4,5},{5,4},{6,7},{7,6},{8,9},{9,8},{10,11... | collective-permute-start | bytes 12582920 | tf_op jit(solution)/shard_map/ppermute | solution.py:46
  343.0 55.8 %collective-permute-start.36 = (bf16[4,64,1024]{2,1,0:T(8,128)(2,1)}, bf16[4,64,1024]{2,1,0:T(8,128)(2,1)S(1)}, u32[]{:S(2)}, u32[]{:S(2)}) collective-permute-start(bf16[4,64,1024]{2,1,0:T(8,128)(2,1)} %get-tuple-element.136), channel_id=1, source_target_pairs={{0,4},{4,0},{8,12},{12,8},{16,20},{20,16},{24,28},{28,24},{1,5},{5... | collective-permute-start | bytes 1572872 | tf_op jit(solution)/shard_map/ppermute | solution.py:46
  344.2 54.6 %collective-permute-start.37 = (bf16[4,64,1024]{2,1,0:T(8,128)(2,1)}, bf16[4,64,1024]{2,1,0:T(8,128)(2,1)S(1)}, u32[]{:S(2)}, u32[]{:S(2)}) collective-permute-start(bf16[4,64,1024]{2,1,0:T(8,128)(2,1)} %get-tuple-element.137), channel_id=1, source_target_pairs={{0,8},{4,12},{8,0},{12,4},{16,24},{20,28},{24,16},{28,20},{1,9},{5... | collective-permute-start | bytes 1572872 | tf_op jit(solution)/shard_map/ppermute | solution.py:46
  344.6 54.2 %collective-permute-start.38 = (bf16[4,64,1024]{2,1,0:T(8,128)(2,1)}, bf16[4,64,1024]{2,1,0:T(8,128)(2,1)S(1)}, u32[]{:S(2)}, u32[]{:S(2)}) collective-permute-start(bf16[4,64,1024]{2,1,0:T(8,128)(2,1)} %get-tuple-element.138), channel_id=1, source_target_pairs={{0,12},{4,8},{8,4},{12,0},{16,28},{20,24},{24,20},{28,16},{1,13},{... | collective-permute-start | bytes 1572872 | tf_op jit(solution)/shard_map/ppermute | solution.py:46
  420.7 54.2 %collective-permute-start.44 = (bf16[2,2,4,4,128,256]{5,4,3,2,1,0:T(8,128)(2,1)}, bf16[2,2,4,4,128,256]{5,4,3,2,1,0:T(8,128)(2,1)}, u32[]{:S(2)}, u32[]{:S(2)}) collective-permute-start(bf16[2,2,4,4,128,256]{5,4,3,2,1,0:T(8,128)(2,1)} %get-tuple-element.147), channel_id=1, source_target_pairs={{0,1},{1,0},{2,3},{3,2},{4,5},{5,4},{6,7},{7,6},{8,9},{9,8},{10,11... | collective-permute-start | bytes 12582920 | tf_op jit(solution)/shard_map/ppermute | solution.py:46
  420.8 48.8 %collective-permute-start.43 = (bf16[2,4,4,128,256]{4,3,2,1,0:T(8,128)(2,1)}, bf16[2,4,4,128,256]{4,3,2,1,0:T(8,128)(2,1)}, u32[]{:S(2)}, u32[]{:S(2)}) collective-permute-start(bf16[2,4,4,128,256]{4,3,2,1,0:T(8,128)(2,1)} %get-tuple-element.206), channel_id=1, source_target_pairs={{0,2},{1,3},{2,0},{3,1},{4,6},{5,7},{6,4},{7,5},{8,10},{9,11},{10,... | collective-permute-start | bytes 6291464 | tf_op jit(solution)/shard_map/ppermute | solution.py:46
  422.4 14.0 %collective-permute-start.40 = (bf16[4,64,1024]{2,1,0:T(8,128)(2,1)S(1)}, bf16[4,64,1024]{2,1,0:T(8,128)(2,1)S(1)}, u32[]{:S(2)}, u32[]{:S(2)}) collective-permute-start(bf16[4,64,1024]{2,1,0:T(8,128)(2,1)S(1)} %copy-done.36), channel_id=1, source_target_pairs={{0,4},{4,0},{8,12},{12,8},{16,20},{20,16},{24,28},{28,24},{1,5},{5... | collective-permute-start | bytes 1572872 | tf_op jit(solution)/shard_map/ppermute | solution.py:46
  423.5 14.8 %collective-permute-start.41 = (bf16[4,64,1024]{2,1,0:T(8,128)(2,1)S(1)}, bf16[4,64,1024]{2,1,0:T(8,128)(2,1)S(1)}, u32[]{:S(2)}, u32[]{:S(2)}) collective-permute-start(bf16[4,64,1024]{2,1,0:T(8,128)(2,1)S(1)} %copy-done.35), channel_id=1, source_target_pairs={{0,8},{4,12},{8,0},{12,4},{16,24},{20,28},{24,16},{28,20},{1,9},{5... | collective-permute-start | bytes 1572872 | tf_op jit(solution)/shard_map/ppermute | solution.py:46
  424.5 24.4 %collective-permute-start.42 = (bf16[4,64,1024]{2,1,0:T(8,128)(2,1)S(1)}, bf16[4,64,1024]{2,1,0:T(8,128)(2,1)}, u32[]{:S(2)}, u32[]{:S(2)}) collective-permute-start(bf16[4,64,1024]{2,1,0:T(8,128)(2,1)S(1)} %copy-done.34), channel_id=1, source_target_pairs={{0,12},{4,8},{8,4},{12,0},{16,28},{20,24},{24,20},{28,16},{1,13},{... | collective-permute-start | bytes 1572872 | tf_op jit(solution)/shard_map/ppermute | solution.py:46
  436.4 78.1 %collective-permute-start.46 = (bf16[2,4,4,128,256]{4,3,2,1,0:T(8,128)(2,1)}, bf16[2,4,4,128,256]{4,3,2,1,0:T(8,128)(2,1)}, u32[]{:S(2)}, u32[]{:S(2)}) collective-permute-start(bf16[2,4,4,128,256]{4,3,2,1,0:T(8,128)(2,1)} %get-tuple-element.204), channel_id=1, source_target_pairs={{0,2},{1,3},{2,0},{3,1},{4,6},{5,7},{6,4},{7,5},{8,10},{9,11},{10,... | collective-permute-start | bytes 6291464 | tf_op jit(solution)/shard_map/ppermute | solution.py:46
  473.7 40.8 %collective-permute-start.45 = (bf16[4,4,128,256]{3,2,1,0:T(8,128)(2,1)}, bf16[4,4,128,256]{3,2,1,0:T(8,128)(2,1)}, u32[]{:S(2)}, u32[]{:S(2)}) collective-permute-start(bf16[4,4,128,256]{3,2,1,0:T(8,128)(2,1)} %get-tuple-element.216), channel_id=1, source_target_pairs={{0,4},{4,0},{8,12},{12,8},{16,20},{20,16},{24,28},{28,24},{1,5},{5... | collective-permute-start | bytes 3145736 | tf_op jit(solution)/shard_map/ppermute | solution.py:46
  479.4 79.7 %collective-permute-start.47 = (bf16[2,4,4,128,256]{4,3,2,1,0:T(8,128)(2,1)}, bf16[2,4,4,128,256]{4,3,2,1,0:T(8,128)(2,1)}, u32[]{:S(2)}, u32[]{:S(2)}) collective-permute-start(bf16[2,4,4,128,256]{4,3,2,1,0:T(8,128)(2,1)} %get-tuple-element.202), channel_id=1, source_target_pairs={{0,2},{1,3},{2,0},{3,1},{4,6},{5,7},{6,4},{7,5},{8,10},{9,11},{10,... | collective-permute-start | bytes 6291464 | tf_op jit(solution)/shard_map/ppermute | solution.py:46
  518.3 24.6 %collective-permute-start.48 = (bf16[4,4,128,256]{3,2,1,0:T(8,128)(2,1)}, bf16[4,4,128,256]{3,2,1,0:T(8,128)(2,1)}, u32[]{:S(2)}, u32[]{:S(2)}) collective-permute-start(bf16[4,4,128,256]{3,2,1,0:T(8,128)(2,1)} %get-tuple-element.214), channel_id=1, source_target_pairs={{0,4},{4,0},{8,12},{12,8},{16,20},{20,16},{24,28},{28,24},{1,5},{5... | collective-permute-start | bytes 3145736 | tf_op jit(solution)/shard_map/ppermute | solution.py:46
  537.0 44.4 %collective-permute-start.65 = (bf16[2,4,2,2,128,256]{5,4,3,2,1,0:T(8,128)(2,1)}, bf16[2,4,2,2,128,256]{5,4,3,2,1,0:T(8,128)(2,1)S(1)}, u32[]{:S(2)}, u32[]{:S(2)}) collective-permute-start(bf16[2,4,2,2,128,256]{5,4,3,2,1,0:T(8,128)(2,1)} %get-tuple-element.165), channel_id=1, source_target_pairs={{0,1},{1,0},{2,3},{3,2},{4,5},{5,4},{6,7},{7,6},{8,9},{9,8},{10,11... | collective-permute-start | bytes 6291464 | tf_op jit(solution)/shard_map/ppermute | solution.py:46
  537.1 53.9 %collective-permute-start.49 = (bf16[4,128,256]{2,1,0:T(8,128)(2,1)}, bf16[4,128,256]{2,1,0:T(8,128)(2,1)}, u32[]{:S(2)}, u32[]{:S(2)}) collective-permute-start(bf16[4,128,256]{2,1,0:T(8,128)(2,1)} %get-tuple-element.231), channel_id=1, source_target_pairs={{0,8},{4,12},{8,16},{12,20},{16,24},{20,28},{24,0},{28,4},{1,9},{5... | collective-permute-start | bytes 786440 | tf_op jit(solution)/shard_map/ppermute | solution.py:51
  537.7 54.8 %collective-permute-start.50 = (bf16[4,128,256]{2,1,0:T(8,128)(2,1)}, bf16[4,128,256]{2,1,0:T(8,128)(2,1)}, u32[]{:S(2)}, u32[]{:S(2)}) collective-permute-start(bf16[4,128,256]{2,1,0:T(8,128)(2,1)} %get-tuple-element.230), channel_id=1, source_target_pairs={{0,16},{4,20},{8,24},{12,28},{16,0},{20,4},{24,8},{28,12},{1,17},{... | collective-permute-start | bytes 786440 | tf_op jit(solution)/shard_map/ppermute | solution.py:51
  542.9 43.9 %collective-permute-start.59 = (bf16[2,2,4,2,128,256]{5,4,3,2,1,0:T(8,128)(2,1)}, bf16[2,2,4,2,128,256]{5,4,3,2,1,0:T(8,128)(2,1)}, u32[]{:S(2)}, u32[]{:S(2)}) collective-permute-start(bf16[2,2,4,2,128,256]{5,4,3,2,1,0:T(8,128)(2,1)} %get-tuple-element.163), channel_id=1, source_target_pairs={{0,1},{1,0},{2,3},{3,2},{4,5},{5,4},{6,7},{7,6},{8,9},{9,8},{10,11... | collective-permute-start | bytes 6291464 | tf_op jit(solution)/shard_map/ppermute | solution.py:46
  559.0 33.4 %collective-permute-start.51 = (bf16[4,128,256]{2,1,0:T(8,128)(2,1)}, bf16[4,128,256]{2,1,0:T(8,128)(2,1)S(1)}, u32[]{:S(2)}, u32[]{:S(2)}) collective-permute-start(bf16[4,128,256]{2,1,0:T(8,128)(2,1)} %get-tuple-element.229), channel_id=1, source_target_pairs={{0,24},{4,28},{8,0},{12,4},{16,8},{20,12},{24,16},{28,20},{1,25},{... | collective-permute-start | bytes 786440 | tf_op jit(solution)/shard_map/ppermute | solution.py:51
  581.4 13.9 %collective-permute-start.52 = (bf16[4,128,256]{2,1,0:T(8,128)(2,1)S(1)}, bf16[4,128,256]{2,1,0:T(8,128)(2,1)S(1)}, u32[]{:S(2)}, u32[]{:S(2)}) collective-permute-start(bf16[4,128,256]{2,1,0:T(8,128)(2,1)S(1)} %copy-done.16), channel_id=1, source_target_pairs={{0,8},{4,12},{8,16},{12,20},{16,24},{20,28},{24,0},{28,4},{1,9},{5... | collective-permute-start | bytes 786440 | tf_op jit(solution)/shard_map/ppermute | solution.py:51
  586.8 26.5 %collective-permute-start.66 = (bf16[4,2,2,128,256]{4,3,2,1,0:T(8,128)(2,1)}, bf16[4,2,2,128,256]{4,3,2,1,0:T(8,128)(2,1)}, u32[]{:S(2)}, u32[]{:S(2)}) collective-permute-start(bf16[4,2,2,128,256]{4,3,2,1,0:T(8,128)(2,1)} %get-tuple-element.208), channel_id=1, source_target_pairs={{0,4},{4,0},{8,12},{12,8},{16,20},{20,16},{24,28},{28,24},{1,5},{5... | collective-permute-start | bytes 3145736 | tf_op jit(solution)/shard_map/ppermute | solution.py:46
  591.0 28.0 %collective-permute-start.60 = (bf16[2,4,2,128,256]{4,3,2,1,0:T(8,128)(2,1)}, bf16[2,4,2,128,256]{4,3,2,1,0:T(8,128)(2,1)}, u32[]{:S(2)}, u32[]{:S(2)}) collective-permute-start(bf16[2,4,2,128,256]{4,3,2,1,0:T(8,128)(2,1)} %get-tuple-element.210), channel_id=1, source_target_pairs={{0,2},{1,3},{2,0},{3,1},{4,6},{5,7},{6,4},{7,5},{8,10},{9,11},{10,... | collective-permute-start | bytes 3145736 | tf_op jit(solution)/shard_map/ppermute | solution.py:46
  592.5 13.6 %collective-permute-start.53 = (bf16[4,128,256]{2,1,0:T(8,128)(2,1)S(1)}, bf16[4,128,256]{2,1,0:T(8,128)(2,1)S(1)}, u32[]{:S(2)}, u32[]{:S(2)}) collective-permute-start(bf16[4,128,256]{2,1,0:T(8,128)(2,1)S(1)} %copy-done.15), channel_id=1, source_target_pairs={{0,16},{4,20},{8,24},{12,28},{16,0},{20,4},{24,8},{28,12},{1,17},{... | collective-permute-start | bytes 786440 | tf_op jit(solution)/shard_map/ppermute | solution.py:51
  592.5 13.7 %collective-permute-start.54 = (bf16[4,128,256]{2,1,0:T(8,128)(2,1)S(1)}, bf16[4,128,256]{2,1,0:T(8,128)(2,1)S(1)}, u32[]{:S(2)}, u32[]{:S(2)}) collective-permute-start(bf16[4,128,256]{2,1,0:T(8,128)(2,1)S(1)} %copy-done.14), channel_id=1, source_target_pairs={{0,24},{4,28},{8,0},{12,4},{16,8},{20,12},{24,16},{28,20},{1,25},{... | collective-permute-start | bytes 786440 | tf_op jit(solution)/shard_map/ppermute | solution.py:51
  595.3 40.5 %collective-permute-start.55 = (bf16[4,4,128,256]{3,2,1,0:T(8,128)(2,1)}, bf16[4,4,128,256]{3,2,1,0:T(8,128)(2,1)}, u32[]{:S(2)}, u32[]{:S(2)}) collective-permute-start(bf16[4,4,128,256]{3,2,1,0:T(8,128)(2,1)} %get-tuple-element.212), channel_id=1, source_target_pairs={{0,4},{4,0},{8,12},{12,8},{16,20},{20,16},{24,28},{28,24},{1,5},{5... | collective-permute-start | bytes 3145736 | tf_op jit(solution)/shard_map/ppermute | solution.py:46
  614.6 22.6 %collective-permute-start.67 = (bf16[2,2,128,256]{3,2,1,0:T(8,128)(2,1)S(1)}, bf16[2,2,128,256]{3,2,1,0:T(8,128)(2,1)S(1)}, u32[]{:S(2)}, u32[]{:S(2)}) collective-permute-start(bf16[2,2,128,256]{3,2,1,0:T(8,128)(2,1)S(1)} %get-tuple-element.217), channel_id=1, source_target_pairs={{0,8},{4,12},{8,16},{12,20},{16,24},{20,28},{24,0},{28,4},{1,9},{5... | collective-permute-start | bytes 786440 | tf_op jit(solution)/shard_map/ppermute | solution.py:51
  616.6 24.0 %collective-permute-start.68 = (bf16[2,2,128,256]{3,2,1,0:T(8,128)(2,1)S(1)}, bf16[2,2,128,256]{3,2,1,0:T(8,128)(2,1)S(1)}, u32[]{:S(2)}, u32[]{:S(2)}) collective-permute-start(bf16[2,2,128,256]{3,2,1,0:T(8,128)(2,1)S(1)} %get-tuple-element.219), channel_id=1, source_target_pairs={{0,16},{4,20},{8,24},{12,28},{16,0},{20,4},{24,8},{28,12},{1,17},{... | collective-permute-start | bytes 786440 | tf_op jit(solution)/shard_map/ppermute | solution.py:51
  618.0 27.4 %collective-permute-start.69 = (bf16[2,2,128,256]{3,2,1,0:T(8,128)(2,1)S(1)}, bf16[2,2,128,256]{3,2,1,0:T(8,128)(2,1)S(1)}, u32[]{:S(2)}, u32[]{:S(2)}) collective-permute-start(bf16[2,2,128,256]{3,2,1,0:T(8,128)(2,1)S(1)} %get-tuple-element.218), channel_id=1, source_target_pairs={{0,24},{4,28},{8,0},{12,4},{16,8},{20,12},{24,16},{28,20},{1,25},{... | collective-permute-start | bytes 786440 | tf_op jit(solution)/shard_map/ppermute | solution.py:51
  621.5 38.5 %collective-permute-start.61 = (bf16[4,2,128,256]{3,2,1,0:T(8,128)(2,1)}, bf16[4,2,128,256]{3,2,1,0:T(8,128)(2,1)S(1)}, u32[]{:S(2)}, u32[]{:S(2)}) collective-permute-start(bf16[4,2,128,256]{3,2,1,0:T(8,128)(2,1)} %get-tuple-element.221), channel_id=1, source_target_pairs={{0,4},{4,0},{8,12},{12,8},{16,20},{20,16},{24,28},{28,24},{1,5},{5... | collective-permute-start | bytes 1572872 | tf_op jit(solution)/shard_map/ppermute | solution.py:46
  637.2 20.4 %collective-permute-start.57 = (bf16[4,128,256]{2,1,0:T(8,128)(2,1)S(1)}, bf16[4,128,256]{2,1,0:T(8,128)(2,1)S(1)}, u32[]{:S(2)}, u32[]{:S(2)}) collective-permute-start(bf16[4,128,256]{2,1,0:T(8,128)(2,1)S(1)} %get-tuple-element.224), channel_id=1, source_target_pairs={{0,16},{4,20},{8,24},{12,28},{16,0},{20,4},{24,8},{28,12},{1,17},{... | collective-permute-start | bytes 786440 | tf_op jit(solution)/shard_map/ppermute | solution.py:51
  640.5 17.1 %collective-permute-start.58 = (bf16[4,128,256]{2,1,0:T(8,128)(2,1)S(1)}, bf16[4,128,256]{2,1,0:T(8,128)(2,1)S(1)}, u32[]{:S(2)}, u32[]{:S(2)}) collective-permute-start(bf16[4,128,256]{2,1,0:T(8,128)(2,1)S(1)} %get-tuple-element.223), channel_id=1, source_target_pairs={{0,24},{4,28},{8,0},{12,4},{16,8},{20,12},{24,16},{28,20},{1,25},{... | collective-permute-start | bytes 786440 | tf_op jit(solution)/shard_map/ppermute | solution.py:51
  647.2 21.5 %collective-permute-start.70 = (bf16[2,128,256]{2,1,0:T(8,128)(2,1)}, bf16[2,128,256]{2,1,0:T(8,128)(2,1)}, u32[]{:S(2)}, u32[]{:S(2)}) collective-permute-start(bf16[2,128,256]{2,1,0:T(8,128)(2,1)} %slice_bitcast_fusion.24), channel_id=1, source_target_pairs={{0,2},{1,3},{2,0},{3,1},{4,6},{5,7},{6,4},{7,5},{8,10},{9,11},{10,... | collective-permute-start | bytes 393224 | tf_op jit(solution)/shard_map/ppermute | solution.py:46
  660.1 11.8 %collective-permute-start.62 = (bf16[2,128,256]{2,1,0:T(8,128)(2,1)S(1)}, bf16[2,128,256]{2,1,0:T(8,128)(2,1)S(1)}, u32[]{:S(2)}, u32[]{:S(2)}) collective-permute-start(bf16[2,128,256]{2,1,0:T(8,128)(2,1)S(1)} %get-tuple-element.253), channel_id=1, source_target_pairs={{0,8},{4,12},{8,16},{12,20},{16,24},{20,28},{24,0},{28,4},{1,9},{5... | collective-permute-start | bytes 393224 | tf_op jit(solution)/shard_map/ppermute | solution.py:51
  689.7 14.0 %collective-permute-start.88 = (bf16[4,128,256]{2,1,0:T(8,128)(2,1)S(1)}, bf16[4,128,256]{2,1,0:T(8,128)(2,1)S(1)}, u32[]{:S(2)}, u32[]{:S(2)}) collective-permute-start(bf16[4,128,256]{2,1,0:T(8,128)(2,1)S(1)} %copy-done.12), channel_id=1, source_target_pairs={{0,1},{1,0},{2,3},{3,2},{4,5},{5,4},{6,7},{7,6},{8,9},{9,8},{10,11... | collective-permute-start | bytes 786440 | tf_op jit(solution)/shard_map/ppermute | solution.py:46
  689.7 12.8 %collective-permute-start.90 = (bf16[4,128,256]{2,1,0:T(8,128)(2,1)S(1)}, bf16[4,128,256]{2,1,0:T(8,128)(2,1)S(1)}, u32[]{:S(2)}, u32[]{:S(2)}) collective-permute-start(bf16[4,128,256]{2,1,0:T(8,128)(2,1)S(1)} %copy-done.13), channel_id=1, source_target_pairs={{0,2},{1,3},{2,0},{3,1},{4,6},{5,7},{6,4},{7,5},{8,10},{9,11},{10,... | collective-permute-start | bytes 786440 | tf_op jit(solution)/shard_map/ppermute | solution.py:46
  702.5 12.1 %collective-permute-start.92 = (bf16[4,128,256]{2,1,0:T(8,128)(2,1)S(1)}, bf16[4,128,256]{2,1,0:T(8,128)(2,1)S(1)}, u32[]{:S(2)}, u32[]{:S(2)}) collective-permute-start(bf16[4,128,256]{2,1,0:T(8,128)(2,1)S(1)} %collective-permute-done.90.refs_5_), channel_id=1, source_target_pairs={{0,1},{1,0},{2,3},{3,2},{4,5},{5,4},{6,7},{7,6},{8,9},{9,8},{10,11... | collective-permute-start | bytes 786440 | tf_op jit(solution)/shard_map/ppermute | solution.py:46
  702.6 11.5 %collective-permute-start.84 = (bf16[4,128,256]{2,1,0:T(8,128)(2,1)S(1)}, bf16[4,128,256]{2,1,0:T(8,128)(2,1)S(1)}, u32[]{:S(2)}, u32[]{:S(2)}) collective-permute-start(bf16[4,128,256]{2,1,0:T(8,128)(2,1)S(1)} %get-tuple-element.196.refs_8_), channel_id=1, source_target_pairs={{0,2},{1,3},{2,0},{3,1},{4,6},{5,7},{6,4},{7,5},{8,10},{9,11},{10,... | collective-permute-start | bytes 786440 | tf_op jit(solution)/shard_map/ppermute | solution.py:46
  707.2 23.2 %collective-permute-start.85 = (bf16[4,128,256]{2,1,0:T(8,128)(2,1)S(1)}, bf16[4,128,256]{2,1,0:T(8,128)(2,1)S(1)}, u32[]{:S(2)}, u32[]{:S(2)}) collective-permute-start(bf16[4,128,256]{2,1,0:T(8,128)(2,1)S(1)} %get-tuple-element.196.refs_8_), channel_id=1, source_target_pairs={{0,1},{1,0},{2,3},{3,2},{4,5},{5,4},{6,7},{7,6},{8,9},{9,8},{10,11... | collective-permute-start | bytes 786440 | tf_op jit(solution)/shard_map/ppermute | solution.py:46
  707.3 21.9 %collective-permute-start.82 = (bf16[2,128,256]{2,1,0:T(8,128)(2,1)S(1)}, bf16[2,128,256]{2,1,0:T(8,128)(2,1)S(1)}, u32[]{:S(2)}, u32[]{:S(2)}) collective-permute-start(bf16[2,128,256]{2,1,0:T(8,128)(2,1)S(1)} %get-tuple-element.192.refs_4_), channel_id=1, source_target_pairs={{0,1},{1,0},{2,3},{3,2},{4,5},{5,4},{6,7},{7,6},{8,9},{9,8},{10,11... | collective-permute-start | bytes 393224 | tf_op jit(solution)/shard_map/ppermute | solution.py:46
  714.1 16.4 %collective-permute-start.83 = (bf16[2,128,256]{2,1,0:T(8,128)(2,1)S(1)}, bf16[2,128,256]{2,1,0:T(8,128)(2,1)S(1)}, u32[]{:S(2)}, u32[]{:S(2)}) collective-permute-start(bf16[2,128,256]{2,1,0:T(8,128)(2,1)S(1)} %collective-permute-done.81.refs_5_), channel_id=1, source_target_pairs={{0,1},{1,0},{2,3},{3,2},{4,5},{5,4},{6,7},{7,6},{8,9},{9,8},{10,11... | collective-permute-start | bytes 393224 | tf_op jit(solution)/shard_map/ppermute | solution.py:46
  714.1 16.5 %collective-permute-start.86 = (bf16[4,128,256]{2,1,0:T(8,128)(2,1)S(1)}, bf16[4,128,256]{2,1,0:T(8,128)(2,1)S(1)}, u32[]{:S(2)}, u32[]{:S(2)}) collective-permute-start(bf16[4,128,256]{2,1,0:T(8,128)(2,1)S(1)} %collective-permute-done.84.refs_9_), channel_id=1, source_target_pairs={{0,1},{1,0},{2,3},{3,2},{4,5},{5,4},{6,7},{7,6},{8,9},{9,8},{10,11... | collective-permute-start | bytes 786440 | tf_op jit(solution)/shard_map/ppermute | solution.py:46
  714.6 14.7 %collective-permute-start.78 = (bf16[2,128,256]{2,1,0:T(8,128)(2,1)S(1)}, bf16[2,128,256]{2,1,0:T(8,128)(2,1)S(1)}, u32[]{:S(2)}, u32[]{:S(2)}) collective-permute-start(bf16[2,128,256]{2,1,0:T(8,128)(2,1)S(1)} %get-tuple-element.194.refs_0_), channel_id=1, source_target_pairs={{0,2},{1,3},{2,0},{3,1},{4,6},{5,7},{6,4},{7,5},{8,10},{9,11},{10,... | collective-permute-start | bytes 393224 | tf_op jit(solution)/shard_map/ppermute | solution.py:46
  (100 other events, 1243.5 us)
Sparse Core Ops, SparseCore 0:
  15.2 143.4 all-gather.4
  161.6 103.0 all-gather.6

commit v3 on v2

--- a/solution.py
+++ b/solution.py
@@ -56,28 +56,15 @@
     return [list(range(first, size, 2)) for first in range(2)]
 
 
-def gather_z(piece):
+def gather_z(piece, *others):
     nz = lax.axis_size("seq") // 2
     if nz <= 4:
-        return jnp.stack([piece] + [shift_z(piece, k) for k in range(1, nz)])
+        return jnp.stack([piece] + [after(shift_z(piece, k), *others) for k in range(1, nz)])
     whole = lax.all_gather(piece, "seq", axis_index_groups=z_groups())
     here = lax.axis_index("seq") // 2
     return jnp.take(whole, (here - jnp.arange(nz)) % nz, axis=0)
 
 
-def scatter_z(parts, *others):
-    nz = lax.axis_size("seq") // 2
-    if nz <= 4:
-        come = [parts[0]] + [shift_z(parts[k], k) for k in range(1, nz)]
-        total = come[0].astype(F32)
-        for item in come[1:]:
-            total = total + after(item, *others).astype(F32)
-        return total.astype(BF)
-    here = lax.axis_index("seq") // 2
-    ordered = jnp.take(jnp.stack(parts), (jnp.arange(nz) - here) % nz, axis=0)
-    return lax.psum_scatter(ordered, "seq", axis_index_groups=z_groups())
-
-
 def column_part(block, start, width):
     return lax.dynamic_slice_in_dim(block, start, width, 2)
 
@@ -87,7 +74,7 @@
     return column_part(block, (place[CORE] * 2 + place[XPOS]) * part, part)
 
 
-def gather_weights(block, kind, place, begin=(), beside_after=(), across_after=(), cross=()):
+def start_gather(block, kind, place, begin=(), then=()):
     width = block.shape[2]
     if kind == "zyx":
         part = width // 4
@@ -95,9 +82,11 @@
     else:
         part = width // 2
         piece = column_part(block, place[CORE] * part, part)
-    piece = after(piece, *begin)
-    below = gather_z(piece)
-    beside = swap(after(below, *beside_after), "seq", 1)
+    below = gather_z(after(piece, *begin), *then)
+    return below, swap(below, "seq", 1)
+
+
+def finish_gather(below, beside, kind, across_after=(), cross=()):
     stacks = [(below, 0, 0), (beside, 1, 0)]
     if kind == "zyx":
         stacks += [(swap(after(s, *across_after), "grp", 2), y, 1) for s, y, _ in stacks]
@@ -106,51 +95,66 @@
     return [s for s, _ in out], [m if kind == "zyx" else (m[0], m[1], None) for _, m in out]
 
 
-def add_low(a, b):
-    return (a.astype(F32) + b.astype(F32)).astype(BF)
+def gather_weights(block, kind, place, begin=()):
+    return finish_gather(*start_gather(block, kind, place, begin), kind)
+
+
+def add_low(*terms):
+    return sum(term.astype(F32) for term in terms).astype(BF)
 
 
 def send_core(parts):
-    return parts[0], swap(parts[1], "grp", 1)
-
-
-def step_one(here, there):
-    return add_low(here[0], there[0]), add_low(here[1], there[1])
-
-
-def send_one(kept, sent, kind):
-    return kept, swap(sent, "grp", 2) if kind == "xyz" else swap(sent, "seq", 1)
-
-
-def step_two(kept, come, kind):
+    return [parts[0], swap(parts[1], "grp", 1)]
+
+
+def step_one(terms, *others):
+    terms = [terms[0], before(terms[1], others)]
+    return [term[0] for term in terms], add_low(*[term[1] for term in terms])
+
+
+def send_one(terms, sent, kind):
+    return terms + [swap(sent, "grp", 2) if kind == "xyz" else swap(sent, "seq", 1)]
+
+
+def step_two(terms, kind, *others):
+    terms = terms[:-1] + [before(terms[-1], others)]
     if kind == "xyz":
-        return add_low(kept[0], come[0]), add_low(kept[1], come[1])
-    sums = [add_low(kept[k], come[k]) for k in range(kept.shape[0])]
-    return sums[0], sums[1:]
-
-
-def send_two(kept, sent, kind, *others):
+        return [term[0] for term in terms], add_low(*[term[1] for term in terms])
+    return step_z(terms)
+
+
+def step_z(terms):
+    nz = terms[0].shape[0]
+    return [term[0] for term in terms], [add_low(*[term[k] for term in terms]) for k in range(1, nz)]
+
+
+def send_z(terms, sent):
+    nz = lax.axis_size("seq") // 2
+    if nz <= 4:
+        return terms + [shift_z(part, k + 1) for k, part in enumerate(sent)]
+    here = lax.axis_index("seq") // 2
+    parts = jnp.stack([add_low(*terms), *sent])
+    ordered = jnp.take(parts, (jnp.arange(nz) - here) % nz, axis=0)
+    return [lax.psum_scatter(ordered, "seq", axis_index_groups=z_groups())]
+
+
+def send_two(terms, sent, kind):
+    return terms + [swap(sent, "seq", 1)] if kind == "xyz" else send_z(terms, sent)
+
+
+def step_three(terms, kind, *others):
+    terms = terms[:-1] + [before(terms[-1], others)]
     if kind == "xyz":
-        return kept, swap(sent, "seq", 1)
-    ends = scatter_z([kept, *sent], *others)
-    return ends[0], ends[1]
-
-
-def step_three(kept, come, kind):
-    if kind == "xyz":
-        sums = [add_low(kept[k], come[k]) for k in range(kept.shape[0])]
-        return sums[0], sums[1:]
-    return kept, come
-
-
-def send_three(kept, sent, kind, *others):
-    if kind == "xyz":
-        return scatter_z([kept, *sent], *others)
-    return add_low(kept, after(swap(sent, "grp", 2), *others))
-
-
-def pinned(state, *others):
-    return state[0], after(state[1], *others)
+        return step_z(terms)
+    return [term[0] for term in terms], add_low(*[term[1] for term in terms])
+
+
+def send_three(terms, sent, kind):
+    return send_z(terms, sent) if kind == "xyz" else terms + [swap(sent, "grp", 2)]
+
+
+def finish(terms, *others):
+    return add_low(*terms[:-1], before(terms[-1], others))
 
 
 def before(value, *states):
@@ -468,44 +472,23 @@
     loads = [(third_ref, third, 0), (cot_ref, cot, 1), (resid_ref, acc, 2)]
     if not first:
         loads.append((dx_in, dx, 3))
-    for source, target, s in loads:
+    for source, target, s in loads[:2]:
         pltpu.make_async_copy(source, target, sems.at[s]).start()
-    start_whole(stack, base, weights, sems.at[4])
+    for b in range(blocks):
+        start_whole(stack, base + 2 * b, weights.at[pl.ds(2 * b, 2)], sems.at[8 + b])
+        if b == 0:
+            for source, target, s in loads[2:]:
+                pltpu.make_async_copy(source, target, sems.at[s]).start()
     for source, target, s in loads[:2]:
         pltpu.make_async_copy(source, target, sems.at[s]).wait()
-    for r in range(tokens // chunk):
-        rows = slice(r * chunk, (r + 1) * chunk)
-        third_t[:, rows] = third[rows, :].T
-        cot_t[:, rows] = cot[rows, :].T
-    wait_all(weights, sems.at[4])
     for source, target, s in loads[2:]:
         pltpu.make_async_copy(source, target, sems.at[s]).wait()
 
-    def send(source, index):
-        start_grads(place, kind, source, index, outs, sems.at[5])
-
-    for b in range(blocks):
-        for r in range(tokens // chunk):
-            rows = slice(r * chunk, (r + 1) * chunk)
-            pre = dot_nn(third[rows, :], weights[b])
-            act_grad = dot_nn(cot[rows, :], weights[blocks + b])
-            act_now, slope = gelu_both(pre)
-            act_now = act_now.astype(BF)
-            grad_now = (act_grad * slope).astype(BF)
-            act[rows, :] = act_now
-            pre_grad[rows, :] = grad_now
-            acc[rows, :] += dot_nt(act_now, weights[blocks + b])
-            back = dot_nt(grad_now, weights[b])
-            if first and b == 0:
-                dx[rows, :] = back
-            else:
-                dx[rows, :] += back
-        staging[b] = dot_nn(third_t[...], pre_grad[...]).astype(BF)
-        send(staging.at[b], b)
-        staging[blocks + b] = dot_nn(cot_t[...], act[...]).astype(BF)
-        send(staging.at[blocks + b], blocks + b)
-    pltpu.make_async_copy(dx, dx_out, sems.at[6]).start()
-    if last:
+    def finish_sums():
+        pltpu.make_async_copy(dx, dx_out, sems.at[6]).start()
+        if not last:
+            pltpu.make_async_copy(acc, resid_out, sems.at[7]).start()
+            return
         low = third
         low[...] = acc[...].astype(BF)
         frames, positions = piece_refs[0].shape[:2]
@@ -524,11 +507,42 @@
                         piece.at[f, pl.ds(tile * per_tile, per_tile)],
                         sems.at[7],
                     ).start()
-        wait_all(low, sems.at[7])
+
+    def send(source, index):
+        start_grads(place, kind, source, index, outs, sems.at[5])
+
+    for b in range(blocks):
+        w_up, w_down = weights.at[2 * b], weights.at[2 * b + 1]
+        wait_all(weights.at[pl.ds(2 * b, 2)], sems.at[8 + b])
+        for r in range(tokens // chunk):
+            rows = slice(r * chunk, (r + 1) * chunk)
+            pre = dot_nn(third[rows, :], w_up[...])
+            act_grad = dot_nn(cot[rows, :], w_down[...])
+            act_now, slope = gelu_both(pre)
+            act_now = act_now.astype(BF)
+            grad_now = (act_grad * slope).astype(BF)
+            act[rows, :] = act_now
+            pre_grad[rows, :] = grad_now
+            if b == 0:
+                third_t[:, rows] = third[rows, :].T
+                cot_t[:, rows] = cot[rows, :].T
+            acc[rows, :] += dot_nt(act_now, w_down[...])
+            back = dot_nt(grad_now, w_up[...])
+            if first and b == 0:
+                dx[rows, :] = back
+            else:
+                dx[rows, :] += back
+        if b == blocks - 1:
+            finish_sums()
+        staging[2 * b] = dot_nn(third_t[...], pre_grad[...]).astype(BF)
+        send(staging.at[2 * b], 2 * b)
+        staging[2 * b + 1] = dot_nn(cot_t[...], act[...]).astype(BF)
+        send(staging.at[2 * b + 1], 2 * b + 1)
+    if last:
+        wait_all(third, sems.at[7])
     else:
-        pltpu.make_async_copy(acc, resid_out, sems.at[7]).start()
-        pltpu.make_async_copy(acc, resid_out, sems.at[7]).wait()
-    pltpu.make_async_copy(dx, dx_out, sems.at[6]).wait()
+        wait_all(acc, sems.at[7])
+    wait_all(dx, sems.at[6])
     wait_all(staging, sems.at[5])
 
 
@@ -647,15 +661,19 @@
 
 def update_body(lots, place, clip, *refs):
     pieces, refs = refs[: 4 * len(lots)], refs[4 * len(lots) :]
-    master, first, second, master_new, first_new, second_new = refs
-    matrix, block = pl.program_id(0), pl.program_id(1)
+    olds, news = refs[:6], refs[6:]
+    array, matrix, block = pl.program_id(0), pl.program_id(1), pl.program_id(2)
     for i, lot in enumerate(lots):
         mine = functools.reduce(
-            jnp.logical_or, [(matrix == m) & (block == b) for m, b in lot]
+            jnp.logical_or,
+            [(array == a) & (matrix == m) & (block == b) for a, m, b in lot],
         )
+        which = lot[0][0]
 
         @pl.when(mine)
-        def _(i=i):
+        def _(i=i, which=which):
+            master, first, second = olds[3 * which : 3 * which + 3]
+            master_new, first_new, second_new = news[3 * which : 3 * which + 3]
             for rel, piece in enumerate(pieces[4 * i : 4 * i + 4]):
                 width = piece.shape[2]
                 column = (place[CORE] ^ (rel // 2)) * 2 + (place[XPOS] ^ (rel % 2))
@@ -764,9 +782,12 @@
     v_s, meta_v_s = gather_weights(
         blocks(attn_master, [(0, 2)]), "zy", place, begin=(qk_s[0],)
     )
+    below_o, beside_o = start_gather(
+        blocks(attn_master, [(0, 3)]), "zy", place, begin=(v_s[0],)
+    )
     lots_in_s, in_s = ((0, 2, meta_qk_s), (2, 1, meta_v_s)), [*qk_s, *v_s]
 
-    ffn_picks = [(m, 2 * group + b) for group in range(2) for m in range(2) for b in range(2)]
+    ffn_picks = [(m, 2 * group + b) for group in range(2) for b in range(2) for m in range(2)]
     early = jnp.concatenate(
         [
             quarter_mine(blocks(attn_master, [(1, b) for b in range(4)]), place),
@@ -840,17 +861,16 @@
         spatial_in_body,
         lots_in_s,
         in_s,
-        [frames_in, code_shift, gains],
+        [before(frames_in, below_o), code_shift, gains],
         [flat_tile, tile(1, width), fixed(3, width)],
         [wide, flat_tile],
         [wide_shape, tile_shape],
         [],
         12,
     )
-    late_all = lax.all_gather(after(late, packed_s), ("seq", "grp"))
     heads_s, lse_s = attention(packed_s, 0)
-    out_s, meta_out_s = gather_weights(
-        blocks(attn_master, [(0, 3)]), "zyx", place, begin=(v_s[0],), across_after=(packed_s,), cross=(heads_s,)
+    out_s, meta_out_s = finish_gather(
+        below_o, beside_o, "zy", cross=(heads_s,)
     )
     lots_out_s = ((0, 1, meta_out_s),)
     pieces = layer(
@@ -865,6 +885,7 @@
         6,
     )
     token_pieces = exchange(pieces)
+    late_all = lax.all_gather(before(late, token_pieces), ("seq", "grp"))
 
     packed_t, heads_t, lse_t, normed_t, tokens_t, resid_two, third = call(
         temporal_fwd_body,
@@ -922,7 +943,7 @@
             + [pltpu.VMEM((tokens, width), F32)] * 2
             + [pltpu.VMEM((4, width, width), BF)]
             + [pltpu.VMEM((tokens, width), BF)] * 2
-            + [pltpu.VMEM((4, width, width), BF), sems((8,))],
+            + [pltpu.VMEM((4, width, width), BF), sems((10,))],
             us=41,
         )
         parts_f.append(outs[:2])
@@ -934,9 +955,9 @@
 
     quarters = {}
     sum_f = send_core(parts_f[1])
-    sum_e = step_one(*pinned(sum_e, dx))
-    dx = before(dx, sum_e)
-    sum_e = send_one(*sum_e, "xyz")
+    sum_e, sent_e = step_one(sum_e, dx)
+    dx = before(dx, sent_e)
+    sum_e = send_one(sum_e, sent_e, "xyz")
     outs = call(
         temporal_bwd_body,
         spots,
@@ -985,64 +1006,79 @@
         )
         return [outs[2 * i : 2 * i + 2] for i in range(len(lots))]
 
-    kinds = ("xyz", "yzx")
-    sum_f = step_one(*pinned(sum_f, grad_t))
+    sum_e, sent_e = step_two(sum_e, "xyz", grad_t)
+    sum_f, sent_f = step_one(sum_f, grad_t)
     (parts_t,) = weight_grads(
         ("xyz",),
-        [normed_t, before(grad_t, sum_f, block_out), heads_t, branch_t],
+        [normed_t, before(grad_t, sent_e, sent_f, block_out), heads_t, branch_t],
         [(0, 0), (0, 1), (0, 2), (1, 0)],
     )
-    sum_f = send_one(*sum_f, "xyz")
-    sum_t = send_core(parts_t)
+    sum_f = send_one(sum_f, sent_f, "xyz")
+    sum_t, sent_t = step_one(send_core(parts_t))
 
     branch_s, heads_grad_s = layer(
         spatial_branch_body,
         lots_out_s,
         out_s,
-        [before(grad_pieces[0], parts_t), *grad_pieces[1:]],
+        [before(grad_pieces[0], sent_t), *grad_pieces[1:]],
         [part_spec] * members,
         [flat_tile] * 2,
         [tile_shape] * 2,
         [],
         7,
     )
-    sum_e = step_two(*pinned(sum_e, branch_s), "xyz")
-    sum_t = step_one(*pinned(sum_t, branch_s))
-    grad_s = attention_back(packed_s, heads_s, before(heads_grad_s, sum_e, sum_t), lse_s, 0)
-    sum_e, sum_t = send_two(*sum_e, "xyz"), send_one(*sum_t, "xyz")
-    sum_e = step_three(*pinned(sum_e, grad_s), "xyz")
-    sum_f = step_two(*pinned(sum_f, grad_s), "xyz")
-    parts_s = weight_grads(
-        kinds,
-        [normed_s, before(grad_s, sum_e, sum_f), heads_s, branch_s],
-        [(0, 0), (0, 1)],
-        [(0, 2), (1, 0)],
-    )
-    quarters["ffn0"] = send_three(*sum_e, "xyz", parts_s[0][0])
-    sum_f = send_two(*sum_f, "xyz")
-    sums_s = [send_core(parts) for parts in parts_s]
-    sum_f = step_three(*pinned(sum_f, parts_s[0][0]), "xyz")
-    sum_t = step_two(*pinned(sum_t, parts_s[0][0]), "xyz")
+    sum_t = send_one(sum_t, sent_t, "xyz")
+    sum_f, sent_f = step_two(sum_f, "xyz", branch_s)
+    grad_s = attention_back(packed_s, heads_s, before(heads_grad_s, sent_f), lse_s, 0)
+    sum_e = send_two(sum_e, after(sent_e, branch_s), "xyz")
+    sum_f = send_two(sum_f, sent_f, "xyz")
+    sum_e, sent_e = step_three(sum_e, "xyz", grad_s)
+    (parts_qk,) = weight_grads(
+        ("xyz",), [normed_s, before(grad_s, sent_e)], [(0, 0), (0, 1)]
+    )
+    sum_e = send_three(sum_e, sent_e, "xyz")
+    sum_qk = send_core(parts_qk)
+    sum_f, sent_f = step_three(sum_f, "xyz", parts_qk[0])
+    sum_t, sent_t = step_two(sum_t, "xyz", parts_qk[0])
+    (parts_vo,) = weight_grads(
+        ("xyz",), [normed_s, before(grad_s, sent_f, sent_t), heads_s, branch_s], [(0, 2), (1, 0)]
+    )
+    sum_f, sum_t = send_three(sum_f, sent_f, "xyz"), send_two(sum_t, sent_t, "xyz")
+    quarters["ffn0"] = finish(sum_e, parts_vo[0])
+    sum_vo = send_core(parts_vo)
+    sum_qk, sent_qk = step_one(sum_qk, parts_vo[0])
+    sum_vo, sent_vo = step_one(sum_vo, sent_qk)
     input_grad, gain_one, columns = layer(
         spatial_end_body,
         lots_in_s,
         in_s,
-        [grad_s, frames_in, code_shift, before(branch_s, parts_s, sum_t, sum_f), gains],
+        [grad_s, frames_in, code_shift, before(branch_s, sent_qk, sent_vo, quarters["ffn0"]), gains],
         [wide, flat_tile, tile(1, width), flat_tile, fixed(3, width)],
         [flat_tile, fixed(1, width), tile(1, width)],
         [tile_shape, gain_shape, shape_of(frames, 1, width, dtype=F32)],
         [],
         14,
     )
-    sum_t = send_two(*sum_t, "xyz")
-    quarters["ffn1"] = send_three(*sum_f, "xyz", columns)
-    sums_s = [step_one(*pinned(s, columns)) for s in sums_s]
-    sums_s = [send_one(*s, kind) for s, kind in zip(sums_s, kinds)]
-    sum_t = step_three(*pinned(sum_t, columns), "xyz")
-    quarters["t"] = send_three(*sum_t, "xyz")
-    sums_s = [send_two(*step_two(*s, kind), kind) for s, kind in zip(sums_s, kinds)]
-    sums_s = [send_three(*step_three(*s, kind), kind) for s, kind in zip(sums_s, kinds)]
-    quarters["qk"], quarters["vo"] = sums_s
+    sum_qk = send_one(sum_qk, sent_qk, "xyz")
+    sum_qk, sent_qk = step_two(sum_qk, "xyz", columns)
+    sum_qk = send_two(sum_qk, sent_qk, "xyz")
+    quarters["ffn1"] = finish(sum_f, columns)
+    sum_t, sent_t = step_three(sum_t, "xyz", columns)
+    sum_t = send_three(sum_t, sent_t, "xyz")
+    sum_vo = send_one(sum_vo, sent_vo, "xyz")
+    sum_vo, sent_vo = step_two(sum_vo, "xyz", sent_qk, sent_t)
+    sum_vo = send_two(sum_vo, sent_vo, "xyz")
+    sum_qk, sent_qk = step_three(sum_qk, "xyz", sent_vo)
+    sum_qk = send_three(sum_qk, sent_qk, "xyz")
+    shared = {
+        name: share_quarters(before(quarters[name], sent_qk)) for name in ("ffn0", "ffn1")
+    }
+    quarters["t"] = finish(sum_t, sent_qk)
+    sum_vo, sent_vo = step_three(sum_vo, "xyz", quarters["t"])
+    sum_vo = send_three(sum_vo, sent_vo, "xyz")
+    quarters["qk"] = finish(sum_qk, sent_vo)
+    shared["t"] = share_quarters(before(quarters["t"], sent_vo))
+    quarters["vo"] = finish(sum_vo, shared["ffn0"], shared["ffn1"])
 
     table_grad = jnp.dot(
         onehot.astype(F32).T, columns[:, 0, :], precision=lax.Precision.HIGHEST
@@ -1058,45 +1094,54 @@
     total_squares = sums[-1, 0] + jnp.sum(small_grad * small_grad)
     grad_norm = jnp.sqrt(total_squares)
     clip_factor = 1.0 / jnp.maximum(grad_norm, 1.0)
-    shared = {name: share_quarters(q) for name, q in quarters.items()}
-
-    def updated(lots, master, first, second):
-        def piece(lot):
-            def at(m, b, *_):
-                entry = 0
-                for k, (matrix, block) in enumerate(lot):
-                    entry = jnp.where((m == matrix) & (b == block), k, entry)
-                return entry, 0, 0
-
-            return pl.BlockSpec((1, local_rows, width // 4), at)
-
-        block = pl.BlockSpec((1, local_rows, width), lambda m, b, *_: (m, 0, b))
-        return call(
-            functools.partial(update_body, [lot for _, lot in lots]),
-            (place, clip_factor.reshape(1)),
-            [p for name, _ in lots for p in shared[name]] + [master, first, second],
-            [piece(lot) for _, lot in lots for _ in range(4)] + [block] * 3,
-            [block] * 3,
-            [shape_of(*master.shape, dtype=F32)] * 3,
-            [],
-            grid=(2, master.shape[2] // width),
-            scalars=2,
-        )
-
-    attn_new = updated(
-        [("qk", [(0, 0), (0, 1)]), ("vo", [(0, 2), (0, 3)]), ("t", [(1, b) for b in range(4)])],
-        attn_master,
-        attn_first,
-        attn_second,
-    )
-    ffn_new = updated([("ffn0", ffn_picks[:4]), ("ffn1", ffn_picks[4:])], ffn_master, ffn_first, ffn_second)
+    for name in ("qk", "vo"):
+        shared[name] = share_quarters(quarters[name])
+
+    lots = [
+        ("qk", [(0, 0, 0), (0, 0, 1)]),
+        ("vo", [(0, 0, 2), (0, 0, 3)]),
+        ("t", [(0, 1, b) for b in range(4)]),
+        ("ffn0", [(1, *pick) for pick in ffn_picks[:4]]),
+        ("ffn1", [(1, *pick) for pick in ffn_picks[4:]]),
+    ]
+
+    def piece_spec_of(lot):
+        def at(a, m, b, *_):
+            entry = 0
+            for k, (array, matrix, block) in enumerate(lot):
+                entry = jnp.where((a == array) & (m == matrix) & (b == block), k, entry)
+            return entry, 0, 0
+
+        return pl.BlockSpec((1, local_rows, width // 4), at)
+
+    columns_n = attn_master.shape[2] // width
+    attn_block = pl.BlockSpec(
+        (1, local_rows, width),
+        lambda a, m, b, *_: (jnp.where(a == 0, m, 1), 0, jnp.where(a == 0, b, columns_n - 1)),
+    )
+    ffn_block = pl.BlockSpec(
+        (1, local_rows, width), lambda a, m, b, *_: (jnp.where(a == 1, m, 0), 0, jnp.where(a == 1, b, 0))
+    )
+    blocks_six = [attn_block] * 3 + [ffn_block] * 3
+    updated = call(
+        functools.partial(update_body, [lot for _, lot in lots]),
+        (place, clip_factor.reshape(1)),
+        [p for name, _ in lots for p in shared[name]]
+        + [attn_master, attn_first, attn_second, ffn_master, ffn_first, ffn_second],
+        [piece_spec_of(lot) for _, lot in lots for _ in range(4)] + blocks_six,
+        blocks_six,
+        [shape_of(*attn_master.shape, dtype=F32)] * 3 + [shape_of(*ffn_master.shape, dtype=F32)] * 3,
+        [],
+        grid=(2, 2, columns_n),
+        scalars=2,
+    )
     small_decay = jnp.where(jnp.arange(3 + CODES)[:, None] >= 3, decay_rate, 0.0)
     small_cols = small_master.shape[1]
     small_mine = lax.dynamic_slice_in_dim(small_grad, seq * small_cols, small_cols, 1)
     small_new = update(
         small_master, small_first, small_second, small_mine * clip_factor, rate_small, small_decay
     )
-    return (block_out, input_grad, grad_norm, *attn_new, *ffn_new, *small_new)
+    return (block_out, input_grad, grad_norm, *updated, *small_new)
 
 
 def solution(mesh):

time: 760 us -> 708 us (0.932)
  waiting for transfers between devices: 218 us -> 173 us
  starting transfers between devices: 117 us -> 101 us
    ppermute x69 -> x65, waiting for transfers between devices: 173 us -> 99.7 us  [swap(): return lax.ppermute(value, axis, [(i, i ^ bit) for i in range(size)])]
    ppermute x24, waiting for transfers between devices: 44.9 us -> 73.2 us  [shift_z(): lax.ppermute(value, 'seq', [(i, (i + 2 * step) % size) for i in range(siz...]
    ppermute x24, starting transfers between devices: 55.2 us -> 38.4 us  [shift_z(): lax.ppermute(value, 'seq', [(i, (i + 2 * step) % size) for i in range(siz...]
    ppermute x69 -> x65, starting transfers between devices: 61.5 us -> 62.8 us  [swap(): return lax.ppermute(value, axis, [(i, i ^ bit) for i in range(size)])]
  transfers between devices with their start and end apart: 95 -> 91, of which waited for: 41 -> 37; matrix products, arithmetic and copies ran while one was open for 8% -> 8% of each run, Pallas kernels for 38% -> 41%
where the time goes in v3:
time: 708 us; the launch traced here: 697 us
  Pallas kernels  326 us (46%)
  waiting for transfers between devices  173 us (24%)
  starting transfers between devices  101 us (14%)
  other arithmetic  60.2 us (9%)
  between operations  21 us (3%)
  local copies, waits for them, and re-layouts  15 us (2%)
    pallas_call x16, Pallas kernels, call(): pl.pallas_call(body, out_shape=out_shape, grid_spec=pltpu.PrefetchScalarG...  326 us
    ppermute x65, waiting for transfers between devices, swap(): return lax.ppermute(value, axis, [(i, i ^ bit) for i in range(size)])  99.7 us
    ppermute x24, waiting for transfers between devices, shift_z(): lax.ppermute(value, 'seq', [(i, (i + 2 * step) % size) for i in range(siz...  73.2 us
    ppermute x65, starting transfers between devices, swap(): return lax.ppermute(value, axis, [(i, i ^ bit) for i in range(size)])  62.8 us
    convert_element_type x15, other arithmetic, add_low(): return sum((term.astype(F32) for term in terms)).astype(BF)  41.7 us
    ppermute x24, starting transfers between devices, shift_z(): lax.ppermute(value, 'seq', [(i, (i + 2 * step) % size) for i in range(siz...  38.4 us
  transfers between devices with their start and end apart: 91, of which 37 were waited for; matrix products, arithmetic and copies ran while one was open for 8% of the time, Pallas kernels for 41%

profile of v3, /device:TPU:0, one launch (start us, length us, event | category | flops | bytes accessed | tf_op | source)
XLA Modules:
  0.0 696.9 jit_solution(15697817668076305477)
XLA Ops:
  7.2 2.5 convert.72
  14.6 3.1 collective-permute-start
  17.7 2.6 collective-permute-start.1
  24.2 4.8 collective-permute-done.1
  30.6 7.5 %collective-permute-start.10 = (bf16[2,11,128]{2,1,0:T(8,128)(2,1)S(1)}, bf16[2,11,128]{2,1,0:T(8,128)(2,1)S(1)}, u32[]{:S(2)}, u32[]{:S(2)}) collective-permute-start(bf16[2,11,128]{2,1,0:T(8,128)(2,1)S(1)} %pad_maximum_fusion.6), channel_id=1, source_target_pairs={{0,8},{4,12},{8,0},{12,4},{16,24},{20,28},{24,16},{28,20},{1,9},{5... | collective-permute-start | bytes 16904 | tf_op jit(solution)/shard_map/ppermute | solution.py:46
  38.2 3.2 collective-permute-start.4
  41.4 2.9 collective-permute-start.5
  44.4 2.6 collective-permute-done.3
  46.9 4.8 collective-permute-done.4
  51.8 3.5 collective-permute-start.6
  58.9 3.0 collective-permute-done.6
  61.9 4.1 collective-permute-start.7
  67.3 10.2 %collective-permute-done.7 = bf16[1,128,512]{2,1,0:T(8,128)(2,1)S(1)} collective-permute-done((bf16[1,128,512]{2,1,0:T(8,128)(2,1)S(1)}, bf16[1,128,512]{2,1,0:T(8,128)(2,1)S(1)}, u32[]{:S(2)}, u32[]{:S(2)}) %collective-permute-start.7) | collective-permute-done | bytes 131104 | tf_op jit(solution)/shard_map/ppermute | solution.py:51
  79.9 4.4 collective-permute-done.8
  85.4 8.3 %collective-permute-done.14.refs_3_ = bf16[4,2,128,256]{3,2,1,0:T(8,128)(2,1)} collective-permute-done((bf16[4,2,128,256]{3,2,1,0:T(8,128)(2,1)}, bf16[4,2,128,256]{3,2,1,0:T(8,128)(2,1)}, u32[]{:S(2)}, u32[]{:S(2)}) %collective-permute-start.14) | collective-permute-done | bytes 524320 | tf_op jit(solution)/shard_map/ppermute | solution.py:46
  97.6 14.5 %shard_map.211 = (bf16[4,256,3072]{2,1,0:T(8,128)(2,1)}, bf16[4,256,1024]{2,1,0:T(8,128)(2,1)}) custom-call(s32[5]{0:T(128)} %stack.86.place, bf16[4,256,1024]{2,1,0:T(8,128)(2,1)} %frames_ref.4, f32[4,1,1024]{2,1,0:T(1,128)} %broadcast_in_dim.33.shift_ref, f32[3,1024]{1,0:T(4,128)} %fusion.56.gain_ref.refs_4_, bf16[4,2,128,256]{3,2,1,0:T(8,128)(2,1)} %copy-done.9, ...), custom_call_target="tpu_custom_call" | custom-call | flops 12000000000 | bytes 1048576 | tf_op jit(solution)/shard_map/pallas_call | solution.py:709
  112.1 22.3 %shard_map.212 = (bf16[4,256,1024]{2,1,0:T(8,128)(2,1)}, f32[4,16,256]{2,1,0:T(8,128)}) custom-call(s32[5]{0:T(128)} %stack.86.place, bf16[4,256,3072]{2,1,0:T(8,128)(2,1)} %get-tuple-element.107.packed_ref), custom_call_target="tpu_custom_call" | custom-call | flops 22000001024 | bytes 1048576 | tf_op jit(solution)/shard_map/pallas_call | solution.py:709
  137.3 8.3 %shard_map.213 = (bf16[4,64,1024]{2,1,0:T(8,128)(2,1)}, bf16[4,64,1024]{2,1,0:T(8,128)(2,1)}, bf16[4,64,1024]{2,1,0:T(8,128)(2,1)}, bf16[4,64,1024]{2,1,0:T(8,128)(2,1)}) custom-call(s32[5]{0:T(128)} %stack.86.place, bf16[4,256,1024]{2,1,0:T(8,128)(2,1)} %get-tuple-element.108.heads_ref, bf16[4,256,1024]{2,1,0:T(8,128)(2,1)} %frames_ref.4, ...), custom_call_target="tpu_custom_call" | custom-call | flops 6000000000 | bytes 1048576 | tf_op jit(solution)/shard_map/pallas_call | solution.py:709
  149.9 10.1 %collective-permute-done.25.refs_1_ = bf16[4,64,1024]{2,1,0:T(8,128)(2,1)} collective-permute-done((bf16[4,64,1024]{2,1,0:T(8,128)(2,1)}, bf16[4,64,1024]{2,1,0:T(8,128)(2,1)}, u32[]{:S(2)}, u32[]{:S(2)}) %collective-permute-start.25) | collective-permute-done | bytes 524320 | tf_op jit(solution)/shard_map/ppermute | solution.py:46
  160.0 8.6 %collective-permute-done.26.refs_2_ = bf16[4,64,1024]{2,1,0:T(8,128)(2,1)} collective-permute-done((bf16[4,64,1024]{2,1,0:T(8,128)(2,1)}, bf16[4,64,1024]{2,1,0:T(8,128)(2,1)}, u32[]{:S(2)}, u32[]{:S(2)}) %collective-permute-start.26) | collective-permute-done | bytes 524320 | tf_op jit(solution)/shard_map/ppermute | solution.py:46
  168.6 12.1 %collective-permute-done.27.refs_3_ = bf16[4,64,1024]{2,1,0:T(8,128)(2,1)} collective-permute-done((bf16[4,64,1024]{2,1,0:T(8,128)(2,1)}, bf16[4,64,1024]{2,1,0:T(8,128)(2,1)}, u32[]{:S(2)}, u32[]{:S(2)}) %collective-permute-start.27) | collective-permute-done | bytes 524320 | tf_op jit(solution)/shard_map/ppermute | solution.py:46
  185.4 37.1 %shard_map.214 = (bf16[4,256,3072]{2,1,0:T(8,128)(2,1)}, bf16[4,256,1024]{2,1,0:T(8,128)(2,1)}, f32[4,16,256]{2,1,0:T(8,128)}, bf16[4,256,1024]{2,1,0:T(8,128)(2...) custom-call(s32[5]{0:T(128)} %stack.86.place, ...), custom_call_target="tpu_custom_call" | custom-call | flops 36999999488 | bytes 1048576 | tf_op jit(solution)/shard_map/pallas_call | solution.py:709
  224.3 4.6 shard_map.215.cot_ref
  228.9 46.1 %shard_map.216 = (bf16[2,2,4,4,128,256]{5,4,3,2,1,0:T(8,128)(2,1)}, bf16[2,2,4,4,128,256]{5,4,3,2,1,0:T(8,128)(2,1)}, f32[1024,1024]{1,0:T(8,128)}, f32[1024,1024]{1,0:T(8,128)}) custom-call(s32[5]{0:T(128)} %stack.86.place, bf16[1024,1024]{1,0:T(8,128)(2,1)} %bitcast.291, bf16[1024,1024]{1,0:T(8,128)(2,1)} %bitcast.289, f32[1024,1024]{1,0:T(8,128)} %bitcast.281, ...), custom_call_target="tpu_custom_call" | custom-call | flops 41000001536 | bytes 1048576 | tf_op jit(solution)/shard_map/pallas_call | solution.py:709
  275.1 38.1 %shard_map.217 = (bf16[2,2,4,4,128,256]{5,4,3,2,1,0:T(8,128)(2,1)}, bf16[2,2,4,4,128,256]{5,4,3,2,1,0:T(8,128)(2,1)}, f32[1024,1024]{1,0:T(8,128)}, bf16[4,64,10...) custom-call(s32[5]{0:T(128)} %stack.86.place, ...), custom_call_target="tpu_custom_call" | custom-call | flops 41000001536 | bytes 1048576 | tf_op jit(solution)/shard_map/pallas_call | solution.py:709
  317.3 4.4 fusion
  322.9 41.5 %shard_map.218 = (bf16[4,256,1024]{2,1,0:T(8,128)(2,1)}, bf16[4,256,3072]{2,1,0:T(8,128)(2,1)}, f32[2,1024]{1,0:T(2,128)}, bf16[4,64,1024]{2,1,0:T(8,128)(2,1)},...) custom-call(s32[5]{0:T(128)} %stack.86.place, ...), custom_call_target="tpu_custom_call" | custom-call | flops 38000001024 | bytes 1048576 | tf_op jit(solution)/shard_map/pallas_call | solution.py:709
  364.4 3.0 fusion.1
  369.3 4.7 shard_map.219
  374.0 3.3 fusion.5
  377.3 15.2 %shard_map.220 = (bf16[2,2,4,4,128,256]{5,4,3,2,1,0:T(8,128)(2,1)}, bf16[2,2,4,4,128,256]{5,4,3,2,1,0:T(8,128)(2,1)}) custom-call(s32[5]{0:T(128)} %stack.86.place, bf16[1024,1024]{1,0:T(8,128)(2,1)} %bitcast.288, bf16[1024,3072]{1,0:T(8,128)(2,1)} %bitcast.280, bf16[1024,1024]{1,0:T(8,128)(2,1)} %bitcast.287, bf16[1024,1024]{1,0:T(8,128)(2,1)} %bitcast.293), custom_call_target="tpu_custom_call" | custom-call | flops 15000000512 | bytes 1048576 | tf_op jit(solution)/shard_map/pallas_call | solution.py:709
  397.0 2.9 collective-permute-done.37
  399.9 5.2 fusion.2
  409.2 10.9 %collective-permute-done.40.refs_3_ = bf16[4,64,1024]{2,1,0:T(8,128)(2,1)} collective-permute-done((bf16[4,64,1024]{2,1,0:T(8,128)(2,1)S(1)}, bf16[4,64,1024]{2,1,0:T(8,128)(2,1)}, u32[]{:S(2)}, u32[]{:S(2)}) %collective-permute-start.40) | collective-permute-done | bytes 524320 | tf_op jit(solution)/shard_map/ppermute | solution.py:46
  420.0 7.9 %shard_map.221 = (bf16[4,256,1024]{2,1,0:T(8,128)(2,1)}, bf16[4,256,1024]{2,1,0:T(8,128)(2,1)}) custom-call(s32[5]{0:T(128)} %stack.86.place, bf16[4,64,1024]{2,1,0:T(8,128)(2,1)} %get-tuple-element.150.refs_0_, bf16[4,64,1024]{2,1,0:T(8,128)(2,1)} %copy-done.36, bf16[4,64,1024]{2,1,0:T(8,128)(2,1)} %copy-done.38, ...), custom_call_target="tpu_custom_call" | custom-call | flops 7000000000 | bytes 1048576 | tf_op jit(solution)/shard_map/pallas_call | solution.py:709
  428.4 12.8 %collective-permute-done.41 = bf16[2,4,4,128,256]{4,3,2,1,0:T(8,128)(2,1)} collective-permute-done((bf16[2,4,4,128,256]{4,3,2,1,0:T(8,128)(2,1)S(1)}, bf16[2,4,4,128,256]{4,3,2,1,0:T(8,128)(2,1)}, u32[]{:S(2)}, u32[]{:S(2)}) %collective-permute-start.41) | collective-permute-done | bytes 2097184 | tf_op jit(solution)/shard_map/ppermute | solution.py:46
  443.6 23.3 %shard_map.222.grad_ref = bf16[4,256,3072]{2,1,0:T(8,128)(2,1)} custom-call(s32[5]{0:T(128)} %stack.86.place, bf16[4,256,3072]{2,1,0:T(8,128)(2,1)} %get-tuple-element.107.packed_ref, bf16[4,256,1024]{2,1,0:T(8,128)(2,1)} %get-tuple-element.108.heads_ref, bf16[4,256,1024]{2,1,0:T(8,128)(2,1)} %get-tuple-element.157.heads_grad_ref, ...), custom_call_target="tpu_custom_call" | custom-call | flops 25999998976 | bytes 1048576 | tf_op jit(solution)/shard_map/pallas_call | solution.py:709
  466.9 2.9 fusion.28
  469.8 9.9 %shard_map.223 = (bf16[2,2,4,2,128,256]{5,4,3,2,1,0:T(8,128)(2,1)}, bf16[2,2,4,2,128,256]{5,4,3,2,1,0:T(8,128)(2,1)}) custom-call(s32[5]{0:T(128)} %stack.86.place, bf16[1024,1024]{1,0:T(8,128)(2,1)} %bitcast.283, bf16[1024,3072]{1,0:T(8,128)(2,1)} %bitcast.278), custom_call_target="tpu_custom_call" | custom-call | flops 15000000512 | bytes 1048576 | tf_op jit(solution)/shard_map/pallas_call | solution.py:709
  479.8 3.1 fusion.25
  482.9 2.8 collective-permute-done.45
  485.7 3.3 fusion.3
  489.0 10.9 %shard_map.224 = (bf16[2,2,4,2,128,256]{5,4,3,2,1,0:T(8,128)(2,1)}, bf16[2,2,4,2,128,256]{5,4,3,2,1,0:T(8,128)(2,1)}) custom-call(s32[5]{0:T(128)} %stack.86.place, bf16[1024,1024]{1,0:T(8,128)(2,1)} %bitcast.284, bf16[1024,3072]{1,0:T(8,128)(2,1)} %bitcast.279, bf16[1024,1024]{1,0:T(8,128)(2,1)} %bitcast.285, bf16[1024,1024]{1,0:T(8,128)(2,1)} %bitcast.286), custom_call_target="tpu_custom_call" | custom-call | flops 15000000512 | bytes 1048576 | tf_op jit(solution)/shard_map/pallas_call | solution.py:709
  503.0 12.3 %collective-permute-done.49 = bf16[4,128,256]{2,1,0:T(8,128)(2,1)S(1)} collective-permute-done((bf16[4,128,256]{2,1,0:T(8,128)(2,1)}, bf16[4,128,256]{2,1,0:T(8,128)(2,1)S(1)}, u32[]{:S(2)}, u32[]{:S(2)}) %collective-permute-start.49) | collective-permute-done | bytes 262176 | tf_op jit(solution)/shard_map/ppermute | solution.py:51
  517.3 9.0 %collective-permute-done.48 = bf16[4,128,256]{2,1,0:T(8,128)(2,1)S(1)} collective-permute-done((bf16[4,128,256]{2,1,0:T(8,128)(2,1)S(1)}, bf16[4,128,256]{2,1,0:T(8,128)(2,1)S(1)}, u32[]{:S(2)}, u32[]{:S(2)}) %collective-permute-start.48) | collective-permute-done | bytes 262176 | tf_op jit(solution)/shard_map/ppermute | solution.py:51
  528.4 2.7 fusion.6
  531.0 7.1 %collective-permute-start.57 = (bf16[2,4,2,128,256]{4,3,2,1,0:T(8,128)(2,1)}, bf16[2,4,2,128,256]{4,3,2,1,0:T(8,128)(2,1)}, u32[]{:S(2)}, u32[]{:S(2)}) collective-permute-start(bf16[2,4,2,128,256]{4,3,2,1,0:T(8,128)(2,1)} %fusion.6), channel_id=1, source_target_pairs={{0,2},{1,3},{2,0},{3,1},{4,6},{5,7},{6,4},{7,5},{8,10},{9,11},{10,... | collective-permute-start | bytes 3145736 | tf_op jit(solution)/shard_map/ppermute | solution.py:46
  539.9 16.2 %shard_map.225 = (bf16[4,256,1024]{2,1,0:T(8,128)(2,1)}, f32[1,1024]{1,0:T(1,128)}, f32[4,1,1024]{2,1,0:T(1,128)}) custom-call(s32[5]{0:T(128)} %stack.86.place, bf16[4,256,3072]{2,1,0:T(8,128)(2,1)} %shard_map.222.grad_ref, bf16[4,256,1024]{2,1,0:T(8,128)(2,1)} %frames_ref.4, f32[4,1,1024]{2,1,0:T(1,128)} %broadcast_in_dim.33.shift_ref, ...), custom_call_target="tpu_custom_call" | custom-call | flops 14000000000 | bytes 1048576 | tf_op jit(solution)/shard_map/pallas_call | solution.py:709
  556.0 6.5 collective-permute-done.57
  562.5 2.3 fusion.9
  566.8 3.0 fusion.11
  569.8 2.9 collective-permute-start.56
  572.7 10.7 %collective-permute-done.59 = bf16[2,4,2,128,256]{4,3,2,1,0:T(8,128)(2,1)} collective-permute-done((bf16[2,4,2,128,256]{4,3,2,1,0:T(8,128)(2,1)S(1)}, bf16[2,4,2,128,256]{4,3,2,1,0:T(8,128)(2,1)}, u32[]{:S(2)}, u32[]{:S(2)}) %collective-permute-start.59) | collective-permute-done | bytes 1048608 | tf_op jit(solution)/shard_map/ppermute | solution.py:46
  584.8 2.9 collective-permute-start.55
  589.4 2.8 multiply_reduce_fusion.1
  593.5 2.3 fusion.47
  599.1 4.5 collective-permute-done.55
  610.5 2.5 collective-permute-done.60
  615.8 5.5 collective-permute-done.61
  625.8 3.1 collective-permute-done.66
  630.2 4.0 collective-permute-done.65
  638.8 3.1 collective-permute-done.74
  649.6 3.1 collective-permute-start.79
  663.6 25.1 %shard_map.226 = (f32[2,128,4096]{2,1,0:T(8,128)}, f32[2,128,4096]{2,1,0:T(8,128)}, f32[2,128,4096]{2,1,0:T(8,128)}, f32[2,128,4096]{2,1,0:T(8,128)}, f32[2,128,4096]{2,1,0:T(8,128)}, /*index=5*/f32[2,128,4096]{2,1,0:T(8,128)}) custom-call(s32[5]{0:T(128)} %stack.86.place, f32[1]{0:T(128)} %bitcast.114.clip, bf16[2,128,256]{2,1,0:T(8,128)(2,1)} %copy-done.15, ...), custom_call_target="tpu_custom_call" | custom-call | flops 10000000000 | bytes 1048576 | tf_op jit(solution)/shard_map/pallas_call | solution.py:709
  (298 shorter events, 106.9 us)
Async XLA Ops:
  7.2 178.3 %all-gather.5.cloned.1.call-start = ((), (), s32[]{:S(2)}) async-start(), calls=%async_computation | async-start | bytes 17301504 | tf_op jit(solution)/shard_map/all_gather | solution.py:798
  14.5 260.6 %all-gather.7.cloned.1.call-start = ((), (), s32[]{:S(2)}) async-start(), calls=%async_computation.1 | async-start | bytes 8650752 | tf_op jit(solution)/shard_map/all_gather | solution.py:888
  14.6 9.5 %collective-permute-start = (bf16[2,128,256]{2,1,0:T(8,128)(2,1)S(1)}, bf16[2,128,256]{2,1,0:T(8,128)(2,1)S(1)}, u32[]{:S(2)}, u32[]{:S(2)}) collective-permute-start(bf16[2,128,256]{2,1,0:T(8,128)(2,1)S(1)} %fusion.50), channel_id=1, source_target_pairs={{0,8},{4,12},{8,16},{12,20},{16,24},{20,28},{24,0},{28,4},{1,9},{5... | collective-permute-start | bytes 393224 | tf_op jit(solution)/shard_map/ppermute | solution.py:51
  17.7 11.2 %collective-permute-start.1 = (bf16[2,128,256]{2,1,0:T(8,128)(2,1)S(1)}, bf16[2,128,256]{2,1,0:T(8,128)(2,1)S(1)}, u32[]{:S(2)}, u32[]{:S(2)}) collective-permute-start(bf16[2,128,256]{2,1,0:T(8,128)(2,1)S(1)} %fusion.50), channel_id=1, source_target_pairs={{0,16},{4,20},{8,24},{12,28},{16,0},{20,4},{24,8},{28,12},{1,17},{... | collective-permute-start | bytes 393224 | tf_op jit(solution)/shard_map/ppermute | solution.py:51
  29.0 29.3 %collective-permute-start.12 = (bf16[4,2,128,256]{3,2,1,0:T(8,128)(2,1)S(1)}, bf16[4,2,128,256]{3,2,1,0:T(8,128)(2,1)}, u32[]{:S(2)}, u32[]{:S(2)}) collective-permute-start(bf16[4,2,128,256]{3,2,1,0:T(8,128)(2,1)S(1)} %pad_maximum_fusion.refs_0_), channel_id=1, source_target_pairs={{0,4},{4,0},{8,12},{12,8},{16,20},{20,16},{24,28},{28,24},{1,5},{5... | collective-permute-start | bytes 1572872 | tf_op jit(solution)/shard_map/ppermute | solution.py:46
  30.6 13.6 %collective-permute-start.10 = (bf16[2,11,128]{2,1,0:T(8,128)(2,1)S(1)}, bf16[2,11,128]{2,1,0:T(8,128)(2,1)S(1)}, u32[]{:S(2)}, u32[]{:S(2)}) collective-permute-start(bf16[2,11,128]{2,1,0:T(8,128)(2,1)S(1)} %pad_maximum_fusion.6), channel_id=1, source_target_pairs={{0,8},{4,12},{8,0},{12,4},{16,24},{20,28},{24,16},{28,20},{1,9},{5... | collective-permute-start | bytes 16904 | tf_op jit(solution)/shard_map/ppermute | solution.py:46
  38.2 13.6 %collective-permute-start.4 = (bf16[1,128,512]{2,1,0:T(8,128)(2,1)S(1)}, bf16[1,128,512]{2,1,0:T(8,128)(2,1)S(1)}, u32[]{:S(2)}, u32[]{:S(2)}) collective-permute-start(bf16[1,128,512]{2,1,0:T(8,128)(2,1)S(1)} %constant_dynamic-slice_fusion.4), channel_id=1, source_target_pairs={{0,16},{4,20},{8,24},{12,28},{16,0},{20,4},{24,8},{28,12},{1,17},{... | collective-permute-start | bytes 393224 | tf_op jit(solution)/shard_map/ppermute | solution.py:51
  41.4 10.4 %collective-permute-start.5 = (bf16[1,128,512]{2,1,0:T(8,128)(2,1)S(1)}, bf16[1,128,512]{2,1,0:T(8,128)(2,1)S(1)}, u32[]{:S(2)}, u32[]{:S(2)}) collective-permute-start(bf16[1,128,512]{2,1,0:T(8,128)(2,1)S(1)} %constant_dynamic-slice_fusion.4), channel_id=1, source_target_pairs={{0,24},{4,28},{8,0},{12,4},{16,8},{20,12},{24,16},{28,20},{1,25},{... | collective-permute-start | bytes 393224 | tf_op jit(solution)/shard_map/ppermute | solution.py:51
  44.3 12.5 %collective-permute-start.11 = (bf16[4,11,128]{2,1,0:T(8,128)(2,1)S(1)}, bf16[4,11,128]{2,1,0:T(8,128)(2,1)S(1)}, u32[]{:S(2)}, u32[]{:S(2)}) collective-permute-start(bf16[4,11,128]{2,1,0:T(8,128)(2,1)S(1)} %pad_maximum_fusion.5), channel_id=1, source_target_pairs={{0,16},{4,20},{8,24},{12,28},{16,0},{20,4},{24,8},{28,12},{1,17},{... | collective-permute-start | bytes 33800 | tf_op jit(solution)/shard_map/ppermute | solution.py:46
  51.8 10.1 %collective-permute-start.6 = (bf16[1,128,512]{2,1,0:T(8,128)(2,1)S(1)}, bf16[1,128,512]{2,1,0:T(8,128)(2,1)S(1)}, u32[]{:S(2)}, u32[]{:S(2)}) collective-permute-start(bf16[1,128,512]{2,1,0:T(8,128)(2,1)S(1)} %constant_dynamic-slice_fusion.5), channel_id=1, source_target_pairs={{0,8},{4,12},{8,16},{12,20},{16,24},{20,28},{24,0},{28,4},{1,9},{5... | collective-permute-start | bytes 393224 | tf_op jit(solution)/shard_map/ppermute | solution.py:51
  55.3 29.0 %collective-permute-start.13 = (bf16[4,2,128,256]{3,2,1,0:T(8,128)(2,1)S(1)}, bf16[4,2,128,256]{3,2,1,0:T(8,128)(2,1)}, u32[]{:S(2)}, u32[]{:S(2)}) collective-permute-start(bf16[4,2,128,256]{3,2,1,0:T(8,128)(2,1)S(1)} %pad_maximum_fusion.refs_0_), channel_id=1, source_target_pairs={{0,2},{1,3},{2,0},{3,1},{4,6},{5,7},{6,4},{7,5},{8,10},{9,11},{10,... | collective-permute-start | bytes 1572872 | tf_op jit(solution)/shard_map/ppermute | solution.py:46
  56.8 28.0 %collective-permute-start.15 = (bf16[4,2,128,256]{3,2,1,0:T(8,128)(2,1)S(1)}, bf16[4,2,128,256]{3,2,1,0:T(8,128)(2,1)}, u32[]{:S(2)}, u32[]{:S(2)}) collective-permute-start(bf16[4,2,128,256]{3,2,1,0:T(8,128)(2,1)S(1)} %pad_maximum_fusion.refs_0_), channel_id=1, source_target_pairs={{0,1},{1,0},{2,3},{3,2},{4,5},{5,4},{6,7},{7,6},{8,9},{9,8},{10,11... | collective-permute-start | bytes 1572872 | tf_op jit(solution)/shard_map/ppermute | solution.py:46
  56.8 28.1 %collective-permute-start.19 = (bf16[4,1,128,512]{3,2,1,0:T(8,128)(2,1)S(1)}, bf16[4,1,128,512]{3,2,1,0:T(8,128)(2,1)}, u32[]{:S(2)}, u32[]{:S(2)}) collective-permute-start(bf16[4,1,128,512]{3,2,1,0:T(8,128)(2,1)S(1)} %pad_maximum_fusion.1.refs_8_), channel_id=1, source_target_pairs={{0,4},{4,0},{8,12},{12,8},{16,20},{20,16},{24,28},{28,24},{1,5},{5... | collective-permute-start | bytes 1572872 | tf_op jit(solution)/shard_map/ppermute | solution.py:46
  58.3 35.4 %collective-permute-start.14 = (bf16[4,2,128,256]{3,2,1,0:T(8,128)(2,1)}, bf16[4,2,128,256]{3,2,1,0:T(8,128)(2,1)}, u32[]{:S(2)}, u32[]{:S(2)}) collective-permute-start(bf16[4,2,128,256]{3,2,1,0:T(8,128)(2,1)} %collective-permute-done.12.refs_1_), channel_id=1, source_target_pairs={{0,2},{1,3},{2,0},{3,1},{4,6},{5,7},{6,4},{7,5},{8,10},{9,11},{10,... | collective-permute-start | bytes 1572872 | tf_op jit(solution)/shard_map/ppermute | solution.py:46
  61.9 15.6 %collective-permute-start.7 = (bf16[1,128,512]{2,1,0:T(8,128)(2,1)S(1)}, bf16[1,128,512]{2,1,0:T(8,128)(2,1)S(1)}, u32[]{:S(2)}, u32[]{:S(2)}) collective-permute-start(bf16[1,128,512]{2,1,0:T(8,128)(2,1)S(1)} %constant_dynamic-slice_fusion.5), channel_id=1, source_target_pairs={{0,16},{4,20},{8,24},{12,28},{16,0},{20,4},{24,8},{28,12},{1,17},{... | collective-permute-start | bytes 393224 | tf_op jit(solution)/shard_map/ppermute | solution.py:51
  84.3 10.9 %collective-permute-start.20 = (bf16[4,1,128,512]{3,2,1,0:T(8,128)(2,1)S(1)}, bf16[4,1,128,512]{3,2,1,0:T(8,128)(2,1)S(1)}, u32[]{:S(2)}, u32[]{:S(2)}) collective-permute-start(bf16[4,1,128,512]{3,2,1,0:T(8,128)(2,1)S(1)} %pad_maximum_fusion.1.refs_8_), channel_id=1, source_target_pairs={{0,1},{1,0},{2,3},{3,2},{4,5},{5,4},{6,7},{7,6},{8,9},{9,8},{10,11... | collective-permute-start | bytes 1572872 | tf_op jit(solution)/shard_map/ppermute | solution.py:46
  84.3 13.2 %collective-permute-start.16 = (bf16[4,2,128,256]{3,2,1,0:T(8,128)(2,1)}, bf16[4,2,128,256]{3,2,1,0:T(8,128)(2,1)}, u32[]{:S(2)}, u32[]{:S(2)}) collective-permute-start(bf16[4,2,128,256]{3,2,1,0:T(8,128)(2,1)} %collective-permute-done.12.refs_1_), channel_id=1, source_target_pairs={{0,1},{1,0},{2,3},{3,2},{4,5},{5,4},{6,7},{7,6},{8,9},{9,8},{10,11... | collective-permute-start | bytes 1572872 | tf_op jit(solution)/shard_map/ppermute | solution.py:46
  84.8 12.7 %collective-permute-start.17 = (bf16[4,2,128,256]{3,2,1,0:T(8,128)(2,1)}, bf16[4,2,128,256]{3,2,1,0:T(8,128)(2,1)}, u32[]{:S(2)}, u32[]{:S(2)}) collective-permute-start(bf16[4,2,128,256]{3,2,1,0:T(8,128)(2,1)} %collective-permute-done.13.refs_2_), channel_id=1, source_target_pairs={{0,1},{1,0},{2,3},{3,2},{4,5},{5,4},{6,7},{7,6},{8,9},{9,8},{10,11... | collective-permute-start | bytes 1572872 | tf_op jit(solution)/shard_map/ppermute | solution.py:46
  84.9 12.6 %collective-permute-start.21 = (bf16[4,1,128,512]{3,2,1,0:T(8,128)(2,1)}, bf16[4,1,128,512]{3,2,1,0:T(8,128)(2,1)}, u32[]{:S(2)}, u32[]{:S(2)}) collective-permute-start(bf16[4,1,128,512]{3,2,1,0:T(8,128)(2,1)} %collective-permute-done.19.refs_9_), channel_id=1, source_target_pairs={{0,1},{1,0},{2,3},{3,2},{4,5},{5,4},{6,7},{7,6},{8,9},{9,8},{10,11... | collective-permute-start | bytes 1572872 | tf_op jit(solution)/shard_map/ppermute | solution.py:46
  96.0 38.3 %collective-permute-start.22 = (bf16[4,1,128,512]{3,2,1,0:T(8,128)(2,1)S(1)}, bf16[4,1,128,512]{3,2,1,0:T(8,128)(2,1)S(1)}, u32[]{:S(2)}, u32[]{:S(2)}) collective-permute-start(bf16[4,1,128,512]{3,2,1,0:T(8,128)(2,1)S(1)} %pad_maximum_fusion.2.refs_0_.refs_4_), channel_id=1, source_target_pairs={{0,4},{4,0},{8,12},{12,8},{16,20},{20,16},{24,28},{28,24},{1,5},{5... | collective-permute-start | bytes 1572872 | tf_op jit(solution)/shard_map/ppermute | solution.py:46
  145.6 14.3 %collective-permute-start.25 = (bf16[4,64,1024]{2,1,0:T(8,128)(2,1)}, bf16[4,64,1024]{2,1,0:T(8,128)(2,1)}, u32[]{:S(2)}, u32[]{:S(2)}) collective-permute-start(bf16[4,64,1024]{2,1,0:T(8,128)(2,1)} %get-tuple-element.112), channel_id=1, source_target_pairs={{0,4},{4,0},{8,12},{12,8},{16,20},{20,16},{24,28},{28,24},{1,5},{5... | collective-permute-start | bytes 1572872 | tf_op jit(solution)/shard_map/ppermute | solution.py:46
  146.1 22.5 %collective-permute-start.26 = (bf16[4,64,1024]{2,1,0:T(8,128)(2,1)}, bf16[4,64,1024]{2,1,0:T(8,128)(2,1)}, u32[]{:S(2)}, u32[]{:S(2)}) collective-permute-start(bf16[4,64,1024]{2,1,0:T(8,128)(2,1)} %get-tuple-element.113), channel_id=1, source_target_pairs={{0,8},{4,12},{8,0},{12,4},{16,24},{20,28},{24,16},{28,20},{1,9},{5... | collective-permute-start | bytes 1572872 | tf_op jit(solution)/shard_map/ppermute | solution.py:46
  147.5 33.2 %collective-permute-start.27 = (bf16[4,64,1024]{2,1,0:T(8,128)(2,1)}, bf16[4,64,1024]{2,1,0:T(8,128)(2,1)}, u32[]{:S(2)}, u32[]{:S(2)}) collective-permute-start(bf16[4,64,1024]{2,1,0:T(8,128)(2,1)} %get-tuple-element.114), channel_id=1, source_target_pairs={{0,12},{4,8},{8,4},{12,0},{16,28},{20,24},{24,20},{28,16},{1,13},{... | collective-permute-start | bytes 1572872 | tf_op jit(solution)/shard_map/ppermute | solution.py:46
  181.9 40.6 %collective-permute-start.30 = (bf16[4,64,1024]{2,1,0:T(8,128)(2,1)}, bf16[4,64,1024]{2,1,0:T(8,128)(2,1)S(1)}, u32[]{:S(2)}, u32[]{:S(2)}) collective-permute-start(bf16[4,64,1024]{2,1,0:T(8,128)(2,1)} %get-tuple-element.120), channel_id=1, source_target_pairs={{0,12},{4,8},{8,4},{12,0},{16,28},{20,24},{24,20},{28,16},{1,13},{... | collective-permute-start | bytes 1572872 | tf_op jit(solution)/shard_map/ppermute | solution.py:46
  183.4 39.1 %collective-permute-start.29 = (bf16[4,64,1024]{2,1,0:T(8,128)(2,1)S(1)}, bf16[4,64,1024]{2,1,0:T(8,128)(2,1)S(1)}, u32[]{:S(2)}, u32[]{:S(2)}) collective-permute-start(bf16[4,64,1024]{2,1,0:T(8,128)(2,1)S(1)} %get-tuple-element.119), channel_id=1, source_target_pairs={{0,8},{4,12},{8,0},{12,4},{16,24},{20,28},{24,16},{28,20},{1,9},{5... | collective-permute-start | bytes 1572872 | tf_op jit(solution)/shard_map/ppermute | solution.py:46
  184.0 38.6 %collective-permute-start.28 = (bf16[4,64,1024]{2,1,0:T(8,128)(2,1)S(1)}, bf16[4,64,1024]{2,1,0:T(8,128)(2,1)S(1)}, u32[]{:S(2)}, u32[]{:S(2)}) collective-permute-start(bf16[4,64,1024]{2,1,0:T(8,128)(2,1)S(1)} %get-tuple-element.118), channel_id=1, source_target_pairs={{0,4},{4,0},{8,12},{12,8},{16,20},{20,16},{24,28},{28,24},{1,5},{5... | collective-permute-start | bytes 1572872 | tf_op jit(solution)/shard_map/ppermute | solution.py:46
  275.0 42.3 %collective-permute-start.31 = (bf16[2,2,4,4,128,256]{5,4,3,2,1,0:T(8,128)(2,1)}, bf16[2,2,4,4,128,256]{5,4,3,2,1,0:T(8,128)(2,1)}, u32[]{:S(2)}, u32[]{:S(2)}) collective-permute-start(bf16[2,2,4,4,128,256]{5,4,3,2,1,0:T(8,128)(2,1)} %get-tuple-element.128), channel_id=1, source_target_pairs={{0,1},{1,0},{2,3},{3,2},{4,5},{5,4},{6,7},{7,6},{8,9},{9,8},{10,11... | collective-permute-start | bytes 12582920 | tf_op jit(solution)/shard_map/ppermute | solution.py:46
  313.3 51.1 %collective-permute-start.36 = (bf16[2,2,4,4,128,256]{5,4,3,2,1,0:T(8,128)(2,1)}, bf16[2,2,4,4,128,256]{5,4,3,2,1,0:T(8,128)(2,1)}, u32[]{:S(2)}, u32[]{:S(2)}) collective-permute-start(bf16[2,2,4,4,128,256]{5,4,3,2,1,0:T(8,128)(2,1)} %get-tuple-element.144), channel_id=1, source_target_pairs={{0,1},{1,0},{2,3},{3,2},{4,5},{5,4},{6,7},{7,6},{8,9},{9,8},{10,11... | collective-permute-start | bytes 12582920 | tf_op jit(solution)/shard_map/ppermute | solution.py:46
  313.8 53.7 %collective-permute-start.32 = (bf16[4,64,1024]{2,1,0:T(8,128)(2,1)}, bf16[4,64,1024]{2,1,0:T(8,128)(2,1)S(1)}, u32[]{:S(2)}, u32[]{:S(2)}) collective-permute-start(bf16[4,64,1024]{2,1,0:T(8,128)(2,1)} %get-tuple-element.137), channel_id=1, source_target_pairs={{0,4},{4,0},{8,12},{12,8},{16,20},{20,16},{24,28},{28,24},{1,5},{5... | collective-permute-start | bytes 1572872 | tf_op jit(solution)/shard_map/ppermute | solution.py:46
  313.8 53.7 %collective-permute-start.33 = (bf16[4,64,1024]{2,1,0:T(8,128)(2,1)}, bf16[4,64,1024]{2,1,0:T(8,128)(2,1)S(1)}, u32[]{:S(2)}, u32[]{:S(2)}) collective-permute-start(bf16[4,64,1024]{2,1,0:T(8,128)(2,1)} %get-tuple-element.138), channel_id=1, source_target_pairs={{0,8},{4,12},{8,0},{12,4},{16,24},{20,28},{24,16},{28,20},{1,9},{5... | collective-permute-start | bytes 1572872 | tf_op jit(solution)/shard_map/ppermute | solution.py:46
  315.0 52.5 %collective-permute-start.34 = (bf16[4,64,1024]{2,1,0:T(8,128)(2,1)}, bf16[4,64,1024]{2,1,0:T(8,128)(2,1)S(1)}, u32[]{:S(2)}, u32[]{:S(2)}) collective-permute-start(bf16[4,64,1024]{2,1,0:T(8,128)(2,1)} %get-tuple-element.139), channel_id=1, source_target_pairs={{0,12},{4,8},{8,4},{12,0},{16,28},{20,24},{24,20},{28,16},{1,13},{... | collective-permute-start | bytes 1572872 | tf_op jit(solution)/shard_map/ppermute | solution.py:46
  321.7 52.3 %collective-permute-start.35 = (bf16[2,4,4,128,256]{4,3,2,1,0:T(8,128)(2,1)}, bf16[2,4,4,128,256]{4,3,2,1,0:T(8,128)(2,1)}, u32[]{:S(2)}, u32[]{:S(2)}) collective-permute-start(bf16[2,4,4,128,256]{4,3,2,1,0:T(8,128)(2,1)} %fusion), channel_id=1, source_target_pairs={{0,2},{1,3},{2,0},{3,1},{4,6},{5,7},{6,4},{7,5},{8,10},{9,11},{10,... | collective-permute-start | bytes 6291464 | tf_op jit(solution)/shard_map/ppermute | solution.py:46
  392.6 48.6 %collective-permute-start.41 = (bf16[2,4,4,128,256]{4,3,2,1,0:T(8,128)(2,1)S(1)}, bf16[2,4,4,128,256]{4,3,2,1,0:T(8,128)(2,1)}, u32[]{:S(2)}, u32[]{:S(2)}) collective-permute-start(bf16[2,4,4,128,256]{4,3,2,1,0:T(8,128)(2,1)S(1)} %fusion.1), channel_id=1, source_target_pairs={{0,2},{1,3},{2,0},{3,1},{4,6},{5,7},{6,4},{7,5},{8,10},{9,11},{10,... | collective-permute-start | bytes 6291464 | tf_op jit(solution)/shard_map/ppermute | solution.py:46
  393.5 14.0 %collective-permute-start.38 = (bf16[4,64,1024]{2,1,0:T(8,128)(2,1)S(1)}, bf16[4,64,1024]{2,1,0:T(8,128)(2,1)S(1)}, u32[]{:S(2)}, u32[]{:S(2)}) collective-permute-start(bf16[4,64,1024]{2,1,0:T(8,128)(2,1)S(1)} %copy-done.31), channel_id=1, source_target_pairs={{0,4},{4,0},{8,12},{12,8},{16,20},{20,16},{24,28},{28,24},{1,5},{5... | collective-permute-start | bytes 1572872 | tf_op jit(solution)/shard_map/ppermute | solution.py:46
  393.5 14.8 %collective-permute-start.39 = (bf16[4,64,1024]{2,1,0:T(8,128)(2,1)S(1)}, bf16[4,64,1024]{2,1,0:T(8,128)(2,1)S(1)}, u32[]{:S(2)}, u32[]{:S(2)}) collective-permute-start(bf16[4,64,1024]{2,1,0:T(8,128)(2,1)S(1)} %copy-done.30), channel_id=1, source_target_pairs={{0,8},{4,12},{8,0},{12,4},{16,24},{20,28},{24,16},{28,20},{1,9},{5... | collective-permute-start | bytes 1572872 | tf_op jit(solution)/shard_map/ppermute | solution.py:46
  394.8 25.2 %collective-permute-start.40 = (bf16[4,64,1024]{2,1,0:T(8,128)(2,1)S(1)}, bf16[4,64,1024]{2,1,0:T(8,128)(2,1)}, u32[]{:S(2)}, u32[]{:S(2)}) collective-permute-start(bf16[4,64,1024]{2,1,0:T(8,128)(2,1)S(1)} %copy-done.29), channel_id=1, source_target_pairs={{0,12},{4,8},{8,4},{12,0},{16,28},{20,24},{24,20},{28,16},{1,13},{... | collective-permute-start | bytes 1572872 | tf_op jit(solution)/shard_map/ppermute | solution.py:46
  405.1 80.6 %collective-permute-start.45 = (bf16[2,4,4,128,256]{4,3,2,1,0:T(8,128)(2,1)}, bf16[2,4,4,128,256]{4,3,2,1,0:T(8,128)(2,1)}, u32[]{:S(2)}, u32[]{:S(2)}) collective-permute-start(bf16[2,4,4,128,256]{4,3,2,1,0:T(8,128)(2,1)} %fusion.2), channel_id=1, source_target_pairs={{0,2},{1,3},{2,0},{3,1},{4,6},{5,7},{6,4},{7,5},{8,10},{9,11},{10,... | collective-permute-start | bytes 6291464 | tf_op jit(solution)/shard_map/ppermute | solution.py:46
  428.0 39.0 %collective-permute-start.42 = (bf16[4,4,128,256]{3,2,1,0:T(8,128)(2,1)}, bf16[4,4,128,256]{3,2,1,0:T(8,128)(2,1)S(1)}, u32[]{:S(2)}, u32[]{:S(2)}) collective-permute-start(bf16[4,4,128,256]{3,2,1,0:T(8,128)(2,1)} %fusion.5), channel_id=1, source_target_pairs={{0,4},{4,0},{8,12},{12,8},{16,20},{20,16},{24,28},{28,24},{1,5},{5... | collective-permute-start | bytes 3145736 | tf_op jit(solution)/shard_map/ppermute | solution.py:46
  443.5 36.2 %collective-permute-start.44 = (bf16[4,4,128,256]{3,2,1,0:T(8,128)(2,1)S(1)}, bf16[4,4,128,256]{3,2,1,0:T(8,128)(2,1)S(1)}, u32[]{:S(2)}, u32[]{:S(2)}) collective-permute-start(bf16[4,4,128,256]{3,2,1,0:T(8,128)(2,1)S(1)} %fusion.4), channel_id=1, source_target_pairs={{0,4},{4,0},{8,12},{12,8},{16,20},{20,16},{24,28},{28,24},{1,5},{5... | collective-permute-start | bytes 3145736 | tf_op jit(solution)/shard_map/ppermute | solution.py:46
  479.7 48.6 %collective-permute-start.43 = (bf16[2,2,4,2,128,256]{5,4,3,2,1,0:T(8,128)(2,1)}, bf16[2,2,4,2,128,256]{5,4,3,2,1,0:T(8,128)(2,1)}, u32[]{:S(2)}, u32[]{:S(2)}) collective-permute-start(bf16[2,2,4,2,128,256]{5,4,3,2,1,0:T(8,128)(2,1)} %get-tuple-element.164), channel_id=1, source_target_pairs={{0,1},{1,0},{2,3},{3,2},{4,5},{5,4},{6,7},{7,6},{8,9},{9,8},{10,11... | collective-permute-start | bytes 6291464 | tf_op jit(solution)/shard_map/ppermute | solution.py:46
  499.9 38.2 %collective-permute-start.46 = (bf16[2,2,4,2,128,256]{5,4,3,2,1,0:T(8,128)(2,1)}, bf16[2,2,4,2,128,256]{5,4,3,2,1,0:T(8,128)(2,1)S(1)}, u32[]{:S(2)}, u32[]{:S(2)}) collective-permute-start(bf16[2,2,4,2,128,256]{5,4,3,2,1,0:T(8,128)(2,1)} %get-tuple-element.170), channel_id=1, source_target_pairs={{0,1},{1,0},{2,3},{3,2},{4,5},{5,4},{6,7},{7,6},{8,9},{9,8},{10,11... | collective-permute-start | bytes 6291464 | tf_op jit(solution)/shard_map/ppermute | solution.py:46
  500.0 15.3 %collective-permute-start.49 = (bf16[4,128,256]{2,1,0:T(8,128)(2,1)}, bf16[4,128,256]{2,1,0:T(8,128)(2,1)S(1)}, u32[]{:S(2)}, u32[]{:S(2)}) collective-permute-start(bf16[4,128,256]{2,1,0:T(8,128)(2,1)} %get-tuple-element.215), channel_id=1, source_target_pairs={{0,24},{4,28},{8,0},{12,4},{16,8},{20,12},{24,16},{28,20},{1,25},{... | collective-permute-start | bytes 786440 | tf_op jit(solution)/shard_map/ppermute | solution.py:51
  501.0 14.4 %collective-permute-start.47 = (bf16[4,128,256]{2,1,0:T(8,128)(2,1)S(1)}, bf16[4,128,256]{2,1,0:T(8,128)(2,1)S(1)}, u32[]{:S(2)}, u32[]{:S(2)}) collective-permute-start(bf16[4,128,256]{2,1,0:T(8,128)(2,1)S(1)} %copy-done.14), channel_id=1, source_target_pairs={{0,8},{4,12},{8,16},{12,20},{16,24},{20,28},{24,0},{28,4},{1,9},{5... | collective-permute-start | bytes 786440 | tf_op jit(solution)/shard_map/ppermute | solution.py:51
  502.1 24.3 %collective-permute-start.48 = (bf16[4,128,256]{2,1,0:T(8,128)(2,1)S(1)}, bf16[4,128,256]{2,1,0:T(8,128)(2,1)S(1)}, u32[]{:S(2)}, u32[]{:S(2)}) collective-permute-start(bf16[4,128,256]{2,1,0:T(8,128)(2,1)S(1)} %get-tuple-element.216), channel_id=1, source_target_pairs={{0,16},{4,20},{8,24},{12,28},{16,0},{20,4},{24,8},{28,12},{1,17},{... | collective-permute-start | bytes 786440 | tf_op jit(solution)/shard_map/ppermute | solution.py:51
  515.3 51.6 %collective-permute-start.52 = (bf16[4,128,256]{2,1,0:T(8,128)(2,1)}, bf16[4,128,256]{2,1,0:T(8,128)(2,1)S(1)}, u32[]{:S(2)}, u32[]{:S(2)}) collective-permute-start(bf16[4,128,256]{2,1,0:T(8,128)(2,1)} %get-tuple-element.212), channel_id=1, source_target_pairs={{0,24},{4,28},{8,0},{12,4},{16,8},{20,12},{24,16},{28,20},{1,25},{... | collective-permute-start | bytes 786440 | tf_op jit(solution)/shard_map/ppermute | solution.py:51
  515.4 69.4 %collective-permute-start.50 = (bf16[4,128,256]{2,1,0:T(8,128)(2,1)}, bf16[4,128,256]{2,1,0:T(8,128)(2,1)S(1)}, u32[]{:S(2)}, u32[]{:S(2)}) collective-permute-start(bf16[4,128,256]{2,1,0:T(8,128)(2,1)} %get-tuple-element.214), channel_id=1, source_target_pairs={{0,8},{4,12},{8,16},{12,20},{16,24},{20,28},{24,0},{28,4},{1,9},{5... | collective-permute-start | bytes 786440 | tf_op jit(solution)/shard_map/ppermute | solution.py:51
  526.4 36.1 %collective-permute-start.53 = (bf16[4,4,128,256]{3,2,1,0:T(8,128)(2,1)}, bf16[4,4,128,256]{3,2,1,0:T(8,128)(2,1)}, u32[]{:S(2)}, u32[]{:S(2)}) collective-permute-start(bf16[4,4,128,256]{3,2,1,0:T(8,128)(2,1)} %fusion.3), channel_id=1, source_target_pairs={{0,4},{4,0},{8,12},{12,8},{16,20},{20,16},{24,28},{28,24},{1,5},{5... | collective-permute-start | bytes 3145736 | tf_op jit(solution)/shard_map/ppermute | solution.py:46
  531.0 31.5 %collective-permute-start.57 = (bf16[2,4,2,128,256]{4,3,2,1,0:T(8,128)(2,1)}, bf16[2,4,2,128,256]{4,3,2,1,0:T(8,128)(2,1)}, u32[]{:S(2)}, u32[]{:S(2)}) collective-permute-start(bf16[2,4,2,128,256]{4,3,2,1,0:T(8,128)(2,1)} %fusion.6), channel_id=1, source_target_pairs={{0,2},{1,3},{2,0},{3,1},{4,6},{5,7},{6,4},{7,5},{8,10},{9,11},{10,... | collective-permute-start | bytes 3145736 | tf_op jit(solution)/shard_map/ppermute | solution.py:46
  539.8 43.6 %collective-permute-start.59 = (bf16[2,4,2,128,256]{4,3,2,1,0:T(8,128)(2,1)S(1)}, bf16[2,4,2,128,256]{4,3,2,1,0:T(8,128)(2,1)}, u32[]{:S(2)}, u32[]{:S(2)}) collective-permute-start(bf16[2,4,2,128,256]{4,3,2,1,0:T(8,128)(2,1)S(1)} %fusion.7), channel_id=1, source_target_pairs={{0,2},{1,3},{2,0},{3,1},{4,6},{5,7},{6,4},{7,5},{8,10},{9,11},{10,... | collective-permute-start | bytes 3145736 | tf_op jit(solution)/shard_map/ppermute | solution.py:46
  562.5 25.2 %collective-permute-start.51 = (bf16[4,128,256]{2,1,0:T(8,128)(2,1)}, bf16[4,128,256]{2,1,0:T(8,128)(2,1)S(1)}, u32[]{:S(2)}, u32[]{:S(2)}) collective-permute-start(bf16[4,128,256]{2,1,0:T(8,128)(2,1)} %get-tuple-element.213), channel_id=1, source_target_pairs={{0,16},{4,20},{8,24},{12,28},{16,0},{20,4},{24,8},{28,12},{1,17},{... | collective-permute-start | bytes 786440 | tf_op jit(solution)/shard_map/ppermute | solution.py:51
  564.8 28.7 %collective-permute-start.58 = (bf16[4,2,128,256]{3,2,1,0:T(8,128)(2,1)}, bf16[4,2,128,256]{3,2,1,0:T(8,128)(2,1)}, u32[]{:S(2)}, u32[]{:S(2)}) collective-permute-start(bf16[4,2,128,256]{3,2,1,0:T(8,128)(2,1)} %fusion.9), channel_id=1, source_target_pairs={{0,4},{4,0},{8,12},{12,8},{16,20},{20,16},{24,28},{28,24},{1,5},{5... | collective-permute-start | bytes 1572872 | tf_op jit(solution)/shard_map/ppermute | solution.py:46
  569.8 27.4 %collective-permute-start.56 = (bf16[4,128,256]{2,1,0:T(8,128)(2,1)}, bf16[4,128,256]{2,1,0:T(8,128)(2,1)}, u32[]{:S(2)}, u32[]{:S(2)}) collective-permute-start(bf16[4,128,256]{2,1,0:T(8,128)(2,1)} %get-tuple-element.210), channel_id=1, source_target_pairs={{0,24},{4,28},{8,0},{12,4},{16,8},{20,12},{24,16},{28,20},{1,25},{... | collective-permute-start | bytes 786440 | tf_op jit(solution)/shard_map/ppermute | solution.py:51
  583.4 15.7 %collective-permute-start.54 = (bf16[4,128,256]{2,1,0:T(8,128)(2,1)}, bf16[4,128,256]{2,1,0:T(8,128)(2,1)}, u32[]{:S(2)}, u32[]{:S(2)}) collective-permute-start(bf16[4,128,256]{2,1,0:T(8,128)(2,1)} %get-tuple-element.211), channel_id=1, source_target_pairs={{0,8},{4,12},{8,16},{12,20},{16,24},{20,28},{24,0},{28,4},{1,9},{5... | collective-permute-start | bytes 786440 | tf_op jit(solution)/shard_map/ppermute | solution.py:51
  584.8 18.8 %collective-permute-start.55 = (bf16[4,128,256]{2,1,0:T(8,128)(2,1)}, bf16[4,128,256]{2,1,0:T(8,128)(2,1)}, u32[]{:S(2)}, u32[]{:S(2)}) collective-permute-start(bf16[4,128,256]{2,1,0:T(8,128)(2,1)} %get-tuple-element.209), channel_id=1, source_target_pairs={{0,16},{4,20},{8,24},{12,28},{16,0},{20,4},{24,8},{28,12},{1,17},{... | collective-permute-start | bytes 786440 | tf_op jit(solution)/shard_map/ppermute | solution.py:51
  587.7 17.4 %collective-permute-start.63 = (bf16[4,2,128,256]{3,2,1,0:T(8,128)(2,1)S(1)}, bf16[4,2,128,256]{3,2,1,0:T(8,128)(2,1)S(1)}, u32[]{:S(2)}, u32[]{:S(2)}) collective-permute-start(bf16[4,2,128,256]{3,2,1,0:T(8,128)(2,1)S(1)} %fusion.8), channel_id=1, source_target_pairs={{0,4},{4,0},{8,12},{12,8},{16,20},{20,16},{24,28},{28,24},{1,5},{5... | collective-permute-start | bytes 1572872 | tf_op jit(solution)/shard_map/ppermute | solution.py:46
  595.9 9.2 %collective-permute-start.62 = (bf16[2,128,256]{2,1,0:T(8,128)(2,1)S(1)}, bf16[2,128,256]{2,1,0:T(8,128)(2,1)S(1)}, u32[]{:S(2)}, u32[]{:S(2)}) collective-permute-start(bf16[2,128,256]{2,1,0:T(8,128)(2,1)S(1)} %get-tuple-element.221), channel_id=1, source_target_pairs={{0,24},{4,28},{8,0},{12,4},{16,8},{20,12},{24,16},{28,20},{1,25},{... | collective-permute-start | bytes 393224 | tf_op jit(solution)/shard_map/ppermute | solution.py:51
  597.3 15.8 %collective-permute-start.70 = (bf16[4,128,256]{2,1,0:T(8,128)(2,1)}, bf16[4,128,256]{2,1,0:T(8,128)(2,1)}, u32[]{:S(2)}, u32[]{:S(2)}) collective-permute-start(bf16[4,128,256]{2,1,0:T(8,128)(2,1)} %get-tuple-element.187.refs_16_), channel_id=1, source_target_pairs={{0,2},{1,3},{2,0},{3,1},{4,6},{5,7},{6,4},{7,5},{8,10},{9,11},{10,... | collective-permute-start | bytes 786440 | tf_op jit(solution)/shard_map/ppermute | solution.py:46
  599.1 22.6 %collective-permute-start.71 = (bf16[4,128,256]{2,1,0:T(8,128)(2,1)}, bf16[4,128,256]{2,1,0:T(8,128)(2,1)}, u32[]{:S(2)}, u32[]{:S(2)}) collective-permute-start(bf16[4,128,256]{2,1,0:T(8,128)(2,1)} %get-tuple-element.187.refs_16_), channel_id=1, source_target_pairs={{0,1},{1,0},{2,3},{3,2},{4,5},{5,4},{6,7},{7,6},{8,9},{9,8},{10,11... | collective-permute-start | bytes 786440 | tf_op jit(solution)/shard_map/ppermute | solution.py:46
  603.6 9.6 %collective-permute-start.67 = (bf16[4,128,256]{2,1,0:T(8,128)(2,1)S(1)}, bf16[4,128,256]{2,1,0:T(8,128)(2,1)}, u32[]{:S(2)}, u32[]{:S(2)}) collective-permute-start(bf16[4,128,256]{2,1,0:T(8,128)(2,1)S(1)} %get-tuple-element.186.refs_12_), channel_id=1, source_target_pairs={{0,2},{1,3},{2,0},{3,1},{4,6},{5,7},{6,4},{7,5},{8,10},{9,11},{10,... | collective-permute-start | bytes 786440 | tf_op jit(solution)/shard_map/ppermute | solution.py:46
  605.1 18.2 %collective-permute-start.68 = (bf16[4,128,256]{2,1,0:T(8,128)(2,1)S(1)}, bf16[4,128,256]{2,1,0:T(8,128)(2,1)}, u32[]{:S(2)}, u32[]{:S(2)}) collective-permute-start(bf16[4,128,256]{2,1,0:T(8,128)(2,1)S(1)} %get-tuple-element.186.refs_12_), channel_id=1, source_target_pairs={{0,1},{1,0},{2,3},{3,2},{4,5},{5,4},{6,7},{7,6},{8,9},{9,8},{10,11... | collective-permute-start | bytes 786440 | tf_op jit(solution)/shard_map/ppermute | solution.py:46
  613.1 12.8 %collective-permute-start.72 = (bf16[4,128,256]{2,1,0:T(8,128)(2,1)}, bf16[4,128,256]{2,1,0:T(8,128)(2,1)}, u32[]{:S(2)}, u32[]{:S(2)}) collective-permute-start(bf16[4,128,256]{2,1,0:T(8,128)(2,1)} %collective-permute-done.70.refs_17_), channel_id=1, source_target_pairs={{0,1},{1,0},{2,3},{3,2},{4,5},{5,4},{6,7},{7,6},{8,9},{9,8},{10,11... | collective-permute-start | bytes 786440 | tf_op jit(solution)/shard_map/ppermute | solution.py:46
  613.2 12.7 %collective-permute-start.69 = (bf16[4,128,256]{2,1,0:T(8,128)(2,1)}, bf16[4,128,256]{2,1,0:T(8,128)(2,1)}, u32[]{:S(2)}, u32[]{:S(2)}) collective-permute-start(bf16[4,128,256]{2,1,0:T(8,128)(2,1)} %collective-permute-done.67.refs_13_), channel_id=1, source_target_pairs={{0,1},{1,0},{2,3},{3,2},{4,5},{5,4},{6,7},{7,6},{8,9},{9,8},{10,11... | collective-permute-start | bytes 786440 | tf_op jit(solution)/shard_map/ppermute | solution.py:46
  623.2 11.0 %collective-permute-start.65 = (bf16[2,128,256]{2,1,0:T(8,128)(2,1)}, bf16[2,128,256]{2,1,0:T(8,128)(2,1)S(1)}, u32[]{:S(2)}, u32[]{:S(2)}) collective-permute-start(bf16[2,128,256]{2,1,0:T(8,128)(2,1)} %get-tuple-element.219), channel_id=1, source_target_pairs={{0,16},{4,20},{8,24},{12,28},{16,0},{20,4},{24,8},{28,12},{1,17},{... | collective-permute-start | bytes 393224 | tf_op jit(solution)/shard_map/ppermute | solution.py:51
  652.8 9.5 %collective-permute-start.87 = (bf16[4,128,256]{2,1,0:T(8,128)(2,1)S(1)}, bf16[4,128,256]{2,1,0:T(8,128)(2,1)S(1)}, u32[]{:S(2)}, u32[]{:S(2)}) collective-permute-start(bf16[4,128,256]{2,1,0:T(8,128)(2,1)S(1)} %get-tuple-element.189.refs_8_), channel_id=1, source_target_pairs={{0,1},{1,0},{2,3},{3,2},{4,5},{5,4},{6,7},{7,6},{8,9},{9,8},{10,11... | collective-permute-start | bytes 786440 | tf_op jit(solution)/shard_map/ppermute | solution.py:46
  (79 other events, 1058.4 us)
Sparse Core Ops, SparseCore 0:
  14.7 150.1 all-gather.4
  180.8 81.9 all-gather.6

commit v4 on v3

--- a/solution.py
+++ b/solution.py
@@ -407,32 +407,37 @@
     piece_refs, gain_ref, stack = refs[:4], refs[4], refs[5]
     packed_ref, heads_ref, lse_ref, normed_ref, tokens_ref, resid_ref, third_ref = refs[6:13]
     weights, tokens, sems = refs[13:]
-    load_whole(stack, weights, sems)
+    load_whole(stack, weights, sems, (QKV, OUT))
     frames, positions = piece_refs[0].shape[0], piece_refs[0].shape[1]
     for j, piece in enumerate(piece_refs):
         tokens[pl.ds((place[MEMBER] ^ j) * frames, frames)] = piece[...]
     low = tokens[...].reshape(tokens_ref.shape[1:])
     tokens_ref[0] = low
     values = low.astype(F32)
-    await_whole(weights, sems)
+    await_whole(weights, sems, *QKV)
     project_in(values, gain_ref[1:2, :], weights, normed_ref, packed_ref)
     attend(packed_ref, heads_ref, lse_ref, video_mask(low.shape[0], positions))
+    await_whole(weights, sems, *OUT)
     resid = values + dot_nn(heads_ref[0], weights[3])
     resid_ref[0] = resid
     xhat, _ = norm_parts(resid)
     third_ref[0] = (xhat * gain_ref[2:3, :]).astype(BF)
 
 
-def load_whole(stack, weights, sems):
+QKV, OUT = (0, 3), (3, 1)
+
+
+def load_whole(stack, weights, sems, order):
     @pl.when(pl.program_id(0) == 0)
     def _():
-        start_whole(stack, 0, weights, sems.at[0])
-
-
-def await_whole(weights, sems):
+        for first, count in order:
+            start_whole(stack, first, weights.at[pl.ds(first, count)], sems.at[first // 3])
+
+
+def await_whole(weights, sems, first, count):
     @pl.when(pl.program_id(0) == 0)
     def _():
-        wait_all(weights, sems.at[0])
+        wait_all(weights.at[pl.ds(first, count)], sems.at[first // 3])
 
 
 def attend_body(positions, place, packed_ref, heads_ref, lse_ref):
@@ -563,17 +568,18 @@
     piece_refs = refs[3:7]
     weights, heads_grad, total, sems = refs[7:]
     step = pl.program_id(0)
-    load_whole(stack, weights, sems)
+    load_whole(stack, weights, sems, (OUT, QKV))
     back, gain_three = norm_back(resid_ref[0], dx_ref[0], gain_ref[2:3, :])
     add_gain(step, gains_out, 1, gain_three)
     grad_two = cot_ref[0].astype(F32) + back
     branch = grad_two.astype(BF)
     branch_ref[0] = branch
-    await_whole(weights, sems)
+    await_whole(weights, sems, *OUT)
     heads_grad[0] = dot_nt(branch, weights[3]).astype(BF)
     frames, positions = piece_refs[0].shape[0], piece_refs[0].shape[1]
     mask = video_mask(branch.shape[0], positions)
     attend_back(packed_ref, heads_ref, heads_grad, lse_ref, grad_ref, mask)
+    await_whole(weights, sems, *QKV)
     normed_grad = project_back(grad_ref, weights)
     back, gain_two = norm_back(tokens_ref[0].astype(F32), normed_grad, gain_ref[1:2, :])
     add_gain(step, gains_out, 0, gain_two)
@@ -894,7 +900,7 @@
         [piece_spec] * members + [fixed(3, width), ANY],
         [wide, flat_tile, lse_spec] + [flat_tile] * 4,
         [wide_shape, tile_shape, lse_shape, tile_shape, tile_shape, tile32_shape, tile_shape],
-        held(4) + [pltpu.VMEM((FPV, spot, width), BF), sems((1,))],
+        held(4) + [pltpu.VMEM((FPV, spot, width), BF), sems((2,))],
         grid=(tiles,),
         us=37,
     )
@@ -969,7 +975,7 @@
         + [
             pltpu.VMEM((1, positions, width), BF),
             pltpu.VMEM((FPV, spot, width), BF),
-            sems((1,)),
+            sems((2,)),
         ],
         grid=(tiles,),
         us=38,
@@ -1006,53 +1012,57 @@
         )
         return [outs[2 * i : 2 * i + 2] for i in range(len(lots))]
 
-    sum_e, sent_e = step_two(sum_e, "xyz", grad_t)
     sum_f, sent_f = step_one(sum_f, grad_t)
-    (parts_t,) = weight_grads(
-        ("xyz",),
-        [normed_t, before(grad_t, sent_e, sent_f, block_out), heads_t, branch_t],
-        [(0, 0), (0, 1), (0, 2), (1, 0)],
-    )
+    sum_e, sent_e = step_two(sum_e, "xyz", grad_t, sent_f)
     sum_f = send_one(sum_f, sent_f, "xyz")
-    sum_t, sent_t = step_one(send_core(parts_t))
 
     branch_s, heads_grad_s = layer(
         spatial_branch_body,
         lots_out_s,
         out_s,
-        [before(grad_pieces[0], sent_t), *grad_pieces[1:]],
+        [before(grad_pieces[0], sent_e, sent_f, block_out), *grad_pieces[1:]],
         [part_spec] * members,
         [flat_tile] * 2,
         [tile_shape] * 2,
         [],
         7,
     )
-    sum_t = send_one(sum_t, sent_t, "xyz")
-    sum_f, sent_f = step_two(sum_f, "xyz", branch_s)
-    grad_s = attention_back(packed_s, heads_s, before(heads_grad_s, sent_f), lse_s, 0)
-    sum_e = send_two(sum_e, after(sent_e, branch_s), "xyz")
-    sum_f = send_two(sum_f, sent_f, "xyz")
-    sum_e, sent_e = step_three(sum_e, "xyz", grad_s)
+    sum_e = send_two(sum_e, before(sent_e, grad_pieces), "xyz")
+    parts_tq, parts_tv = weight_grads(
+        ("xyz", "yzx"),
+        [normed_t, before(grad_t, branch_s), heads_t, branch_t],
+        [(0, 0), (0, 1)],
+        [(0, 2), (1, 0)],
+    )
+    sum_tq, sum_tv = send_core(parts_tq), send_core(parts_tv)
+    sum_e, sent_e = step_three(sum_e, "xyz", parts_tq[0])
+    sum_f, sent_f = step_two(sum_f, "xyz", parts_tq[0])
+    grad_s = attention_back(packed_s, heads_s, before(heads_grad_s, sent_e, sent_f), lse_s, 0)
+    sum_e, sum_f = send_three(sum_e, sent_e, "xyz"), send_two(sum_f, sent_f, "xyz")
+    sum_tq, sent_tq = step_one(sum_tq, grad_s)
+    sum_tv, sent_tv = step_one(sum_tv, grad_s)
+    sum_f, sent_f = step_three(sum_f, "xyz", grad_s)
     (parts_qk,) = weight_grads(
-        ("xyz",), [normed_s, before(grad_s, sent_e)], [(0, 0), (0, 1)]
-    )
-    sum_e = send_three(sum_e, sent_e, "xyz")
+        ("xyz",), [normed_s, before(grad_s, sent_tq, sent_tv, sent_f)], [(0, 0), (0, 1)]
+    )
+    sum_tq, sum_tv = send_one(sum_tq, sent_tq, "xyz"), send_one(sum_tv, sent_tv, "yzx")
+    sum_f = send_three(sum_f, sent_f, "xyz")
+    quarters["ffn0"] = finish(sum_e, parts_qk[0])
     sum_qk = send_core(parts_qk)
-    sum_f, sent_f = step_three(sum_f, "xyz", parts_qk[0])
-    sum_t, sent_t = step_two(sum_t, "xyz", parts_qk[0])
     (parts_vo,) = weight_grads(
-        ("xyz",), [normed_s, before(grad_s, sent_f, sent_t), heads_s, branch_s], [(0, 2), (1, 0)]
-    )
-    sum_f, sum_t = send_three(sum_f, sent_f, "xyz"), send_two(sum_t, sent_t, "xyz")
-    quarters["ffn0"] = finish(sum_e, parts_vo[0])
+        ("xyz",),
+        [normed_s, before(grad_s, parts_qk, quarters["ffn0"]), heads_s, branch_s],
+        [(0, 2), (1, 0)],
+    )
     sum_vo = send_core(parts_vo)
     sum_qk, sent_qk = step_one(sum_qk, parts_vo[0])
-    sum_vo, sent_vo = step_one(sum_vo, sent_qk)
+    sum_tq, sent_tq = step_two(sum_tq, "xyz", parts_vo[0])
+    sum_tv, sent_tv = step_two(sum_tv, "yzx", parts_vo[0])
     input_grad, gain_one, columns = layer(
         spatial_end_body,
         lots_in_s,
         in_s,
-        [grad_s, frames_in, code_shift, before(branch_s, sent_qk, sent_vo, quarters["ffn0"]), gains],
+        [grad_s, frames_in, code_shift, before(branch_s, sent_qk, sent_tq, sent_tv), gains],
         [wide, flat_tile, tile(1, width), flat_tile, fixed(3, width)],
         [flat_tile, fixed(1, width), tile(1, width)],
         [tile_shape, gain_shape, shape_of(frames, 1, width, dtype=F32)],
@@ -1060,30 +1070,33 @@
         14,
     )
     sum_qk = send_one(sum_qk, sent_qk, "xyz")
-    sum_qk, sent_qk = step_two(sum_qk, "xyz", columns)
+    sum_tq, sum_tv = send_two(sum_tq, sent_tq, "xyz"), send_two(sum_tv, sent_tv, "yzx")
+    sum_vo, sent_vo = step_one(sum_vo, columns)
+    sum_vo = send_one(sum_vo, sent_vo, "xyz")
+    sum_qk, sent_qk = step_two(sum_qk, "xyz", columns, sent_vo)
     sum_qk = send_two(sum_qk, sent_qk, "xyz")
-    quarters["ffn1"] = finish(sum_f, columns)
-    sum_t, sent_t = step_three(sum_t, "xyz", columns)
-    sum_t = send_three(sum_t, sent_t, "xyz")
-    sum_vo = send_one(sum_vo, sent_vo, "xyz")
-    sum_vo, sent_vo = step_two(sum_vo, "xyz", sent_qk, sent_t)
+    sum_tq, sent_tq = step_three(sum_tq, "xyz", columns, sent_qk)
+    sum_tv, sent_tv = step_three(sum_tv, "yzx", columns, sent_qk)
+    sum_tq, sum_tv = send_three(sum_tq, sent_tq, "xyz"), send_three(sum_tv, sent_tv, "yzx")
+    quarters["ffn1"] = finish(sum_f, columns, sent_tq)
+    sum_qk, sent_qk = step_three(sum_qk, "xyz", sent_tq, sent_tv)
+    sum_qk = send_three(sum_qk, sent_qk, "xyz")
+    ffn_quarter = before(jnp.concatenate([quarters["ffn0"], quarters["ffn1"]]), sent_qk)
+    ffn_shared = share_quarters(ffn_quarter)
+    sum_vo, sent_vo = step_two(sum_vo, "xyz", sent_qk)
     sum_vo = send_two(sum_vo, sent_vo, "xyz")
-    sum_qk, sent_qk = step_three(sum_qk, "xyz", sent_vo)
-    sum_qk = send_three(sum_qk, sent_qk, "xyz")
-    shared = {
-        name: share_quarters(before(quarters[name], sent_qk)) for name in ("ffn0", "ffn1")
-    }
-    quarters["t"] = finish(sum_t, sent_qk)
-    sum_vo, sent_vo = step_three(sum_vo, "xyz", quarters["t"])
+    quarters["tq"], quarters["tv"] = finish(sum_tq, sent_vo), finish(sum_tv, sent_vo)
+    sum_vo, sent_vo = step_three(sum_vo, "xyz", quarters["tq"], quarters["tv"])
     sum_vo = send_three(sum_vo, sent_vo, "xyz")
     quarters["qk"] = finish(sum_qk, sent_vo)
-    shared["t"] = share_quarters(before(quarters["t"], sent_vo))
-    quarters["vo"] = finish(sum_vo, shared["ffn0"], shared["ffn1"])
+    quarters["vo"] = finish(sum_vo, ffn_shared)
+    attn_quarter = jnp.concatenate([quarters[name] for name in ("qk", "vo", "tq", "tv")])
+    attn_shared = share_quarters(attn_quarter)
 
     table_grad = jnp.dot(
         onehot.astype(F32).T, columns[:, 0, :], precision=lax.Precision.HIGHEST
     )
-    squares = sum(jnp.sum(jnp.square(q.astype(F32))) for q in quarters.values())
+    squares = sum(jnp.sum(jnp.square(q.astype(F32))) for q in (attn_quarter, ffn_quarter))
     sums = all_sum(
         jnp.concatenate(
             [gain_one, gains_two, table_grad, jnp.broadcast_to(squares, (1, width))], axis=0
@@ -1094,15 +1107,9 @@
     total_squares = sums[-1, 0] + jnp.sum(small_grad * small_grad)
     grad_norm = jnp.sqrt(total_squares)
     clip_factor = 1.0 / jnp.maximum(grad_norm, 1.0)
-    for name in ("qk", "vo"):
-        shared[name] = share_quarters(quarters[name])
-
     lots = [
-        ("qk", [(0, 0, 0), (0, 0, 1)]),
-        ("vo", [(0, 0, 2), (0, 0, 3)]),
-        ("t", [(0, 1, b) for b in range(4)]),
-        ("ffn0", [(1, *pick) for pick in ffn_picks[:4]]),
-        ("ffn1", [(1, *pick) for pick in ffn_picks[4:]]),
+        (attn_shared, [(0, m, b) for m in range(2) for b in range(4)]),
+        (ffn_shared, [(1, *pick) for pick in ffn_picks]),
     ]
 
     def piece_spec_of(lot):
@@ -1126,7 +1133,7 @@
     updated = call(
         functools.partial(update_body, [lot for _, lot in lots]),
         (place, clip_factor.reshape(1)),
-        [p for name, _ in lots for p in shared[name]]
+        [piece for pieces, _ in lots for piece in pieces]
         + [attn_master, attn_first, attn_second, ffn_master, ffn_first, ffn_second],
         [piece_spec_of(lot) for _, lot in lots for _ in range(4)] + blocks_six,
         blocks_six,

time: 708 us -> 668 us (0.944)
  waiting for transfers between devices: 173 us -> 144 us
    ppermute x24 -> x27, waiting for transfers between devices: 73.2 us -> 53.5 us  [shift_z(): lax.ppermute(value, 'seq', [(i, (i + 2 * step) % size) for i in range(siz...]
    ppermute x24 -> x27, starting transfers between devices: 38.4 us -> 52.4 us  [shift_z(): lax.ppermute(value, 'seq', [(i, (i + 2 * step) % size) for i in range(siz...]
    ppermute x65 -> x59, starting transfers between devices: 62.8 us -> 50.4 us  [swap(): return lax.ppermute(value, axis, [(i, i ^ bit) for i in range(size)])]
    reduce_sum x5 -> x2, other arithmetic: 10.9 us -> 1.74 us  [shards(): jnp.sum(jnp.square(q.astype(F32)))]
    ppermute x65 -> x59, waiting for transfers between devices: 99.7 us -> 90.7 us  [swap(): return lax.ppermute(value, axis, [(i, i ^ bit) for i in range(size)])]
    convert_element_type x15 -> x24, other arithmetic: 41.7 us -> 45 us  [add_low(): return sum((term.astype(F32) for term in terms)).astype(BF)]
  transfers between devices with their start and end apart: 91 -> 88, of which waited for: 37 -> 34; matrix products, arithmetic and copies ran while one was open for 8% -> 8% of each run, Pallas kernels for 41% -> 45%
where the time goes in v4:
time: 668 us; the launch traced here: 657 us
  Pallas kernels  325 us (49%)
  waiting for transfers between devices  144 us (22%)
  starting transfers between devices  103 us (15%)
  other arithmetic  54.5 us (8%)
  between operations  19 us (3%)
  local copies, waits for them, and re-layouts  11.5 us (2%)
    pallas_call x16, Pallas kernels, call(): pl.pallas_call(body, out_shape=out_shape, grid_spec=pltpu.PrefetchScalarG...  325 us
    ppermute x59, waiting for transfers between devices, swap(): return lax.ppermute(value, axis, [(i, i ^ bit) for i in range(size)])  90.7 us
    ppermute x27, waiting for transfers between devices, shift_z(): lax.ppermute(value, 'seq', [(i, (i + 2 * step) % size) for i in range(siz...  53.5 us
    ppermute x27, starting transfers between devices, shift_z(): lax.ppermute(value, 'seq', [(i, (i + 2 * step) % size) for i in range(siz...  52.4 us
    ppermute x59, starting transfers between devices, swap(): return lax.ppermute(value, axis, [(i, i ^ bit) for i in range(size)])  50.4 us
    convert_element_type x24, other arithmetic, add_low(): return sum((term.astype(F32) for term in terms)).astype(BF)  45 us
  transfers between devices with their start and end apart: 88, of which 34 were waited for; matrix products, arithmetic and copies ran while one was open for 8% of the time, Pallas kernels for 45%

profile of v4, /device:TPU:0, one launch (start us, length us, event | category | flops | bytes accessed | tf_op | source)
XLA Modules:
  0.0 657.2 jit_solution(10066876638194928150)
XLA Ops:
  7.2 2.5 convert.83
  14.6 3.1 collective-permute-start
  17.7 2.6 collective-permute-start.1
  24.2 4.8 collective-permute-done.1
  30.6 7.5 %collective-permute-start.10 = (bf16[2,11,128]{2,1,0:T(8,128)(2,1)S(1)}, bf16[2,11,128]{2,1,0:T(8,128)(2,1)S(1)}, u32[]{:S(2)}, u32[]{:S(2)}) collective-permute-start(bf16[2,11,128]{2,1,0:T(8,128)(2,1)S(1)} %pad_maximum_fusion.8), channel_id=1, source_target_pairs={{0,8},{4,12},{8,0},{12,4},{16,24},{20,28},{24,16},{28,20},{1,9},{5... | collective-permute-start | bytes 16904 | tf_op jit(solution)/shard_map/ppermute | solution.py:46
  38.2 3.2 collective-permute-start.4
  41.4 2.9 collective-permute-start.5
  44.4 2.6 collective-permute-done.3
  46.9 4.8 collective-permute-done.4
  51.8 3.5 collective-permute-start.6
  58.9 3.0 collective-permute-done.6
  61.9 4.1 collective-permute-start.7
  67.3 10.3 %collective-permute-done.7 = bf16[1,128,512]{2,1,0:T(8,128)(2,1)S(1)} collective-permute-done((bf16[1,128,512]{2,1,0:T(8,128)(2,1)S(1)}, bf16[1,128,512]{2,1,0:T(8,128)(2,1)S(1)}, u32[]{:S(2)}, u32[]{:S(2)}) %collective-permute-start.7) | collective-permute-done | bytes 131104 | tf_op jit(solution)/shard_map/ppermute | solution.py:51
  77.5 2.3 collective-permute-start.8
  79.9 4.4 collective-permute-done.8
  85.4 8.3 %collective-permute-done.14.refs_3_ = bf16[4,2,128,256]{3,2,1,0:T(8,128)(2,1)} collective-permute-done((bf16[4,2,128,256]{3,2,1,0:T(8,128)(2,1)}, bf16[4,2,128,256]{3,2,1,0:T(8,128)(2,1)}, u32[]{:S(2)}, u32[]{:S(2)}) %collective-permute-start.14) | collective-permute-done | bytes 524320 | tf_op jit(solution)/shard_map/ppermute | solution.py:46
  97.6 14.5 %shard_map.211 = (bf16[4,256,3072]{2,1,0:T(8,128)(2,1)}, bf16[4,256,1024]{2,1,0:T(8,128)(2,1)}) custom-call(s32[5]{0:T(128)} %stack.86.place, bf16[4,256,1024]{2,1,0:T(8,128)(2,1)} %frames_ref.4, f32[4,1,1024]{2,1,0:T(1,128)} %broadcast_in_dim.33.shift_ref, f32[3,1024]{1,0:T(4,128)} %fusion.63.gain_ref.refs_4_, bf16[4,2,128,256]{3,2,1,0:T(8,128)(2,1)} %copy-done.11, ...), custom_call_target="tpu_custom_call" | custom-call | flops 12000000000 | bytes 1048576 | tf_op jit(solution)/shard_map/pallas_call | solution.py:715
  112.1 22.3 %shard_map.212 = (bf16[4,256,1024]{2,1,0:T(8,128)(2,1)}, f32[4,16,256]{2,1,0:T(8,128)}) custom-call(s32[5]{0:T(128)} %stack.86.place, bf16[4,256,3072]{2,1,0:T(8,128)(2,1)} %get-tuple-element.112.packed_ref), custom_call_target="tpu_custom_call" | custom-call | flops 22000001024 | bytes 1048576 | tf_op jit(solution)/shard_map/pallas_call | solution.py:715
  137.2 8.3 %shard_map.213 = (bf16[4,64,1024]{2,1,0:T(8,128)(2,1)}, bf16[4,64,1024]{2,1,0:T(8,128)(2,1)}, bf16[4,64,1024]{2,1,0:T(8,128)(2,1)}, bf16[4,64,1024]{2,1,0:T(8,128)(2,1)}) custom-call(s32[5]{0:T(128)} %stack.86.place, bf16[4,256,1024]{2,1,0:T(8,128)(2,1)} %get-tuple-element.113.heads_ref, bf16[4,256,1024]{2,1,0:T(8,128)(2,1)} %frames_ref.4, ...), custom_call_target="tpu_custom_call" | custom-call | flops 6000000000 | bytes 1048576 | tf_op jit(solution)/shard_map/pallas_call | solution.py:715
  149.9 10.1 %collective-permute-done.25.refs_1_ = bf16[4,64,1024]{2,1,0:T(8,128)(2,1)} collective-permute-done((bf16[4,64,1024]{2,1,0:T(8,128)(2,1)}, bf16[4,64,1024]{2,1,0:T(8,128)(2,1)}, u32[]{:S(2)}, u32[]{:S(2)}) %collective-permute-start.25) | collective-permute-done | bytes 524320 | tf_op jit(solution)/shard_map/ppermute | solution.py:46
  159.9 8.7 %collective-permute-done.26.refs_2_ = bf16[4,64,1024]{2,1,0:T(8,128)(2,1)} collective-permute-done((bf16[4,64,1024]{2,1,0:T(8,128)(2,1)}, bf16[4,64,1024]{2,1,0:T(8,128)(2,1)}, u32[]{:S(2)}, u32[]{:S(2)}) %collective-permute-start.26) | collective-permute-done | bytes 524320 | tf_op jit(solution)/shard_map/ppermute | solution.py:46
  168.6 12.1 %collective-permute-done.27.refs_3_ = bf16[4,64,1024]{2,1,0:T(8,128)(2,1)} collective-permute-done((bf16[4,64,1024]{2,1,0:T(8,128)(2,1)}, bf16[4,64,1024]{2,1,0:T(8,128)(2,1)}, u32[]{:S(2)}, u32[]{:S(2)}) %collective-permute-start.27) | collective-permute-done | bytes 524320 | tf_op jit(solution)/shard_map/ppermute | solution.py:46
  185.5 36.7 %shard_map.214 = (bf16[4,256,3072]{2,1,0:T(8,128)(2,1)}, bf16[4,256,1024]{2,1,0:T(8,128)(2,1)}, f32[4,16,256]{2,1,0:T(8,128)}, bf16[4,256,1024]{2,1,0:T(8,128)(2...) custom-call(s32[5]{0:T(128)} %stack.86.place, ...), custom_call_target="tpu_custom_call" | custom-call | flops 36999999488 | bytes 1048576 | tf_op jit(solution)/shard_map/pallas_call | solution.py:715
  224.0 4.6 shard_map.215.cot_ref
  228.5 45.7 %shard_map.216 = (bf16[2,2,4,4,128,256]{5,4,3,2,1,0:T(8,128)(2,1)}, bf16[2,2,4,4,128,256]{5,4,3,2,1,0:T(8,128)(2,1)}, f32[1024,1024]{1,0:T(8,128)}, f32[1024,1024]{1,0:T(8,128)}) custom-call(s32[5]{0:T(128)} %stack.86.place, bf16[1024,1024]{1,0:T(8,128)(2,1)} %bitcast.330, bf16[1024,1024]{1,0:T(8,128)(2,1)} %bitcast.328, f32[1024,1024]{1,0:T(8,128)} %bitcast.319, ...), custom_call_target="tpu_custom_call" | custom-call | flops 41000001536 | bytes 1048576 | tf_op jit(solution)/shard_map/pallas_call | solution.py:715
  274.3 38.2 %shard_map.217 = (bf16[2,2,4,4,128,256]{5,4,3,2,1,0:T(8,128)(2,1)}, bf16[2,2,4,4,128,256]{5,4,3,2,1,0:T(8,128)(2,1)}, f32[1024,1024]{1,0:T(8,128)}, bf16[4,64,10...) custom-call(s32[5]{0:T(128)} %stack.86.place, ...), custom_call_target="tpu_custom_call" | custom-call | flops 41000001536 | bytes 1048576 | tf_op jit(solution)/shard_map/pallas_call | solution.py:715
  316.5 4.4 fusion
  322.0 41.0 %shard_map.218 = (bf16[4,256,1024]{2,1,0:T(8,128)(2,1)}, bf16[4,256,3072]{2,1,0:T(8,128)(2,1)}, f32[2,1024]{1,0:T(2,128)}, bf16[4,64,1024]{2,1,0:T(8,128)(2,1)},...) custom-call(s32[5]{0:T(128)} %stack.86.place, ...), custom_call_target="tpu_custom_call" | custom-call | flops 38000001024 | bytes 1048576 | tf_op jit(solution)/shard_map/pallas_call | solution.py:715
  363.4 3.1 fusion.1
  366.9 2.9 collective-permute-start.39
  370.7 4.5 shard_map.219
  375.2 2.3 fusion.3
  377.6 4.2 collective-permute-done.38.refs_2_
  381.7 10.0 %collective-permute-done.39.refs_3_ = bf16[4,64,1024]{2,1,0:T(8,128)(2,1)} collective-permute-done((bf16[4,64,1024]{2,1,0:T(8,128)(2,1)S(1)}, bf16[4,64,1024]{2,1,0:T(8,128)(2,1)}, u32[]{:S(2)}, u32[]{:S(2)}) %collective-permute-start.39) | collective-permute-done | bytes 524320 | tf_op jit(solution)/shard_map/ppermute | solution.py:46
  391.8 7.9 %shard_map.220 = (bf16[4,256,1024]{2,1,0:T(8,128)(2,1)}, bf16[4,256,1024]{2,1,0:T(8,128)(2,1)}) custom-call(s32[5]{0:T(128)} %stack.86.place, bf16[4,64,1024]{2,1,0:T(8,128)(2,1)} %get-tuple-element.150.refs_0_, bf16[4,64,1024]{2,1,0:T(8,128)(2,1)} %collective-permute-done.37.refs_1_, bf16[4,64,1024]{2,1,0:T(8,128)(2,1)} %collective-permute-done.38.refs_2_, ...), custom_call_target="tpu_custom_call" | custom-call | flops 7000000000 | bytes 1048576 | tf_op jit(solution)/shard_map/pallas_call | solution.py:715
  400.1 15.1 %shard_map.221 = (bf16[2,2,4,2,128,256]{5,4,3,2,1,0:T(8,128)(2,1)}, bf16[2,2,4,2,128,256]{5,4,3,2,1,0:T(8,128)(2,1)}, bf16[2,4,2,2,128,256]{5,4,3,2,1,0:T(8,128)(2,1)}, bf16[2,4,2,2,128,256]{5,4,3,2,1,0:T(8,128)(2,1)}) custom-call(s32[5]{0:T(128)} %stack.86.place, bf16[1024,1024]{1,0:T(8,128)(2,1)} %bitcast.326, bf16[1024,3072]{1,0:T(8,128)(2,1)} %bitcast.318, ...), custom_call_target="tpu_custom_call" | custom-call | flops 15000000512 | bytes 1048576 | tf_op jit(solution)/shard_map/pallas_call | solution.py:715
  415.6 2.3 fusion.2
  419.8 6.2 collective-permute-done.40
  426.0 3.0 fusion.25
  431.0 23.3 %shard_map.222.grad_ref = bf16[4,256,3072]{2,1,0:T(8,128)(2,1)} custom-call(s32[5]{0:T(128)} %stack.86.place, bf16[4,256,3072]{2,1,0:T(8,128)(2,1)} %get-tuple-element.112.packed_ref, bf16[4,256,1024]{2,1,0:T(8,128)(2,1)} %get-tuple-element.113.heads_ref, bf16[4,256,1024]{2,1,0:T(8,128)(2,1)} %get-tuple-element.163.heads_grad_ref, ...), custom_call_target="tpu_custom_call" | custom-call | flops 25999998976 | bytes 1048576 | tf_op jit(solution)/shard_map/pallas_call | solution.py:715
  455.7 2.8 fusion.22
  458.5 2.8 collective-permute-start.72
  462.9 2.5 fusion.5
  465.4 9.9 %shard_map.223 = (bf16[2,2,4,2,128,256]{5,4,3,2,1,0:T(8,128)(2,1)}, bf16[2,2,4,2,128,256]{5,4,3,2,1,0:T(8,128)(2,1)}) custom-call(s32[5]{0:T(128)} %stack.86.place, bf16[1024,1024]{1,0:T(8,128)(2,1)} %bitcast.321, bf16[1024,3072]{1,0:T(8,128)(2,1)} %bitcast.316), custom_call_target="tpu_custom_call" | custom-call | flops 15000000512 | bytes 1048576 | tf_op jit(solution)/shard_map/pallas_call | solution.py:715
  478.4 10.7 %shard_map.224 = (bf16[2,2,4,2,128,256]{5,4,3,2,1,0:T(8,128)(2,1)}, bf16[2,2,4,2,128,256]{5,4,3,2,1,0:T(8,128)(2,1)}) custom-call(s32[5]{0:T(128)} %stack.86.place, bf16[1024,1024]{1,0:T(8,128)(2,1)} %bitcast.322, bf16[1024,3072]{1,0:T(8,128)(2,1)} %bitcast.317, bf16[1024,1024]{1,0:T(8,128)(2,1)} %bitcast.323, bf16[1024,1024]{1,0:T(8,128)(2,1)} %bitcast.324), custom_call_target="tpu_custom_call" | custom-call | flops 15000000512 | bytes 1048576 | tf_op jit(solution)/shard_map/pallas_call | solution.py:715
  489.1 4.6 collective-permute-done.50
  494.6 2.6 fusion.15
  500.8 16.1 %shard_map.225 = (bf16[4,256,1024]{2,1,0:T(8,128)(2,1)}, f32[1,1024]{1,0:T(1,128)}, f32[4,1,1024]{2,1,0:T(1,128)}) custom-call(s32[5]{0:T(128)} %stack.86.place, bf16[4,256,3072]{2,1,0:T(8,128)(2,1)} %shard_map.222.grad_ref, bf16[4,256,1024]{2,1,0:T(8,128)(2,1)} %frames_ref.4, f32[4,1,1024]{2,1,0:T(1,128)} %broadcast_in_dim.33.shift_ref, ...), custom_call_target="tpu_custom_call" | custom-call | flops 14000000000 | bytes 1048576 | tf_op jit(solution)/shard_map/pallas_call | solution.py:715
  520.0 5.9 collective-permute-done.51
  525.9 3.0 collective-permute-start.57
  534.1 3.3 collective-permute-start.55
  542.4 2.9 collective-permute-done.55
  545.3 5.3 collective-permute-start.63
  550.6 6.6 %collective-permute-done.56 = bf16[2,2,128,256]{3,2,1,0:T(8,128)(2,1)S(1)} collective-permute-done((bf16[2,2,128,256]{3,2,1,0:T(8,128)(2,1)S(1)}, bf16[2,2,128,256]{3,2,1,0:T(8,128)(2,1)S(1)}, u32[]{:S(2)}, u32[]{:S(2)}) %collective-permute-start.56) | collective-permute-done | bytes 262176 | tf_op jit(solution)/shard_map/ppermute | solution.py:51
  564.8 3.5 collective-permute-start.60
  571.1 3.8 collective-permute-done.73.refs_5_
  576.4 2.6 collective-permute-start.59
  582.5 4.2 collective-permute-done.59
  587.8 2.8 collective-permute-done.69
  590.5 6.2 collective-permute-done.68
  602.4 2.7 collective-permute-done.77
  606.5 2.8 collective-permute-start.81
  613.2 4.1 collective-permute-done.83.refs_1_
  623.2 25.8 %shard_map.226 = (f32[2,128,4096]{2,1,0:T(8,128)}, f32[2,128,4096]{2,1,0:T(8,128)}, f32[2,128,4096]{2,1,0:T(8,128)}, f32[2,128,4096]{2,1,0:T(8,128)}, f32[2,128,4096]{2,1,0:T(8,128)}, /*index=5*/f32[2,128,4096]{2,1,0:T(8,128)}) custom-call(s32[5]{0:T(128)} %stack.86.place, f32[1]{0:T(128)} %bitcast.131.clip, bf16[8,128,256]{2,1,0:T(8,128)(2,1)} %copy-done.14, ...), custom_call_target="tpu_custom_call" | custom-call | flops 10000000000 | bytes 1048576 | tf_op jit(solution)/shard_map/pallas_call | solution.py:715
  (281 shorter events, 99.7 us)
Async XLA Ops:
  7.2 178.3 %all-gather.5.cloned.1.call-start = ((), (), s32[]{:S(2)}) async-start(), calls=%async_computation | async-start | bytes 17301504 | tf_op jit(solution)/shard_map/all_gather | solution.py:804
  14.5 259.8 %all-gather.7.cloned.1.call-start = ((), (), s32[]{:S(2)}) async-start(), calls=%async_computation.1 | async-start | bytes 8650752 | tf_op jit(solution)/shard_map/all_gather | solution.py:894
  17.7 11.2 %collective-permute-start.1 = (bf16[2,128,256]{2,1,0:T(8,128)(2,1)S(1)}, bf16[2,128,256]{2,1,0:T(8,128)(2,1)S(1)}, u32[]{:S(2)}, u32[]{:S(2)}) collective-permute-start(bf16[2,128,256]{2,1,0:T(8,128)(2,1)S(1)} %fusion.57), channel_id=1, source_target_pairs={{0,16},{4,20},{8,24},{12,28},{16,0},{20,4},{24,8},{28,12},{1,17},{... | collective-permute-start | bytes 393224 | tf_op jit(solution)/shard_map/ppermute | solution.py:51
  29.0 29.3 %collective-permute-start.12 = (bf16[4,2,128,256]{3,2,1,0:T(8,128)(2,1)S(1)}, bf16[4,2,128,256]{3,2,1,0:T(8,128)(2,1)}, u32[]{:S(2)}, u32[]{:S(2)}) collective-permute-start(bf16[4,2,128,256]{3,2,1,0:T(8,128)(2,1)S(1)} %pad_maximum_fusion.refs_0_), channel_id=1, source_target_pairs={{0,4},{4,0},{8,12},{12,8},{16,20},{20,16},{24,28},{28,24},{1,5},{5... | collective-permute-start | bytes 1572872 | tf_op jit(solution)/shard_map/ppermute | solution.py:46
  30.6 13.6 %collective-permute-start.10 = (bf16[2,11,128]{2,1,0:T(8,128)(2,1)S(1)}, bf16[2,11,128]{2,1,0:T(8,128)(2,1)S(1)}, u32[]{:S(2)}, u32[]{:S(2)}) collective-permute-start(bf16[2,11,128]{2,1,0:T(8,128)(2,1)S(1)} %pad_maximum_fusion.8), channel_id=1, source_target_pairs={{0,8},{4,12},{8,0},{12,4},{16,24},{20,28},{24,16},{28,20},{1,9},{5... | collective-permute-start | bytes 16904 | tf_op jit(solution)/shard_map/ppermute | solution.py:46
  38.2 13.6 %collective-permute-start.4 = (bf16[1,128,512]{2,1,0:T(8,128)(2,1)S(1)}, bf16[1,128,512]{2,1,0:T(8,128)(2,1)S(1)}, u32[]{:S(2)}, u32[]{:S(2)}) collective-permute-start(bf16[1,128,512]{2,1,0:T(8,128)(2,1)S(1)} %constant_dynamic-slice_fusion.4), channel_id=1, source_target_pairs={{0,16},{4,20},{8,24},{12,28},{16,0},{20,4},{24,8},{28,12},{1,17},{... | collective-permute-start | bytes 393224 | tf_op jit(solution)/shard_map/ppermute | solution.py:51
  44.3 12.5 %collective-permute-start.11 = (bf16[4,11,128]{2,1,0:T(8,128)(2,1)S(1)}, bf16[4,11,128]{2,1,0:T(8,128)(2,1)S(1)}, u32[]{:S(2)}, u32[]{:S(2)}) collective-permute-start(bf16[4,11,128]{2,1,0:T(8,128)(2,1)S(1)} %pad_maximum_fusion.7), channel_id=1, source_target_pairs={{0,16},{4,20},{8,24},{12,28},{16,0},{20,4},{24,8},{28,12},{1,17},{... | collective-permute-start | bytes 33800 | tf_op jit(solution)/shard_map/ppermute | solution.py:46
  55.3 29.0 %collective-permute-start.13 = (bf16[4,2,128,256]{3,2,1,0:T(8,128)(2,1)S(1)}, bf16[4,2,128,256]{3,2,1,0:T(8,128)(2,1)}, u32[]{:S(2)}, u32[]{:S(2)}) collective-permute-start(bf16[4,2,128,256]{3,2,1,0:T(8,128)(2,1)S(1)} %pad_maximum_fusion.refs_0_), channel_id=1, source_target_pairs={{0,2},{1,3},{2,0},{3,1},{4,6},{5,7},{6,4},{7,5},{8,10},{9,11},{10,... | collective-permute-start | bytes 1572872 | tf_op jit(solution)/shard_map/ppermute | solution.py:46
  56.8 28.0 %collective-permute-start.15 = (bf16[4,2,128,256]{3,2,1,0:T(8,128)(2,1)S(1)}, bf16[4,2,128,256]{3,2,1,0:T(8,128)(2,1)}, u32[]{:S(2)}, u32[]{:S(2)}) collective-permute-start(bf16[4,2,128,256]{3,2,1,0:T(8,128)(2,1)S(1)} %pad_maximum_fusion.refs_0_), channel_id=1, source_target_pairs={{0,1},{1,0},{2,3},{3,2},{4,5},{5,4},{6,7},{7,6},{8,9},{9,8},{10,11... | collective-permute-start | bytes 1572872 | tf_op jit(solution)/shard_map/ppermute | solution.py:46
  56.8 28.1 %collective-permute-start.19 = (bf16[4,1,128,512]{3,2,1,0:T(8,128)(2,1)S(1)}, bf16[4,1,128,512]{3,2,1,0:T(8,128)(2,1)}, u32[]{:S(2)}, u32[]{:S(2)}) collective-permute-start(bf16[4,1,128,512]{3,2,1,0:T(8,128)(2,1)S(1)} %pad_maximum_fusion.1.refs_8_), channel_id=1, source_target_pairs={{0,4},{4,0},{8,12},{12,8},{16,20},{20,16},{24,28},{28,24},{1,5},{5... | collective-permute-start | bytes 1572872 | tf_op jit(solution)/shard_map/ppermute | solution.py:46
  58.3 35.4 %collective-permute-start.14 = (bf16[4,2,128,256]{3,2,1,0:T(8,128)(2,1)}, bf16[4,2,128,256]{3,2,1,0:T(8,128)(2,1)}, u32[]{:S(2)}, u32[]{:S(2)}) collective-permute-start(bf16[4,2,128,256]{3,2,1,0:T(8,128)(2,1)} %collective-permute-done.12.refs_1_), channel_id=1, source_target_pairs={{0,2},{1,3},{2,0},{3,1},{4,6},{5,7},{6,4},{7,5},{8,10},{9,11},{10,... | collective-permute-start | bytes 1572872 | tf_op jit(solution)/shard_map/ppermute | solution.py:46
  61.9 15.6 %collective-permute-start.7 = (bf16[1,128,512]{2,1,0:T(8,128)(2,1)S(1)}, bf16[1,128,512]{2,1,0:T(8,128)(2,1)S(1)}, u32[]{:S(2)}, u32[]{:S(2)}) collective-permute-start(bf16[1,128,512]{2,1,0:T(8,128)(2,1)S(1)} %constant_dynamic-slice_fusion.5), channel_id=1, source_target_pairs={{0,16},{4,20},{8,24},{12,28},{16,0},{20,4},{24,8},{28,12},{1,17},{... | collective-permute-start | bytes 393224 | tf_op jit(solution)/shard_map/ppermute | solution.py:51
  84.3 13.2 %collective-permute-start.16 = (bf16[4,2,128,256]{3,2,1,0:T(8,128)(2,1)}, bf16[4,2,128,256]{3,2,1,0:T(8,128)(2,1)}, u32[]{:S(2)}, u32[]{:S(2)}) collective-permute-start(bf16[4,2,128,256]{3,2,1,0:T(8,128)(2,1)} %collective-permute-done.12.refs_1_), channel_id=1, source_target_pairs={{0,1},{1,0},{2,3},{3,2},{4,5},{5,4},{6,7},{7,6},{8,9},{9,8},{10,11... | collective-permute-start | bytes 1572872 | tf_op jit(solution)/shard_map/ppermute | solution.py:46
  84.8 12.7 %collective-permute-start.17 = (bf16[4,2,128,256]{3,2,1,0:T(8,128)(2,1)}, bf16[4,2,128,256]{3,2,1,0:T(8,128)(2,1)}, u32[]{:S(2)}, u32[]{:S(2)}) collective-permute-start(bf16[4,2,128,256]{3,2,1,0:T(8,128)(2,1)} %collective-permute-done.13.refs_2_), channel_id=1, source_target_pairs={{0,1},{1,0},{2,3},{3,2},{4,5},{5,4},{6,7},{7,6},{8,9},{9,8},{10,11... | collective-permute-start | bytes 1572872 | tf_op jit(solution)/shard_map/ppermute | solution.py:46
  84.9 12.6 %collective-permute-start.21 = (bf16[4,1,128,512]{3,2,1,0:T(8,128)(2,1)}, bf16[4,1,128,512]{3,2,1,0:T(8,128)(2,1)}, u32[]{:S(2)}, u32[]{:S(2)}) collective-permute-start(bf16[4,1,128,512]{3,2,1,0:T(8,128)(2,1)} %collective-permute-done.19.refs_9_), channel_id=1, source_target_pairs={{0,1},{1,0},{2,3},{3,2},{4,5},{5,4},{6,7},{7,6},{8,9},{9,8},{10,11... | collective-permute-start | bytes 1572872 | tf_op jit(solution)/shard_map/ppermute | solution.py:46
  96.0 38.3 %collective-permute-start.22 = (bf16[4,1,128,512]{3,2,1,0:T(8,128)(2,1)S(1)}, bf16[4,1,128,512]{3,2,1,0:T(8,128)(2,1)S(1)}, u32[]{:S(2)}, u32[]{:S(2)}) collective-permute-start(bf16[4,1,128,512]{3,2,1,0:T(8,128)(2,1)S(1)} %pad_maximum_fusion.2.refs_0_.refs_4_), channel_id=1, source_target_pairs={{0,4},{4,0},{8,12},{12,8},{16,20},{20,16},{24,28},{28,24},{1,5},{5... | collective-permute-start | bytes 1572872 | tf_op jit(solution)/shard_map/ppermute | solution.py:46
  145.6 14.3 %collective-permute-start.25 = (bf16[4,64,1024]{2,1,0:T(8,128)(2,1)}, bf16[4,64,1024]{2,1,0:T(8,128)(2,1)}, u32[]{:S(2)}, u32[]{:S(2)}) collective-permute-start(bf16[4,64,1024]{2,1,0:T(8,128)(2,1)} %get-tuple-element.117), channel_id=1, source_target_pairs={{0,4},{4,0},{8,12},{12,8},{16,20},{20,16},{24,28},{28,24},{1,5},{5... | collective-permute-start | bytes 1572872 | tf_op jit(solution)/shard_map/ppermute | solution.py:46
  146.0 22.6 %collective-permute-start.26 = (bf16[4,64,1024]{2,1,0:T(8,128)(2,1)}, bf16[4,64,1024]{2,1,0:T(8,128)(2,1)}, u32[]{:S(2)}, u32[]{:S(2)}) collective-permute-start(bf16[4,64,1024]{2,1,0:T(8,128)(2,1)} %get-tuple-element.118), channel_id=1, source_target_pairs={{0,8},{4,12},{8,0},{12,4},{16,24},{20,28},{24,16},{28,20},{1,9},{5... | collective-permute-start | bytes 1572872 | tf_op jit(solution)/shard_map/ppermute | solution.py:46
  147.4 33.3 %collective-permute-start.27 = (bf16[4,64,1024]{2,1,0:T(8,128)(2,1)}, bf16[4,64,1024]{2,1,0:T(8,128)(2,1)}, u32[]{:S(2)}, u32[]{:S(2)}) collective-permute-start(bf16[4,64,1024]{2,1,0:T(8,128)(2,1)} %get-tuple-element.119), channel_id=1, source_target_pairs={{0,12},{4,8},{8,4},{12,0},{16,28},{20,24},{24,20},{28,16},{1,13},{... | collective-permute-start | bytes 1572872 | tf_op jit(solution)/shard_map/ppermute | solution.py:46
  182.0 40.2 %collective-permute-start.30 = (bf16[4,64,1024]{2,1,0:T(8,128)(2,1)}, bf16[4,64,1024]{2,1,0:T(8,128)(2,1)S(1)}, u32[]{:S(2)}, u32[]{:S(2)}) collective-permute-start(bf16[4,64,1024]{2,1,0:T(8,128)(2,1)} %get-tuple-element.125), channel_id=1, source_target_pairs={{0,12},{4,8},{8,4},{12,0},{16,28},{20,24},{24,20},{28,16},{1,13},{... | collective-permute-start | bytes 1572872 | tf_op jit(solution)/shard_map/ppermute | solution.py:46
  183.4 38.8 %collective-permute-start.29 = (bf16[4,64,1024]{2,1,0:T(8,128)(2,1)S(1)}, bf16[4,64,1024]{2,1,0:T(8,128)(2,1)S(1)}, u32[]{:S(2)}, u32[]{:S(2)}) collective-permute-start(bf16[4,64,1024]{2,1,0:T(8,128)(2,1)S(1)} %get-tuple-element.124), channel_id=1, source_target_pairs={{0,8},{4,12},{8,0},{12,4},{16,24},{20,28},{24,16},{28,20},{1,9},{5... | collective-permute-start | bytes 1572872 | tf_op jit(solution)/shard_map/ppermute | solution.py:46
  184.0 38.2 %collective-permute-start.28 = (bf16[4,64,1024]{2,1,0:T(8,128)(2,1)S(1)}, bf16[4,64,1024]{2,1,0:T(8,128)(2,1)S(1)}, u32[]{:S(2)}, u32[]{:S(2)}) collective-permute-start(bf16[4,64,1024]{2,1,0:T(8,128)(2,1)S(1)} %get-tuple-element.123), channel_id=1, source_target_pairs={{0,4},{4,0},{8,12},{12,8},{16,20},{20,16},{24,28},{28,24},{1,5},{5... | collective-permute-start | bytes 1572872 | tf_op jit(solution)/shard_map/ppermute | solution.py:46
  274.2 42.3 %collective-permute-start.31 = (bf16[2,2,4,4,128,256]{5,4,3,2,1,0:T(8,128)(2,1)}, bf16[2,2,4,4,128,256]{5,4,3,2,1,0:T(8,128)(2,1)}, u32[]{:S(2)}, u32[]{:S(2)}) collective-permute-start(bf16[2,2,4,4,128,256]{5,4,3,2,1,0:T(8,128)(2,1)} %get-tuple-element.133), channel_id=1, source_target_pairs={{0,1},{1,0},{2,3},{3,2},{4,5},{5,4},{6,7},{7,6},{8,9},{9,8},{10,11... | collective-permute-start | bytes 12582920 | tf_op jit(solution)/shard_map/ppermute | solution.py:46
  312.5 50.5 %collective-permute-start.36 = (bf16[2,2,4,4,128,256]{5,4,3,2,1,0:T(8,128)(2,1)}, bf16[2,2,4,4,128,256]{5,4,3,2,1,0:T(8,128)(2,1)}, u32[]{:S(2)}, u32[]{:S(2)}) collective-permute-start(bf16[2,2,4,4,128,256]{5,4,3,2,1,0:T(8,128)(2,1)} %get-tuple-element.147), channel_id=1, source_target_pairs={{0,1},{1,0},{2,3},{3,2},{4,5},{5,4},{6,7},{7,6},{8,9},{9,8},{10,11... | collective-permute-start | bytes 12582920 | tf_op jit(solution)/shard_map/ppermute | solution.py:46
  313.0 53.4 %collective-permute-start.32 = (bf16[4,64,1024]{2,1,0:T(8,128)(2,1)}, bf16[4,64,1024]{2,1,0:T(8,128)(2,1)S(1)}, u32[]{:S(2)}, u32[]{:S(2)}) collective-permute-start(bf16[4,64,1024]{2,1,0:T(8,128)(2,1)} %get-tuple-element.142), channel_id=1, source_target_pairs={{0,4},{4,0},{8,12},{12,8},{16,20},{20,16},{24,28},{28,24},{1,5},{5... | collective-permute-start | bytes 1572872 | tf_op jit(solution)/shard_map/ppermute | solution.py:46
  313.1 53.8 %collective-permute-start.33 = (bf16[4,64,1024]{2,1,0:T(8,128)(2,1)}, bf16[4,64,1024]{2,1,0:T(8,128)(2,1)S(1)}, u32[]{:S(2)}, u32[]{:S(2)}) collective-permute-start(bf16[4,64,1024]{2,1,0:T(8,128)(2,1)} %get-tuple-element.143), channel_id=1, source_target_pairs={{0,8},{4,12},{8,0},{12,4},{16,24},{20,28},{24,16},{28,20},{1,9},{5... | collective-permute-start | bytes 1572872 | tf_op jit(solution)/shard_map/ppermute | solution.py:46
  314.5 55.3 %collective-permute-start.34 = (bf16[4,64,1024]{2,1,0:T(8,128)(2,1)}, bf16[4,64,1024]{2,1,0:T(8,128)(2,1)}, u32[]{:S(2)}, u32[]{:S(2)}) collective-permute-start(bf16[4,64,1024]{2,1,0:T(8,128)(2,1)} %get-tuple-element.144), channel_id=1, source_target_pairs={{0,12},{4,8},{8,4},{12,0},{16,28},{20,24},{24,20},{28,16},{1,13},{... | collective-permute-start | bytes 1572872 | tf_op jit(solution)/shard_map/ppermute | solution.py:46
  320.9 54.3 %collective-permute-start.35 = (bf16[2,4,4,128,256]{4,3,2,1,0:T(8,128)(2,1)}, bf16[2,4,4,128,256]{4,3,2,1,0:T(8,128)(2,1)}, u32[]{:S(2)}, u32[]{:S(2)}) collective-permute-start(bf16[2,4,4,128,256]{4,3,2,1,0:T(8,128)(2,1)} %fusion), channel_id=1, source_target_pairs={{0,2},{1,3},{2,0},{3,1},{4,6},{5,7},{6,4},{7,5},{8,10},{9,11},{10,... | collective-permute-start | bytes 6291464 | tf_op jit(solution)/shard_map/ppermute | solution.py:46
  363.0 14.6 %collective-permute-start.37 = (bf16[4,64,1024]{2,1,0:T(8,128)(2,1)}, bf16[4,64,1024]{2,1,0:T(8,128)(2,1)}, u32[]{:S(2)}, u32[]{:S(2)}) collective-permute-start(bf16[4,64,1024]{2,1,0:T(8,128)(2,1)} %get-tuple-element.151), channel_id=1, source_target_pairs={{0,4},{4,0},{8,12},{12,8},{16,20},{20,16},{24,28},{28,24},{1,5},{5... | collective-permute-start | bytes 1572872 | tf_op jit(solution)/shard_map/ppermute | solution.py:46
  366.5 15.2 %collective-permute-start.38 = (bf16[4,64,1024]{2,1,0:T(8,128)(2,1)}, bf16[4,64,1024]{2,1,0:T(8,128)(2,1)}, u32[]{:S(2)}, u32[]{:S(2)}) collective-permute-start(bf16[4,64,1024]{2,1,0:T(8,128)(2,1)} %get-tuple-element.152), channel_id=1, source_target_pairs={{0,8},{4,12},{8,0},{12,4},{16,24},{20,28},{24,16},{28,20},{1,9},{5... | collective-permute-start | bytes 1572872 | tf_op jit(solution)/shard_map/ppermute | solution.py:46
  366.9 24.8 %collective-permute-start.39 = (bf16[4,64,1024]{2,1,0:T(8,128)(2,1)S(1)}, bf16[4,64,1024]{2,1,0:T(8,128)(2,1)}, u32[]{:S(2)}, u32[]{:S(2)}) collective-permute-start(bf16[4,64,1024]{2,1,0:T(8,128)(2,1)S(1)} %copy-done.35), channel_id=1, source_target_pairs={{0,12},{4,8},{8,4},{12,0},{16,28},{20,24},{24,20},{28,16},{1,13},{... | collective-permute-start | bytes 1572872 | tf_op jit(solution)/shard_map/ppermute | solution.py:46
  369.8 45.8 %collective-permute-start.41 = (bf16[2,4,4,128,256]{4,3,2,1,0:T(8,128)(2,1)S(1)}, bf16[2,4,4,128,256]{4,3,2,1,0:T(8,128)(2,1)}, u32[]{:S(2)}, u32[]{:S(2)}) collective-permute-start(bf16[2,4,4,128,256]{4,3,2,1,0:T(8,128)(2,1)S(1)} %fusion.1), channel_id=1, source_target_pairs={{0,2},{1,3},{2,0},{3,1},{4,6},{5,7},{6,4},{7,5},{8,10},{9,11},{10,... | collective-permute-start | bytes 6291464 | tf_op jit(solution)/shard_map/ppermute | solution.py:46
  399.7 26.3 %collective-permute-start.40 = (bf16[4,4,128,256]{3,2,1,0:T(8,128)(2,1)S(1)}, bf16[4,4,128,256]{3,2,1,0:T(8,128)(2,1)}, u32[]{:S(2)}, u32[]{:S(2)}) collective-permute-start(bf16[4,4,128,256]{3,2,1,0:T(8,128)(2,1)S(1)} %fusion.3), channel_id=1, source_target_pairs={{0,4},{4,0},{8,12},{12,8},{16,20},{20,16},{24,28},{28,24},{1,5},{5... | collective-permute-start | bytes 3145736 | tf_op jit(solution)/shard_map/ppermute | solution.py:46
  417.9 36.4 %collective-permute-start.44 = (bf16[4,4,128,256]{3,2,1,0:T(8,128)(2,1)S(1)}, bf16[4,4,128,256]{3,2,1,0:T(8,128)(2,1)S(1)}, u32[]{:S(2)}, u32[]{:S(2)}) collective-permute-start(bf16[4,4,128,256]{3,2,1,0:T(8,128)(2,1)S(1)} %fusion.2), channel_id=1, source_target_pairs={{0,4},{4,0},{8,12},{12,8},{16,20},{20,16},{24,28},{28,24},{1,5},{5... | collective-permute-start | bytes 3145736 | tf_op jit(solution)/shard_map/ppermute | solution.py:46
  419.3 39.3 %collective-permute-start.43 = (bf16[2,4,2,2,128,256]{5,4,3,2,1,0:T(8,128)(2,1)}, bf16[2,4,2,2,128,256]{5,4,3,2,1,0:T(8,128)(2,1)}, u32[]{:S(2)}, u32[]{:S(2)}) collective-permute-start(bf16[2,4,2,2,128,256]{5,4,3,2,1,0:T(8,128)(2,1)} %get-tuple-element.169), channel_id=1, source_target_pairs={{0,1},{1,0},{2,3},{3,2},{4,5},{5,4},{6,7},{7,6},{8,9},{9,8},{10,11... | collective-permute-start | bytes 6291464 | tf_op jit(solution)/shard_map/ppermute | solution.py:46
  419.3 42.0 %collective-permute-start.42 = (bf16[2,2,4,2,128,256]{5,4,3,2,1,0:T(8,128)(2,1)}, bf16[2,2,4,2,128,256]{5,4,3,2,1,0:T(8,128)(2,1)}, u32[]{:S(2)}, u32[]{:S(2)}) collective-permute-start(bf16[2,2,4,2,128,256]{5,4,3,2,1,0:T(8,128)(2,1)} %get-tuple-element.166), channel_id=1, source_target_pairs={{0,1},{1,0},{2,3},{3,2},{4,5},{5,4},{6,7},{7,6},{8,9},{9,8},{10,11... | collective-permute-start | bytes 6291464 | tf_op jit(solution)/shard_map/ppermute | solution.py:46
  429.0 46.3 %collective-permute-start.48 = (bf16[4,128,256]{2,1,0:T(8,128)(2,1)}, bf16[4,128,256]{2,1,0:T(8,128)(2,1)S(1)}, u32[]{:S(2)}, u32[]{:S(2)}) collective-permute-start(bf16[4,128,256]{2,1,0:T(8,128)(2,1)} %get-tuple-element.214), channel_id=1, source_target_pairs={{0,24},{4,28},{8,0},{12,4},{16,8},{20,12},{24,16},{28,20},{1,25},{... | collective-permute-start | bytes 786440 | tf_op jit(solution)/shard_map/ppermute | solution.py:51
  430.3 45.5 %collective-permute-start.46 = (bf16[4,128,256]{2,1,0:T(8,128)(2,1)}, bf16[4,128,256]{2,1,0:T(8,128)(2,1)S(1)}, u32[]{:S(2)}, u32[]{:S(2)}) collective-permute-start(bf16[4,128,256]{2,1,0:T(8,128)(2,1)} %get-tuple-element.216), channel_id=1, source_target_pairs={{0,8},{4,12},{8,16},{12,20},{16,24},{20,28},{24,0},{28,4},{1,9},{5... | collective-permute-start | bytes 786440 | tf_op jit(solution)/shard_map/ppermute | solution.py:51
  454.3 21.9 %collective-permute-start.47 = (bf16[4,128,256]{2,1,0:T(8,128)(2,1)}, bf16[4,128,256]{2,1,0:T(8,128)(2,1)S(1)}, u32[]{:S(2)}, u32[]{:S(2)}) collective-permute-start(bf16[4,128,256]{2,1,0:T(8,128)(2,1)} %get-tuple-element.215), channel_id=1, source_target_pairs={{0,16},{4,20},{8,24},{12,28},{16,0},{20,4},{24,8},{28,12},{1,17},{... | collective-permute-start | bytes 786440 | tf_op jit(solution)/shard_map/ppermute | solution.py:51
  458.5 75.5 %collective-permute-start.72 = (bf16[4,128,256]{2,1,0:T(8,128)(2,1)}, bf16[4,128,256]{2,1,0:T(8,128)(2,1)}, u32[]{:S(2)}, u32[]{:S(2)}) collective-permute-start(bf16[4,128,256]{2,1,0:T(8,128)(2,1)} %get-tuple-element.211), channel_id=1, source_target_pairs={{0,24},{4,28},{8,0},{12,4},{16,8},{20,12},{24,16},{28,20},{1,25},{... | collective-permute-start | bytes 786440 | tf_op jit(solution)/shard_map/ppermute | solution.py:51
  461.3 76.1 %collective-permute-start.70 = (bf16[4,128,256]{2,1,0:T(8,128)(2,1)}, bf16[4,128,256]{2,1,0:T(8,128)(2,1)}, u32[]{:S(2)}, u32[]{:S(2)}) collective-permute-start(bf16[4,128,256]{2,1,0:T(8,128)(2,1)} %get-tuple-element.213), channel_id=1, source_target_pairs={{0,8},{4,12},{8,16},{12,20},{16,24},{20,28},{24,0},{28,4},{1,9},{5... | collective-permute-start | bytes 786440 | tf_op jit(solution)/shard_map/ppermute | solution.py:51
  475.3 18.4 %collective-permute-start.50 = (bf16[4,2,2,128,256]{4,3,2,1,0:T(8,128)(2,1)}, bf16[4,2,2,128,256]{4,3,2,1,0:T(8,128)(2,1)}, u32[]{:S(2)}, u32[]{:S(2)}) collective-permute-start(bf16[4,2,2,128,256]{4,3,2,1,0:T(8,128)(2,1)} %fusion.5), channel_id=1, source_target_pairs={{0,4},{4,0},{8,12},{12,8},{16,20},{20,16},{24,28},{28,24},{1,5},{5... | collective-permute-start | bytes 3145736 | tf_op jit(solution)/shard_map/ppermute | solution.py:46
  475.7 18.8 %collective-permute-start.49 = (bf16[2,4,2,128,256]{4,3,2,1,0:T(8,128)(2,1)S(1)}, bf16[2,4,2,128,256]{4,3,2,1,0:T(8,128)(2,1)}, u32[]{:S(2)}, u32[]{:S(2)}) collective-permute-start(bf16[2,4,2,128,256]{4,3,2,1,0:T(8,128)(2,1)S(1)} %fusion.4), channel_id=1, source_target_pairs={{0,2},{1,3},{2,0},{3,1},{4,6},{5,7},{6,4},{7,5},{8,10},{9,11},{10,... | collective-permute-start | bytes 3145736 | tf_op jit(solution)/shard_map/ppermute | solution.py:46
  476.9 21.8 %collective-permute-start.45 = (bf16[2,2,4,2,128,256]{5,4,3,2,1,0:T(8,128)(2,1)}, bf16[2,2,4,2,128,256]{5,4,3,2,1,0:T(8,128)(2,1)}, u32[]{:S(2)}, u32[]{:S(2)}) collective-permute-start(bf16[2,2,4,2,128,256]{5,4,3,2,1,0:T(8,128)(2,1)} %get-tuple-element.174), channel_id=1, source_target_pairs={{0,1},{1,0},{2,3},{3,2},{4,5},{5,4},{6,7},{7,6},{8,9},{9,8},{10,11... | collective-permute-start | bytes 6291464 | tf_op jit(solution)/shard_map/ppermute | solution.py:46
  493.7 43.9 %collective-permute-start.71 = (bf16[4,128,256]{2,1,0:T(8,128)(2,1)}, bf16[4,128,256]{2,1,0:T(8,128)(2,1)}, u32[]{:S(2)}, u32[]{:S(2)}) collective-permute-start(bf16[4,128,256]{2,1,0:T(8,128)(2,1)} %get-tuple-element.212), channel_id=1, source_target_pairs={{0,16},{4,20},{8,24},{12,28},{16,0},{20,4},{24,8},{28,12},{1,17},{... | collective-permute-start | bytes 786440 | tf_op jit(solution)/shard_map/ppermute | solution.py:51
  494.6 22.4 %collective-permute-start.52 = (bf16[2,2,4,2,128,256]{5,4,3,2,1,0:T(8,128)(2,1)}, bf16[2,2,4,2,128,256]{5,4,3,2,1,0:T(8,128)(2,1)}, u32[]{:S(2)}, u32[]{:S(2)}) collective-permute-start(bf16[2,2,4,2,128,256]{5,4,3,2,1,0:T(8,128)(2,1)} %get-tuple-element.186), channel_id=1, source_target_pairs={{0,1},{1,0},{2,3},{3,2},{4,5},{5,4},{6,7},{7,6},{8,9},{9,8},{10,11... | collective-permute-start | bytes 6291464 | tf_op jit(solution)/shard_map/ppermute | solution.py:46
  500.3 25.6 %collective-permute-start.51 = (bf16[2,4,2,128,256]{4,3,2,1,0:T(8,128)(2,1)S(1)}, bf16[2,4,2,128,256]{4,3,2,1,0:T(8,128)(2,1)}, u32[]{:S(2)}, u32[]{:S(2)}) collective-permute-start(bf16[2,4,2,128,256]{4,3,2,1,0:T(8,128)(2,1)S(1)} %fusion.6), channel_id=1, source_target_pairs={{0,2},{1,3},{2,0},{3,1},{4,6},{5,7},{6,4},{7,5},{8,10},{9,11},{10,... | collective-permute-start | bytes 3145736 | tf_op jit(solution)/shard_map/ppermute | solution.py:46
  517.0 14.0 %collective-permute-start.54 = (bf16[4,2,128,256]{3,2,1,0:T(8,128)(2,1)S(1)}, bf16[4,2,128,256]{3,2,1,0:T(8,128)(2,1)S(1)}, u32[]{:S(2)}, u32[]{:S(2)}) collective-permute-start(bf16[4,2,128,256]{3,2,1,0:T(8,128)(2,1)S(1)} %fusion.10), channel_id=1, source_target_pairs={{0,4},{4,0},{8,12},{12,8},{16,20},{20,16},{24,28},{28,24},{1,5},{5... | collective-permute-start | bytes 1572872 | tf_op jit(solution)/shard_map/ppermute | solution.py:46
  525.9 14.8 %collective-permute-start.57 = (bf16[2,2,128,256]{3,2,1,0:T(8,128)(2,1)S(1)}, bf16[2,2,128,256]{3,2,1,0:T(8,128)(2,1)S(1)}, u32[]{:S(2)}, u32[]{:S(2)}) collective-permute-start(bf16[2,2,128,256]{3,2,1,0:T(8,128)(2,1)S(1)} %copy-done.17), channel_id=1, source_target_pairs={{0,24},{4,28},{8,0},{12,4},{16,8},{20,12},{24,16},{28,20},{1,25},{... | collective-permute-start | bytes 786440 | tf_op jit(solution)/shard_map/ppermute | solution.py:51
  531.0 29.3 %collective-permute-start.61 = (bf16[2,4,2,128,256]{4,3,2,1,0:T(8,128)(2,1)S(1)}, bf16[2,4,2,128,256]{4,3,2,1,0:T(8,128)(2,1)S(1)}, u32[]{:S(2)}, u32[]{:S(2)}) collective-permute-start(bf16[2,4,2,128,256]{4,3,2,1,0:T(8,128)(2,1)S(1)} %fusion.7), channel_id=1, source_target_pairs={{0,2},{1,3},{2,0},{3,1},{4,6},{5,7},{6,4},{7,5},{8,10},{9,11},{10,... | collective-permute-start | bytes 3145736 | tf_op jit(solution)/shard_map/ppermute | solution.py:46
  534.1 11.2 %collective-permute-start.55 = (bf16[2,2,128,256]{3,2,1,0:T(8,128)(2,1)S(1)}, bf16[2,2,128,256]{3,2,1,0:T(8,128)(2,1)S(1)}, u32[]{:S(2)}, u32[]{:S(2)}) collective-permute-start(bf16[2,2,128,256]{3,2,1,0:T(8,128)(2,1)S(1)} %copy-done.16), channel_id=1, source_target_pairs={{0,8},{4,12},{8,16},{12,20},{16,24},{20,28},{24,0},{28,4},{1,9},{5... | collective-permute-start | bytes 786440 | tf_op jit(solution)/shard_map/ppermute | solution.py:51
  537.4 19.8 %collective-permute-start.56 = (bf16[2,2,128,256]{3,2,1,0:T(8,128)(2,1)S(1)}, bf16[2,2,128,256]{3,2,1,0:T(8,128)(2,1)S(1)}, u32[]{:S(2)}, u32[]{:S(2)}) collective-permute-start(bf16[2,2,128,256]{3,2,1,0:T(8,128)(2,1)S(1)} %copy-done.15), channel_id=1, source_target_pairs={{0,16},{4,20},{8,24},{12,28},{16,0},{20,4},{24,8},{28,12},{1,17},{... | collective-permute-start | bytes 786440 | tf_op jit(solution)/shard_map/ppermute | solution.py:51
  537.7 20.6 %collective-permute-start.53 = (bf16[4,2,128,256]{3,2,1,0:T(8,128)(2,1)S(1)}, bf16[4,2,128,256]{3,2,1,0:T(8,128)(2,1)S(1)}, u32[]{:S(2)}, u32[]{:S(2)}) collective-permute-start(bf16[4,2,128,256]{3,2,1,0:T(8,128)(2,1)S(1)} %fusion.9), channel_id=1, source_target_pairs={{0,4},{4,0},{8,12},{12,8},{16,20},{20,16},{24,28},{28,24},{1,5},{5... | collective-permute-start | bytes 1572872 | tf_op jit(solution)/shard_map/ppermute | solution.py:46
  540.7 22.5 %collective-permute-start.65 = (bf16[2,128,256]{2,1,0:T(8,128)(2,1)S(1)}, bf16[2,128,256]{2,1,0:T(8,128)(2,1)S(1)}, u32[]{:S(2)}, u32[]{:S(2)}) collective-permute-start(bf16[2,128,256]{2,1,0:T(8,128)(2,1)S(1)} %get-tuple-element.223), channel_id=1, source_target_pairs={{0,24},{4,28},{8,0},{12,4},{16,8},{20,12},{24,16},{28,20},{1,25},{... | collective-permute-start | bytes 393224 | tf_op jit(solution)/shard_map/ppermute | solution.py:51
  545.3 24.1 %collective-permute-start.63 = (bf16[2,128,256]{2,1,0:T(8,128)(2,1)S(1)}, bf16[2,128,256]{2,1,0:T(8,128)(2,1)S(1)}, u32[]{:S(2)}, u32[]{:S(2)}) collective-permute-start(bf16[2,128,256]{2,1,0:T(8,128)(2,1)S(1)} %get-tuple-element.225), channel_id=1, source_target_pairs={{0,8},{4,12},{8,16},{12,20},{16,24},{20,28},{24,0},{28,4},{1,9},{5... | collective-permute-start | bytes 393224 | tf_op jit(solution)/shard_map/ppermute | solution.py:51
  557.2 12.7 %collective-permute-start.64 = (bf16[2,128,256]{2,1,0:T(8,128)(2,1)S(1)}, bf16[2,128,256]{2,1,0:T(8,128)(2,1)S(1)}, u32[]{:S(2)}, u32[]{:S(2)}) collective-permute-start(bf16[2,128,256]{2,1,0:T(8,128)(2,1)S(1)} %get-tuple-element.224), channel_id=1, source_target_pairs={{0,16},{4,20},{8,24},{12,28},{16,0},{20,4},{24,8},{28,12},{1,17},{... | collective-permute-start | bytes 393224 | tf_op jit(solution)/shard_map/ppermute | solution.py:51
  560.3 14.7 %collective-permute-start.73 = (bf16[8,128,256]{2,1,0:T(8,128)(2,1)S(1)}, bf16[8,128,256]{2,1,0:T(8,128)(2,1)S(1)}, u32[]{:S(2)}, u32[]{:S(2)}) collective-permute-start(bf16[8,128,256]{2,1,0:T(8,128)(2,1)S(1)} %pad_maximum_fusion.4.refs_4_), channel_id=1, source_target_pairs={{0,2},{1,3},{2,0},{3,1},{4,6},{5,7},{6,4},{7,5},{8,10},{9,11},{10,... | collective-permute-start | bytes 1572872 | tf_op jit(solution)/shard_map/ppermute | solution.py:46
  563.2 13.3 %collective-permute-start.62 = (bf16[4,2,128,256]{3,2,1,0:T(8,128)(2,1)S(1)}, bf16[4,2,128,256]{3,2,1,0:T(8,128)(2,1)S(1)}, u32[]{:S(2)}, u32[]{:S(2)}) collective-permute-start(bf16[4,2,128,256]{3,2,1,0:T(8,128)(2,1)S(1)} %fusion.8), channel_id=1, source_target_pairs={{0,4},{4,0},{8,12},{12,8},{16,20},{20,16},{24,28},{28,24},{1,5},{5... | collective-permute-start | bytes 1572872 | tf_op jit(solution)/shard_map/ppermute | solution.py:46
  564.8 15.6 %collective-permute-start.60 = (bf16[2,128,256]{2,1,0:T(8,128)(2,1)S(1)}, bf16[2,128,256]{2,1,0:T(8,128)(2,1)S(1)}, u32[]{:S(2)}, u32[]{:S(2)}) collective-permute-start(bf16[2,128,256]{2,1,0:T(8,128)(2,1)S(1)} %get-tuple-element.220), channel_id=1, source_target_pairs={{0,24},{4,28},{8,0},{12,4},{16,8},{20,12},{24,16},{28,20},{1,25},{... | collective-permute-start | bytes 393224 | tf_op jit(solution)/shard_map/ppermute | solution.py:51
  569.4 11.4 %collective-permute-start.58 = (bf16[2,128,256]{2,1,0:T(8,128)(2,1)S(1)}, bf16[2,128,256]{2,1,0:T(8,128)(2,1)S(1)}, u32[]{:S(2)}, u32[]{:S(2)}) collective-permute-start(bf16[2,128,256]{2,1,0:T(8,128)(2,1)S(1)} %get-tuple-element.222), channel_id=1, source_target_pairs={{0,8},{4,12},{8,16},{12,20},{16,24},{20,28},{24,0},{28,4},{1,9},{5... | collective-permute-start | bytes 393224 | tf_op jit(solution)/shard_map/ppermute | solution.py:51
  570.0 17.8 %collective-permute-start.74 = (bf16[8,128,256]{2,1,0:T(8,128)(2,1)S(1)}, bf16[8,128,256]{2,1,0:T(8,128)(2,1)S(1)}, u32[]{:S(2)}, u32[]{:S(2)}) collective-permute-start(bf16[8,128,256]{2,1,0:T(8,128)(2,1)S(1)} %pad_maximum_fusion.4.refs_4_), channel_id=1, source_target_pairs={{0,1},{1,0},{2,3},{3,2},{4,5},{5,4},{6,7},{7,6},{8,9},{9,8},{10,11... | collective-permute-start | bytes 1572872 | tf_op jit(solution)/shard_map/ppermute | solution.py:46
  575.0 15.6 %collective-permute-start.75 = (bf16[8,128,256]{2,1,0:T(8,128)(2,1)S(1)}, bf16[8,128,256]{2,1,0:T(8,128)(2,1)S(1)}, u32[]{:S(2)}, u32[]{:S(2)}) collective-permute-start(bf16[8,128,256]{2,1,0:T(8,128)(2,1)S(1)} %collective-permute-done.73.refs_5_), channel_id=1, source_target_pairs={{0,1},{1,0},{2,3},{3,2},{4,5},{5,4},{6,7},{7,6},{8,9},{9,8},{10,11... | collective-permute-start | bytes 1572872 | tf_op jit(solution)/shard_map/ppermute | solution.py:46
  602.0 15.3 %collective-permute-start.83 = (bf16[8,128,256]{2,1,0:T(8,128)(2,1)S(1)}, bf16[8,128,256]{2,1,0:T(8,128)(2,1)S(1)}, u32[]{:S(2)}, u32[]{:S(2)}) collective-permute-start(bf16[8,128,256]{2,1,0:T(8,128)(2,1)S(1)} %get-tuple-element.210.refs_0_), channel_id=1, source_target_pairs={{0,2},{1,3},{2,0},{3,1},{4,6},{5,7},{6,4},{7,5},{8,10},{9,11},{10,... | collective-permute-start | bytes 1572872 | tf_op jit(solution)/shard_map/ppermute | solution.py:46
  609.3 13.0 %collective-permute-start.84 = (bf16[8,128,256]{2,1,0:T(8,128)(2,1)S(1)}, bf16[8,128,256]{2,1,0:T(8,128)(2,1)S(1)}, u32[]{:S(2)}, u32[]{:S(2)}) collective-permute-start(bf16[8,128,256]{2,1,0:T(8,128)(2,1)S(1)} %get-tuple-element.210.refs_0_), channel_id=1, source_target_pairs={{0,1},{1,0},{2,3},{3,2},{4,5},{5,4},{6,7},{7,6},{8,9},{9,8},{10,11... | collective-permute-start | bytes 1572872 | tf_op jit(solution)/shard_map/ppermute | solution.py:46
  (67 other events, 910.8 us)
Sparse Core Ops, SparseCore 0:
  14.7 150.1 all-gather.4
  180.8 82.0 all-gather.6

commit v5 on v4

--- a/solution.py
+++ b/solution.py
@@ -364,21 +364,23 @@
         start_weights(place, stacks, metas, weights.at[pl.ds(first, count)], sems.at[i])
 
 
-def wait_layer(lots, weights, sems):
+def wait_layer(lots, weights, sems, block=None):
     for i, (first, count, _) in enumerate(lots):
-        wait_all(weights.at[pl.ds(first, count)], sems.at[i])
+        if block is None or block == first:
+            wait_all(weights.at[pl.ds(first, count)], sems.at[i])
 
 
 def stacks_of(lots):
     return sum(len(metas) for _, _, metas in lots)
 
 
-def project_in(values, gain, weights, normed_ref, packed_ref):
+def project_in(values, gain, weights, normed_ref, packed_ref, ready=lambda b: None):
     xhat, _ = norm_parts(values)
     normed = (xhat * gain).astype(BF)
     normed_ref[0] = normed
     width = normed.shape[1]
     for b in range(3):
+        ready(b)
         packed_ref[0, :, b * width : (b + 1) * width] = dot_nn(normed, weights[b]).astype(BF)
 
 
@@ -388,19 +390,19 @@
         start_layer(place, lots, stacks, weights, sems)
 
 
-def await_layer(lots, weights, sems):
+def await_layer(lots, weights, sems, block=None):
     @pl.when(pl.program_id(0) == 0)
     def _():
-        wait_layer(lots, weights, sems)
+        wait_layer(lots, weights, sems, block)
 
 
 def spatial_in_body(lots, place, frames_ref, shift_ref, gain_ref, *refs):
     n = stacks_of(lots)
     stacks, (packed_ref, normed_ref, weights, sems) = refs[:n], refs[n:]
     load_layer(place, lots, stacks, weights, sems)
-    await_layer(lots, weights, sems)
     values = frames_ref[0].astype(F32) + shift_ref[0]
-    project_in(values, gain_ref[0:1, :], weights, normed_ref, packed_ref)
+    ready = functools.partial(await_layer, lots, weights, sems)
+    project_in(values, gain_ref[0:1, :], weights, normed_ref, packed_ref, ready)
 
 
 def temporal_fwd_body(place, *refs):
@@ -606,10 +608,12 @@
     attend_back(packed_ref, heads_ref, heads_grad_ref, lse_ref, grad_ref, mask)
 
 
-def project_back(grad_ref, weights):
+def project_back(grad_ref, weights, ready=lambda b: None):
     width = weights.shape[1]
+    ready(0)
     out = dot_nt(grad_ref[0, :, :width], weights[0])
     for b in range(1, 3):
+        ready(b)
         out = out + dot_nt(grad_ref[0, :, b * width : (b + 1) * width], weights[b])
     return out
 
@@ -618,8 +622,9 @@
     n = stacks_of(lots)
     stacks, (input_ref, gain_out, column_out, weights, sems) = refs[:n], refs[n:]
     load_layer(place, lots, stacks, weights, sems)
-    await_layer(lots, weights, sems)
-    normed_grad = project_back(grad_ref, weights)
+    normed_grad = project_back(
+        grad_ref, weights, functools.partial(await_layer, lots, weights, sems)
+    )
     values = frames_ref[0].astype(F32) + shift_ref[0]
     back, gain_one = norm_back(values, normed_grad, gain_ref[0:1, :])
     add_gain(pl.program_id(0), gain_out, 0, gain_one)
@@ -629,31 +634,39 @@
 
 
 def weight_grad_body(kinds, lots, place, *refs):
-    pairs = 1 + max(pair for lot in lots for pair, _ in lot)
+    uses = [use for lot in lots for use in lot]
+    pairs = 1 + max(pair for pair, _ in uses)
     sides, refs = refs[: 2 * pairs], refs[2 * pairs :]
     outs, refs = refs[: 2 * len(lots)], refs[2 * len(lots) :]
-    held, refs = refs[: 2 * pairs], refs[2 * pairs :]
-    turned, (staging, sems) = refs[:pairs], refs[pairs:]
-    for s, (source, target) in enumerate(zip(sides, held)):
-        pltpu.make_async_copy(source, target, sems.at[s]).start()
-    tokens, width = held[0].shape
+    lefts, turned, refs = refs[:pairs], refs[pairs : 2 * pairs], refs[2 * pairs :]
+    rights, staging, sems = refs
+    tokens, width = lefts[0].shape
     chunk = 256
-    done = set()
+    seen = []
+    for at, (pair, block) in enumerate(uses):
+        if pair not in seen:
+            seen.append(pair)
+            pltpu.make_async_copy(sides[2 * pair], lefts[pair], sems.at[pair]).start()
+        pltpu.make_async_copy(
+            sides[2 * pair + 1].at[:, pl.ds(block * width, width)], rights.at[at], sems.at[pairs + at]
+        ).start()
+    seen = []
     at = 0
     for i, lot in enumerate(lots):
-        for index, (pair, block) in enumerate(lot):
-            if pair not in done:
-                done.add(pair)
-                wait_all(held[2 * pair], sems.at[2 * pair])
+        for index, (pair, _) in enumerate(lot):
+            if pair not in seen:
+                seen.append(pair)
+                wait_all(lefts[pair], sems.at[pair])
                 for r in range(tokens // chunk):
                     rows = slice(r * chunk, (r + 1) * chunk)
-                    turned[pair][:, rows] = held[2 * pair][rows, :].T
-                wait_all(held[2 * pair + 1], sems.at[2 * pair + 1])
-            columns = slice(block * width, (block + 1) * width)
-            staging[at] = dot_nn(turned[pair][...], held[2 * pair + 1][:, columns]).astype(BF)
-            start_grads(place, kinds[i], staging.at[at], index, outs[2 * i : 2 * i + 2], sems.at[2 * pairs])
+                    turned[pair][:, rows] = lefts[pair][rows, :].T
+            wait_all(rights.at[at], sems.at[pairs + at])
+            staging[at] = dot_nn(turned[pair][...], rights[at]).astype(BF)
+            start_grads(
+                place, kinds[i], staging.at[at], index, outs[2 * i : 2 * i + 2], sems.at[pairs + len(uses)]
+            )
             at += 1
-    wait_all(staging, sems.at[2 * pairs])
+    wait_all(staging, sems.at[pairs + len(uses)])
 
 
 def update(weight, moment_one, moment_two, gradient, step_rate, decay_coef):
@@ -1005,9 +1018,11 @@
             [ANY] * len(sides),
             [ANY] * (2 * len(lots)),
             [split_shape(kind, len(lot)) for kind, lot in zip(kinds, lots) for _ in range(2)],
-            [pltpu.VMEM(side.shape, BF) for side in sides]
+            [pltpu.VMEM((tokens, width), BF)] * (len(sides) // 2)
             + [pltpu.VMEM((width, tokens), BF)] * (len(sides) // 2)
-            + [pltpu.VMEM((sum(map(len, lots)), width, width), BF), sems((len(sides) + 1,))],
+            + [pltpu.VMEM((sum(map(len, lots)), tokens, width), BF)]
+            + [pltpu.VMEM((sum(map(len, lots)), width, width), BF)]
+            + [sems((len(sides) // 2 + sum(map(len, lots)) + 1,))],
             us=15,
         )
         return [outs[2 * i : 2 * i + 2] for i in range(len(lots))]
@@ -1076,19 +1091,21 @@
     sum_qk, sent_qk = step_two(sum_qk, "xyz", columns, sent_vo)
     sum_qk = send_two(sum_qk, sent_qk, "xyz")
     sum_tq, sent_tq = step_three(sum_tq, "xyz", columns, sent_qk)
-    sum_tv, sent_tv = step_three(sum_tv, "yzx", columns, sent_qk)
-    sum_tq, sum_tv = send_three(sum_tq, sent_tq, "xyz"), send_three(sum_tv, sent_tv, "yzx")
+    sum_tq = send_three(sum_tq, sent_tq, "xyz")
     quarters["ffn1"] = finish(sum_f, columns, sent_tq)
-    sum_qk, sent_qk = step_three(sum_qk, "xyz", sent_tq, sent_tv)
+    sum_qk, sent_qk = step_three(sum_qk, "xyz", sent_tq)
     sum_qk = send_three(sum_qk, sent_qk, "xyz")
     ffn_quarter = before(jnp.concatenate([quarters["ffn0"], quarters["ffn1"]]), sent_qk)
     ffn_shared = share_quarters(ffn_quarter)
     sum_vo, sent_vo = step_two(sum_vo, "xyz", sent_qk)
     sum_vo = send_two(sum_vo, sent_vo, "xyz")
-    quarters["tq"], quarters["tv"] = finish(sum_tq, sent_vo), finish(sum_tv, sent_vo)
-    sum_vo, sent_vo = step_three(sum_vo, "xyz", quarters["tq"], quarters["tv"])
+    sum_tv, sent_tv = step_three(sum_tv, "yzx", sent_vo)
+    sum_tv = send_three(sum_tv, sent_tv, "yzx")
+    quarters["tq"] = finish(sum_tq, sent_tv)
+    sum_vo, sent_vo = step_three(sum_vo, "xyz", quarters["tq"])
     sum_vo = send_three(sum_vo, sent_vo, "xyz")
     quarters["qk"] = finish(sum_qk, sent_vo)
+    quarters["tv"] = finish(sum_tv, sent_vo)
     quarters["vo"] = finish(sum_vo, ffn_shared)
     attn_quarter = jnp.concatenate([quarters[name] for name in ("qk", "vo", "tq", "tv")])
     attn_shared = share_quarters(attn_quarter)

time: 668 us -> 664 us (level)
  transfers between devices with their start and end apart: 88 -> 88, of which waited for: 34 -> 33; matrix products, arithmetic and copies ran while one was open for 8% -> 8% of each run, Pallas kernels for 45% -> 45%
where the time goes in v5:
time: 664 us; the launch traced here: 659 us
  Pallas kernels  321 us (48%)
  waiting for transfers between devices  145 us (22%)
  starting transfers between devices  108 us (16%)
  other arithmetic  54.7 us (8%)
  between operations  19.1 us (3%)
  local copies, waits for them, and re-layouts  11.5 us (2%)
    pallas_call x16, Pallas kernels, call(): pl.pallas_call(body, out_shape=out_shape, grid_spec=pltpu.PrefetchScalarG...  321 us
    ppermute x59, waiting for transfers between devices, swap(): return lax.ppermute(value, axis, [(i, i ^ bit) for i in range(size)])  96.3 us
    ppermute x27, starting transfers between devices, shift_z(): lax.ppermute(value, 'seq', [(i, (i + 2 * step) % size) for i in range(siz...  55 us
    ppermute x59, starting transfers between devices, swap(): return lax.ppermute(value, axis, [(i, i ^ bit) for i in range(size)])  52.6 us
    ppermute x27, waiting for transfers between devices, shift_z(): lax.ppermute(value, 'seq', [(i, (i + 2 * step) % size) for i in range(siz...  48.2 us
    convert_element_type x24, other arithmetic, add_low(): return sum((term.astype(F32) for term in terms)).astype(BF)  45.2 us
  transfers between devices with their start and end apart: 88, of which 33 were waited for; matrix products, arithmetic and copies ran while one was open for 8% of the time, Pallas kernels for 45%

profile of v5, /device:TPU:0, one launch (start us, length us, event | category | flops | bytes accessed | tf_op | source)
XLA Modules:
  0.0 658.9 jit_solution(538038269688395080)
XLA Ops:
  7.2 2.5 convert.83
  14.6 3.1 collective-permute-start
  17.7 2.6 collective-permute-start.1
  24.2 4.8 collective-permute-done.1
  30.6 7.5 %collective-permute-start.10 = (bf16[2,11,128]{2,1,0:T(8,128)(2,1)S(1)}, bf16[2,11,128]{2,1,0:T(8,128)(2,1)S(1)}, u32[]{:S(2)}, u32[]{:S(2)}) collective-permute-start(bf16[2,11,128]{2,1,0:T(8,128)(2,1)S(1)} %pad_maximum_fusion.8), channel_id=1, source_target_pairs={{0,8},{4,12},{8,0},{12,4},{16,24},{20,28},{24,16},{28,20},{1,9},{5... | collective-permute-start | bytes 16904 | tf_op jit(solution)/shard_map/ppermute | solution.py:46
  38.2 3.2 collective-permute-start.4
  41.4 2.9 collective-permute-start.5
  44.4 2.6 collective-permute-done.3
  46.9 4.8 collective-permute-done.4
  51.8 3.5 collective-permute-start.6
  58.9 3.0 collective-permute-done.6
  61.9 4.1 collective-permute-start.7
  67.3 10.3 %collective-permute-done.7 = bf16[1,128,512]{2,1,0:T(8,128)(2,1)S(1)} collective-permute-done((bf16[1,128,512]{2,1,0:T(8,128)(2,1)S(1)}, bf16[1,128,512]{2,1,0:T(8,128)(2,1)S(1)}, u32[]{:S(2)}, u32[]{:S(2)}) %collective-permute-start.7) | collective-permute-done | bytes 131104 | tf_op jit(solution)/shard_map/ppermute | solution.py:51
  77.5 2.3 collective-permute-start.8
  79.9 4.4 collective-permute-done.8
  85.4 8.3 %collective-permute-done.14.refs_3_ = bf16[4,2,128,256]{3,2,1,0:T(8,128)(2,1)} collective-permute-done((bf16[4,2,128,256]{3,2,1,0:T(8,128)(2,1)}, bf16[4,2,128,256]{3,2,1,0:T(8,128)(2,1)}, u32[]{:S(2)}, u32[]{:S(2)}) %collective-permute-start.14) | collective-permute-done | bytes 524320 | tf_op jit(solution)/shard_map/ppermute | solution.py:46
  97.6 14.2 %shard_map.211 = (bf16[4,256,3072]{2,1,0:T(8,128)(2,1)}, bf16[4,256,1024]{2,1,0:T(8,128)(2,1)}) custom-call(s32[5]{0:T(128)} %stack.86.place, bf16[4,256,1024]{2,1,0:T(8,128)(2,1)} %frames_ref.4, f32[4,1,1024]{2,1,0:T(1,128)} %broadcast_in_dim.33.shift_ref, f32[3,1024]{1,0:T(4,128)} %fusion.63.gain_ref.refs_4_, bf16[4,2,128,256]{3,2,1,0:T(8,128)(2,1)} %copy-done.11, ...), custom_call_target="tpu_custom_call" | custom-call | flops 12000000000 | bytes 1048576 | tf_op jit(solution)/shard_map/pallas_call | solution.py:728
  111.7 22.3 %shard_map.212 = (bf16[4,256,1024]{2,1,0:T(8,128)(2,1)}, f32[4,16,256]{2,1,0:T(8,128)}) custom-call(s32[5]{0:T(128)} %stack.86.place, bf16[4,256,3072]{2,1,0:T(8,128)(2,1)} %get-tuple-element.112.packed_ref), custom_call_target="tpu_custom_call" | custom-call | flops 22000001024 | bytes 1048576 | tf_op jit(solution)/shard_map/pallas_call | solution.py:728
  136.9 8.4 %shard_map.213 = (bf16[4,64,1024]{2,1,0:T(8,128)(2,1)}, bf16[4,64,1024]{2,1,0:T(8,128)(2,1)}, bf16[4,64,1024]{2,1,0:T(8,128)(2,1)}, bf16[4,64,1024]{2,1,0:T(8,128)(2,1)}) custom-call(s32[5]{0:T(128)} %stack.86.place, bf16[4,256,1024]{2,1,0:T(8,128)(2,1)} %get-tuple-element.113.heads_ref, bf16[4,256,1024]{2,1,0:T(8,128)(2,1)} %frames_ref.4, ...), custom_call_target="tpu_custom_call" | custom-call | flops 6000000000 | bytes 1048576 | tf_op jit(solution)/shard_map/pallas_call | solution.py:728
  149.6 10.1 %collective-permute-done.25.refs_1_ = bf16[4,64,1024]{2,1,0:T(8,128)(2,1)} collective-permute-done((bf16[4,64,1024]{2,1,0:T(8,128)(2,1)}, bf16[4,64,1024]{2,1,0:T(8,128)(2,1)}, u32[]{:S(2)}, u32[]{:S(2)}) %collective-permute-start.25) | collective-permute-done | bytes 524320 | tf_op jit(solution)/shard_map/ppermute | solution.py:46
  159.7 8.9 %collective-permute-done.26.refs_2_ = bf16[4,64,1024]{2,1,0:T(8,128)(2,1)} collective-permute-done((bf16[4,64,1024]{2,1,0:T(8,128)(2,1)}, bf16[4,64,1024]{2,1,0:T(8,128)(2,1)}, u32[]{:S(2)}, u32[]{:S(2)}) %collective-permute-start.26) | collective-permute-done | bytes 524320 | tf_op jit(solution)/shard_map/ppermute | solution.py:46
  168.6 12.1 %collective-permute-done.27.refs_3_ = bf16[4,64,1024]{2,1,0:T(8,128)(2,1)} collective-permute-done((bf16[4,64,1024]{2,1,0:T(8,128)(2,1)}, bf16[4,64,1024]{2,1,0:T(8,128)(2,1)}, u32[]{:S(2)}, u32[]{:S(2)}) %collective-permute-start.27) | collective-permute-done | bytes 524320 | tf_op jit(solution)/shard_map/ppermute | solution.py:46
  185.4 36.7 %shard_map.214 = (bf16[4,256,3072]{2,1,0:T(8,128)(2,1)}, bf16[4,256,1024]{2,1,0:T(8,128)(2,1)}, f32[4,16,256]{2,1,0:T(8,128)}, bf16[4,256,1024]{2,1,0:T(8,128)(2...) custom-call(s32[5]{0:T(128)} %stack.86.place, ...), custom_call_target="tpu_custom_call" | custom-call | flops 36999999488 | bytes 1048576 | tf_op jit(solution)/shard_map/pallas_call | solution.py:728
  223.9 4.6 shard_map.215.cot_ref
  228.5 45.5 %shard_map.216 = (bf16[2,2,4,4,128,256]{5,4,3,2,1,0:T(8,128)(2,1)}, bf16[2,2,4,4,128,256]{5,4,3,2,1,0:T(8,128)(2,1)}, f32[1024,1024]{1,0:T(8,128)}, f32[1024,1024]{1,0:T(8,128)}) custom-call(s32[5]{0:T(128)} %stack.86.place, bf16[1024,1024]{1,0:T(8,128)(2,1)} %bitcast.330, bf16[1024,1024]{1,0:T(8,128)(2,1)} %bitcast.328, f32[1024,1024]{1,0:T(8,128)} %bitcast.319, ...), custom_call_target="tpu_custom_call" | custom-call | flops 41000001536 | bytes 1048576 | tf_op jit(solution)/shard_map/pallas_call | solution.py:728
  274.1 38.2 %shard_map.217 = (bf16[2,2,4,4,128,256]{5,4,3,2,1,0:T(8,128)(2,1)}, bf16[2,2,4,4,128,256]{5,4,3,2,1,0:T(8,128)(2,1)}, f32[1024,1024]{1,0:T(8,128)}, bf16[4,64,10...) custom-call(s32[5]{0:T(128)} %stack.86.place, ...), custom_call_target="tpu_custom_call" | custom-call | flops 41000001536 | bytes 1048576 | tf_op jit(solution)/shard_map/pallas_call | solution.py:728
  316.3 4.4 fusion
  321.9 41.2 %shard_map.218 = (bf16[4,256,1024]{2,1,0:T(8,128)(2,1)}, bf16[4,256,3072]{2,1,0:T(8,128)(2,1)}, f32[2,1024]{1,0:T(2,128)}, bf16[4,64,1024]{2,1,0:T(8,128)(2,1)},...) custom-call(s32[5]{0:T(128)} %stack.86.place, ...), custom_call_target="tpu_custom_call" | custom-call | flops 38000001024 | bytes 1048576 | tf_op jit(solution)/shard_map/pallas_call | solution.py:728
  363.6 3.1 fusion.1
  367.1 2.7 collective-permute-start.39
  370.7 4.5 shard_map.219
  375.2 2.3 fusion.3
  377.6 4.4 collective-permute-done.38.refs_2_
  381.9 9.9 %collective-permute-done.39.refs_3_ = bf16[4,64,1024]{2,1,0:T(8,128)(2,1)} collective-permute-done((bf16[4,64,1024]{2,1,0:T(8,128)(2,1)S(1)}, bf16[4,64,1024]{2,1,0:T(8,128)(2,1)}, u32[]{:S(2)}, u32[]{:S(2)}) %collective-permute-start.39) | collective-permute-done | bytes 524320 | tf_op jit(solution)/shard_map/ppermute | solution.py:46
  391.8 7.9 %shard_map.220 = (bf16[4,256,1024]{2,1,0:T(8,128)(2,1)}, bf16[4,256,1024]{2,1,0:T(8,128)(2,1)}) custom-call(s32[5]{0:T(128)} %stack.86.place, bf16[4,64,1024]{2,1,0:T(8,128)(2,1)} %get-tuple-element.150.refs_0_, bf16[4,64,1024]{2,1,0:T(8,128)(2,1)} %collective-permute-done.37.refs_1_, bf16[4,64,1024]{2,1,0:T(8,128)(2,1)} %collective-permute-done.38.refs_2_, ...), custom_call_target="tpu_custom_call" | custom-call | flops 7000000000 | bytes 1048576 | tf_op jit(solution)/shard_map/pallas_call | solution.py:728
  400.3 14.3 %shard_map.221 = (bf16[2,2,4,2,128,256]{5,4,3,2,1,0:T(8,128)(2,1)}, bf16[2,2,4,2,128,256]{5,4,3,2,1,0:T(8,128)(2,1)}, bf16[2,4,2,2,128,256]{5,4,3,2,1,0:T(8,128)(2,1)}, bf16[2,4,2,2,128,256]{5,4,3,2,1,0:T(8,128)(2,1)}) custom-call(s32[5]{0:T(128)} %stack.86.place, bf16[1024,1024]{1,0:T(8,128)(2,1)} %bitcast.326, bf16[1024,3072]{1,0:T(8,128)(2,1)} %bitcast.318, ...), custom_call_target="tpu_custom_call" | custom-call | flops 15000000512 | bytes 1048576 | tf_op jit(solution)/shard_map/pallas_call | solution.py:728
  415.6 2.3 fusion.2
  419.1 7.0 %collective-permute-done.40 = bf16[4,4,128,256]{3,2,1,0:T(8,128)(2,1)} collective-permute-done((bf16[4,4,128,256]{3,2,1,0:T(8,128)(2,1)S(1)}, bf16[4,4,128,256]{3,2,1,0:T(8,128)(2,1)}, u32[]{:S(2)}, u32[]{:S(2)}) %collective-permute-start.40) | collective-permute-done | bytes 1048608 | tf_op jit(solution)/shard_map/ppermute | solution.py:46
  426.0 3.0 fusion.25
  431.1 23.1 %shard_map.222.grad_ref = bf16[4,256,3072]{2,1,0:T(8,128)(2,1)} custom-call(s32[5]{0:T(128)} %stack.86.place, bf16[4,256,3072]{2,1,0:T(8,128)(2,1)} %get-tuple-element.112.packed_ref, bf16[4,256,1024]{2,1,0:T(8,128)(2,1)} %get-tuple-element.113.heads_ref, bf16[4,256,1024]{2,1,0:T(8,128)(2,1)} %get-tuple-element.163.heads_grad_ref, ...), custom_call_target="tpu_custom_call" | custom-call | flops 25999998976 | bytes 1048576 | tf_op jit(solution)/shard_map/pallas_call | solution.py:728
  455.7 2.8 fusion.22
  458.5 2.8 collective-permute-start.71
  462.9 2.5 fusion.5
  465.4 8.9 %shard_map.223 = (bf16[2,2,4,2,128,256]{5,4,3,2,1,0:T(8,128)(2,1)}, bf16[2,2,4,2,128,256]{5,4,3,2,1,0:T(8,128)(2,1)}) custom-call(s32[5]{0:T(128)} %stack.86.place, bf16[1024,1024]{1,0:T(8,128)(2,1)} %bitcast.321, bf16[1024,3072]{1,0:T(8,128)(2,1)} %bitcast.316), custom_call_target="tpu_custom_call" | custom-call | flops 15000000512 | bytes 1048576 | tf_op jit(solution)/shard_map/pallas_call | solution.py:728
  477.4 9.5 %shard_map.224 = (bf16[2,2,4,2,128,256]{5,4,3,2,1,0:T(8,128)(2,1)}, bf16[2,2,4,2,128,256]{5,4,3,2,1,0:T(8,128)(2,1)}) custom-call(s32[5]{0:T(128)} %stack.86.place, bf16[1024,1024]{1,0:T(8,128)(2,1)} %bitcast.322, bf16[1024,3072]{1,0:T(8,128)(2,1)} %bitcast.317, bf16[1024,1024]{1,0:T(8,128)(2,1)} %bitcast.323, bf16[1024,1024]{1,0:T(8,128)(2,1)} %bitcast.324), custom_call_target="tpu_custom_call" | custom-call | flops 15000000512 | bytes 1048576 | tf_op jit(solution)/shard_map/pallas_call | solution.py:728
  486.9 5.5 collective-permute-done.50
  493.3 2.6 fusion.15
  499.5 15.9 %shard_map.225 = (bf16[4,256,1024]{2,1,0:T(8,128)(2,1)}, f32[1,1024]{1,0:T(1,128)}, f32[4,1,1024]{2,1,0:T(1,128)}) custom-call(s32[5]{0:T(128)} %stack.86.place, bf16[4,256,3072]{2,1,0:T(8,128)(2,1)} %shard_map.222.grad_ref, bf16[4,256,1024]{2,1,0:T(8,128)(2,1)} %frames_ref.4, f32[4,1,1024]{2,1,0:T(1,128)} %broadcast_in_dim.33.shift_ref, ...), custom_call_target="tpu_custom_call" | custom-call | flops 14000000000 | bytes 1048576 | tf_op jit(solution)/shard_map/pallas_call | solution.py:728
  518.8 5.8 collective-permute-done.51
  526.5 3.0 collective-permute-done.54
  532.0 3.3 collective-permute-start.65
  538.7 3.8 collective-permute-done.53
  542.6 3.2 collective-permute-start.62
  547.2 2.0 collective-permute-done.58
  549.2 3.3 collective-permute-start.60
  553.8 5.2 collective-permute-start.61
  560.0 6.6 collective-permute-done.64
  577.3 2.1 collective-permute-done.75
  579.3 4.2 collective-permute-start.68
  587.7 5.2 collective-permute-done.66
  592.9 5.5 collective-permute-done.67
  608.6 2.5 collective-permute-start.81
  614.8 2.4 collective-permute-start.82
  624.9 25.8 %shard_map.226 = (f32[2,128,4096]{2,1,0:T(8,128)}, f32[2,128,4096]{2,1,0:T(8,128)}, f32[2,128,4096]{2,1,0:T(8,128)}, f32[2,128,4096]{2,1,0:T(8,128)}, f32[2,128,4096]{2,1,0:T(8,128)}, /*index=5*/f32[2,128,4096]{2,1,0:T(8,128)}) custom-call(s32[5]{0:T(128)} %stack.86.place, f32[1]{0:T(128)} %bitcast.131.clip, bf16[8,128,256]{2,1,0:T(8,128)(2,1)} %copy-done.14, ...), custom_call_target="tpu_custom_call" | custom-call | flops 10000000000 | bytes 1048576 | tf_op jit(solution)/shard_map/pallas_call | solution.py:728
  (281 shorter events, 104.6 us)
Async XLA Ops:
  7.2 178.2 %all-gather.5.cloned.1.call-start = ((), (), s32[]{:S(2)}) async-start(), calls=%async_computation | async-start | bytes 17301504 | tf_op jit(solution)/shard_map/all_gather | solution.py:817
  14.5 259.6 %all-gather.7.cloned.1.call-start = ((), (), s32[]{:S(2)}) async-start(), calls=%async_computation.1 | async-start | bytes 8650752 | tf_op jit(solution)/shard_map/all_gather | solution.py:907
  17.7 11.2 %collective-permute-start.1 = (bf16[2,128,256]{2,1,0:T(8,128)(2,1)S(1)}, bf16[2,128,256]{2,1,0:T(8,128)(2,1)S(1)}, u32[]{:S(2)}, u32[]{:S(2)}) collective-permute-start(bf16[2,128,256]{2,1,0:T(8,128)(2,1)S(1)} %fusion.57), channel_id=1, source_target_pairs={{0,16},{4,20},{8,24},{12,28},{16,0},{20,4},{24,8},{28,12},{1,17},{... | collective-permute-start | bytes 393224 | tf_op jit(solution)/shard_map/ppermute | solution.py:51
  29.0 29.3 %collective-permute-start.12 = (bf16[4,2,128,256]{3,2,1,0:T(8,128)(2,1)S(1)}, bf16[4,2,128,256]{3,2,1,0:T(8,128)(2,1)}, u32[]{:S(2)}, u32[]{:S(2)}) collective-permute-start(bf16[4,2,128,256]{3,2,1,0:T(8,128)(2,1)S(1)} %pad_maximum_fusion.refs_0_), channel_id=1, source_target_pairs={{0,4},{4,0},{8,12},{12,8},{16,20},{20,16},{24,28},{28,24},{1,5},{5... | collective-permute-start | bytes 1572872 | tf_op jit(solution)/shard_map/ppermute | solution.py:46
  30.6 13.6 %collective-permute-start.10 = (bf16[2,11,128]{2,1,0:T(8,128)(2,1)S(1)}, bf16[2,11,128]{2,1,0:T(8,128)(2,1)S(1)}, u32[]{:S(2)}, u32[]{:S(2)}) collective-permute-start(bf16[2,11,128]{2,1,0:T(8,128)(2,1)S(1)} %pad_maximum_fusion.8), channel_id=1, source_target_pairs={{0,8},{4,12},{8,0},{12,4},{16,24},{20,28},{24,16},{28,20},{1,9},{5... | collective-permute-start | bytes 16904 | tf_op jit(solution)/shard_map/ppermute | solution.py:46
  38.2 13.6 %collective-permute-start.4 = (bf16[1,128,512]{2,1,0:T(8,128)(2,1)S(1)}, bf16[1,128,512]{2,1,0:T(8,128)(2,1)S(1)}, u32[]{:S(2)}, u32[]{:S(2)}) collective-permute-start(bf16[1,128,512]{2,1,0:T(8,128)(2,1)S(1)} %constant_dynamic-slice_fusion.4), channel_id=1, source_target_pairs={{0,16},{4,20},{8,24},{12,28},{16,0},{20,4},{24,8},{28,12},{1,17},{... | collective-permute-start | bytes 393224 | tf_op jit(solution)/shard_map/ppermute | solution.py:51
  44.3 12.5 %collective-permute-start.11 = (bf16[4,11,128]{2,1,0:T(8,128)(2,1)S(1)}, bf16[4,11,128]{2,1,0:T(8,128)(2,1)S(1)}, u32[]{:S(2)}, u32[]{:S(2)}) collective-permute-start(bf16[4,11,128]{2,1,0:T(8,128)(2,1)S(1)} %pad_maximum_fusion.7), channel_id=1, source_target_pairs={{0,16},{4,20},{8,24},{12,28},{16,0},{20,4},{24,8},{28,12},{1,17},{... | collective-permute-start | bytes 33800 | tf_op jit(solution)/shard_map/ppermute | solution.py:46
  55.3 29.0 %collective-permute-start.13 = (bf16[4,2,128,256]{3,2,1,0:T(8,128)(2,1)S(1)}, bf16[4,2,128,256]{3,2,1,0:T(8,128)(2,1)}, u32[]{:S(2)}, u32[]{:S(2)}) collective-permute-start(bf16[4,2,128,256]{3,2,1,0:T(8,128)(2,1)S(1)} %pad_maximum_fusion.refs_0_), channel_id=1, source_target_pairs={{0,2},{1,3},{2,0},{3,1},{4,6},{5,7},{6,4},{7,5},{8,10},{9,11},{10,... | collective-permute-start | bytes 1572872 | tf_op jit(solution)/shard_map/ppermute | solution.py:46
  56.8 28.0 %collective-permute-start.15 = (bf16[4,2,128,256]{3,2,1,0:T(8,128)(2,1)S(1)}, bf16[4,2,128,256]{3,2,1,0:T(8,128)(2,1)}, u32[]{:S(2)}, u32[]{:S(2)}) collective-permute-start(bf16[4,2,128,256]{3,2,1,0:T(8,128)(2,1)S(1)} %pad_maximum_fusion.refs_0_), channel_id=1, source_target_pairs={{0,1},{1,0},{2,3},{3,2},{4,5},{5,4},{6,7},{7,6},{8,9},{9,8},{10,11... | collective-permute-start | bytes 1572872 | tf_op jit(solution)/shard_map/ppermute | solution.py:46
  56.8 28.1 %collective-permute-start.19 = (bf16[4,1,128,512]{3,2,1,0:T(8,128)(2,1)S(1)}, bf16[4,1,128,512]{3,2,1,0:T(8,128)(2,1)}, u32[]{:S(2)}, u32[]{:S(2)}) collective-permute-start(bf16[4,1,128,512]{3,2,1,0:T(8,128)(2,1)S(1)} %pad_maximum_fusion.1.refs_8_), channel_id=1, source_target_pairs={{0,4},{4,0},{8,12},{12,8},{16,20},{20,16},{24,28},{28,24},{1,5},{5... | collective-permute-start | bytes 1572872 | tf_op jit(solution)/shard_map/ppermute | solution.py:46
  58.3 35.4 %collective-permute-start.14 = (bf16[4,2,128,256]{3,2,1,0:T(8,128)(2,1)}, bf16[4,2,128,256]{3,2,1,0:T(8,128)(2,1)}, u32[]{:S(2)}, u32[]{:S(2)}) collective-permute-start(bf16[4,2,128,256]{3,2,1,0:T(8,128)(2,1)} %collective-permute-done.12.refs_1_), channel_id=1, source_target_pairs={{0,2},{1,3},{2,0},{3,1},{4,6},{5,7},{6,4},{7,5},{8,10},{9,11},{10,... | collective-permute-start | bytes 1572872 | tf_op jit(solution)/shard_map/ppermute | solution.py:46
  61.9 15.6 %collective-permute-start.7 = (bf16[1,128,512]{2,1,0:T(8,128)(2,1)S(1)}, bf16[1,128,512]{2,1,0:T(8,128)(2,1)S(1)}, u32[]{:S(2)}, u32[]{:S(2)}) collective-permute-start(bf16[1,128,512]{2,1,0:T(8,128)(2,1)S(1)} %constant_dynamic-slice_fusion.5), channel_id=1, source_target_pairs={{0,16},{4,20},{8,24},{12,28},{16,0},{20,4},{24,8},{28,12},{1,17},{... | collective-permute-start | bytes 393224 | tf_op jit(solution)/shard_map/ppermute | solution.py:51
  84.3 10.9 %collective-permute-start.20 = (bf16[4,1,128,512]{3,2,1,0:T(8,128)(2,1)S(1)}, bf16[4,1,128,512]{3,2,1,0:T(8,128)(2,1)S(1)}, u32[]{:S(2)}, u32[]{:S(2)}) collective-permute-start(bf16[4,1,128,512]{3,2,1,0:T(8,128)(2,1)S(1)} %pad_maximum_fusion.1.refs_8_), channel_id=1, source_target_pairs={{0,1},{1,0},{2,3},{3,2},{4,5},{5,4},{6,7},{7,6},{8,9},{9,8},{10,11... | collective-permute-start | bytes 1572872 | tf_op jit(solution)/shard_map/ppermute | solution.py:46
  84.3 13.2 %collective-permute-start.16 = (bf16[4,2,128,256]{3,2,1,0:T(8,128)(2,1)}, bf16[4,2,128,256]{3,2,1,0:T(8,128)(2,1)}, u32[]{:S(2)}, u32[]{:S(2)}) collective-permute-start(bf16[4,2,128,256]{3,2,1,0:T(8,128)(2,1)} %collective-permute-done.12.refs_1_), channel_id=1, source_target_pairs={{0,1},{1,0},{2,3},{3,2},{4,5},{5,4},{6,7},{7,6},{8,9},{9,8},{10,11... | collective-permute-start | bytes 1572872 | tf_op jit(solution)/shard_map/ppermute | solution.py:46
  84.8 12.7 %collective-permute-start.17 = (bf16[4,2,128,256]{3,2,1,0:T(8,128)(2,1)}, bf16[4,2,128,256]{3,2,1,0:T(8,128)(2,1)}, u32[]{:S(2)}, u32[]{:S(2)}) collective-permute-start(bf16[4,2,128,256]{3,2,1,0:T(8,128)(2,1)} %collective-permute-done.13.refs_2_), channel_id=1, source_target_pairs={{0,1},{1,0},{2,3},{3,2},{4,5},{5,4},{6,7},{7,6},{8,9},{9,8},{10,11... | collective-permute-start | bytes 1572872 | tf_op jit(solution)/shard_map/ppermute | solution.py:46
  84.9 12.6 %collective-permute-start.21 = (bf16[4,1,128,512]{3,2,1,0:T(8,128)(2,1)}, bf16[4,1,128,512]{3,2,1,0:T(8,128)(2,1)}, u32[]{:S(2)}, u32[]{:S(2)}) collective-permute-start(bf16[4,1,128,512]{3,2,1,0:T(8,128)(2,1)} %collective-permute-done.19.refs_9_), channel_id=1, source_target_pairs={{0,1},{1,0},{2,3},{3,2},{4,5},{5,4},{6,7},{7,6},{8,9},{9,8},{10,11... | collective-permute-start | bytes 1572872 | tf_op jit(solution)/shard_map/ppermute | solution.py:46
  96.0 38.0 %collective-permute-start.22 = (bf16[4,1,128,512]{3,2,1,0:T(8,128)(2,1)S(1)}, bf16[4,1,128,512]{3,2,1,0:T(8,128)(2,1)S(1)}, u32[]{:S(2)}, u32[]{:S(2)}) collective-permute-start(bf16[4,1,128,512]{3,2,1,0:T(8,128)(2,1)S(1)} %pad_maximum_fusion.2.refs_0_.refs_4_), channel_id=1, source_target_pairs={{0,4},{4,0},{8,12},{12,8},{16,20},{20,16},{24,28},{28,24},{1,5},{5... | collective-permute-start | bytes 1572872 | tf_op jit(solution)/shard_map/ppermute | solution.py:46
  145.3 14.4 %collective-permute-start.25 = (bf16[4,64,1024]{2,1,0:T(8,128)(2,1)}, bf16[4,64,1024]{2,1,0:T(8,128)(2,1)}, u32[]{:S(2)}, u32[]{:S(2)}) collective-permute-start(bf16[4,64,1024]{2,1,0:T(8,128)(2,1)} %get-tuple-element.117), channel_id=1, source_target_pairs={{0,4},{4,0},{8,12},{12,8},{16,20},{20,16},{24,28},{28,24},{1,5},{5... | collective-permute-start | bytes 1572872 | tf_op jit(solution)/shard_map/ppermute | solution.py:46
  146.6 22.0 %collective-permute-start.26 = (bf16[4,64,1024]{2,1,0:T(8,128)(2,1)}, bf16[4,64,1024]{2,1,0:T(8,128)(2,1)}, u32[]{:S(2)}, u32[]{:S(2)}) collective-permute-start(bf16[4,64,1024]{2,1,0:T(8,128)(2,1)} %get-tuple-element.118), channel_id=1, source_target_pairs={{0,8},{4,12},{8,0},{12,4},{16,24},{20,28},{24,16},{28,20},{1,9},{5... | collective-permute-start | bytes 1572872 | tf_op jit(solution)/shard_map/ppermute | solution.py:46
  148.0 32.6 %collective-permute-start.27 = (bf16[4,64,1024]{2,1,0:T(8,128)(2,1)}, bf16[4,64,1024]{2,1,0:T(8,128)(2,1)}, u32[]{:S(2)}, u32[]{:S(2)}) collective-permute-start(bf16[4,64,1024]{2,1,0:T(8,128)(2,1)} %get-tuple-element.119), channel_id=1, source_target_pairs={{0,12},{4,8},{8,4},{12,0},{16,28},{20,24},{24,20},{28,16},{1,13},{... | collective-permute-start | bytes 1572872 | tf_op jit(solution)/shard_map/ppermute | solution.py:46
  181.9 40.2 %collective-permute-start.30 = (bf16[4,64,1024]{2,1,0:T(8,128)(2,1)}, bf16[4,64,1024]{2,1,0:T(8,128)(2,1)S(1)}, u32[]{:S(2)}, u32[]{:S(2)}) collective-permute-start(bf16[4,64,1024]{2,1,0:T(8,128)(2,1)} %get-tuple-element.125), channel_id=1, source_target_pairs={{0,12},{4,8},{8,4},{12,0},{16,28},{20,24},{24,20},{28,16},{1,13},{... | collective-permute-start | bytes 1572872 | tf_op jit(solution)/shard_map/ppermute | solution.py:46
  183.4 38.7 %collective-permute-start.29 = (bf16[4,64,1024]{2,1,0:T(8,128)(2,1)S(1)}, bf16[4,64,1024]{2,1,0:T(8,128)(2,1)S(1)}, u32[]{:S(2)}, u32[]{:S(2)}) collective-permute-start(bf16[4,64,1024]{2,1,0:T(8,128)(2,1)S(1)} %get-tuple-element.124), channel_id=1, source_target_pairs={{0,8},{4,12},{8,0},{12,4},{16,24},{20,28},{24,16},{28,20},{1,9},{5... | collective-permute-start | bytes 1572872 | tf_op jit(solution)/shard_map/ppermute | solution.py:46
  184.0 38.2 %collective-permute-start.28 = (bf16[4,64,1024]{2,1,0:T(8,128)(2,1)S(1)}, bf16[4,64,1024]{2,1,0:T(8,128)(2,1)S(1)}, u32[]{:S(2)}, u32[]{:S(2)}) collective-permute-start(bf16[4,64,1024]{2,1,0:T(8,128)(2,1)S(1)} %get-tuple-element.123), channel_id=1, source_target_pairs={{0,4},{4,0},{8,12},{12,8},{16,20},{20,16},{24,28},{28,24},{1,5},{5... | collective-permute-start | bytes 1572872 | tf_op jit(solution)/shard_map/ppermute | solution.py:46
  274.0 42.3 %collective-permute-start.31 = (bf16[2,2,4,4,128,256]{5,4,3,2,1,0:T(8,128)(2,1)}, bf16[2,2,4,4,128,256]{5,4,3,2,1,0:T(8,128)(2,1)}, u32[]{:S(2)}, u32[]{:S(2)}) collective-permute-start(bf16[2,2,4,4,128,256]{5,4,3,2,1,0:T(8,128)(2,1)} %get-tuple-element.133), channel_id=1, source_target_pairs={{0,1},{1,0},{2,3},{3,2},{4,5},{5,4},{6,7},{7,6},{8,9},{9,8},{10,11... | collective-permute-start | bytes 12582920 | tf_op jit(solution)/shard_map/ppermute | solution.py:46
  312.3 50.7 %collective-permute-start.36 = (bf16[2,2,4,4,128,256]{5,4,3,2,1,0:T(8,128)(2,1)}, bf16[2,2,4,4,128,256]{5,4,3,2,1,0:T(8,128)(2,1)}, u32[]{:S(2)}, u32[]{:S(2)}) collective-permute-start(bf16[2,2,4,4,128,256]{5,4,3,2,1,0:T(8,128)(2,1)} %get-tuple-element.147), channel_id=1, source_target_pairs={{0,1},{1,0},{2,3},{3,2},{4,5},{5,4},{6,7},{7,6},{8,9},{9,8},{10,11... | collective-permute-start | bytes 12582920 | tf_op jit(solution)/shard_map/ppermute | solution.py:46
  312.8 53.9 %collective-permute-start.32 = (bf16[4,64,1024]{2,1,0:T(8,128)(2,1)}, bf16[4,64,1024]{2,1,0:T(8,128)(2,1)S(1)}, u32[]{:S(2)}, u32[]{:S(2)}) collective-permute-start(bf16[4,64,1024]{2,1,0:T(8,128)(2,1)} %get-tuple-element.142), channel_id=1, source_target_pairs={{0,4},{4,0},{8,12},{12,8},{16,20},{20,16},{24,28},{28,24},{1,5},{5... | collective-permute-start | bytes 1572872 | tf_op jit(solution)/shard_map/ppermute | solution.py:46
  313.1 54.0 %collective-permute-start.33 = (bf16[4,64,1024]{2,1,0:T(8,128)(2,1)}, bf16[4,64,1024]{2,1,0:T(8,128)(2,1)S(1)}, u32[]{:S(2)}, u32[]{:S(2)}) collective-permute-start(bf16[4,64,1024]{2,1,0:T(8,128)(2,1)} %get-tuple-element.143), channel_id=1, source_target_pairs={{0,8},{4,12},{8,0},{12,4},{16,24},{20,28},{24,16},{28,20},{1,9},{5... | collective-permute-start | bytes 1572872 | tf_op jit(solution)/shard_map/ppermute | solution.py:46
  314.5 55.3 %collective-permute-start.34 = (bf16[4,64,1024]{2,1,0:T(8,128)(2,1)}, bf16[4,64,1024]{2,1,0:T(8,128)(2,1)}, u32[]{:S(2)}, u32[]{:S(2)}) collective-permute-start(bf16[4,64,1024]{2,1,0:T(8,128)(2,1)} %get-tuple-element.144), channel_id=1, source_target_pairs={{0,12},{4,8},{8,4},{12,0},{16,28},{20,24},{24,20},{28,16},{1,13},{... | collective-permute-start | bytes 1572872 | tf_op jit(solution)/shard_map/ppermute | solution.py:46
  320.7 54.5 %collective-permute-start.35 = (bf16[2,4,4,128,256]{4,3,2,1,0:T(8,128)(2,1)}, bf16[2,4,4,128,256]{4,3,2,1,0:T(8,128)(2,1)}, u32[]{:S(2)}, u32[]{:S(2)}) collective-permute-start(bf16[2,4,4,128,256]{4,3,2,1,0:T(8,128)(2,1)} %fusion), channel_id=1, source_target_pairs={{0,2},{1,3},{2,0},{3,1},{4,6},{5,7},{6,4},{7,5},{8,10},{9,11},{10,... | collective-permute-start | bytes 6291464 | tf_op jit(solution)/shard_map/ppermute | solution.py:46
  363.0 14.5 %collective-permute-start.37 = (bf16[4,64,1024]{2,1,0:T(8,128)(2,1)}, bf16[4,64,1024]{2,1,0:T(8,128)(2,1)}, u32[]{:S(2)}, u32[]{:S(2)}) collective-permute-start(bf16[4,64,1024]{2,1,0:T(8,128)(2,1)} %get-tuple-element.151), channel_id=1, source_target_pairs={{0,4},{4,0},{8,12},{12,8},{16,20},{20,16},{24,28},{28,24},{1,5},{5... | collective-permute-start | bytes 1572872 | tf_op jit(solution)/shard_map/ppermute | solution.py:46
  366.7 15.2 %collective-permute-start.38 = (bf16[4,64,1024]{2,1,0:T(8,128)(2,1)}, bf16[4,64,1024]{2,1,0:T(8,128)(2,1)}, u32[]{:S(2)}, u32[]{:S(2)}) collective-permute-start(bf16[4,64,1024]{2,1,0:T(8,128)(2,1)} %get-tuple-element.152), channel_id=1, source_target_pairs={{0,8},{4,12},{8,0},{12,4},{16,24},{20,28},{24,16},{28,20},{1,9},{5... | collective-permute-start | bytes 1572872 | tf_op jit(solution)/shard_map/ppermute | solution.py:46
  367.1 24.7 %collective-permute-start.39 = (bf16[4,64,1024]{2,1,0:T(8,128)(2,1)S(1)}, bf16[4,64,1024]{2,1,0:T(8,128)(2,1)}, u32[]{:S(2)}, u32[]{:S(2)}) collective-permute-start(bf16[4,64,1024]{2,1,0:T(8,128)(2,1)S(1)} %copy-done.35), channel_id=1, source_target_pairs={{0,12},{4,8},{8,4},{12,0},{16,28},{20,24},{24,20},{28,16},{1,13},{... | collective-permute-start | bytes 1572872 | tf_op jit(solution)/shard_map/ppermute | solution.py:46
  369.9 45.8 %collective-permute-start.41 = (bf16[2,4,4,128,256]{4,3,2,1,0:T(8,128)(2,1)S(1)}, bf16[2,4,4,128,256]{4,3,2,1,0:T(8,128)(2,1)}, u32[]{:S(2)}, u32[]{:S(2)}) collective-permute-start(bf16[2,4,4,128,256]{4,3,2,1,0:T(8,128)(2,1)S(1)} %fusion.1), channel_id=1, source_target_pairs={{0,2},{1,3},{2,0},{3,1},{4,6},{5,7},{6,4},{7,5},{8,10},{9,11},{10,... | collective-permute-start | bytes 6291464 | tf_op jit(solution)/shard_map/ppermute | solution.py:46
  399.8 26.3 %collective-permute-start.40 = (bf16[4,4,128,256]{3,2,1,0:T(8,128)(2,1)S(1)}, bf16[4,4,128,256]{3,2,1,0:T(8,128)(2,1)}, u32[]{:S(2)}, u32[]{:S(2)}) collective-permute-start(bf16[4,4,128,256]{3,2,1,0:T(8,128)(2,1)S(1)} %fusion.3), channel_id=1, source_target_pairs={{0,4},{4,0},{8,12},{12,8},{16,20},{20,16},{24,28},{28,24},{1,5},{5... | collective-permute-start | bytes 3145736 | tf_op jit(solution)/shard_map/ppermute | solution.py:46
  418.0 36.2 %collective-permute-start.44 = (bf16[4,4,128,256]{3,2,1,0:T(8,128)(2,1)S(1)}, bf16[4,4,128,256]{3,2,1,0:T(8,128)(2,1)S(1)}, u32[]{:S(2)}, u32[]{:S(2)}) collective-permute-start(bf16[4,4,128,256]{3,2,1,0:T(8,128)(2,1)S(1)} %fusion.2), channel_id=1, source_target_pairs={{0,4},{4,0},{8,12},{12,8},{16,20},{20,16},{24,28},{28,24},{1,5},{5... | collective-permute-start | bytes 3145736 | tf_op jit(solution)/shard_map/ppermute | solution.py:46
  418.6 39.9 %collective-permute-start.43 = (bf16[2,4,2,2,128,256]{5,4,3,2,1,0:T(8,128)(2,1)}, bf16[2,4,2,2,128,256]{5,4,3,2,1,0:T(8,128)(2,1)}, u32[]{:S(2)}, u32[]{:S(2)}) collective-permute-start(bf16[2,4,2,2,128,256]{5,4,3,2,1,0:T(8,128)(2,1)} %get-tuple-element.169), channel_id=1, source_target_pairs={{0,1},{1,0},{2,3},{3,2},{4,5},{5,4},{6,7},{7,6},{8,9},{9,8},{10,11... | collective-permute-start | bytes 6291464 | tf_op jit(solution)/shard_map/ppermute | solution.py:46
  418.6 42.7 %collective-permute-start.42 = (bf16[2,2,4,2,128,256]{5,4,3,2,1,0:T(8,128)(2,1)}, bf16[2,2,4,2,128,256]{5,4,3,2,1,0:T(8,128)(2,1)}, u32[]{:S(2)}, u32[]{:S(2)}) collective-permute-start(bf16[2,2,4,2,128,256]{5,4,3,2,1,0:T(8,128)(2,1)} %get-tuple-element.166), channel_id=1, source_target_pairs={{0,1},{1,0},{2,3},{3,2},{4,5},{5,4},{6,7},{7,6},{8,9},{9,8},{10,11... | collective-permute-start | bytes 6291464 | tf_op jit(solution)/shard_map/ppermute | solution.py:46
  429.0 45.3 %collective-permute-start.48 = (bf16[4,128,256]{2,1,0:T(8,128)(2,1)}, bf16[4,128,256]{2,1,0:T(8,128)(2,1)S(1)}, u32[]{:S(2)}, u32[]{:S(2)}) collective-permute-start(bf16[4,128,256]{2,1,0:T(8,128)(2,1)} %get-tuple-element.214), channel_id=1, source_target_pairs={{0,24},{4,28},{8,0},{12,4},{16,8},{20,12},{24,16},{28,20},{1,25},{... | collective-permute-start | bytes 786440 | tf_op jit(solution)/shard_map/ppermute | solution.py:51
  430.5 44.3 %collective-permute-start.46 = (bf16[4,128,256]{2,1,0:T(8,128)(2,1)}, bf16[4,128,256]{2,1,0:T(8,128)(2,1)S(1)}, u32[]{:S(2)}, u32[]{:S(2)}) collective-permute-start(bf16[4,128,256]{2,1,0:T(8,128)(2,1)} %get-tuple-element.216), channel_id=1, source_target_pairs={{0,8},{4,12},{8,16},{12,20},{16,24},{20,28},{24,0},{28,4},{1,9},{5... | collective-permute-start | bytes 786440 | tf_op jit(solution)/shard_map/ppermute | solution.py:51
  454.2 21.0 %collective-permute-start.47 = (bf16[4,128,256]{2,1,0:T(8,128)(2,1)}, bf16[4,128,256]{2,1,0:T(8,128)(2,1)S(1)}, u32[]{:S(2)}, u32[]{:S(2)}) collective-permute-start(bf16[4,128,256]{2,1,0:T(8,128)(2,1)} %get-tuple-element.215), channel_id=1, source_target_pairs={{0,16},{4,20},{8,24},{12,28},{16,0},{20,4},{24,8},{28,12},{1,17},{... | collective-permute-start | bytes 786440 | tf_op jit(solution)/shard_map/ppermute | solution.py:51
  458.5 73.5 %collective-permute-start.71 = (bf16[4,128,256]{2,1,0:T(8,128)(2,1)}, bf16[4,128,256]{2,1,0:T(8,128)(2,1)}, u32[]{:S(2)}, u32[]{:S(2)}) collective-permute-start(bf16[4,128,256]{2,1,0:T(8,128)(2,1)} %get-tuple-element.211), channel_id=1, source_target_pairs={{0,24},{4,28},{8,0},{12,4},{16,8},{20,12},{24,16},{28,20},{1,25},{... | collective-permute-start | bytes 786440 | tf_op jit(solution)/shard_map/ppermute | solution.py:51
  461.3 74.1 %collective-permute-start.69 = (bf16[4,128,256]{2,1,0:T(8,128)(2,1)}, bf16[4,128,256]{2,1,0:T(8,128)(2,1)}, u32[]{:S(2)}, u32[]{:S(2)}) collective-permute-start(bf16[4,128,256]{2,1,0:T(8,128)(2,1)} %get-tuple-element.213), channel_id=1, source_target_pairs={{0,8},{4,12},{8,16},{12,20},{16,24},{20,28},{24,0},{28,4},{1,9},{5... | collective-permute-start | bytes 786440 | tf_op jit(solution)/shard_map/ppermute | solution.py:51
  474.3 18.2 %collective-permute-start.50 = (bf16[4,2,2,128,256]{4,3,2,1,0:T(8,128)(2,1)}, bf16[4,2,2,128,256]{4,3,2,1,0:T(8,128)(2,1)}, u32[]{:S(2)}, u32[]{:S(2)}) collective-permute-start(bf16[4,2,2,128,256]{4,3,2,1,0:T(8,128)(2,1)} %fusion.5), channel_id=1, source_target_pairs={{0,4},{4,0},{8,12},{12,8},{16,20},{20,16},{24,28},{28,24},{1,5},{5... | collective-permute-start | bytes 3145736 | tf_op jit(solution)/shard_map/ppermute | solution.py:46
  474.7 18.5 %collective-permute-start.49 = (bf16[2,4,2,128,256]{4,3,2,1,0:T(8,128)(2,1)S(1)}, bf16[2,4,2,128,256]{4,3,2,1,0:T(8,128)(2,1)}, u32[]{:S(2)}, u32[]{:S(2)}) collective-permute-start(bf16[2,4,2,128,256]{4,3,2,1,0:T(8,128)(2,1)S(1)} %fusion.4), channel_id=1, source_target_pairs={{0,2},{1,3},{2,0},{3,1},{4,6},{5,7},{6,4},{7,5},{8,10},{9,11},{10,... | collective-permute-start | bytes 3145736 | tf_op jit(solution)/shard_map/ppermute | solution.py:46
  475.9 21.5 %collective-permute-start.45 = (bf16[2,2,4,2,128,256]{5,4,3,2,1,0:T(8,128)(2,1)}, bf16[2,2,4,2,128,256]{5,4,3,2,1,0:T(8,128)(2,1)}, u32[]{:S(2)}, u32[]{:S(2)}) collective-permute-start(bf16[2,2,4,2,128,256]{5,4,3,2,1,0:T(8,128)(2,1)} %get-tuple-element.174), channel_id=1, source_target_pairs={{0,1},{1,0},{2,3},{3,2},{4,5},{5,4},{6,7},{7,6},{8,9},{9,8},{10,11... | collective-permute-start | bytes 6291464 | tf_op jit(solution)/shard_map/ppermute | solution.py:46
  492.5 43.0 %collective-permute-start.70 = (bf16[4,128,256]{2,1,0:T(8,128)(2,1)}, bf16[4,128,256]{2,1,0:T(8,128)(2,1)}, u32[]{:S(2)}, u32[]{:S(2)}) collective-permute-start(bf16[4,128,256]{2,1,0:T(8,128)(2,1)} %get-tuple-element.212), channel_id=1, source_target_pairs={{0,16},{4,20},{8,24},{12,28},{16,0},{20,4},{24,8},{28,12},{1,17},{... | collective-permute-start | bytes 786440 | tf_op jit(solution)/shard_map/ppermute | solution.py:51
  493.3 22.2 %collective-permute-start.52 = (bf16[2,2,4,2,128,256]{5,4,3,2,1,0:T(8,128)(2,1)}, bf16[2,2,4,2,128,256]{5,4,3,2,1,0:T(8,128)(2,1)}, u32[]{:S(2)}, u32[]{:S(2)}) collective-permute-start(bf16[2,2,4,2,128,256]{5,4,3,2,1,0:T(8,128)(2,1)} %get-tuple-element.186), channel_id=1, source_target_pairs={{0,1},{1,0},{2,3},{3,2},{4,5},{5,4},{6,7},{7,6},{8,9},{9,8},{10,11... | collective-permute-start | bytes 6291464 | tf_op jit(solution)/shard_map/ppermute | solution.py:46
  499.0 25.6 %collective-permute-start.51 = (bf16[2,4,2,128,256]{4,3,2,1,0:T(8,128)(2,1)S(1)}, bf16[2,4,2,128,256]{4,3,2,1,0:T(8,128)(2,1)}, u32[]{:S(2)}, u32[]{:S(2)}) collective-permute-start(bf16[2,4,2,128,256]{4,3,2,1,0:T(8,128)(2,1)S(1)} %fusion.6), channel_id=1, source_target_pairs={{0,2},{1,3},{2,0},{3,1},{4,6},{5,7},{6,4},{7,5},{8,10},{9,11},{10,... | collective-permute-start | bytes 3145736 | tf_op jit(solution)/shard_map/ppermute | solution.py:46
  515.5 14.0 %collective-permute-start.54 = (bf16[4,2,128,256]{3,2,1,0:T(8,128)(2,1)S(1)}, bf16[4,2,128,256]{3,2,1,0:T(8,128)(2,1)S(1)}, u32[]{:S(2)}, u32[]{:S(2)}) collective-permute-start(bf16[4,2,128,256]{3,2,1,0:T(8,128)(2,1)S(1)} %fusion.10), channel_id=1, source_target_pairs={{0,4},{4,0},{8,12},{12,8},{16,20},{20,16},{24,28},{28,24},{1,5},{5... | collective-permute-start | bytes 1572872 | tf_op jit(solution)/shard_map/ppermute | solution.py:46
  524.6 24.6 %collective-permute-start.58 = (bf16[2,4,2,128,256]{4,3,2,1,0:T(8,128)(2,1)S(1)}, bf16[2,4,2,128,256]{4,3,2,1,0:T(8,128)(2,1)S(1)}, u32[]{:S(2)}, u32[]{:S(2)}) collective-permute-start(bf16[2,4,2,128,256]{4,3,2,1,0:T(8,128)(2,1)S(1)} %fusion.7), channel_id=1, source_target_pairs={{0,2},{1,3},{2,0},{3,1},{4,6},{5,7},{6,4},{7,5},{8,10},{9,11},{10,... | collective-permute-start | bytes 3145736 | tf_op jit(solution)/shard_map/ppermute | solution.py:46
  529.5 13.1 %collective-permute-start.53 = (bf16[4,2,128,256]{3,2,1,0:T(8,128)(2,1)S(1)}, bf16[4,2,128,256]{3,2,1,0:T(8,128)(2,1)S(1)}, u32[]{:S(2)}, u32[]{:S(2)}) collective-permute-start(bf16[4,2,128,256]{3,2,1,0:T(8,128)(2,1)S(1)} %fusion.9), channel_id=1, source_target_pairs={{0,4},{4,0},{8,12},{12,8},{16,20},{20,16},{24,28},{28,24},{1,5},{5... | collective-permute-start | bytes 1572872 | tf_op jit(solution)/shard_map/ppermute | solution.py:46
  532.0 21.7 %collective-permute-start.65 = (bf16[2,2,128,256]{3,2,1,0:T(8,128)(2,1)S(1)}, bf16[2,2,128,256]{3,2,1,0:T(8,128)(2,1)S(1)}, u32[]{:S(2)}, u32[]{:S(2)}) collective-permute-start(bf16[2,2,128,256]{3,2,1,0:T(8,128)(2,1)S(1)} %copy-done.17), channel_id=1, source_target_pairs={{0,24},{4,28},{8,0},{12,4},{16,8},{20,12},{24,16},{28,20},{1,25},{... | collective-permute-start | bytes 786440 | tf_op jit(solution)/shard_map/ppermute | solution.py:51
  535.4 23.5 %collective-permute-start.63 = (bf16[2,2,128,256]{3,2,1,0:T(8,128)(2,1)S(1)}, bf16[2,2,128,256]{3,2,1,0:T(8,128)(2,1)S(1)}, u32[]{:S(2)}, u32[]{:S(2)}) collective-permute-start(bf16[2,2,128,256]{3,2,1,0:T(8,128)(2,1)S(1)} %copy-done.16), channel_id=1, source_target_pairs={{0,8},{4,12},{8,16},{12,20},{16,24},{20,28},{24,0},{28,4},{1,9},{5... | collective-permute-start | bytes 786440 | tf_op jit(solution)/shard_map/ppermute | solution.py:51
  535.5 31.0 %collective-permute-start.64 = (bf16[2,2,128,256]{3,2,1,0:T(8,128)(2,1)S(1)}, bf16[2,2,128,256]{3,2,1,0:T(8,128)(2,1)S(1)}, u32[]{:S(2)}, u32[]{:S(2)}) collective-permute-start(bf16[2,2,128,256]{3,2,1,0:T(8,128)(2,1)S(1)} %copy-done.15), channel_id=1, source_target_pairs={{0,16},{4,20},{8,24},{12,28},{16,0},{20,4},{24,8},{28,12},{1,17},{... | collective-permute-start | bytes 786440 | tf_op jit(solution)/shard_map/ppermute | solution.py:51
  542.6 26.7 %collective-permute-start.62 = (bf16[2,128,256]{2,1,0:T(8,128)(2,1)S(1)}, bf16[2,128,256]{2,1,0:T(8,128)(2,1)S(1)}, u32[]{:S(2)}, u32[]{:S(2)}) collective-permute-start(bf16[2,128,256]{2,1,0:T(8,128)(2,1)S(1)} %get-tuple-element.223), channel_id=1, source_target_pairs={{0,24},{4,28},{8,0},{12,4},{16,8},{20,12},{24,16},{28,20},{1,25},{... | collective-permute-start | bytes 393224 | tf_op jit(solution)/shard_map/ppermute | solution.py:51
  549.2 21.3 %collective-permute-start.60 = (bf16[2,128,256]{2,1,0:T(8,128)(2,1)S(1)}, bf16[2,128,256]{2,1,0:T(8,128)(2,1)S(1)}, u32[]{:S(2)}, u32[]{:S(2)}) collective-permute-start(bf16[2,128,256]{2,1,0:T(8,128)(2,1)S(1)} %get-tuple-element.225), channel_id=1, source_target_pairs={{0,8},{4,12},{8,16},{12,20},{16,24},{20,28},{24,0},{28,4},{1,9},{5... | collective-permute-start | bytes 393224 | tf_op jit(solution)/shard_map/ppermute | solution.py:51
  553.8 18.4 %collective-permute-start.61 = (bf16[2,128,256]{2,1,0:T(8,128)(2,1)S(1)}, bf16[2,128,256]{2,1,0:T(8,128)(2,1)S(1)}, u32[]{:S(2)}, u32[]{:S(2)}) collective-permute-start(bf16[2,128,256]{2,1,0:T(8,128)(2,1)S(1)} %get-tuple-element.224), channel_id=1, source_target_pairs={{0,16},{4,20},{8,24},{12,28},{16,0},{20,4},{24,8},{28,12},{1,17},{... | collective-permute-start | bytes 393224 | tf_op jit(solution)/shard_map/ppermute | solution.py:51
  558.9 14.4 %collective-permute-start.59 = (bf16[4,2,128,256]{3,2,1,0:T(8,128)(2,1)S(1)}, bf16[4,2,128,256]{3,2,1,0:T(8,128)(2,1)S(1)}, u32[]{:S(2)}, u32[]{:S(2)}) collective-permute-start(bf16[4,2,128,256]{3,2,1,0:T(8,128)(2,1)S(1)} %fusion.8), channel_id=1, source_target_pairs={{0,4},{4,0},{8,12},{12,8},{16,20},{20,16},{24,28},{28,24},{1,5},{5... | collective-permute-start | bytes 1572872 | tf_op jit(solution)/shard_map/ppermute | solution.py:46
  570.5 14.2 %collective-permute-start.55 = (bf16[2,128,256]{2,1,0:T(8,128)(2,1)S(1)}, bf16[2,128,256]{2,1,0:T(8,128)(2,1)S(1)}, u32[]{:S(2)}, u32[]{:S(2)}) collective-permute-start(bf16[2,128,256]{2,1,0:T(8,128)(2,1)S(1)} %get-tuple-element.222), channel_id=1, source_target_pairs={{0,8},{4,12},{8,16},{12,20},{16,24},{20,28},{24,0},{28,4},{1,9},{5... | collective-permute-start | bytes 393224 | tf_op jit(solution)/shard_map/ppermute | solution.py:51
  572.2 15.5 %collective-permute-start.73 = (bf16[8,128,256]{2,1,0:T(8,128)(2,1)S(1)}, bf16[8,128,256]{2,1,0:T(8,128)(2,1)S(1)}, u32[]{:S(2)}, u32[]{:S(2)}) collective-permute-start(bf16[8,128,256]{2,1,0:T(8,128)(2,1)S(1)} %pad_maximum_fusion.4.refs_4_), channel_id=1, source_target_pairs={{0,1},{1,0},{2,3},{3,2},{4,5},{5,4},{6,7},{7,6},{8,9},{9,8},{10,11... | collective-permute-start | bytes 1572872 | tf_op jit(solution)/shard_map/ppermute | solution.py:46
  575.7 12.0 %collective-permute-start.74 = (bf16[8,128,256]{2,1,0:T(8,128)(2,1)S(1)}, bf16[8,128,256]{2,1,0:T(8,128)(2,1)S(1)}, u32[]{:S(2)}, u32[]{:S(2)}) collective-permute-start(bf16[8,128,256]{2,1,0:T(8,128)(2,1)S(1)} %collective-permute-done.72.refs_5_), channel_id=1, source_target_pairs={{0,1},{1,0},{2,3},{3,2},{4,5},{5,4},{6,7},{7,6},{8,9},{9,8},{10,11... | collective-permute-start | bytes 1572872 | tf_op jit(solution)/shard_map/ppermute | solution.py:46
  585.0 13.4 %collective-permute-start.67 = (bf16[2,128,256]{2,1,0:T(8,128)(2,1)S(1)}, bf16[2,128,256]{2,1,0:T(8,128)(2,1)S(1)}, u32[]{:S(2)}, u32[]{:S(2)}) collective-permute-start(bf16[2,128,256]{2,1,0:T(8,128)(2,1)S(1)} %get-tuple-element.218), channel_id=1, source_target_pairs={{0,16},{4,20},{8,24},{12,28},{16,0},{20,4},{24,8},{28,12},{1,17},{... | collective-permute-start | bytes 393224 | tf_op jit(solution)/shard_map/ppermute | solution.py:51
  603.7 15.4 %collective-permute-start.83 = (bf16[8,128,256]{2,1,0:T(8,128)(2,1)S(1)}, bf16[8,128,256]{2,1,0:T(8,128)(2,1)S(1)}, u32[]{:S(2)}, u32[]{:S(2)}) collective-permute-start(bf16[8,128,256]{2,1,0:T(8,128)(2,1)S(1)} %get-tuple-element.210.refs_0_), channel_id=1, source_target_pairs={{0,2},{1,3},{2,0},{3,1},{4,6},{5,7},{6,4},{7,5},{8,10},{9,11},{10,... | collective-permute-start | bytes 1572872 | tf_op jit(solution)/shard_map/ppermute | solution.py:46
  611.1 12.8 %collective-permute-start.84 = (bf16[8,128,256]{2,1,0:T(8,128)(2,1)S(1)}, bf16[8,128,256]{2,1,0:T(8,128)(2,1)S(1)}, u32[]{:S(2)}, u32[]{:S(2)}) collective-permute-start(bf16[8,128,256]{2,1,0:T(8,128)(2,1)S(1)} %get-tuple-element.210.refs_0_), channel_id=1, source_target_pairs={{0,1},{1,0},{2,3},{3,2},{4,5},{5,4},{6,7},{7,6},{8,9},{9,8},{10,11... | collective-permute-start | bytes 1572872 | tf_op jit(solution)/shard_map/ppermute | solution.py:46
  (67 other events, 871.1 us)
Sparse Core Ops, SparseCore 0:
  14.7 149.5 all-gather.4
  180.8 82.2 all-gather.6
